TPU v7x, 128 devices: a whole 4x4x4 slice. The times are simulated.
128 devices in a mesh: azim: 32 (over y, z, core), rad: 4 (over x).
Axes of the slice: x: 4, y: 4, z: 4, core: 2. Of those that a mesh axis runs over, the one named last changes fastest.
Arguments:
- prior_hydrostatic_load: float32 [256, 256, 1024], P('azim', 'rad'), may hold values from -6 to 6
- predicted_outflow_per_step: float32 [256, 256, 1024], P('azim', 'rad'), may hold values from -6 to 6
- parcel_specific_mass_recip: float32 [256, 256, 1024], P('azim', 'rad'), may hold values from 1 to 10
- melt_heat_state: float32 [256, 256, 1024], P('azim', 'rad'), may hold values from -6 to 6
- passage_parcel_label: int32 [32, 4, 4, 1024], P('azim', 'rad'), may hold values from 0 to 523775
- passage_boundary_vertex: int32 [32, 4, 4, 1024], P('azim', 'rad'), may hold values from 0 to 2047
- passage_face_share: float32 [32, 4, 4, 1024], P('azim', 'rad'), may hold values from 0.1 to 1
- passage_live_tally: int32 [32, 4, 4], P('azim', 'rad'), may hold values from 1 to 1024, as said below
- boundary_elevation_prior: float32 [8192], P('rad'), may hold values from -3 to 3
- boundary_weight_restoring: float32 [8192], P('rad'), may hold values from 0.05 to 0.5
- boundary_load_discontinuity: float32 [8192], P('rad'), may hold values from -6 to 6
- tile_approx_solve: float32 [16, 16, 512], P(None, None, 'rad'), may hold values from -0.03 to 0.28, as said below
Outputs:
- pressure: float32 [256, 256, 1024], P('azim', 'rad')
- front_height: float32 [8192], P('rad')
Inputs may be any that keep to these rules, and one draw needn't show every extreme that they name: `passage_live_tally`: in every draw one group j receives 1024 live slots from every radial slab of one azimuthal sector. `tile_approx_solve`: one given matrix for each block of 16 consecutive nodes.
All inputs are finite; a program needn't handle non-finite values.
Results may differ from a plain program's by a relative error of at most 0.0003.
Values sent between devices are 32-bit elements; how exact they have to be, the bound alone decides.
No kernel may reach another device: no remote copies, remote signals or barrier semaphores. Data moves between devices by JAX's collectives and lax.ppermute only.
A program may use at most 128 MiB of HBM per device.

v0:
```python
import math

import jax
import jax.numpy as jnp
from jax import lax
from jax.sharding import PartitionSpec as P

SWEEPS = 4
ITERS = 4


OMEGA = 0.9
AXIAL = 0.25
STEFAN = 1.0
SHRINK = 0.3
COUPLE = 0.2


def with_halo(block, sides, width, periodic):
    for axis, dim in sides:
        count = lax.axis_size(axis)
        forward = [(i, i + 1) for i in range(count - 1)]
        if periodic:
            forward.append((count - 1, 0))
        backward = [(target, source) for source, target in forward]
        low = lax.ppermute(
            lax.slice_in_dim(block, block.shape[dim] - width, None, axis=dim), axis, forward
        )
        high = lax.ppermute(lax.slice_in_dim(block, 0, width, axis=dim), axis, backward)
        block = jnp.concatenate([low, block, high], axis=dim)
    return block


def face_terms(beta_halo, extra, radial_first, total_radial, total_theta):
    center = beta_halo[1:-1, 1:-1]
    theta_up = 0.5 * (center + beta_halo[2:, 1:-1])
    theta_down = 0.5 * (center + beta_halo[:-2, 1:-1])
    radial_rows = radial_first + jnp.arange(center.shape[1], dtype=jnp.int32) - extra
    outer_open = (radial_rows != total_radial - 1)[None, :, None]
    inner_open = (radial_rows != 0)[None, :, None]
    radial_out = jnp.where(outer_open, 0.5 * (center + beta_halo[1:-1, 2:]), 0.0)
    radial_in = jnp.where(inner_open, 0.5 * (center + beta_halo[1:-1, :-2]), 0.0)
    above = jnp.concatenate([center[:, :, 1:], center[:, :, -1:]], axis=2)
    below = jnp.concatenate([center[:, :, :1], center[:, :, :-1]], axis=2)
    axial_up = 0.5 * (center + above)
    bottom_open = (jnp.arange(center.shape[2], dtype=jnp.int32) != 0)[None, None, :]
    axial_down = jnp.where(bottom_open, 0.5 * (center + below), 0.0)
    radius = 0.25 * total_radial + radial_rows.astype(jnp.float32) + 0.5
    angular = ((total_theta / (2.0 * math.pi)) ** 2 / (radius * radius))[None, :, None]
    a_tp = theta_up * angular
    a_tm = theta_down * angular
    a_rp = radial_out * ((radius + 0.5) / radius)[None, :, None]
    a_rm = radial_in * ((radius - 0.5) / radius)[None, :, None]
    a_zp = AXIAL * axial_up
    a_zm = AXIAL * axial_down
    diagonal = a_tp + a_tm + a_rp + a_rm + a_zp + a_zm
    return (a_tp, a_tm, a_rp, a_rm, a_zp, a_zm, diagonal)


def jacobi_sweep(extended, terms, source):
    a_tp, a_tm, a_rp, a_rm, a_zp, a_zm, diagonal = terms
    center = extended[1:-1, 1:-1]
    zeros = jnp.zeros_like(center[:, :, :1])
    upper = jnp.concatenate([center[:, :, 1:], zeros], axis=2)
    lower = jnp.concatenate([zeros, center[:, :, :-1]], axis=2)
    beside = (
        a_tp * extended[2:, 1:-1]
        + a_tm * extended[:-2, 1:-1]
        + a_rp * extended[1:-1, 2:]
        + a_rm * extended[1:-1, :-2]
        + a_zp * upper
        + a_zm * lower
    )
    return (1.0 - OMEGA) * center + OMEGA * (beside - source) / diagonal


def front_halo(height):
    return with_halo(height, (("rad", 0),), 1, False)


def per_device(
    prior_hydrostatic_load,
    predicted_outflow_per_step,
    parcel_specific_mass_recip,
    melt_heat_state,
    passage_parcel_label,
    passage_boundary_vertex,
    passage_face_share,
    passage_live_tally,
    boundary_elevation_prior,
    boundary_weight_restoring,
    boundary_load_discontinuity,
    tile_approx_solve,
):
    theta_cells, radial_cells, axial_cells = prior_hydrostatic_load.shape
    total_theta = theta_cells * lax.axis_size("azim")
    groups = lax.axis_size("rad")
    total_radial = radial_cells * groups
    radial_first = lax.axis_index("rad") * radial_cells
    group_nodes = boundary_elevation_prior.shape[0]
    block_size = tile_approx_solve.shape[0]
    slots = passage_parcel_label.shape[-1]
    cell_codes = passage_parcel_label.reshape(groups, slots)
    node_ids = passage_boundary_vertex.reshape(groups, slots)
    weights = passage_face_share.reshape(groups, slots)
    counts = passage_live_tally.reshape(groups)
    live_slots = jnp.arange(slots, dtype=jnp.int32)[None, :] < counts[:, None]
    column = cell_codes // (axial_cells - 1)
    unrolled_location = column * axial_cells + cell_codes % (axial_cells - 1)
    heat_state_parcels = melt_heat_state.reshape(-1)
    heat_state_discontinuity = (
        heat_state_parcels[unrolled_location + 1] - heat_state_parcels[unrolled_location]
    )
    contribution = jnp.where(live_slots, weights * heat_state_discontinuity, 0.0)
    owner_group = jnp.arange(groups, dtype=jnp.int32)[:, None]
    target = owner_group * group_nodes + node_ids
    partial_value = jax.ops.segment_sum(
        contribution.reshape(-1), target.reshape(-1), num_segments=groups * group_nodes
    ).reshape(groups, group_nodes)
    summed = lax.psum(partial_value, "azim")
    node_flux = lax.psum_scatter(summed, "rad", scatter_dimension=0, tiled=True).reshape(
        group_nodes
    )
    front_force = boundary_load_discontinuity + COUPLE * node_flux
    height = boundary_elevation_prior
    for repeat in range(ITERS):
        padded = front_halo(height)
        applied = (2.0 + boundary_weight_restoring) * height - padded[:-2] - padded[2:]
        residual = front_force - applied
        blocks = residual.reshape(-1, block_size).T
        update = jnp.einsum(
            "ijb,jb->ib", tile_approx_solve, blocks, precision=lax.Precision.HIGHEST
        )
        height = height + update.T.reshape(-1)
    padded = front_halo(height)
    growth = height - boundary_elevation_prior
    front_slope = padded[2:] - padded[:-2]
    row_table = jnp.stack([growth, front_slope, node_flux])
    node_table = lax.all_gather(row_table, "rad", axis=1, tiled=True)
    picked = node_table[:, target]
    area_factor = jnp.sqrt(1.0 + picked[1] * picked[1])
    cell_term = jnp.where(live_slots, weights * (picked[2] - STEFAN * picked[0]) * area_factor, 0.0)
    front_source = jax.ops.segment_sum(
        cell_term.reshape(-1),
        unrolled_location.reshape(-1),
        num_segments=theta_cells * radial_cells * axial_cells,
    ).reshape(prior_hydrostatic_load.shape)
    source = predicted_outflow_per_step + SHRINK * front_source
    pressure = prior_hydrostatic_load
    beta_halo = with_halo(parcel_specific_mass_recip, (("azim", 0), ("rad", 1)), 1, True)
    terms = face_terms(beta_halo, 0, radial_first, total_radial, total_theta)
    for repeat in range(SWEEPS):
        extended = with_halo(pressure, (("azim", 0), ("rad", 1)), 1, True)
        pressure = jacobi_sweep(extended, terms, source)
    return (pressure, height)


def solution(mesh):
    placed = (
        P("azim", "rad", None),
        P("azim", "rad", None),
        P("azim", "rad", None),
        P("azim", "rad", None),
        P("azim", "rad", None, None),
        P("azim", "rad", None, None),
        P("azim", "rad", None, None),
        P("azim", "rad", None),
        P("rad"),
        P("rad"),
        P("rad"),
        P(None, None, "rad"),
    )
    return jax.shard_map(
        per_device,
        mesh=mesh,
        in_specs=placed,
        out_specs=(P("azim", "rad", None), P("rad")),
        check_vma=False,
    )
```

profile of v0, /device:TPU:2, one launch (start us, length us, event | category | flops | bytes accessed | tf_op | source)
XLA Modules:
  0.0 498.4 jit_solution(4012917140817705280)
XLA Ops:
  0.7 1.5 fusion.126
  2.2 3.4 collective-permute-start.8
  5.6 2.9 collective-permute-start.9
  8.5 1.9 fusion.121
  10.4 5.4 %collective-permute-start.1 = (f32[1,64,1024]{2,1,0:T(8,128)}, f32[1,64,1024]{2,1,0:T(8,128)}, u32[]{:S(2)}, u32[]{:S(2)}) collective-permute-start(f32[1,64,1024]{2,1,0:T(8,128)} %get-tuple-element.44), channel_id=1, source_target_pairs={{4,0},{8,4},{12,8},{16,12},{20,16},{24,20},{28,24},{32,28},{36,32}... | collective-permute-start | bytes 786440 | tf_op jit(solution)/shard_map/ppermute | solution.py:29
  15.8 1.9 fusion.119
  22.2 6.9 %fusion.118 = (f32[8,64,1023]{2,1,0:T(8,128)}, f32[8,64,1023]{2,1,0:T(8,128)}, f32[8,64,1023]{2,1,0:T(8,128)}, f32[8,64,1023]{2,1,0:T(8,128)}) fusion(f32[8,64,1024]{2,1,0:T(8,128)S(1)} %copy-done, f32[8,64,1024]{2,1,0:T(8,128)} %param.12), kind=kLoop, calls=%fused_computation.213 | loop fusion | bytes 16760832 | tf_op jit(solution)/shard_map/slice | solution.py:44
  33.4 2.1 copy.44
  35.5 23.0 %gather_fusion.1 = f32[4096]{0:T(1024)S(1)} fusion(f32[524288]{0:T(1024)S(1)} %bitcast.133, s32[4096]{0:T(1024)S(1)} %get-tuple-element.64), kind=kCustom, calls=%fused_computation.1 | custom fusion | bytes 49152 | tf_op jit(solution)/shard_map/gather | solution.py:112
  58.6 23.0 %gather_fusion = f32[4096]{0:T(1024)S(1)} fusion(f32[524288]{0:T(1024)S(1)} %bitcast.134, s32[4096]{0:T(1024)S(1)} %get-tuple-element.65), kind=kCustom, calls=%fused_computation | custom fusion | bytes 49152 | tf_op jit(solution)/shard_map/gather | solution.py:112
  81.7 22.1 %scatter_custom_fusion = f32[8192]{0:T(1024)S(1)} fusion(s32[4096]{0:T(1024)S(1)} %bitcast.155, f32[4096]{0:T(1024)S(1)} %fusion.77, f32[]{:T(128)} %constant.33.clone.1), kind=kCustom, calls=%fused_computation.152 | custom fusion | flops 4096 | bytes 32772 | tf_op jit(solution)/shard_map/scatter-add | solution.py:117
  104.2 30.7 %all-reduce.8 = f32[4,2048]{0,1:T(8,128)S(1)} all-reduce(f32[4,2048]{0,1:T(8,128)S(1)} %copy.22), channel_id=2, replica_groups=mesh['azim'=32,'rad'=4] {'rad'}, use_global_device_ids=true, to_apply=%region_2.3.clone | all-reduce | flops 8192 | bytes 65536
  136.5 134.3 %psum.8 = f32[1,2048]{0,1:T(8,128)S(1)} all-reduce(f32[1,2048]{0,1:T(8,128)S(1)} %constant_dynamic-slice_fusion), channel_id=1, replica_groups=mesh['azim'=32,'rad'=4] {'azim'}, use_global_device_ids=true, to_apply=%region_1.2 | all-reduce | flops 2048 | bytes 16384 | tf_op jit(solution)/shard_map/psum | solution.py:120
  271.4 1.3 fusion.97
  274.5 4.4 collective-permute-start.10
  278.9 1.7 collective-permute-done.10
  280.6 1.9 collective-permute-start.11
  282.6 3.5 collective-permute-done.11
  286.1 1.3 fusion.94
  289.2 3.9 collective-permute-start.12
  293.1 1.7 collective-permute-done.12
  294.9 2.1 collective-permute-start.13
  297.0 3.3 collective-permute-done.13
  300.3 1.3 fusion.91
  303.4 3.9 collective-permute-start.14
  307.3 1.7 collective-permute-done.14
  309.1 1.9 collective-permute-start.15
  311.0 3.5 collective-permute-done.15
  314.5 1.3 fusion.88
  317.7 1.9 collective-permute-start.16
  320.0 3.3 collective-permute-done.16
  323.3 3.9 collective-permute-start.17
  327.2 1.7 collective-permute-done.17
  328.9 1.3 fusion.86
  330.2 1.4 copy.24
  331.6 1.8 pad_maximum_fusion.32
  333.4 29.7 %all_gather.3 = f32[3,8192]{0,1:T(8,128)} all-gather(f32[3,2048]{0,1:T(8,128)S(1)} %pad_maximum_fusion.32), channel_id=1, replica_groups=mesh['azim'=32,'rad'=4] {'rad'}, dimensions={1}, use_global_device_ids=true | all-gather | bytes 122880 | tf_op jit(solution)/shard_map/all_gather | solution.py:139
  363.1 16.4 %gather_fusion.2 = f32[4096,3]{1,0:T(8,128)} fusion(f32[3,8192]{0,1:T(8,128)} %all_gather.3, s32[4096]{0:T(1024)S(1)} %bitcast_clamp_fusion), kind=kCustom, calls=%fused_computation.2 | custom fusion | bytes 114688 | tf_op jit(solution)/shard_map/gather | solution.py:140
  379.5 2.4 copy.25
  381.9 23.3 %scatter_custom_fusion.1 = f32[524288]{0:T(1024)} fusion(s32[4096]{0:T(1024)S(1)} %bitcast.156, f32[4096]{0:T(1024)S(1)} %fusion.76, f32[]{:T(128)} %constant.33.clone.1), kind=kCustom, calls=%fused_computation.111 | custom fusion | flops 4096 | bytes 2097156 | tf_op jit(solution)/shard_map/scatter-add | solution.py:143
  406.7 1.2 collective-permute-start.6
  410.1 1.1 constant_dynamic-update-slice_fusion.3
  411.2 1.5 copy-done.11
  412.8 3.0 collective-permute-start.5
  415.8 1.5 broadcast_multiply_fusion
  417.4 2.8 mul.287
  420.3 14.5 %fusion.46 = (f32[8,64,1024]{2,1,0:T(8,128)S(1)}, f32[8,64,1024]{2,1,0:T(8,128)}, f32[8,64,1024]{2,1,0:T(8,128)}, f32[8,64,1024]{2,1,0:T(8,128)}, f32[8,64,1024]{2,1,0:T(8,128)}, /*index=5*/f32[8,64,1024]{2,1,0:T(8,128)}) fusion(f32[10,64,1024]{2,1,0:T(8,128)} %copy-done.11, f32[10,1,1024]{2,1,0:T(1,128)S(1)} %collective-permute-done.7, ...), kind=kLoop, calls=%fused_computation.76 | loop fusion | flops 26214400 | bytes 35813248 | tf_op jit(solution)/shard_map/add | solution.py:74
  434.9 5.1 %collective-permute-start.18 = (f32[1,64,1024]{2,1,0:T(8,128)S(1)}, f32[1,64,1024]{2,1,0:T(8,128)S(1)}, u32[]{:S(2)}, u32[]{:S(2)}) collective-permute-start(f32[1,64,1024]{2,1,0:T(8,128)S(1)} %get-tuple-element.35), channel_id=1, source_target_pairs={{4,0},{8,4},{12,8},{16,12},{20,16},{24,20},{28,24},{32,28},{36,32}... | collective-permute-start | bytes 786440 | tf_op jit(solution)/shard_map/ppermute | solution.py:29
  440.0 4.0 collective-permute-done.19
  444.1 2.1 collective-permute-start.20
  446.3 2.9 fusion.115
  451.2 5.6 %fusion.33 = f32[8,64,1024]{2,1,0:T(8,128)S(1)} fusion(f32[8,64,1024]{2,1,0:T(8,128)S(1)} %copy-done.7, f32[8,64,1024]{2,1,0:T(8,128)S(1)} %copy-done.6, f32[10,1,1024]{2,1,0:T(1,128)S(1)} %collective-permute-done.21, f32[1,64,1024]{2,1,0:T(8,128)S(1)} %collective-permute-done.18, f32[8,64,1024]{2,1,0:T(8,128)S(1)} %get-tuple-element.2, ...), kind=kLoop, calls=%fused_computation.55 | loop fusion | flops 18350080 | bytes 22098176 | tf_op jit(solution)/shard_map/add | solution.py:74
  456.8 5.1 %collective-permute-start.22 = (f32[1,64,1024]{2,1,0:T(8,128)S(1)}, f32[1,64,1024]{2,1,0:T(8,128)S(1)}, u32[]{:S(2)}, u32[]{:S(2)}) collective-permute-start(f32[1,64,1024]{2,1,0:T(8,128)S(1)} %get-tuple-element.31), channel_id=1, source_target_pairs={{4,0},{8,4},{12,8},{16,12},{20,16},{24,20},{28,24},{32,28},{36,32}... | collective-permute-start | bytes 786440 | tf_op jit(solution)/shard_map/ppermute | solution.py:29
  461.9 4.1 collective-permute-done.23
  466.0 1.9 collective-permute-start.24
  468.1 2.1 fusion.113
  470.2 1.8 collective-permute-done.25
  472.0 5.2 %fusion.20 = f32[8,64,1024]{2,1,0:T(8,128)S(1)} fusion(f32[8,64,1024]{2,1,0:T(8,128)S(1)} %copy-done.8, f32[8,64,1024]{2,1,0:T(8,128)S(1)} %copy-done.6, f32[10,1,1024]{2,1,0:T(1,128)S(1)} %collective-permute-done.25, f32[1,64,1024]{2,1,0:T(8,128)S(1)} %collective-permute-done.22, f32[8,64,1024]{2,1,0:T(8,128)S(1)} %fusion.33, ...), kind=kLoop, calls=%fused_computation.34 | loop fusion | flops 18350080 | bytes 22098176 | tf_op jit(solution)/shard_map/add | solution.py:74
  477.3 5.1 %collective-permute-start.26 = (f32[1,64,1024]{2,1,0:T(8,128)S(1)}, f32[1,64,1024]{2,1,0:T(8,128)S(1)}, u32[]{:S(2)}, u32[]{:S(2)}) collective-permute-start(f32[1,64,1024]{2,1,0:T(8,128)S(1)} %get-tuple-element.27), channel_id=1, source_target_pairs={{4,0},{8,4},{12,8},{16,12},{20,16},{24,20},{28,24},{32,28},{36,32}... | collective-permute-start | bytes 786440 | tf_op jit(solution)/shard_map/ppermute | solution.py:29
  482.4 4.1 collective-permute-done.27
  486.5 2.1 collective-permute-start.28
  489.5 1.1 collective-permute-done.28
  490.6 2.0 collective-permute-done.29
  492.6 5.8 %fusion.7 = f32[8,64,1024]{2,1,0:T(8,128)} fusion(f32[8,64,1024]{2,1,0:T(8,128)S(1)} %copy-done.8, f32[8,64,1024]{2,1,0:T(8,128)S(1)} %copy-done.6, f32[10,1,1024]{2,1,0:T(1,128)S(1)} %collective-permute-done.29, f32[1,64,1024]{2,1,0:T(8,128)S(1)} %collective-permute-done.26, f32[8,64,1024]{2,1,0:T(8,128)S(1)} %fusion.20, ...), kind=kLoop, calls=%fused_computation.13 | loop fusion | flops 18350080 | bytes 22098176 | tf_op jit(solution)/shard_map/add | solution.py:74
  (168 shorter events, 26.0 us)
Async XLA Ops:
  0.6 20.7 %copy-start = (f32[8,64,1024]{2,1,0:T(8,128)S(1)}, f32[8,64,1024]{2,1,0:T(8,128)}, u32[]{:S(2)}) copy-start(f32[8,64,1024]{2,1,0:T(8,128)} %param.14) | copy-start | bytes 6291460
  0.6 19.3 %copy-start.21 = (s32[1,1,4,1024]{3,2,1,0:T(4,128)S(1)}, s32[1,1,4,1024]{3,2,1,0:T(4,128)}, u32[]{:S(2)}) copy-start(s32[1,1,4,1024]{3,2,1,0:T(4,128)} %param.17) | copy-start | bytes 49156
  0.7 20.0 %copy-start.14 = (s32[1,1,4,1024]{3,2,1,0:T(4,128)S(1)}, s32[1,1,4,1024]{3,2,1,0:T(4,128)}, u32[]{:S(2)}) copy-start(s32[1,1,4,1024]{3,2,1,0:T(4,128)} %param.16) | copy-start | bytes 49156
  2.2 269.1 %collective-permute-start.8 = (f32[1]{0:T(128)}, f32[1]{0:T(128)}, u32[]{:S(2)}, u32[]{:S(2)}) collective-permute-start(f32[1]{0:T(128)} %get-tuple-element.58), channel_id=1, source_target_pairs={{0,1},{1,2},{2,3},{4,5},{5,6},{6,7},{8,9},{9,10},{10,11},{12,13},{... | collective-permute-start | bytes 20 | tf_op jit(solution)/shard_map/ppermute | solution.py:26
  5.6 265.8 %collective-permute-start.9 = (f32[1]{0:T(128)}, f32[1]{0:T(128)}, u32[]{:S(2)}, u32[]{:S(2)}) collective-permute-start(f32[1]{0:T(128)} %get-tuple-element.59), channel_id=1, source_target_pairs={{1,0},{2,1},{3,2},{5,4},{6,5},{7,6},{9,8},{10,9},{11,10},{13,12},{... | collective-permute-start | bytes 20 | tf_op jit(solution)/shard_map/ppermute | solution.py:29
  10.4 399.7 %collective-permute-start.1 = (f32[1,64,1024]{2,1,0:T(8,128)}, f32[1,64,1024]{2,1,0:T(8,128)}, u32[]{:S(2)}, u32[]{:S(2)}) collective-permute-start(f32[1,64,1024]{2,1,0:T(8,128)} %get-tuple-element.44), channel_id=1, source_target_pairs={{4,0},{8,4},{12,8},{16,12},{20,16},{24,20},{28,24},{32,28},{36,32}... | collective-permute-start | bytes 786440 | tf_op jit(solution)/shard_map/ppermute | solution.py:29
  15.8 393.1 %collective-permute-start.3 = (f32[1,64,1024]{2,1,0:T(8,128)}, f32[1,64,1024]{2,1,0:T(8,128)}, u32[]{:S(2)}, u32[]{:S(2)}) collective-permute-start(f32[1,64,1024]{2,1,0:T(8,128)} %get-tuple-element.45), channel_id=1, source_target_pairs={{0,4},{4,8},{8,12},{12,16},{16,20},{20,24},{24,28},{28,32},{32,36}... | collective-permute-start | bytes 786440 | tf_op jit(solution)/shard_map/ppermute | solution.py:26
  17.7 387.6 %collective-permute-start.2 = (f32[1,64,1024]{2,1,0:T(8,128)}, f32[1,64,1024]{2,1,0:T(8,128)S(1)}, u32[]{:S(2)}, u32[]{:S(2)}) collective-permute-start(f32[1,64,1024]{2,1,0:T(8,128)} %get-tuple-element.40), channel_id=1, source_target_pairs={{0,4},{4,8},{8,12},{12,16},{16,20},{20,24},{24,28},{28,32},{32,36}... | collective-permute-start | bytes 786440 | tf_op jit(solution)/shard_map/ppermute | solution.py:26
  22.2 6.9 %copy-start.36 = (s32[1,1,4]{2,1,0:T(1,128)S(1)}, s32[1,1,4]{2,1,0:T(1,128)}, u32[]{:S(2)}) copy-start(s32[1,1,4]{2,1,0:T(1,128)} %param.19) | copy-start | bytes 52
  22.2 10.6 %copy-start.15 = (f32[16,16,128]{2,1,0:T(8,128)S(1)}, f32[16,16,128]{2,1,0:T(8,128)}, u32[]{:S(2)}) copy-start(f32[16,16,128]{2,1,0:T(8,128)} %param.23) | copy-start | bytes 393220
  58.5 23.1 %copy-start.19 = (s32[1,1,4,1024]{3,1,2,0:T(1,128)S(1)}, s32[1,1,4,1024]{3,1,2,0:T(1,128)}, u32[]{:S(2)}) copy-start(s32[1,1,4,1024]{3,1,2,0:T(1,128)} %copy.43) | copy-start | bytes 49156
  58.5 23.1 %copy-start.20 = (s32[1,1,4,1024]{3,1,2,0:T(1,128)S(1)}, s32[1,1,4,1024]{3,1,2,0:T(1,128)}, u32[]{:S(2)}) copy-start(s32[1,1,4,1024]{3,1,2,0:T(1,128)} %copy.42) | copy-start | bytes 49156
  58.5 23.1 %copy-start.18 = (f32[1,1,4,1024]{3,2,1,0:T(4,128)S(1)}, f32[1,1,4,1024]{3,2,1,0:T(4,128)}, u32[]{:S(2)}) copy-start(f32[1,1,4,1024]{3,2,1,0:T(4,128)} %param.18) | copy-start | bytes 49156
  58.5 23.1 %copy-start.28 = (pred[1,8,4,128]{3,2,1,0:T(4,128)(4,1)S(1)}, pred[1,8,4,128]{3,2,1,0:T(4,128)(4,1)}, u32[]{:S(2)}) copy-start(pred[1,8,4,128]{3,2,1,0:T(4,128)(4,1)} %fusion.84) | copy-start | bytes 12292
  81.6 53.3 %copy-start.37 = (u32[128]{0:T(128)S(1)}, u32[128]{0:T(128)}, u32[]{:S(2)}) copy-start(u32[128]{0:T(128)} %constant.102) | copy-start | bytes 1540
  136.5 134.7 %copy-start.23 = (pred[1,1,4,1024]{3,1,2,0:T(4,128)(4,1)S(1)}, pred[1,1,4,1024]{3,1,2,0:T(4,128)(4,1)}, u32[]{:S(2)}) copy-start(pred[1,1,4,1024]{3,1,2,0:T(4,128)(4,1)} %copy.37) | copy-start | bytes 12292
  136.5 134.7 %copy-start.24 = (s32[1,1,4,1024]{3,1,2,0:T(1,128)S(1)}, s32[1,1,4,1024]{3,1,2,0:T(1,128)}, u32[]{:S(2)}) copy-start(s32[1,1,4,1024]{3,1,2,0:T(1,128)} %copy.39) | copy-start | bytes 49156
  136.5 134.7 %copy-start.25 = (s32[1,1,4,1024]{3,1,2,0:T(1,128)S(1)}, s32[1,1,4,1024]{3,1,2,0:T(1,128)}, u32[]{:S(2)}) copy-start(s32[1,1,4,1024]{3,1,2,0:T(1,128)} %copy.38) | copy-start | bytes 49156
  136.5 134.9 %copy-start.16 = (f32[2048]{0:T(1024)S(1)}, f32[2048]{0:T(1024)}, u32[]{:S(2)}) copy-start(f32[2048]{0:T(1024)} %param.21) | copy-start | bytes 24580
  136.5 134.9 %copy-start.17 = (f32[2048]{0:T(1024)S(1)}, f32[2048]{0:T(1024)}, u32[]{:S(2)}) copy-start(f32[2048]{0:T(1024)} %param.20) | copy-start | bytes 24580
  136.5 134.9 %copy-start.30 = (f32[2048]{0:T(1024)S(1)}, f32[2048]{0:T(1024)}, u32[]{:S(2)}) copy-start(f32[2048]{0:T(1024)} %param.22) | copy-start | bytes 24580
  271.3 134.2 %collective-permute-start = (f32[1,64,1024]{2,1,0:T(8,128)}, f32[1,64,1024]{2,1,0:T(8,128)}, u32[]{:S(2)}, u32[]{:S(2)}) collective-permute-start(f32[1,64,1024]{2,1,0:T(8,128)} %get-tuple-element.41), channel_id=1, source_target_pairs={{4,0},{8,4},{12,8},{16,12},{20,16},{24,20},{28,24},{32,28},{36,32}... | collective-permute-start | bytes 786440 | tf_op jit(solution)/shard_map/ppermute | solution.py:29
  274.5 6.2 %collective-permute-start.10 = (f32[1]{0:T(128)}, f32[1]{0:T(128)}, u32[]{:S(2)}, u32[]{:S(2)}) collective-permute-start(f32[1]{0:T(128)} %get-tuple-element.56), channel_id=1, source_target_pairs={{0,1},{1,2},{2,3},{4,5},{5,6},{6,7},{8,9},{9,10},{10,11},{12,13},{... | collective-permute-start | bytes 20 | tf_op jit(solution)/shard_map/ppermute | solution.py:26
  280.6 5.5 %collective-permute-start.11 = (f32[1]{0:T(128)}, f32[1]{0:T(128)}, u32[]{:S(2)}, u32[]{:S(2)}) collective-permute-start(f32[1]{0:T(128)} %get-tuple-element.57), channel_id=1, source_target_pairs={{1,0},{2,1},{3,2},{5,4},{6,5},{7,6},{9,8},{10,9},{11,10},{13,12},{... | collective-permute-start | bytes 20 | tf_op jit(solution)/shard_map/ppermute | solution.py:29
  289.2 5.7 %collective-permute-start.12 = (f32[1]{0:T(128)}, f32[1]{0:T(128)}, u32[]{:S(2)}, u32[]{:S(2)}) collective-permute-start(f32[1]{0:T(128)} %get-tuple-element.54), channel_id=1, source_target_pairs={{0,1},{1,2},{2,3},{4,5},{5,6},{6,7},{8,9},{9,10},{10,11},{12,13},{... | collective-permute-start | bytes 20 | tf_op jit(solution)/shard_map/ppermute | solution.py:26
  294.9 5.4 %collective-permute-start.13 = (f32[1]{0:T(128)}, f32[1]{0:T(128)}, u32[]{:S(2)}, u32[]{:S(2)}) collective-permute-start(f32[1]{0:T(128)} %get-tuple-element.55), channel_id=1, source_target_pairs={{1,0},{2,1},{3,2},{5,4},{6,5},{7,6},{9,8},{10,9},{11,10},{13,12},{... | collective-permute-start | bytes 20 | tf_op jit(solution)/shard_map/ppermute | solution.py:29
  303.4 5.7 %collective-permute-start.14 = (f32[1]{0:T(128)}, f32[1]{0:T(128)}, u32[]{:S(2)}, u32[]{:S(2)}) collective-permute-start(f32[1]{0:T(128)} %get-tuple-element.52), channel_id=1, source_target_pairs={{0,1},{1,2},{2,3},{4,5},{5,6},{6,7},{8,9},{9,10},{10,11},{12,13},{... | collective-permute-start | bytes 20 | tf_op jit(solution)/shard_map/ppermute | solution.py:26
  309.1 5.4 %collective-permute-start.15 = (f32[1]{0:T(128)}, f32[1]{0:T(128)}, u32[]{:S(2)}, u32[]{:S(2)}) collective-permute-start(f32[1]{0:T(128)} %get-tuple-element.53), channel_id=1, source_target_pairs={{1,0},{2,1},{3,2},{5,4},{6,5},{7,6},{9,8},{10,9},{11,10},{13,12},{... | collective-permute-start | bytes 20 | tf_op jit(solution)/shard_map/ppermute | solution.py:29
  317.0 16.4 %copy-start.27 = (f32[2048]{0:T(1024)}, f32[2048]{0:T(1024)S(1)}, u32[]{:S(2)}) copy-start(f32[2048]{0:T(1024)S(1)} %get-tuple-element.9) | copy-start | bytes 24580
  317.7 5.6 %collective-permute-start.16 = (f32[1]{0:T(128)}, f32[1]{0:T(128)}, u32[]{:S(2)}, u32[]{:S(2)}) collective-permute-start(f32[1]{0:T(128)} %get-tuple-element.50), channel_id=1, source_target_pairs={{1,0},{2,1},{3,2},{5,4},{6,5},{7,6},{9,8},{10,9},{11,10},{13,12},{... | collective-permute-start | bytes 20 | tf_op jit(solution)/shard_map/ppermute | solution.py:29
  323.3 5.6 %collective-permute-start.17 = (f32[1]{0:T(128)}, f32[1]{0:T(128)}, u32[]{:S(2)}, u32[]{:S(2)}) collective-permute-start(f32[1]{0:T(128)} %get-tuple-element.51), channel_id=1, source_target_pairs={{0,1},{1,2},{2,3},{4,5},{5,6},{6,7},{8,9},{9,10},{10,11},{12,13},{... | collective-permute-start | bytes 20 | tf_op jit(solution)/shard_map/ppermute | solution.py:26
  379.5 25.8 %copy-start.1 = (f32[8,64,1024]{2,1,0:T(8,128)S(1)}, f32[8,64,1024]{2,1,0:T(8,128)}, u32[]{:S(2)}) copy-start(f32[8,64,1024]{2,1,0:T(8,128)} %param.14) | copy-start | bytes 6291460
  405.3 4.5 copy-start.2
  406.7 13.4 %collective-permute-start.6 = (f32[10,1,1024]{2,1,0:T(1,128)S(1)}, f32[10,1,1024]{2,1,0:T(1,128)S(1)}, u32[]{:S(2)}, u32[]{:S(2)}) collective-permute-start(f32[10,1,1024]{2,1,0:T(1,128)S(1)} %get-tuple-element.20), channel_id=1, source_target_pairs={{0,1},{1,2},{2,3},{3,0},{4,5},{5,6},{6,7},{7,4},{8,9},{9,10},{10,1... | collective-permute-start | bytes 122888 | tf_op jit(solution)/shard_map/ppermute | solution.py:26
  407.9 12.2 %collective-permute-start.4 = (f32[10,1,1024]{2,1,0:T(1,128)S(1)}, f32[10,1,1024]{2,1,0:T(1,128)S(1)}, u32[]{:S(2)}, u32[]{:S(2)}) collective-permute-start(f32[10,1,1024]{2,1,0:T(1,128)S(1)} %get-tuple-element.21), channel_id=1, source_target_pairs={{1,0},{2,1},{3,2},{0,3},{5,4},{6,5},{7,6},{4,7},{9,8},{10,9},{11,1... | collective-permute-start | bytes 122888 | tf_op jit(solution)/shard_map/ppermute | solution.py:29
  409.8 6.0 %copy-start.9 = (f32[524288]{0:T(1024)S(1)}, f32[524288]{0:T(1024)}, u32[]{:S(2)}) copy-start(f32[524288]{0:T(1024)} %scatter_custom_fusion.1) | copy-start | bytes 6291460
  412.8 7.4 %collective-permute-start.5 = (f32[10,1,1024]{2,1,0:T(1,128)S(1)}, f32[10,1,1024]{2,1,0:T(1,128)S(1)}, u32[]{:S(2)}, u32[]{:S(2)}) collective-permute-start(f32[10,1,1024]{2,1,0:T(1,128)S(1)} %get-tuple-element.22), channel_id=1, source_target_pairs={{1,0},{2,1},{3,2},{0,3},{5,4},{6,5},{7,6},{4,7},{9,8},{10,9},{11,1... | collective-permute-start | bytes 122888 | tf_op jit(solution)/shard_map/ppermute | solution.py:29
  415.8 4.4 collective-permute-start.7
  417.3 2.9 copy-start.12
  417.3 2.9 copy-start.13
  417.3 2.9 copy-start.29
  417.3 2.9 copy-start.31
  417.3 2.9 copy-start.32
  417.3 2.9 copy-start.33
  417.4 2.9 copy-start.34
  417.4 2.9 copy-start.35
  434.8 9.2 %collective-permute-start.19 = (f32[1,64,1024]{2,1,0:T(8,128)S(1)}, f32[1,64,1024]{2,1,0:T(8,128)S(1)}, u32[]{:S(2)}, u32[]{:S(2)}) collective-permute-start(f32[1,64,1024]{2,1,0:T(8,128)S(1)} %get-tuple-element.34), channel_id=1, source_target_pairs={{0,4},{4,8},{8,12},{12,16},{16,20},{20,24},{24,28},{28,32},{32,36}... | collective-permute-start | bytes 786440 | tf_op jit(solution)/shard_map/ppermute | solution.py:26
  434.9 9.1 %collective-permute-start.18 = (f32[1,64,1024]{2,1,0:T(8,128)S(1)}, f32[1,64,1024]{2,1,0:T(8,128)S(1)}, u32[]{:S(2)}, u32[]{:S(2)}) collective-permute-start(f32[1,64,1024]{2,1,0:T(8,128)S(1)} %get-tuple-element.35), channel_id=1, source_target_pairs={{4,0},{8,4},{12,8},{16,12},{20,16},{24,20},{28,24},{32,28},{36,32}... | collective-permute-start | bytes 786440 | tf_op jit(solution)/shard_map/ppermute | solution.py:29
  444.0 6.2 %copy-start.7 = (f32[8,64,1024]{2,1,0:T(8,128)S(1)}, f32[8,64,1024]{2,1,0:T(8,128)}, u32[]{:S(2)}) copy-start(f32[8,64,1024]{2,1,0:T(8,128)} %get-tuple-element.7) | copy-start | bytes 6291460
  444.1 5.1 %collective-permute-start.20 = (f32[10,1,1024]{2,1,0:T(1,128)S(1)}, f32[10,1,1024]{2,1,0:T(1,128)S(1)}, u32[]{:S(2)}, u32[]{:S(2)}) collective-permute-start(f32[10,1,1024]{2,1,0:T(1,128)S(1)} %get-tuple-element.18), channel_id=1, source_target_pairs={{1,0},{2,1},{3,2},{0,3},{5,4},{6,5},{7,6},{4,7},{9,8},{10,9},{11,1... | collective-permute-start | bytes 122888 | tf_op jit(solution)/shard_map/ppermute | solution.py:29
  446.2 4.1 copy-start.3
  446.2 4.1 copy-start.4
  446.2 4.4 copy-start.5
  446.2 5.0 copy-start.6
  446.2 4.1 collective-permute-start.21
  456.8 9.2 %collective-permute-start.23 = (f32[1,64,1024]{2,1,0:T(8,128)S(1)}, f32[1,64,1024]{2,1,0:T(8,128)S(1)}, u32[]{:S(2)}, u32[]{:S(2)}) collective-permute-start(f32[1,64,1024]{2,1,0:T(8,128)S(1)} %get-tuple-element.30), channel_id=1, source_target_pairs={{0,4},{4,8},{8,12},{12,16},{16,20},{20,24},{24,28},{28,32},{32,36}... | collective-permute-start | bytes 786440 | tf_op jit(solution)/shard_map/ppermute | solution.py:26
  456.8 9.1 %collective-permute-start.22 = (f32[1,64,1024]{2,1,0:T(8,128)S(1)}, f32[1,64,1024]{2,1,0:T(8,128)S(1)}, u32[]{:S(2)}, u32[]{:S(2)}) collective-permute-start(f32[1,64,1024]{2,1,0:T(8,128)S(1)} %get-tuple-element.31), channel_id=1, source_target_pairs={{4,0},{8,4},{12,8},{16,12},{20,16},{24,20},{28,24},{32,28},{36,32}... | collective-permute-start | bytes 786440 | tf_op jit(solution)/shard_map/ppermute | solution.py:29
  466.0 4.2 collective-permute-start.24
  468.0 4.0 copy-start.8
  468.0 4.0 collective-permute-start.25
  477.3 9.2 %collective-permute-start.27 = (f32[1,64,1024]{2,1,0:T(8,128)S(1)}, f32[1,64,1024]{2,1,0:T(8,128)S(1)}, u32[]{:S(2)}, u32[]{:S(2)}) collective-permute-start(f32[1,64,1024]{2,1,0:T(8,128)S(1)} %get-tuple-element.26), channel_id=1, source_target_pairs={{0,4},{4,8},{8,12},{12,16},{16,20},{20,24},{24,28},{28,32},{32,36}... | collective-permute-start | bytes 786440 | tf_op jit(solution)/shard_map/ppermute | solution.py:26
  477.3 9.1 %collective-permute-start.26 = (f32[1,64,1024]{2,1,0:T(8,128)S(1)}, f32[1,64,1024]{2,1,0:T(8,128)S(1)}, u32[]{:S(2)}, u32[]{:S(2)}) collective-permute-start(f32[1,64,1024]{2,1,0:T(8,128)S(1)} %get-tuple-element.27), channel_id=1, source_target_pairs={{4,0},{8,4},{12,8},{16,12},{20,16},{24,20},{28,24},{32,28},{36,32}... | collective-permute-start | bytes 786440 | tf_op jit(solution)/shard_map/ppermute | solution.py:29
  486.5 4.1 collective-permute-start.28
  488.6 4.0 collective-permute-start.29
  (4 other events, 7.9 us)
where the time goes:
time: 500 us; the launch traced here: 498 us
  blocking collectives  195 us (39%)
  local copies, waits for them, and re-layouts  105 us (21%)
  other arithmetic  91.4 us (18%)
  starting transfers between devices  62.6 us (13%)
  waiting for transfers between devices  38.8 us (8%)
    psum x1, blocking collectives, per_device(): summed = lax.psum(partial_value, 'azim')  134 us
    ppermute x15, starting transfers between devices, with_halo(): lax.ppermute(lax.slice_in_dim(block, 0, width, axis=dim), axis, backward)  41.4 us
    add x4, other arithmetic, jacobi_sweep(): return (1.0 - OMEGA) * center + OMEGA * (beside - source) / diagonal  31.1 us
    unnamed x1, blocking collectives  30.7 us
    all_gather x1, blocking collectives, per_device(): node_table = lax.all_gather(row_table, 'rad', axis=1, tiled=True)  29.7 us
    ppermute x15, waiting for transfers between devices, with_halo(): lax.ppermute(lax.slice_in_dim(block, block.shape[dim] - width, None, axis...  23.9 us
    scatter-add x1, other arithmetic, per_device(): jax.ops.segment_sum(cell_term.reshape(-1), unrolled_location.reshape(-1),...  23.3 us
    gather x1, local copies, waits for them, and re-layouts, per_device(): heat_state_parcels[unrolled_location]  23 us
  transfers between devices with their start and end apart: 30, of which 15 were waited for; matrix products, arithmetic and copies ran while one was open for 33% of the time, Pallas kernels for 0%

commit v1 on v0

v1 whole, which is shorter than its diff:
```python
import functools
import math

import jax
import jax.numpy as jnp
from jax import lax
from jax.experimental import pallas as pl
from jax.experimental.pallas import tpu as pltpu
from jax.sharding import PartitionSpec as P

SWEEPS = 4
ITERS = 4
OMEGA = 0.9
AXIAL = 0.25
STEFAN = 1.0
SHRINK = 0.3
COUPLE = 0.2

F32 = jnp.float32
I32 = jnp.int32
BF16 = jnp.bfloat16

T, R, Z = 8, 64, 1024
H = 4
TE = T + 2 * H
RE = R + 16
RT = RE // 8
GROUPS, SLOTS, NB, BS = 4, 1024, 128, 16
UNROLL = 16


def iota(shape, dim):
    return lax.broadcasted_iota(I32, shape, dim)


def pieces(x):
    h = x.astype(BF16)
    rest = x - h.astype(F32)
    m = rest.astype(BF16)
    return h, m, (rest - m.astype(F32)).astype(BF16)


def at8(i):
    return pl.ds(pl.multiple_of(i * 8, 8), 8)


def flux_kernel(cnt, row, heat, lane, vert, share, out, diff, picked):
    def make(q, _):
        x = heat[q // 8, at8(q % 8), :]
        d = pltpu.roll(x, Z - 1, 1) - x
        for zc in range(8):
            diff[at8(q * 8 + zc), :] = d[:, zc * 128:(zc + 1) * 128]
        return 0

    lax.fori_loop(0, T * R // 8, make, 0, unroll=2)
    for j in range(GROUPS):
        def body(b, _):
            base = pl.multiple_of(b * UNROLL, UNROLL)
            for u in range(UNROLL):
                picked[pl.ds(base + u, 1), :] = diff[pl.ds(row[j, base + u], 1), :]
            return 0

        lax.fori_loop(0, (cnt[j] + UNROLL - 1) // UNROLL, body, 0)
        vals = []
        for kb in range(SLOTS // 128):
            cut = slice(kb * 128, (kb + 1) * 128)
            hit = iota((128, 128), 0) == lane[j:j + 1, cut]
            vals.append(jnp.sum(jnp.where(hit, picked[cut, :].T, 0.0), axis=0, keepdims=True))
        live = iota((1, SLOTS), 1) < cnt[j]
        val = jnp.where(live, share[j:j + 1, :] * jnp.concatenate(vals, axis=1), 0.0)
        v = vert[j:j + 1, :]
        inner = iota((BS, SLOTS), 0) == (v & (BS - 1))
        left = jnp.concatenate(
            [jnp.where(inner, p.astype(F32), 0.0).astype(BF16) for p in pieces(val)], axis=0)
        right = jnp.where(iota((NB, SLOTS), 0) == (v >> 4), 1.0, 0.0).astype(BF16)
        o = lax.dot_general(left, right, (((1,), (1,)), ((), ())), preferred_element_type=F32)
        out[j * BS:(j + 1) * BS, :] = o[:BS] + o[BS:2 * BS] + o[2 * BS:]


def front_kernel(kref, cnt, row, flux, f0, f1, f2, f3, lane, vert, share, pred,
                 src, hout, front, gtab, height, terms, *acc):
    k = kref[0]

    def zero(q, _):
        for a in acc:
            a[at8(q), :] = jnp.zeros((8, 128), F32)
        return 0

    lax.fori_loop(0, T * R, zero, 0, unroll=4)
    for s, f in enumerate((f0, f1, f2, f3)):
        front[lax.rem(k + GROUPS - s, GROUPS)] = f[...]

    def neighbours(h):
        last = jnp.concatenate([h[g][BS - 1:BS, :] for g in range(GROUPS)], axis=0)
        first = jnp.concatenate([h[g][0:1, :] for g in range(GROUPS)], axis=0)
        zrow = jnp.zeros((1, 128), F32)
        lr = pltpu.roll(last, 1, 1)
        fr = pltpu.roll(first, 127, 1)
        col = iota((GROUPS, 128), 1)
        lr = jnp.where(col == 0, jnp.concatenate([zrow, lr[:-1]], axis=0), lr)
        fr = jnp.where(col == 127, jnp.concatenate([fr[1:], zrow], axis=0), fr)
        down = [jnp.concatenate([lr[g:g + 1], h[g][:BS - 1]], axis=0) for g in range(GROUPS)]
        up = [jnp.concatenate([h[g][1:], fr[g:g + 1]], axis=0) for g in range(GROUPS)]
        return down, up

    prior = [front[g, 256:272, :] for g in range(GROUPS)]
    h = list(prior)
    for _ in range(ITERS):
        down, up = neighbours(h)
        for g in range(GROUPS):
            applied = (2.0 + front[g, 272:288, :]) * h[g] - down[g] - up[g]
            res = front[g, 288:304, :] + COUPLE * flux[g * BS:(g + 1) * BS, :] - applied
            prod = front[g, 0:256, :].reshape(BS, BS, 128) * res[None]
            h[g] = h[g] + jnp.sum(prod, axis=1)
    down, up = neighbours(h)
    for g in range(GROUPS):
        slope = up[g] - down[g]
        growth = h[g] - prior[g]
        height[g] = h[g]
        gtab[g] = (flux[g * BS:(g + 1) * BS, :] - STEFAN * growth) * jnp.sqrt(1.0 + slope * slope)
    hout[...] = height[k]
    for j in range(GROUPS):
        v = vert[j:j + 1, :]
        right = jnp.where(iota((NB, SLOTS), 0) == (v >> 4), 1.0, 0.0).astype(BF16)
        x = jnp.dot(jnp.concatenate(pieces(gtab[j]), axis=0), right, preferred_element_type=F32)
        x = x[:BS] + x[BS:2 * BS] + x[2 * BS:]
        inner = iota((BS, SLOTS), 0) == (v & (BS - 1))
        term = jnp.sum(jnp.where(inner, x, 0.0), axis=0, keepdims=True) * share[j:j + 1, :]
        term = jnp.where(iota((1, SLOTS), 1) < cnt[j], term, 0.0)
        for kb in range(SLOTS // 128):
            cut = slice(kb * 128, (kb + 1) * 128)
            hit = iota((128, 128), 0) == lane[j:j + 1, cut]
            terms[j, cut, :] = jnp.where(hit, term[:, cut], 0.0).T
    most = jnp.maximum(jnp.maximum(cnt[0], cnt[1]), jnp.maximum(cnt[2], cnt[3]))

    def add(b, _):
        for u in range(UNROLL):
            s = b * UNROLL + u
            for j in range(GROUPS):
                at = pl.ds(row[j, s], 1)
                acc[j][at, :] = acc[j][at, :] + terms[j, pl.ds(s, 1), :]
        return 0

    lax.fori_loop(0, (most + UNROLL - 1) // UNROLL, add, 0)

    def finish(q, _):
        d = q // 8
        for zc in range(8):
            a = at8(q * 8 + zc)
            s = (acc[0][a, :] + acc[1][a, :]) + (acc[2][a, :] + acc[3][a, :])
            cut = slice(zc * 128, (zc + 1) * 128)
            src[d, at8(q % 8), cut] = pred[d, at8(q % 8), cut] + SHRINK * s
        return 0

    lax.fori_loop(0, T * R // 8, finish, 0)


def place(ref, own, lo, hi, rlo, rhi, c0, c1, c2, c3):
    mid, a, b = pl.ds(H, T), pl.ds(0, H), pl.ds(H + T, H)
    rm, r0, r1 = pl.ds(8, R), pl.ds(0, 8), pl.ds(8 + R, 8)
    return [(own, ref.at[mid, rm]), (lo, ref.at[a, rm]), (hi, ref.at[b, rm]),
            (rlo, ref.at[mid, r0]), (rhi, ref.at[mid, r1]),
            (c0, ref.at[a, r0]), (c1, ref.at[a, r1]), (c2, ref.at[b, r0]), (c3, ref.at[b, r1])]


def sweep_kernel(kref, *refs):
    fields, out = refs[:27], refs[27]
    pa, pb, th, rr, zz, ww, ss, sems = refs[28:]
    k = kref[0]
    copies = []
    for n, ref in enumerate((pb, pa, ss)):
        cs = [pltpu.make_async_copy(a, b, sems.at[n, m])
              for m, (a, b) in enumerate(place(ref, *fields[9 * n:9 * n + 9]))]
        for c in cs:
            c.start()
        copies.append(cs)
    for c in copies[0]:
        c.wait()
    sub = iota((8, Z), 0)
    lane = iota((8, Z), 1)
    beta = pb

    def gidx(it):
        return k * R + (it * 8 - 8) + sub

    def radius(it):
        return 0.25 * 256 + gidx(it).astype(F32) + 0.5

    angular = (256 / (2.0 * math.pi)) ** 2

    def theta(t, _):
        for it in range(RT):
            c = slice(it * 8, it * 8 + 8)
            th[t, c, :] = (beta[t, c, :] + beta[t + 1, c, :]) * ((0.5 * angular) / radius(it))
        return 0

    lax.fori_loop(0, TE - 1, theta, 0)

    def coef(t, _):
        prev = jnp.zeros((8, Z), F32)
        nxt = beta[t, 0:8, :]
        for it in range(RT):
            c = slice(it * 8, it * 8 + 8)
            b, ra, gi = nxt, radius(it), gidx(it)
            if it + 1 < RT:
                nxt = beta[t, it * 8 + 8:it * 8 + 16, :]
            bu = jnp.where(sub == 7, pltpu.roll(nxt, 7, 0), pltpu.roll(b, 7, 0))
            face = jnp.where((gi >= 0) & (gi < 255), (0.5 * (b + bu)) * (ra + 0.5), 0.0)
            rolled = pltpu.roll(face, 1, 0)
            below = jnp.where(sub == 0, prev, rolled)
            prev = rolled
            zu = jnp.where(lane == Z - 1, b, 0.5 * (b + pltpu.roll(b, Z - 1, 1))) * (AXIAL * ra)
            zcut = jnp.where(lane == Z - 1, 0.0, zu)
            d = th[t, c, :] + th[t - 1, c, :] + face + below + zu + pltpu.roll(zcut, 1, 1)
            ww[t, c, :] = jnp.where(d > 0.0, OMEGA / jnp.where(d > 0.0, d, 1.0), 0.0)
            rr[t, c, :] = face
            zz[t, c, :] = zcut
        return 0

    lax.fori_loop(1, TE - 1, coef, 0)
    for cs in copies[1:]:
        for c in cs:
            c.wait()

    def scale(t, _):
        for it in range(RT):
            c = slice(it * 8, it * 8 + 8)
            ss[t, c, :] = ss[t, c, :] * radius(it)
        return 0

    lax.fori_loop(1, TE - 1, scale, 0)

    def sweep(old, new, t, first, last, shift, rows):
        prev = jnp.zeros((8, Z), F32)
        if first > 0:
            c = slice(first * 8 - 8, first * 8)
            prev = pltpu.roll(rr[t, c, :] * old[t, c, :], 1, 0)
        nxt = old[t, first * 8:first * 8 + 8, :]
        nroll = pltpu.roll(nxt, 7, 0)
        for it in range(first, last):
            c = slice(it * 8, it * 8 + 8)
            p, proll = nxt, nroll
            if it + 1 < RT:
                nxt = old[t, it * 8 + 8:it * 8 + 16, :]
                nroll = pltpu.roll(nxt, 7, 0)
            r, z = rr[t, c, :], zz[t, c, :]
            acc = th[t, c, :] * old[t + 1, c, :] + th[t - 1, c, :] * old[t - 1, c, :]
            acc = acc + r * jnp.where(sub == 7, nroll, proll)
            rolled = pltpu.roll(r * p, 1, 0)
            acc = acc + jnp.where(sub == 0, prev, rolled)
            prev = rolled
            acc = acc + z * pltpu.roll(p, Z - 1, 1) + pltpu.roll(z * p, 1, 1)
            o = slice(it * 8 - rows, it * 8 - rows + 8)
            new[t - shift, o, :] = (1.0 - OMEGA) * p + ww[t, c, :] * (acc - ss[t, c, :])

    bufs = (pa, pb)
    for n in range(1, SWEEPS + 1):
        old, new = bufs[(n - 1) % 2], bufs[n % 2]
        if n < SWEEPS:
            lax.fori_loop(n, TE - n, lambda t, _: (sweep(old, new, t, 0, RT, 0, 0), 0)[1], 0)
        else:
            lax.fori_loop(n, TE - n, lambda t, _: (sweep(old, out, t, 1, RT - 1, H, 8), 0)[1], 0)


def shift_pairs(dt, dk):
    pairs = []
    for a in range(32):
        for k in range(4):
            if 0 <= k + dk < 4:
                pairs.append((a * 4 + k, ((a + dt) % 32) * 4 + k + dk))
    return pairs


def halos(x):
    both = ("azim", "rad")
    send = lambda y, dt, dk: lax.ppermute(y, both, shift_pairs(dt, dk))
    a, b = x[T - H:], x[:H]
    lo, hi = send(a, 1, 0), send(b, -1, 0)
    rlo, rhi = send(x[:, R - 8:], 0, 1), send(x[:, :8], 0, -1)
    c0, c1 = send(a[:, R - 8:], 1, 1), send(a[:, :8], 1, -1)
    c2, c3 = send(b[:, R - 8:], -1, 1), send(b[:, :8], -1, -1)
    return x, lo, hi, rlo, rhi, c0, c1, c2, c3


def at(y, z, c):
    return (y % 4 * 4 + z % 4) * 2 + c


def azim_pairs(dy, dz, flip):
    return [(at(y, z, c), at(y + dy, z + dz, c ^ flip))
            for y in range(4) for z in range(4) for c in range(2)]


def total(x):
    x = x + lax.ppermute(x, "azim", azim_pairs(0, 0, 1))
    x = x + sum(lax.ppermute(x, "azim", azim_pairs(0, s, 0)) for s in (1, 2, 3))
    x = x + sum(lax.ppermute(x, "azim", azim_pairs(s, 0, 0)) for s in (1, 2, 3))
    return x + sum(lax.ppermute(x, "rad", [(i, (i + s) % 4) for i in range(4)]) for s in (1, 2, 3))


VM = pl.BlockSpec(memory_space=pltpu.VMEM)
SM = pl.BlockSpec(memory_space=pltpu.SMEM)
ANY = pl.BlockSpec(memory_space=pl.ANY)
PARAMS = pltpu.CompilerParams(vmem_limit_bytes=56 << 20)


def per_device(load, outflow, beta, heat, label, vertex, share, tally, prior, weight, jump, solve):
    label = label.reshape(GROUPS, SLOTS)
    vertex = vertex.reshape(GROUPS, SLOTS)
    share = share.reshape(GROUPS, SLOTS)
    tally = tally.reshape(GROUPS)
    hi = label >> 10
    low = hi + (label & 1023)
    carry = (low >= Z - 1).astype(I32)
    column, axial = hi + carry, low - (Z - 1) * carry
    row = ((column >> 3) << 6) + ((axial >> 7) << 3) + (column & 7)
    lane = axial & 127
    kidx = lax.axis_index("rad").astype(I32).reshape(1)

    flip = lambda v: v.reshape(NB, BS).T
    front = jnp.concatenate([solve.reshape(BS * BS, NB), flip(prior), flip(weight), flip(jump)], axis=0)
    fronts = [front] + [
        lax.ppermute(front, "rad", [(i, (i + s) % 4) for i in range(4)]) for s in (1, 2, 3)]
    beta_parts = halos(beta)
    load_parts = halos(load)

    partial = pl.pallas_call(
        flux_kernel, out_shape=jax.ShapeDtypeStruct((GROUPS * BS, NB), F32),
        in_specs=[SM, SM, VM, VM, VM, VM], out_specs=VM,
        scratch_shapes=[pltpu.VMEM((T * R * 8, 128), F32), pltpu.VMEM((SLOTS, 128), F32)],
        compiler_params=PARAMS, name="flux",
        cost_estimate=pl.CostEstimate(flops=20000000, bytes_accessed=2 << 20, transcendentals=0),
    )(tally, row, heat, lane, vertex, share)
    flux = total(partial)
    source, height = pl.pallas_call(
        front_kernel,
        out_shape=(jax.ShapeDtypeStruct((T, R, Z), F32), jax.ShapeDtypeStruct((BS, NB), F32)),
        in_specs=[SM, SM, SM] + [VM] * 9, out_specs=(VM, VM),
        scratch_shapes=[pltpu.VMEM((GROUPS, 304, NB), F32), pltpu.VMEM((GROUPS, BS, NB), F32),
                        pltpu.VMEM((GROUPS, BS, NB), F32), pltpu.VMEM((GROUPS, SLOTS, 128), F32)]
        + [pltpu.VMEM((T * R * 8, 128), F32)] * GROUPS,
        compiler_params=PARAMS, name="front",
        cost_estimate=pl.CostEstimate(flops=20000000, bytes_accessed=4 << 20, transcendentals=0),
    )(kidx, tally, row, flux, *fronts, lane, vertex, share, outflow)
    source_parts = halos(source)
    ext = pltpu.VMEM((TE, RE, Z), F32)
    pressure = pl.pallas_call(
        sweep_kernel, out_shape=jax.ShapeDtypeStruct((T, R, Z), F32),
        in_specs=[SM] + [ANY] * 27, out_specs=VM,
        scratch_shapes=[ext] * 7 + [pltpu.SemaphoreType.DMA((3, 9))],
        compiler_params=PARAMS, name="sweeps",
        cost_estimate=pl.CostEstimate(flops=40000000, bytes_accessed=16 << 20, transcendentals=0),
    )(kidx, *beta_parts, *load_parts, *source_parts)
    return pressure, height.T.reshape(NB * BS)


def solution(mesh):
    cells = P("azim", "rad", None)
    slots = P("azim", "rad", None, None)
    return jax.shard_map(
        per_device,
        mesh=mesh,
        in_specs=(cells, cells, cells, cells, slots, slots, slots, cells,
                  P("rad"), P("rad"), P("rad"), P(None, None, "rad")),
        out_specs=(cells, P("rad")),
        check_vma=False,
    )
```

time: 500 us -> 190 us (0.38)
  blocking collectives: 195 us -> 0 us
  local copies, waits for them, and re-layouts: 105 us -> 12.8 us
  other arithmetic: 91.4 us -> 3.68 us
  Pallas kernels: 0 us -> 39.9 us
  starting transfers between devices: 62.6 us -> 93 us
    psum x1 -> x0, blocking collectives: 134 us -> none  [per_device(): summed = lax.psum(partial_value, 'azim')]
    gather x4 -> x0, local copies, waits for them, and re-layouts: 64.8 us -> none  [the longest x1 23 us: per_device(): heat_state_parcels[unrolled_location]]
    scatter-add x2 -> x0, other arithmetic: 45.5 us -> none  [the longest x1 23.3 us: per_device(): jax.ops.segment_sum(cell_term.reshape(-1), unrolled_location.reshape(-1),...]
    pallas_call x0 -> x3, Pallas kernels: none -> 39.9 us  [the longest x1 21.6 us: per_device(): pl.pallas_call(sweep_kernel, out_shape=jax.ShapeDtypeStruct((T, R, Z), F3...]
    unnamed x1 -> x0, blocking collectives: 30.7 us -> none
    ppermute x30 -> x37, starting transfers between devices: 62.6 us -> 93 us  [the longest x24 81.5 us: halos(): send = lambda y, dt, dk: lax.ppermute(y, both, shift_pairs(dt, dk))]
    all_gather x1 -> x0, blocking collectives: 29.7 us -> none  [per_device(): node_table = lax.all_gather(row_table, 'rad', axis=1, tiled=True)]
    add x9 -> x4, other arithmetic: 31.2 us -> 2.16 us  [the longest x1 1.37 us: total(): x + sum((lax.ppermute(x, 'rad', [(i, (i + s) % 4) for i in range(4)]) for...]
  transfers between devices with their start and end apart: 30 -> 37, of which waited for: 15 -> 12; matrix products, arithmetic and copies ran while one was open for 33% -> 7% of each run, Pallas kernels for 0% -> 5%
where the time goes in v1:
time: 190 us; the launch traced here: 188 us
  starting transfers between devices  93 us (49%)
  Pallas kernels  39.9 us (21%)
  waiting for transfers between devices  37.7 us (20%)
  local copies, waits for them, and re-layouts  12.8 us (7%)
  other arithmetic  3.68 us (2%)
    ppermute x24, starting transfers between devices, halos(): send = lambda y, dt, dk: lax.ppermute(y, both, shift_pairs(dt, dk))  81.5 us
    ppermute x24, waiting for transfers between devices, halos(): send = lambda y, dt, dk: lax.ppermute(y, both, shift_pairs(dt, dk))  30.6 us
    pallas_call x1, Pallas kernels, per_device(): pl.pallas_call(sweep_kernel, out_shape=jax.ShapeDtypeStruct((T, R, Z), F3...  21.6 us
    pallas_call x1, Pallas kernels, per_device(): pl.pallas_call(flux_kernel, out_shape=jax.ShapeDtypeStruct((GROUPS * BS,...  9.42 us
    pallas_call x1, Pallas kernels, per_device(): pl.pallas_call(front_kernel, out_shape=(jax.ShapeDtypeStruct((T, R, Z), F...  8.82 us
    slice x3, local copies, waits for them, and re-layouts, halos(): a, b = (x[T - H:], x[:H])  4.64 us
  transfers between devices with their start and end apart: 37, of which 12 were waited for; matrix products, arithmetic and copies ran while one was open for 7% of the time, Pallas kernels for 5%

profile of v1, /device:TPU:2, one launch (start us, length us, event | category | flops | bytes accessed | tf_op | source)
XLA Modules:
  0.0 188.4 jit_solution(12295204188426064061)
XLA Ops:
  0.6 1.5 broadcast_and_fusion
  2.1 9.4 %flux.1 = f32[64,128]{1,0:T(8,128)} custom-call(s32[4]{0:T(128)} %bitcast.49, s32[4,1024]{1,0:T(4,128)} %get-tuple-element.31.row, f32[8,64,1024]{2,1,0:T(8,128)} %heat.1, s32[4,1024]{1,0:T(4,128)} %get-tuple-element.30.lane, s32[4,1024]{1,0:T(4,128)} %bitcast.41, f32[4,1024]{1,0:T(4,128)} %bitcast.43), custom_call_target="tpu_custom_call" | custom-call | flops 20000000 | bytes 2097152 | tf_op jit(solution)/shard_map/flux/pallas_call | solution.py:327
  11.6 0.8 fusion.4
  12.4 13.4 %collective-permute-start.15 = (f32[4,8,1024]{2,1,0:T(8,128)}, f32[4,8,1024]{2,1,0:T(8,128)S(1)}, u32[]{:S(2)}, u32[]{:S(2)}) collective-permute-start(f32[4,8,1024]{2,1,0:T(8,128)} %get-tuple-element.14), channel_id=1, source_target_pairs={{1,124},{2,125},{3,126},{5,0},{6,1},{7,2},{9,4},{10,5},{11,6},{13,... | collective-permute-start | bytes 393224 | tf_op jit(solution)/shard_map/ppermute | solution.py:276
  25.8 1.9 %collective-permute-start.14 = (f32[4,8,1024]{2,1,0:T(8,128)}, f32[4,8,1024]{2,1,0:T(8,128)S(1)}, u32[]{:S(2)}, u32[]{:S(2)}) collective-permute-start(f32[4,8,1024]{2,1,0:T(8,128)} %get-tuple-element.15), channel_id=1, source_target_pairs={{0,125},{1,126},{2,127},{4,1},{5,2},{6,3},{8,5},{9,6},{10,7},{12,9... | collective-permute-start | bytes 393224 | tf_op jit(solution)/shard_map/ppermute | solution.py:276
  27.7 0.8 add.46
  28.5 0.1 collective-permute-start.18
  28.6 1.9 %collective-permute-start.17 = (f32[64,128]{1,0:T(8,128)S(1)}, f32[64,128]{1,0:T(8,128)S(1)}, u32[]{:S(2)}, u32[]{:S(2)}) collective-permute-start(f32[64,128]{1,0:T(8,128)S(1)} %add.46), channel_id=1, source_target_pairs={{0,8},{4,12},{8,16},{12,20},{16,24},{20,28},{24,0},{28,4},{32,40},... | collective-permute-start | bytes 98312 | tf_op jit(solution)/shard_map/ppermute | solution.py:296
  30.5 1.6 fusion.6
  32.1 0.3 collective-permute-done.19
  32.4 1.6 collective-permute-done.18
  34.0 1.1 collective-permute-done.17
  35.2 0.9 collective-permute-start.21
  36.0 1.2 collective-permute-start.20
  37.3 1.5 fusion.9
  38.8 0.3 collective-permute-done.22
  39.1 1.6 collective-permute-done.21
  40.7 1.1 collective-permute-done.20
  41.8 2.2 %collective-permute-start.25 = (f32[64,128]{1,0:T(8,128)S(1)}, f32[64,128]{1,0:T(8,128)S(1)}, u32[]{:S(2)}, u32[]{:S(2)}) collective-permute-start(f32[64,128]{1,0:T(8,128)S(1)} %add_add_fusion.1), channel_id=1, source_target_pairs={{0,3},{1,0},{2,1},{3,2},{4,7},{5,4},{6,5},{7,6},{8,11},{9,8},{10,9... | collective-permute-start | bytes 98312 | tf_op jit(solution)/shard_map/ppermute | solution.py:298
  44.0 1.6 collective-permute-start.23
  45.5 0.9 fusion.7
  46.4 1.9 %collective-permute-start.13 = (f32[4,8,1024]{2,1,0:T(8,128)S(1)}, f32[4,8,1024]{2,1,0:T(8,128)S(1)}, u32[]{:S(2)}, u32[]{:S(2)}) collective-permute-start(f32[4,8,1024]{2,1,0:T(8,128)S(1)} %get-tuple-element.16), channel_id=1, source_target_pairs={{1,4},{2,5},{3,6},{5,8},{6,9},{7,10},{9,12},{10,13},{11,14},{13,16... | collective-permute-start | bytes 393224 | tf_op jit(solution)/shard_map/ppermute | solution.py:276
  48.3 1.1 collective-permute-done.24
  49.4 2.9 %collective-permute-start.12 = (f32[4,8,1024]{2,1,0:T(8,128)S(1)}, f32[4,8,1024]{2,1,0:T(8,128)S(1)}, u32[]{:S(2)}, u32[]{:S(2)}) collective-permute-start(f32[4,8,1024]{2,1,0:T(8,128)S(1)} %get-tuple-element.17), channel_id=1, source_target_pairs={{0,5},{1,6},{2,7},{4,9},{5,10},{6,11},{8,13},{9,14},{10,15},{12,17... | collective-permute-start | bytes 393224 | tf_op jit(solution)/shard_map/ppermute | solution.py:276
  52.3 6.9 %collective-permute-start.7 = (f32[4,8,1024]{2,1,0:T(8,128)}, f32[4,8,1024]{2,1,0:T(8,128)S(1)}, u32[]{:S(2)}, u32[]{:S(2)}) collective-permute-start(f32[4,8,1024]{2,1,0:T(8,128)} %get-tuple-element.22), channel_id=1, source_target_pairs={{1,124},{2,125},{3,126},{5,0},{6,1},{7,2},{9,4},{10,5},{11,6},{13,... | collective-permute-start | bytes 393224 | tf_op jit(solution)/shard_map/ppermute | solution.py:276
  59.2 0.8 fusion.5
  60.0 0.1 reshape.41
  60.2 0.1 reshape.42
  60.3 0.1 reshape.43
  60.7 2.9 %collective-permute-start.27 = (f32[304,128]{1,0:T(8,128)S(1)}, f32[304,128]{1,0:T(8,128)}, u32[]{:S(2)}, u32[]{:S(2)}) collective-permute-start(f32[304,128]{1,0:T(8,128)S(1)} %pad_maximum_fusion.f0), channel_id=1, source_target_pairs={{0,2},{1,3},{2,0},{3,1},{4,6},{5,7},{6,4},{7,5},{8,10},{9,11},{10,... | collective-permute-start | bytes 466952 | tf_op jit(solution)/shard_map/ppermute | solution.py:323
  63.6 0.5 collective-permute-start.26
  64.1 3.2 %collective-permute-start.6 = (f32[4,8,1024]{2,1,0:T(8,128)}, f32[4,8,1024]{2,1,0:T(8,128)}, u32[]{:S(2)}, u32[]{:S(2)}) collective-permute-start(f32[4,8,1024]{2,1,0:T(8,128)} %get-tuple-element.23), channel_id=1, source_target_pairs={{0,125},{1,126},{2,127},{4,1},{5,2},{6,3},{8,5},{9,6},{10,7},{12,9... | collective-permute-start | bytes 393224 | tf_op jit(solution)/shard_map/ppermute | solution.py:276
  67.4 0.6 copy-done.20
  68.0 1.4 collective-permute-start.9
  69.4 0.8 fusion.8
  70.3 1.2 collective-permute-done.6.refs_7_
  71.5 1.9 %collective-permute-start.5 = (f32[4,8,1024]{2,1,0:T(8,128)}, f32[4,8,1024]{2,1,0:T(8,128)S(1)}, u32[]{:S(2)}, u32[]{:S(2)}) collective-permute-start(f32[4,8,1024]{2,1,0:T(8,128)} %get-tuple-element.24), channel_id=1, source_target_pairs={{1,4},{2,5},{3,6},{5,8},{6,9},{7,10},{9,12},{10,13},{11,14},{13,16... | collective-permute-start | bytes 393224 | tf_op jit(solution)/shard_map/ppermute | solution.py:276
  73.4 2.9 %collective-permute-start.4 = (f32[4,8,1024]{2,1,0:T(8,128)}, f32[4,8,1024]{2,1,0:T(8,128)S(1)}, u32[]{:S(2)}, u32[]{:S(2)}) collective-permute-start(f32[4,8,1024]{2,1,0:T(8,128)} %get-tuple-element.25), channel_id=1, source_target_pairs={{0,5},{1,6},{2,7},{4,9},{5,10},{6,11},{8,13},{9,14},{10,15},{12,17... | collective-permute-start | bytes 393224 | tf_op jit(solution)/shard_map/ppermute | solution.py:276
  76.4 2.7 %collective-permute-start.11 = (f32[8,8,1024]{2,1,0:T(8,128)}, f32[8,8,1024]{2,1,0:T(8,128)S(1)}, u32[]{:S(2)}, u32[]{:S(2)}) collective-permute-start(f32[8,8,1024]{2,1,0:T(8,128)} %get-tuple-element.18), channel_id=1, source_target_pairs={{1,0},{2,1},{3,2},{5,4},{6,5},{7,6},{9,8},{10,9},{11,10},{13,12},{... | collective-permute-start | bytes 786440 | tf_op jit(solution)/shard_map/ppermute | solution.py:276
  79.0 3.2 %collective-permute-start.10 = (f32[8,8,1024]{2,1,0:T(8,128)}, f32[8,8,1024]{2,1,0:T(8,128)S(1)}, u32[]{:S(2)}, u32[]{:S(2)}) collective-permute-start(f32[8,8,1024]{2,1,0:T(8,128)} %get-tuple-element.19), channel_id=1, source_target_pairs={{0,1},{1,2},{2,3},{4,5},{5,6},{6,7},{8,9},{9,10},{10,11},{12,13},{... | collective-permute-start | bytes 786440 | tf_op jit(solution)/shard_map/ppermute | solution.py:276
  82.2 1.4 add_add_fusion.flux
  83.6 8.8 %front.1 = (f32[8,64,1024]{2,1,0:T(8,128)}, f32[16,128]{1,0:T(8,128)}) custom-call(s32[1]{0:T(128)} %bitcast.kref, s32[4]{0:T(128)} %bitcast.50, s32[4,1024]{1,0:T(4,128)} %get-tuple-element.31.row, f32[64,128]{1,0:T(8,128)} %add_add_fusion.flux, f32[304,128]{1,0:T(8,128)} %copy-done.6, f32[304,128]{1,0:T(8,128)} %collective-permute-done.26.f1, ...), custom_call_target="tpu_custom_call" | custom-call | flops 20000000 | bytes 4194304 | tf_op jit(solution)/shard_map/front/pallas_call | solution.py:335
  92.4 6.1 %collective-permute-start.3 = (f32[8,8,1024]{2,1,0:T(8,128)S(1)}, f32[8,8,1024]{2,1,0:T(8,128)S(1)}, u32[]{:S(2)}, u32[]{:S(2)}) collective-permute-start(f32[8,8,1024]{2,1,0:T(8,128)S(1)} %copy-done.14), channel_id=1, source_target_pairs={{1,0},{2,1},{3,2},{5,4},{6,5},{7,6},{9,8},{10,9},{11,10},{13,12},{... | collective-permute-start | bytes 786440 | tf_op jit(solution)/shard_map/ppermute | solution.py:276
  98.6 1.9 %collective-permute-start.2 = (f32[8,8,1024]{2,1,0:T(8,128)S(1)}, f32[8,8,1024]{2,1,0:T(8,128)S(1)}, u32[]{:S(2)}, u32[]{:S(2)}) collective-permute-start(f32[8,8,1024]{2,1,0:T(8,128)S(1)} %copy-done.13), channel_id=1, source_target_pairs={{0,1},{1,2},{2,3},{4,5},{5,6},{6,7},{8,9},{9,10},{10,11},{12,13},{... | collective-permute-start | bytes 786440 | tf_op jit(solution)/shard_map/ppermute | solution.py:276
  100.5 1.1 fusion.1
  101.7 7.3 %collective-permute-start.36 = (f32[4,8,1024]{2,1,0:T(8,128)S(1)}, f32[4,8,1024]{2,1,0:T(8,128)S(1)}, u32[]{:S(2)}, u32[]{:S(2)}) collective-permute-start(f32[4,8,1024]{2,1,0:T(8,128)S(1)} %get-tuple-element.6), channel_id=1, source_target_pairs={{1,124},{2,125},{3,126},{5,0},{6,1},{7,2},{9,4},{10,5},{11,6},{13,... | collective-permute-start | bytes 393224 | tf_op jit(solution)/shard_map/ppermute | solution.py:276
  109.1 3.1 %collective-permute-start.35 = (f32[4,8,1024]{2,1,0:T(8,128)S(1)}, f32[4,8,1024]{2,1,0:T(8,128)S(1)}, u32[]{:S(2)}, u32[]{:S(2)}) collective-permute-start(f32[4,8,1024]{2,1,0:T(8,128)S(1)} %get-tuple-element.7), channel_id=1, source_target_pairs={{0,125},{1,126},{2,127},{4,1},{5,2},{6,3},{8,5},{9,6},{10,7},{12,9... | collective-permute-start | bytes 393224 | tf_op jit(solution)/shard_map/ppermute | solution.py:276
  112.2 1.1 fusion.2
  113.3 2.5 %collective-permute-start.34 = (f32[4,8,1024]{2,1,0:T(8,128)S(1)}, f32[4,8,1024]{2,1,0:T(8,128)S(1)}, u32[]{:S(2)}, u32[]{:S(2)}) collective-permute-start(f32[4,8,1024]{2,1,0:T(8,128)S(1)} %get-tuple-element.8), channel_id=1, source_target_pairs={{1,4},{2,5},{3,6},{5,8},{6,9},{7,10},{9,12},{10,13},{11,14},{13,16... | collective-permute-start | bytes 393224 | tf_op jit(solution)/shard_map/ppermute | solution.py:276
  115.8 1.9 %collective-permute-start.33 = (f32[4,8,1024]{2,1,0:T(8,128)S(1)}, f32[4,8,1024]{2,1,0:T(8,128)S(1)}, u32[]{:S(2)}, u32[]{:S(2)}) collective-permute-start(f32[4,8,1024]{2,1,0:T(8,128)S(1)} %get-tuple-element.9), channel_id=1, source_target_pairs={{0,5},{1,6},{2,7},{4,9},{5,10},{6,11},{8,13},{9,14},{10,15},{12,17... | collective-permute-start | bytes 393224 | tf_op jit(solution)/shard_map/ppermute | solution.py:276
  117.7 2.2 %collective-permute-start.32 = (f32[8,8,1024]{2,1,0:T(8,128)S(1)}, f32[8,8,1024]{2,1,0:T(8,128)S(1)}, u32[]{:S(2)}, u32[]{:S(2)}) collective-permute-start(f32[8,8,1024]{2,1,0:T(8,128)S(1)} %get-tuple-element.10), channel_id=1, source_target_pairs={{1,0},{2,1},{3,2},{5,4},{6,5},{7,6},{9,8},{10,9},{11,10},{13,12},{... | collective-permute-start | bytes 786440 | tf_op jit(solution)/shard_map/ppermute | solution.py:276
  119.9 3.8 %collective-permute-start.31 = (f32[8,8,1024]{2,1,0:T(8,128)S(1)}, f32[8,8,1024]{2,1,0:T(8,128)S(1)}, u32[]{:S(2)}, u32[]{:S(2)}) collective-permute-start(f32[8,8,1024]{2,1,0:T(8,128)S(1)} %get-tuple-element.11), channel_id=1, source_target_pairs={{0,1},{1,2},{2,3},{4,5},{5,6},{6,7},{8,9},{9,10},{10,11},{12,13},{... | collective-permute-start | bytes 786440 | tf_op jit(solution)/shard_map/ppermute | solution.py:276
  123.7 1.6 fusion.3
  125.4 0.6 copy-done.25
  126.0 0.2 collective-permute-done.33.refs_23_
  126.3 5.3 %collective-permute-start.1 = (f32[4,64,1024]{2,1,0:T(8,128)}, f32[4,64,1024]{2,1,0:T(8,128)S(1)}, u32[]{:S(2)}, u32[]{:S(2)}) collective-permute-start(f32[4,64,1024]{2,1,0:T(8,128)} %get-tuple-element.28), channel_id=1, source_target_pairs={{0,124},{1,125},{2,126},{3,127},{4,0},{5,1},{6,2},{7,3},{8,4},{9,5... | collective-permute-start | bytes 3145736 | tf_op jit(solution)/shard_map/ppermute | solution.py:276
  131.6 5.0 %collective-permute-start.30 = (f32[4,64,1024]{2,1,0:T(8,128)}, f32[4,64,1024]{2,1,0:T(8,128)}, u32[]{:S(2)}, u32[]{:S(2)}) collective-permute-start(f32[4,64,1024]{2,1,0:T(8,128)} %get-tuple-element.12), channel_id=1, source_target_pairs={{0,124},{1,125},{2,126},{3,127},{4,0},{5,1},{6,2},{7,3},{8,4},{9,5... | collective-permute-start | bytes 3145736 | tf_op jit(solution)/shard_map/ppermute | solution.py:276
  136.7 0.1 collective-permute-start.29
  136.8 0.1 copy.17
  136.9 0.7 reshape.44
  137.6 6.6 %collective-permute-done.8.refs_10_ = f32[4,64,1024]{2,1,0:T(8,128)S(1)} collective-permute-done((f32[4,64,1024]{2,1,0:T(8,128)}, f32[4,64,1024]{2,1,0:T(8,128)S(1)}, u32[]{:S(2)}, u32[]{:S(2)}) %collective-permute-start.8) | collective-permute-done | bytes 1048608 | tf_op jit(solution)/shard_map/ppermute | solution.py:276
  144.2 11.3 %collective-permute-done.refs_1_ = f32[4,64,1024]{2,1,0:T(8,128)} collective-permute-done((f32[4,64,1024]{2,1,0:T(8,128)}, f32[4,64,1024]{2,1,0:T(8,128)}, u32[]{:S(2)}, u32[]{:S(2)}) %collective-permute-start) | collective-permute-done | bytes 1048608 | tf_op jit(solution)/shard_map/ppermute | solution.py:276
  155.5 11.2 %collective-permute-done.29.refs_19_ = f32[4,64,1024]{2,1,0:T(8,128)} collective-permute-done((f32[4,64,1024]{2,1,0:T(8,128)}, f32[4,64,1024]{2,1,0:T(8,128)}, u32[]{:S(2)}, u32[]{:S(2)}) %collective-permute-start.29) | collective-permute-done | bytes 1048608 | tf_op jit(solution)/shard_map/ppermute | solution.py:276
  166.8 21.6 %sweeps.1 = f32[8,64,1024]{2,1,0:T(8,128)} custom-call(s32[1]{0:T(128)} %bitcast.kref, f32[8,64,1024]{2,1,0:T(8,128)} %refs_0_.1, f32[4,64,1024]{2,1,0:T(8,128)} %collective-permute-done.refs_1_, f32[4,64,1024]{2,1,0:T(8,128)} %copy-done.5, f32[8,8,1024]{2,1,0:T(8,128)} %copy-done.10, f32[8,8,1024]{2,1,0:T(8,128)} %copy-done.9, f32[4,8,1024]{2,1,0:T(8,128)} %copy-done.22, ...), custom_call_target="tpu_custom_call" | custom-call | flops 40000000 | bytes 16777216 | tf_op jit(solution)/shard_map/sweeps/pallas_call | solution.py:347
  (102 shorter events, 0.6 us)
Async XLA Ops:
  0.6 11.0 %copy-start.1 = (f32[8,64,1024]{2,1,0:T(8,128)S(1)}, f32[8,64,1024]{2,1,0:T(8,128)}, u32[]{:S(2)}) copy-start(f32[8,64,1024]{2,1,0:T(8,128)} %refs_9_.1) | copy-start | bytes 6291460
  11.6 16.1 %collective-permute-start.16 = (f32[64,128]{1,0:T(8,128)}, f32[64,128]{1,0:T(8,128)S(1)}, u32[]{:S(2)}, u32[]{:S(2)}) collective-permute-start(f32[64,128]{1,0:T(8,128)} %flux.1), channel_id=1, source_target_pairs={{0,4},{4,0},{8,12},{12,8},{16,20},{20,16},{24,28},{28,24},{32,36},... | collective-permute-start | bytes 98312 | tf_op jit(solution)/shard_map/ppermute | solution.py:295
  12.4 48.2 %collective-permute-start.15 = (f32[4,8,1024]{2,1,0:T(8,128)}, f32[4,8,1024]{2,1,0:T(8,128)S(1)}, u32[]{:S(2)}, u32[]{:S(2)}) collective-permute-start(f32[4,8,1024]{2,1,0:T(8,128)} %get-tuple-element.14), channel_id=1, source_target_pairs={{1,124},{2,125},{3,126},{5,0},{6,1},{7,2},{9,4},{10,5},{11,6},{13,... | collective-permute-start | bytes 393224 | tf_op jit(solution)/shard_map/ppermute | solution.py:276
  25.8 34.9 %collective-permute-start.14 = (f32[4,8,1024]{2,1,0:T(8,128)}, f32[4,8,1024]{2,1,0:T(8,128)S(1)}, u32[]{:S(2)}, u32[]{:S(2)}) collective-permute-start(f32[4,8,1024]{2,1,0:T(8,128)} %get-tuple-element.15), channel_id=1, source_target_pairs={{0,125},{1,126},{2,127},{4,1},{5,2},{6,3},{8,5},{9,6},{10,7},{12,9... | collective-permute-start | bytes 393224 | tf_op jit(solution)/shard_map/ppermute | solution.py:276
  28.5 8.8 %copy-start = (f32[8,64,1024]{2,1,0:T(8,128)S(1)}, f32[8,64,1024]{2,1,0:T(8,128)}, u32[]{:S(2)}) copy-start(f32[8,64,1024]{2,1,0:T(8,128)} %refs_0_.1) | copy-start | bytes 6291460
  28.5 3.9 %collective-permute-start.19 = (f32[64,128]{1,0:T(8,128)S(1)}, f32[64,128]{1,0:T(8,128)S(1)}, u32[]{:S(2)}, u32[]{:S(2)}) collective-permute-start(f32[64,128]{1,0:T(8,128)S(1)} %add.46), channel_id=1, source_target_pairs={{0,24},{4,28},{8,0},{12,4},{16,8},{20,12},{24,16},{28,20},{32,56},... | collective-permute-start | bytes 98312 | tf_op jit(solution)/shard_map/ppermute | solution.py:296
  28.5 5.5 %collective-permute-start.18 = (f32[64,128]{1,0:T(8,128)S(1)}, f32[64,128]{1,0:T(8,128)S(1)}, u32[]{:S(2)}, u32[]{:S(2)}) collective-permute-start(f32[64,128]{1,0:T(8,128)S(1)} %add.46), channel_id=1, source_target_pairs={{0,16},{4,20},{8,24},{12,28},{16,0},{20,4},{24,8},{28,12},{32,48},... | collective-permute-start | bytes 98312 | tf_op jit(solution)/shard_map/ppermute | solution.py:296
  28.6 6.5 %collective-permute-start.17 = (f32[64,128]{1,0:T(8,128)S(1)}, f32[64,128]{1,0:T(8,128)S(1)}, u32[]{:S(2)}, u32[]{:S(2)}) collective-permute-start(f32[64,128]{1,0:T(8,128)S(1)} %add.46), channel_id=1, source_target_pairs={{0,8},{4,12},{8,16},{12,20},{16,24},{20,28},{24,0},{28,4},{32,40},... | collective-permute-start | bytes 98312 | tf_op jit(solution)/shard_map/ppermute | solution.py:296
  35.1 4.0 %collective-permute-start.22 = (f32[64,128]{1,0:T(8,128)S(1)}, f32[64,128]{1,0:T(8,128)S(1)}, u32[]{:S(2)}, u32[]{:S(2)}) collective-permute-start(f32[64,128]{1,0:T(8,128)S(1)} %add_add_fusion.2), channel_id=1, source_target_pairs={{0,96},{4,100},{8,104},{12,108},{16,112},{20,116},{24,120},{28,124... | collective-permute-start | bytes 98312 | tf_op jit(solution)/shard_map/ppermute | solution.py:297
  35.2 5.5 %collective-permute-start.21 = (f32[64,128]{1,0:T(8,128)S(1)}, f32[64,128]{1,0:T(8,128)S(1)}, u32[]{:S(2)}, u32[]{:S(2)}) collective-permute-start(f32[64,128]{1,0:T(8,128)S(1)} %add_add_fusion.2), channel_id=1, source_target_pairs={{0,64},{4,68},{8,72},{12,76},{16,80},{20,84},{24,88},{28,92},{32,9... | collective-permute-start | bytes 98312 | tf_op jit(solution)/shard_map/ppermute | solution.py:297
  36.0 5.7 %collective-permute-start.20 = (f32[64,128]{1,0:T(8,128)S(1)}, f32[64,128]{1,0:T(8,128)S(1)}, u32[]{:S(2)}, u32[]{:S(2)}) collective-permute-start(f32[64,128]{1,0:T(8,128)S(1)} %add_add_fusion.2), channel_id=1, source_target_pairs={{0,32},{4,36},{8,40},{12,44},{16,48},{20,52},{24,56},{28,60},{32,6... | collective-permute-start | bytes 98312 | tf_op jit(solution)/shard_map/ppermute | solution.py:297
  38.8 21.3 %copy-start.29 = (f32[2048]{0:T(1024)S(1)}, f32[2048]{0:T(1024)}, u32[]{:S(2)}) copy-start(f32[2048]{0:T(1024)} %param.20) | copy-start | bytes 24580
  38.8 21.4 %copy-start.30 = (f32[2048]{0:T(1024)S(1)}, f32[2048]{0:T(1024)}, u32[]{:S(2)}) copy-start(f32[2048]{0:T(1024)} %param.21) | copy-start | bytes 24580
  38.8 21.6 %copy-start.31 = (f32[2048]{0:T(1024)S(1)}, f32[2048]{0:T(1024)}, u32[]{:S(2)}) copy-start(f32[2048]{0:T(1024)} %param.22) | copy-start | bytes 24580
  38.8 21.7 %copy-start.27 = (f32[16,16,128]{2,1,0:T(8,128)S(1)}, f32[16,16,128]{2,1,0:T(8,128)}, u32[]{:S(2)}) copy-start(f32[16,16,128]{2,1,0:T(8,128)} %param.23) | copy-start | bytes 393220
  41.8 4.6 %collective-permute-start.25 = (f32[64,128]{1,0:T(8,128)S(1)}, f32[64,128]{1,0:T(8,128)S(1)}, u32[]{:S(2)}, u32[]{:S(2)}) collective-permute-start(f32[64,128]{1,0:T(8,128)S(1)} %add_add_fusion.1), channel_id=1, source_target_pairs={{0,3},{1,0},{2,1},{3,2},{4,7},{5,4},{6,5},{7,6},{8,11},{9,8},{10,9... | collective-permute-start | bytes 98312 | tf_op jit(solution)/shard_map/ppermute | solution.py:298
  44.0 5.4 %collective-permute-start.24 = (f32[64,128]{1,0:T(8,128)S(1)}, f32[64,128]{1,0:T(8,128)S(1)}, u32[]{:S(2)}, u32[]{:S(2)}) collective-permute-start(f32[64,128]{1,0:T(8,128)S(1)} %add_add_fusion.1), channel_id=1, source_target_pairs={{0,2},{1,3},{2,0},{3,1},{4,6},{5,7},{6,4},{7,5},{8,10},{9,11},{10,... | collective-permute-start | bytes 98312 | tf_op jit(solution)/shard_map/ppermute | solution.py:298
  44.0 8.3 %collective-permute-start.23 = (f32[64,128]{1,0:T(8,128)S(1)}, f32[64,128]{1,0:T(8,128)S(1)}, u32[]{:S(2)}, u32[]{:S(2)}) collective-permute-start(f32[64,128]{1,0:T(8,128)S(1)} %add_add_fusion.1), channel_id=1, source_target_pairs={{0,1},{1,2},{2,3},{3,0},{4,5},{5,6},{6,7},{7,4},{8,9},{9,10},{10,1... | collective-permute-start | bytes 98312 | tf_op jit(solution)/shard_map/ppermute | solution.py:298
  46.4 17.2 %collective-permute-start.13 = (f32[4,8,1024]{2,1,0:T(8,128)S(1)}, f32[4,8,1024]{2,1,0:T(8,128)S(1)}, u32[]{:S(2)}, u32[]{:S(2)}) collective-permute-start(f32[4,8,1024]{2,1,0:T(8,128)S(1)} %get-tuple-element.16), channel_id=1, source_target_pairs={{1,4},{2,5},{3,6},{5,8},{6,9},{7,10},{9,12},{10,13},{11,14},{13,16... | collective-permute-start | bytes 393224 | tf_op jit(solution)/shard_map/ppermute | solution.py:276
  49.4 14.7 %collective-permute-start.12 = (f32[4,8,1024]{2,1,0:T(8,128)S(1)}, f32[4,8,1024]{2,1,0:T(8,128)S(1)}, u32[]{:S(2)}, u32[]{:S(2)}) collective-permute-start(f32[4,8,1024]{2,1,0:T(8,128)S(1)} %get-tuple-element.17), channel_id=1, source_target_pairs={{0,5},{1,6},{2,7},{4,9},{5,10},{6,11},{8,13},{9,14},{10,15},{12,17... | collective-permute-start | bytes 393224 | tf_op jit(solution)/shard_map/ppermute | solution.py:276
  52.3 15.1 %copy-start.28 = (f32[64,128]{1,0:T(8,128)}, f32[64,128]{1,0:T(8,128)S(1)}, u32[]{:S(2)}) copy-start(f32[64,128]{1,0:T(8,128)S(1)} %collective-permute-done.23) | copy-start | bytes 98308
  52.3 15.0 %collective-permute-start.7 = (f32[4,8,1024]{2,1,0:T(8,128)}, f32[4,8,1024]{2,1,0:T(8,128)S(1)}, u32[]{:S(2)}, u32[]{:S(2)}) collective-permute-start(f32[4,8,1024]{2,1,0:T(8,128)} %get-tuple-element.22), channel_id=1, source_target_pairs={{1,124},{2,125},{3,126},{5,0},{6,1},{7,2},{9,4},{10,5},{11,6},{13,... | collective-permute-start | bytes 393224 | tf_op jit(solution)/shard_map/ppermute | solution.py:276
  60.5 23.1 %copy-start.6 = (f32[304,128]{1,0:T(8,128)}, f32[304,128]{1,0:T(8,128)S(1)}, u32[]{:S(2)}) copy-start(f32[304,128]{1,0:T(8,128)S(1)} %pad_maximum_fusion.f0) | copy-start | bytes 466948
  60.6 6.8 %copy-start.16 = (f32[4,8,1024]{2,1,0:T(8,128)}, f32[4,8,1024]{2,1,0:T(8,128)S(1)}, u32[]{:S(2)}) copy-start(f32[4,8,1024]{2,1,0:T(8,128)S(1)} %collective-permute-done.15.refs_17_) | copy-start | bytes 393220
  60.6 12.8 %collective-permute-start.28 = (f32[304,128]{1,0:T(8,128)S(1)}, f32[304,128]{1,0:T(8,128)S(1)}, u32[]{:S(2)}, u32[]{:S(2)}) collective-permute-start(f32[304,128]{1,0:T(8,128)S(1)} %pad_maximum_fusion.f0), channel_id=1, source_target_pairs={{0,3},{1,0},{2,1},{3,2},{4,7},{5,4},{6,5},{7,6},{8,11},{9,8},{10,9... | collective-permute-start | bytes 466952 | tf_op jit(solution)/shard_map/ppermute | solution.py:323
  60.7 6.7 %copy-start.17 = (f32[4,8,1024]{2,1,0:T(8,128)}, f32[4,8,1024]{2,1,0:T(8,128)S(1)}, u32[]{:S(2)}) copy-start(f32[4,8,1024]{2,1,0:T(8,128)S(1)} %collective-permute-done.14.refs_16_) | copy-start | bytes 393220
  60.7 15.7 %collective-permute-start.27 = (f32[304,128]{1,0:T(8,128)S(1)}, f32[304,128]{1,0:T(8,128)}, u32[]{:S(2)}, u32[]{:S(2)}) collective-permute-start(f32[304,128]{1,0:T(8,128)S(1)} %pad_maximum_fusion.f0), channel_id=1, source_target_pairs={{0,2},{1,3},{2,0},{3,1},{4,6},{5,7},{6,4},{7,5},{8,10},{9,11},{10,... | collective-permute-start | bytes 466952 | tf_op jit(solution)/shard_map/ppermute | solution.py:323
  63.6 15.5 %collective-permute-start.26 = (f32[304,128]{1,0:T(8,128)S(1)}, f32[304,128]{1,0:T(8,128)}, u32[]{:S(2)}, u32[]{:S(2)}) collective-permute-start(f32[304,128]{1,0:T(8,128)S(1)} %pad_maximum_fusion.f0), channel_id=1, source_target_pairs={{0,1},{1,2},{2,3},{3,0},{4,5},{5,6},{6,7},{7,4},{8,9},{9,10},{10,1... | collective-permute-start | bytes 466952 | tf_op jit(solution)/shard_map/ppermute | solution.py:323
  64.1 7.4 %collective-permute-start.6 = (f32[4,8,1024]{2,1,0:T(8,128)}, f32[4,8,1024]{2,1,0:T(8,128)}, u32[]{:S(2)}, u32[]{:S(2)}) collective-permute-start(f32[4,8,1024]{2,1,0:T(8,128)} %get-tuple-element.23), channel_id=1, source_target_pairs={{0,125},{1,126},{2,127},{4,1},{5,2},{6,3},{8,5},{9,6},{10,7},{12,9... | collective-permute-start | bytes 393224 | tf_op jit(solution)/shard_map/ppermute | solution.py:276
  68.0 68.6 %collective-permute-start.9 = (f32[4,64,1024]{2,1,0:T(8,128)}, f32[4,64,1024]{2,1,0:T(8,128)S(1)}, u32[]{:S(2)}, u32[]{:S(2)}) collective-permute-start(f32[4,64,1024]{2,1,0:T(8,128)} %get-tuple-element.20), channel_id=1, source_target_pairs={{0,124},{1,125},{2,126},{3,127},{4,0},{5,1},{6,2},{7,3},{8,4},{9,5... | collective-permute-start | bytes 3145736 | tf_op jit(solution)/shard_map/ppermute | solution.py:276
  70.3 22.2 %copy-start.14 = (f32[8,8,1024]{2,1,0:T(8,128)S(1)}, f32[8,8,1024]{2,1,0:T(8,128)}, u32[]{:S(2)}) copy-start(f32[8,8,1024]{2,1,0:T(8,128)} %get-tuple-element.26) | copy-start | bytes 786436
  70.3 28.3 %copy-start.13 = (f32[8,8,1024]{2,1,0:T(8,128)S(1)}, f32[8,8,1024]{2,1,0:T(8,128)}, u32[]{:S(2)}) copy-start(f32[8,8,1024]{2,1,0:T(8,128)} %get-tuple-element.27) | copy-start | bytes 786436
  71.5 21.0 %collective-permute-start.5 = (f32[4,8,1024]{2,1,0:T(8,128)}, f32[4,8,1024]{2,1,0:T(8,128)S(1)}, u32[]{:S(2)}, u32[]{:S(2)}) collective-permute-start(f32[4,8,1024]{2,1,0:T(8,128)} %get-tuple-element.24), channel_id=1, source_target_pairs={{1,4},{2,5},{3,6},{5,8},{6,9},{7,10},{9,12},{10,13},{11,14},{13,16... | collective-permute-start | bytes 393224 | tf_op jit(solution)/shard_map/ppermute | solution.py:276
  73.4 10.2 %copy-start.15 = (f32[304,128]{1,0:T(8,128)}, f32[304,128]{1,0:T(8,128)S(1)}, u32[]{:S(2)}) copy-start(f32[304,128]{1,0:T(8,128)S(1)} %collective-permute-done.28.f3) | copy-start | bytes 466948
  73.4 25.2 %collective-permute-start.4 = (f32[4,8,1024]{2,1,0:T(8,128)}, f32[4,8,1024]{2,1,0:T(8,128)S(1)}, u32[]{:S(2)}, u32[]{:S(2)}) collective-permute-start(f32[4,8,1024]{2,1,0:T(8,128)} %get-tuple-element.25), channel_id=1, source_target_pairs={{0,5},{1,6},{2,7},{4,9},{5,10},{6,11},{8,13},{9,14},{10,15},{12,17... | collective-permute-start | bytes 393224 | tf_op jit(solution)/shard_map/ppermute | solution.py:276
  76.4 25.3 %collective-permute-start.11 = (f32[8,8,1024]{2,1,0:T(8,128)}, f32[8,8,1024]{2,1,0:T(8,128)S(1)}, u32[]{:S(2)}, u32[]{:S(2)}) collective-permute-start(f32[8,8,1024]{2,1,0:T(8,128)} %get-tuple-element.18), channel_id=1, source_target_pairs={{1,0},{2,1},{3,2},{5,4},{6,5},{7,6},{9,8},{10,9},{11,10},{13,12},{... | collective-permute-start | bytes 786440 | tf_op jit(solution)/shard_map/ppermute | solution.py:276
  79.0 30.0 %collective-permute-start.10 = (f32[8,8,1024]{2,1,0:T(8,128)}, f32[8,8,1024]{2,1,0:T(8,128)S(1)}, u32[]{:S(2)}, u32[]{:S(2)}) collective-permute-start(f32[8,8,1024]{2,1,0:T(8,128)} %get-tuple-element.19), channel_id=1, source_target_pairs={{0,1},{1,2},{2,3},{4,5},{5,6},{6,7},{8,9},{9,10},{10,11},{12,13},{... | collective-permute-start | bytes 786440 | tf_op jit(solution)/shard_map/ppermute | solution.py:276
  92.4 31.3 %copy-start.2 = (f32[8,64,1024]{2,1,0:T(8,128)S(1)}, f32[8,64,1024]{2,1,0:T(8,128)}, u32[]{:S(2)}) copy-start(f32[8,64,1024]{2,1,0:T(8,128)} %get-tuple-element.4.refs_18_) | copy-start | bytes 6291460
  92.4 32.9 %copy-start.21 = (f32[4,8,1024]{2,1,0:T(8,128)}, f32[4,8,1024]{2,1,0:T(8,128)S(1)}, u32[]{:S(2)}) copy-start(f32[4,8,1024]{2,1,0:T(8,128)S(1)} %collective-permute-done.5.refs_6_) | copy-start | bytes 393220
  92.4 20.8 %collective-permute-start.3 = (f32[8,8,1024]{2,1,0:T(8,128)S(1)}, f32[8,8,1024]{2,1,0:T(8,128)S(1)}, u32[]{:S(2)}, u32[]{:S(2)}) collective-permute-start(f32[8,8,1024]{2,1,0:T(8,128)S(1)} %copy-done.14), channel_id=1, source_target_pairs={{1,0},{2,1},{3,2},{5,4},{6,5},{7,6},{9,8},{10,9},{11,10},{13,12},{... | collective-permute-start | bytes 786440 | tf_op jit(solution)/shard_map/ppermute | solution.py:276
  98.6 26.8 %copy-start.22 = (f32[4,8,1024]{2,1,0:T(8,128)}, f32[4,8,1024]{2,1,0:T(8,128)S(1)}, u32[]{:S(2)}) copy-start(f32[4,8,1024]{2,1,0:T(8,128)S(1)} %collective-permute-done.4.refs_5_) | copy-start | bytes 393220
  98.6 17.1 %collective-permute-start.2 = (f32[8,8,1024]{2,1,0:T(8,128)S(1)}, f32[8,8,1024]{2,1,0:T(8,128)S(1)}, u32[]{:S(2)}, u32[]{:S(2)}) collective-permute-start(f32[8,8,1024]{2,1,0:T(8,128)S(1)} %copy-done.13), channel_id=1, source_target_pairs={{0,1},{1,2},{2,3},{4,5},{5,6},{6,7},{8,9},{9,10},{10,11},{12,13},{... | collective-permute-start | bytes 786440 | tf_op jit(solution)/shard_map/ppermute | solution.py:276
  101.7 23.7 %copy-start.7 = (f32[8,8,1024]{2,1,0:T(8,128)}, f32[8,8,1024]{2,1,0:T(8,128)S(1)}, u32[]{:S(2)}) copy-start(f32[8,8,1024]{2,1,0:T(8,128)S(1)} %collective-permute-done.11.refs_13_) | copy-start | bytes 786436
  101.7 16.0 %collective-permute-start.36 = (f32[4,8,1024]{2,1,0:T(8,128)S(1)}, f32[4,8,1024]{2,1,0:T(8,128)S(1)}, u32[]{:S(2)}, u32[]{:S(2)}) collective-permute-start(f32[4,8,1024]{2,1,0:T(8,128)S(1)} %get-tuple-element.6), channel_id=1, source_target_pairs={{1,124},{2,125},{3,126},{5,0},{6,1},{7,2},{9,4},{10,5},{11,6},{13,... | collective-permute-start | bytes 393224 | tf_op jit(solution)/shard_map/ppermute | solution.py:276
  109.0 16.3 %copy-start.8 = (f32[8,8,1024]{2,1,0:T(8,128)}, f32[8,8,1024]{2,1,0:T(8,128)S(1)}, u32[]{:S(2)}) copy-start(f32[8,8,1024]{2,1,0:T(8,128)S(1)} %collective-permute-done.10.refs_12_) | copy-start | bytes 786436
  109.1 10.9 %collective-permute-start.35 = (f32[4,8,1024]{2,1,0:T(8,128)S(1)}, f32[4,8,1024]{2,1,0:T(8,128)S(1)}, u32[]{:S(2)}, u32[]{:S(2)}) collective-permute-start(f32[4,8,1024]{2,1,0:T(8,128)S(1)} %get-tuple-element.7), channel_id=1, source_target_pairs={{0,125},{1,126},{2,127},{4,1},{5,2},{6,3},{8,5},{9,6},{10,7},{12,9... | collective-permute-start | bytes 393224 | tf_op jit(solution)/shard_map/ppermute | solution.py:276
  113.3 12.1 %copy-start.9 = (f32[8,8,1024]{2,1,0:T(8,128)}, f32[8,8,1024]{2,1,0:T(8,128)S(1)}, u32[]{:S(2)}) copy-start(f32[8,8,1024]{2,1,0:T(8,128)S(1)} %collective-permute-done.3.refs_4_) | copy-start | bytes 786436
  113.3 12.1 %collective-permute-start.34 = (f32[4,8,1024]{2,1,0:T(8,128)S(1)}, f32[4,8,1024]{2,1,0:T(8,128)S(1)}, u32[]{:S(2)}, u32[]{:S(2)}) collective-permute-start(f32[4,8,1024]{2,1,0:T(8,128)S(1)} %get-tuple-element.8), channel_id=1, source_target_pairs={{1,4},{2,5},{3,6},{5,8},{6,9},{7,10},{9,12},{10,13},{11,14},{13,16... | collective-permute-start | bytes 393224 | tf_op jit(solution)/shard_map/ppermute | solution.py:276
  115.7 9.6 %copy-start.10 = (f32[8,8,1024]{2,1,0:T(8,128)}, f32[8,8,1024]{2,1,0:T(8,128)S(1)}, u32[]{:S(2)}) copy-start(f32[8,8,1024]{2,1,0:T(8,128)S(1)} %collective-permute-done.2.refs_3_) | copy-start | bytes 786436
  115.8 10.5 %collective-permute-start.33 = (f32[4,8,1024]{2,1,0:T(8,128)S(1)}, f32[4,8,1024]{2,1,0:T(8,128)S(1)}, u32[]{:S(2)}, u32[]{:S(2)}) collective-permute-start(f32[4,8,1024]{2,1,0:T(8,128)S(1)} %get-tuple-element.9), channel_id=1, source_target_pairs={{0,5},{1,6},{2,7},{4,9},{5,10},{6,11},{8,13},{9,14},{10,15},{12,17... | collective-permute-start | bytes 393224 | tf_op jit(solution)/shard_map/ppermute | solution.py:276
  117.7 7.7 %copy-start.23 = (f32[4,8,1024]{2,1,0:T(8,128)}, f32[4,8,1024]{2,1,0:T(8,128)S(1)}, u32[]{:S(2)}) copy-start(f32[4,8,1024]{2,1,0:T(8,128)S(1)} %collective-permute-done.36.refs_26_) | copy-start | bytes 393220
  117.7 13.9 %collective-permute-start.32 = (f32[8,8,1024]{2,1,0:T(8,128)S(1)}, f32[8,8,1024]{2,1,0:T(8,128)S(1)}, u32[]{:S(2)}, u32[]{:S(2)}) collective-permute-start(f32[8,8,1024]{2,1,0:T(8,128)S(1)} %get-tuple-element.10), channel_id=1, source_target_pairs={{1,0},{2,1},{3,2},{5,4},{6,5},{7,6},{9,8},{10,9},{11,10},{13,12},{... | collective-permute-start | bytes 786440 | tf_op jit(solution)/shard_map/ppermute | solution.py:276
  119.9 5.5 %copy-start.24 = (f32[4,8,1024]{2,1,0:T(8,128)}, f32[4,8,1024]{2,1,0:T(8,128)S(1)}, u32[]{:S(2)}) copy-start(f32[4,8,1024]{2,1,0:T(8,128)S(1)} %collective-permute-done.35.refs_25_) | copy-start | bytes 393220
  119.9 16.8 %copy-start.32 = (f32[16,128]{1,0:T(8,128)S(1)}, f32[16,128]{1,0:T(8,128)}, u32[]{:S(2)}) copy-start(f32[16,128]{1,0:T(8,128)} %get-tuple-element.5) | copy-start | bytes 24580
  119.9 11.6 %collective-permute-start.31 = (f32[8,8,1024]{2,1,0:T(8,128)S(1)}, f32[8,8,1024]{2,1,0:T(8,128)S(1)}, u32[]{:S(2)}, u32[]{:S(2)}) collective-permute-start(f32[8,8,1024]{2,1,0:T(8,128)S(1)} %get-tuple-element.11), channel_id=1, source_target_pairs={{0,1},{1,2},{2,3},{4,5},{5,6},{6,7},{8,9},{9,10},{10,11},{12,13},{... | collective-permute-start | bytes 786440 | tf_op jit(solution)/shard_map/ppermute | solution.py:276
  126.0 18.1 %collective-permute-start.8 = (f32[4,64,1024]{2,1,0:T(8,128)}, f32[4,64,1024]{2,1,0:T(8,128)S(1)}, u32[]{:S(2)}, u32[]{:S(2)}) collective-permute-start(f32[4,64,1024]{2,1,0:T(8,128)} %get-tuple-element.21), channel_id=1, source_target_pairs={{0,4},{1,5},{2,6},{3,7},{4,8},{5,9},{6,10},{7,11},{8,12},{9,13},{1... | collective-permute-start | bytes 3145736 | tf_op jit(solution)/shard_map/ppermute | solution.py:276
  126.3 10.5 %copy-start.26 = (f32[4,8,1024]{2,1,0:T(8,128)}, f32[4,8,1024]{2,1,0:T(8,128)S(1)}, u32[]{:S(2)}) copy-start(f32[4,8,1024]{2,1,0:T(8,128)S(1)} %collective-permute-done.33.refs_23_) | copy-start | bytes 393220
  126.3 17.9 %collective-permute-start.1 = (f32[4,64,1024]{2,1,0:T(8,128)}, f32[4,64,1024]{2,1,0:T(8,128)S(1)}, u32[]{:S(2)}, u32[]{:S(2)}) collective-permute-start(f32[4,64,1024]{2,1,0:T(8,128)} %get-tuple-element.28), channel_id=1, source_target_pairs={{0,124},{1,125},{2,126},{3,127},{4,0},{5,1},{6,2},{7,3},{8,4},{9,5... | collective-permute-start | bytes 3145736 | tf_op jit(solution)/shard_map/ppermute | solution.py:276
  131.6 23.9 %collective-permute-start = (f32[4,64,1024]{2,1,0:T(8,128)}, f32[4,64,1024]{2,1,0:T(8,128)}, u32[]{:S(2)}, u32[]{:S(2)}) collective-permute-start(f32[4,64,1024]{2,1,0:T(8,128)} %get-tuple-element.29), channel_id=1, source_target_pairs={{0,4},{1,5},{2,6},{3,7},{4,8},{5,9},{6,10},{7,11},{8,12},{9,13},{1... | collective-permute-start | bytes 3145736 | tf_op jit(solution)/shard_map/ppermute | solution.py:276
  131.6 23.9 %collective-permute-start.30 = (f32[4,64,1024]{2,1,0:T(8,128)}, f32[4,64,1024]{2,1,0:T(8,128)}, u32[]{:S(2)}, u32[]{:S(2)}) collective-permute-start(f32[4,64,1024]{2,1,0:T(8,128)} %get-tuple-element.12), channel_id=1, source_target_pairs={{0,124},{1,125},{2,126},{3,127},{4,0},{5,1},{6,2},{7,3},{8,4},{9,5... | collective-permute-start | bytes 3145736 | tf_op jit(solution)/shard_map/ppermute | solution.py:276
  136.7 30.1 %copy-start.3 = (f32[4,64,1024]{2,1,0:T(8,128)}, f32[4,64,1024]{2,1,0:T(8,128)S(1)}, u32[]{:S(2)}) copy-start(f32[4,64,1024]{2,1,0:T(8,128)S(1)} %collective-permute-done.9.refs_11_) | copy-start | bytes 3145732
  136.7 30.1 %collective-permute-start.29 = (f32[4,64,1024]{2,1,0:T(8,128)}, f32[4,64,1024]{2,1,0:T(8,128)}, u32[]{:S(2)}, u32[]{:S(2)}) collective-permute-start(f32[4,64,1024]{2,1,0:T(8,128)} %get-tuple-element.13), channel_id=1, source_target_pairs={{0,4},{1,5},{2,6},{3,7},{4,8},{5,9},{6,10},{7,11},{8,12},{9,13},{1... | collective-permute-start | bytes 3145736 | tf_op jit(solution)/shard_map/ppermute | solution.py:276
  144.2 22.6 %copy-start.4 = (f32[4,64,1024]{2,1,0:T(8,128)}, f32[4,64,1024]{2,1,0:T(8,128)S(1)}, u32[]{:S(2)}) copy-start(f32[4,64,1024]{2,1,0:T(8,128)S(1)} %collective-permute-done.8.refs_10_) | copy-start | bytes 3145732
  144.2 22.6 %copy-start.5 = (f32[4,64,1024]{2,1,0:T(8,128)}, f32[4,64,1024]{2,1,0:T(8,128)S(1)}, u32[]{:S(2)}) copy-start(f32[4,64,1024]{2,1,0:T(8,128)S(1)} %collective-permute-done.1.refs_2_) | copy-start | bytes 3145732
  (6 other events, 18.5 us)

commit v2 on v1

v2 whole, which is shorter than its diff:
```python
import functools
import math

import jax
import jax.numpy as jnp
from jax import lax
from jax.experimental import pallas as pl
from jax.experimental.pallas import tpu as pltpu
from jax.sharding import PartitionSpec as P

SWEEPS = 4
ITERS = 4
OMEGA = 0.9
AXIAL = 0.25
STEFAN = 1.0
SHRINK = 0.3
COUPLE = 0.2

F32 = jnp.float32
I32 = jnp.int32
BF16 = jnp.bfloat16

T, R, Z = 8, 64, 1024
H = 4
TE = T + 2 * H
RE = R + 8
RT = RE // 8
GROUPS, SLOTS, NB, BS = 4, 1024, 128, 16
UNROLL = 16
AZIM = ("y", "z", "core")


def iota(shape, dim):
    return lax.broadcasted_iota(I32, shape, dim)


def pieces(x):
    h = x.astype(BF16)
    rest = x - h.astype(F32)
    m = rest.astype(BF16)
    return h, m, (rest - m.astype(F32)).astype(BF16)


def at8(i):
    return pl.ds(pl.multiple_of(i * 8, 8), 8)


def flux_kernel(cnt, row, heat, lane, vert, share, out, diff, picked):
    def make(q, _):
        x = heat[q // 8, at8(q % 8), :]
        d = pltpu.roll(x, Z - 1, 1) - x
        for zc in range(8):
            diff[at8(q * 8 + zc), :] = d[:, zc * 128:(zc + 1) * 128]
        return 0

    lax.fori_loop(0, T * R // 8, make, 0, unroll=4)
    for j in range(GROUPS):
        def body(b, _):
            base = pl.multiple_of(b * UNROLL, UNROLL)
            for u in range(UNROLL):
                picked[pl.ds(base + u, 1), :] = diff[pl.ds(row[j, base + u], 1), :]
            return 0

        lax.fori_loop(0, (cnt[j] + UNROLL - 1) // UNROLL, body, 0)
        vals = []
        for kb in range(SLOTS // 128):
            cut = slice(kb * 128, (kb + 1) * 128)
            hit = iota((128, 128), 0) == lane[j:j + 1, cut]
            vals.append(jnp.sum(jnp.where(hit, picked[cut, :].T, 0.0), axis=0, keepdims=True))
        live = iota((1, SLOTS), 1) < cnt[j]
        val = jnp.where(live, share[j:j + 1, :] * jnp.concatenate(vals, axis=1), 0.0)
        v = vert[j:j + 1, :]
        inner = iota((BS, SLOTS), 0) == (v & (BS - 1))
        left = jnp.concatenate(
            [jnp.where(inner, p.astype(F32), 0.0).astype(BF16) for p in pieces(val)], axis=0)
        right = jnp.where(iota((NB, SLOTS), 0) == (v >> 4), 1.0, 0.0).astype(BF16)
        o = lax.dot_general(left, right, (((1,), (1,)), ((), ())), preferred_element_type=F32)
        out[j * BS:(j + 1) * BS, :] = o[:BS] + o[BS:2 * BS] + o[2 * BS:]


def front_kernel(kref, cnt, row, flux, f0, f1, f2, f3, lane, vert, share, pred, *refs):
    front_body(kref, cnt, row, flux, f0, f1, f2, f3, lane, vert, share, pred, *refs[5:])


def front_body(kref, cnt, row, parts, f0, f1, f2, f3, lane, vert, share, pred,
                 src, sup, sdown, srup, srdown, hout, front, gtab, height, terms, total, *acc):
    k = kref[0]
    sums = parts[0]
    for n in range(1, parts.shape[0]):
        sums = sums + parts[n]
    total[...] = sums
    flux = total

    def zero(q, _):
        for a in acc:
            a[at8(q), :] = jnp.zeros((8, 128), F32)
        return 0

    lax.fori_loop(0, T * R, zero, 0, unroll=4)
    for s, f in enumerate((f0, f1, f2, f3)):
        front[lax.rem(k + GROUPS - s, GROUPS)] = f[...]

    def neighbours(h):
        last = jnp.concatenate([h[g][BS - 1:BS, :] for g in range(GROUPS)], axis=0)
        first = jnp.concatenate([h[g][0:1, :] for g in range(GROUPS)], axis=0)
        zrow = jnp.zeros((1, 128), F32)
        lr = pltpu.roll(last, 1, 1)
        fr = pltpu.roll(first, 127, 1)
        col = iota((GROUPS, 128), 1)
        lr = jnp.where(col == 0, jnp.concatenate([zrow, lr[:-1]], axis=0), lr)
        fr = jnp.where(col == 127, jnp.concatenate([fr[1:], zrow], axis=0), fr)
        down = [jnp.concatenate([lr[g:g + 1], h[g][:BS - 1]], axis=0) for g in range(GROUPS)]
        up = [jnp.concatenate([h[g][1:], fr[g:g + 1]], axis=0) for g in range(GROUPS)]
        return down, up

    prior = [front[g, 256:272, :] for g in range(GROUPS)]
    h = list(prior)
    for _ in range(ITERS):
        down, up = neighbours(h)
        for g in range(GROUPS):
            applied = (2.0 + front[g, 272:288, :]) * h[g] - down[g] - up[g]
            res = front[g, 288:304, :] + COUPLE * flux[g * BS:(g + 1) * BS, :] - applied
            prod = front[g, 0:256, :].reshape(BS, BS, 128) * res[None]
            h[g] = h[g] + jnp.sum(prod, axis=1)
    down, up = neighbours(h)
    for g in range(GROUPS):
        slope = up[g] - down[g]
        growth = h[g] - prior[g]
        height[g] = h[g]
        gtab[g] = (flux[g * BS:(g + 1) * BS, :] - STEFAN * growth) * jnp.sqrt(1.0 + slope * slope)
    hout[...] = height[k]
    for j in range(GROUPS):
        v = vert[j:j + 1, :]
        right = jnp.where(iota((NB, SLOTS), 0) == (v >> 4), 1.0, 0.0).astype(BF16)
        x = jnp.dot(jnp.concatenate(pieces(gtab[j]), axis=0), right, preferred_element_type=F32)
        x = x[:BS] + x[BS:2 * BS] + x[2 * BS:]
        inner = iota((BS, SLOTS), 0) == (v & (BS - 1))
        term = jnp.sum(jnp.where(inner, x, 0.0), axis=0, keepdims=True) * share[j:j + 1, :]
        term = jnp.where(iota((1, SLOTS), 1) < cnt[j], term, 0.0)
        for kb in range(SLOTS // 128):
            cut = slice(kb * 128, (kb + 1) * 128)
            hit = iota((128, 128), 0) == lane[j:j + 1, cut]
            terms[j, cut, :] = jnp.where(hit, term[:, cut], 0.0).T
    most = jnp.maximum(jnp.maximum(cnt[0], cnt[1]), jnp.maximum(cnt[2], cnt[3]))

    def add(b, _):
        for u in range(UNROLL):
            s = b * UNROLL + u
            for j in range(GROUPS):
                at = pl.ds(row[j, s], 1)
                acc[j][at, :] = acc[j][at, :] + terms[j, pl.ds(s, 1), :]
        return 0

    lax.fori_loop(0, (most + UNROLL - 1) // UNROLL, add, 0)

    def finish(q, _):
        d = q // 8
        for zc in range(8):
            a = at8(q * 8 + zc)
            s = (acc[0][a, :] + acc[1][a, :]) + (acc[2][a, :] + acc[3][a, :])
            cut = slice(zc * 128, (zc + 1) * 128)
            src[d, at8(q % 8), cut] = pred[d, at8(q % 8), cut] + SHRINK * s
        return 0

    lax.fori_loop(0, T * R // 8, finish, 0)
    sup[...] = src[T - H + 1:]
    sdown[...] = src[:H - 1]
    srup[...] = src[:, R - 8:, :]
    srdown[...] = src[:, :8, :]


def pack_kernel(load, beta, up, down, rup, rdown, sems):
    copies = []
    for n, f in enumerate((load, beta)):
        copies += [(f.at[pl.ds(T - H, H)], up.at[pl.ds(n * H, H)]),
                   (f.at[pl.ds(0, H)], down.at[pl.ds(n * H, H)]),
                   (f.at[:, pl.ds(R - 8, 8)], rup.at[pl.ds(n * T, T)]),
                   (f.at[:, pl.ds(0, 8)], rdown.at[pl.ds(n * T, T)])]
    copies = [pltpu.make_async_copy(a, b, sems.at[m]) for m, (a, b) in enumerate(copies)]
    for c in copies:
        c.start()
    for c in copies:
        c.wait()


def shift_azim(x, d):
    return lax.ppermute(x, AZIM, [(i, (i + d) % 32) for i in range(32)])


def shift_rad(x, d):
    return lax.ppermute(x, "rad", [(i, i + d) for i in range(4) if 0 <= i + d < 4])


def ring_tile(from_above, from_below):
    return jnp.where(iota(from_above.shape, 1) < 4, from_above, from_below)


def wide(x):
    return jnp.concatenate([x] * (Z // 128), axis=1)


def sweep_kernel(kref, load, beta_in, lo, hi, side, clo, chi, src, slo, shi, sside, sclo, schi,
                 out, pa, pb, th, rr, zz, ww, ss, sems):
    k = kref[0]
    mid, below, above = pl.ds(H, T), pl.ds(0, H), pl.ds(H + T, H)
    below3, above3 = pl.ds(1, H - 1), pl.ds(H + T, H - 1)
    rows, ring = pl.ds(0, R), pl.ds(R, 8)

    def part(x, n, count):
        return x.at[pl.ds(n * count, count)]

    def field(ref, own, n):
        return [(own, ref.at[mid, rows]), (part(lo, n, H), ref.at[below, rows]),
                (part(hi, n, H), ref.at[above, rows]), (part(side, n, T), ref.at[mid, ring]),
                (part(clo, n, H), ref.at[below, ring]), (part(chi, n, H), ref.at[above, ring])]

    groups = [field(pb, beta_in, 1), field(pa, load, 0),
              [(src, ss.at[mid, rows]), (slo, ss.at[below3, rows]), (shi, ss.at[above3, rows]),
               (sside, ss.at[mid, ring]), (sclo, ss.at[below3, ring]), (schi, ss.at[above3, ring])]]
    copies = []
    for n, g in enumerate(groups):
        cs = [pltpu.make_async_copy(a, b, sems.at[n, m]) for m, (a, b) in enumerate(g)]
        for c in cs:
            c.start()
        copies.append(cs)
    for c in copies[0]:
        c.wait()
    sub = iota((8, Z), 0)
    top, bottom = sub == 7, sub == 0
    last_lane = iota((8, Z), 1) == Z - 1
    s8 = iota((8, 128), 0)
    beta = pb

    def gidx(it):
        return k * R + (it * 8 + s8 if it < RT - 1 else jnp.where(s8 < 4, R + s8, s8 - 8))

    def radius(it):
        return 0.25 * 256 + gidx(it).astype(F32) + 0.5

    angular = (256 / (2.0 * math.pi)) ** 2

    def cut(it):
        it = it % RT
        return slice(it * 8, it * 8 + 8)

    def coefs(it, _):
        ra, gi = radius(it), gidx(it)
        return wide((0.5 * angular) / ra), wide(jnp.where((gi >= 0) & (gi < 255), 0.5 * (ra + 0.5), 0.0)), wide(AXIAL * ra)

    for it in range(RT):
        c = cut(it)
        ang, rad, axi = coefs(it, 0)
        th[0, c, :] = (beta[0, c, :] + beta[1, c, :]) * ang

        def coef(t, _):
            b = beta[t, c, :]
            bu = jnp.where(top, pltpu.roll(beta[t, cut(it + 1), :], 7, 0), pltpu.roll(b, 7, 0))
            rr[t, c, :] = (b + bu) * rad
            th[t, c, :] = (b + beta[t + 1, c, :]) * ang
            zz[t, c, :] = jnp.where(last_lane, b, 0.5 * (b + pltpu.roll(b, Z - 1, 1))) * axi
            return 0

        lax.fori_loop(1, TE - 1, coef, 0)

    def diag(t, _):
        for it in range(RT):
            c = cut(it)
            face, z = rr[t, c, :], zz[t, c, :]
            other = jnp.where(bottom, pltpu.roll(rr[t, cut(it - 1), :], 1, 0), pltpu.roll(face, 1, 0))
            zcut = jnp.where(last_lane, 0.0, z)
            zz[t, c, :] = zcut
            d = (th[t, c, :] + th[t - 1, c, :]) + (face + other) + (z + pltpu.roll(zcut, 1, 1))
            ww[t, c, :] = OMEGA / jnp.where(d > 0.0, d, 1.0)
        return 0

    lax.fori_loop(1, TE - 1, diag, 0)
    for cs in copies[1:]:
        for c in cs:
            c.wait()
    for it in range(RT):
        c = cut(it)
        ra = wide(radius(it))

        def scale(t, _):
            ss[t, c, :] = ss[t, c, :] * ra
            return 0

        lax.fori_loop(1, TE - 1, scale, 0, unroll=2)

    def sweep(old, new, t, tiles, shift):
        prev = pltpu.roll(rr[t, cut(-1), :] * old[t, cut(-1), :], 1, 0)
        nxt = old[t, cut(0), :]
        nroll = pltpu.roll(nxt, 7, 0)
        for it in range(tiles):
            c = cut(it)
            p, proll = nxt, nroll
            nxt = old[t, cut(it + 1), :]
            nroll = pltpu.roll(nxt, 7, 0)
            r, z = rr[t, c, :], zz[t, c, :]
            acc = th[t, c, :] * old[t + 1, c, :] + th[t - 1, c, :] * old[t - 1, c, :]
            acc = acc + r * jnp.where(top, nroll, proll)
            rolled = pltpu.roll(r * p, 1, 0)
            acc = acc + jnp.where(bottom, prev, rolled)
            prev = rolled
            acc = acc + z * pltpu.roll(p, Z - 1, 1) + pltpu.roll(z * p, 1, 1)
            new[t - shift, c, :] = (1.0 - OMEGA) * p + ww[t, c, :] * (acc - ss[t, c, :])
        return 0

    bufs = (pa, pb)
    for n in range(1, SWEEPS + 1):
        old, new = bufs[(n - 1) % 2], bufs[n % 2]
        if n < SWEEPS:
            lax.fori_loop(n, TE - n, lambda t, _: sweep(old, new, t, RT, 0), 0)
        else:
            lax.fori_loop(n, TE - n, lambda t, _: sweep(old, out, t, RT - 1, H), 0)


def from_all(x, axes, count):
    return lax.all_to_all(jnp.broadcast_to(x[None], (count,) + x.shape), axes, 0, 0)


def sum_kernel(parts, *refs):
    out = refs[-1]
    s = parts[0]
    for n in range(1, parts.shape[0]):
        s = s + parts[n]
    out[...] = s


VM = pl.BlockSpec(memory_space=pltpu.VMEM)
SM = pl.BlockSpec(memory_space=pltpu.SMEM)
ANY = pl.BlockSpec(memory_space=pl.ANY)
PARAMS = pltpu.CompilerParams(vmem_limit_bytes=56 << 20)


def per_device(load, outflow, beta, heat, label, vertex, share, tally, prior, weight, jump, solve):
    label = label.reshape(GROUPS, SLOTS)
    vertex = vertex.reshape(GROUPS, SLOTS)
    share = share.reshape(GROUPS, SLOTS)
    tally = tally.reshape(GROUPS)
    hi = label >> 10
    low = hi + (label & 1023)
    carry = (low >= Z - 1).astype(I32)
    column, axial = hi + carry, low - (Z - 1) * carry
    row = ((column >> 3) << 6) + ((axial >> 7) << 3) + (column & 7)
    lane = axial & 127
    kidx = lax.axis_index("rad").astype(I32).reshape(1)

    flip = lambda v: v.reshape(NB, BS).T
    front = jnp.concatenate([solve.reshape(BS * BS, NB), flip(prior), flip(weight), flip(jump)], axis=0)
    fronts = [front] + [
        lax.ppermute(front, "rad", [(i, (i + s) % 4) for i in range(4)]) for s in (1, 2, 3)]

    plane = lambda n: jax.ShapeDtypeStruct((n, R, Z), F32)
    tile = lambda n: jax.ShapeDtypeStruct((n, 8, Z), F32)
    up, down, rup, rdown = pl.pallas_call(
        pack_kernel, out_shape=(plane(2 * H), plane(2 * H), tile(2 * T), tile(2 * T)),
        in_specs=[ANY] * 2, out_specs=(ANY,) * 4,
        scratch_shapes=[pltpu.SemaphoreType.DMA((8,))], compiler_params=PARAMS, name="pack",
    )(load, beta)
    up, down, rup, rdown, heat = lax.optimization_barrier((up, down, rup, rdown, heat))
    lo, hi = shift_azim(up, 1), shift_azim(down, -1)
    rhi, rlo = shift_rad(rdown, -1), shift_rad(rup, 1)
    side = ring_tile(rhi, rlo)
    edge = lambda s: jnp.concatenate([side[s:s + H], side[T + s:T + s + H]], axis=0)
    clo, chi = shift_azim(edge(T - H), 1), shift_azim(edge(0), -1)
    partial = pl.pallas_call(
        flux_kernel, out_shape=jax.ShapeDtypeStruct((GROUPS * BS, NB), F32),
        in_specs=[SM, SM, VM, VM, VM, VM], out_specs=VM,
        scratch_shapes=[pltpu.VMEM((T * R * 8, 128), F32), pltpu.VMEM((SLOTS, 128), F32)],
        compiler_params=PARAMS, name="flux",
        cost_estimate=pl.CostEstimate(flops=20000000, bytes_accessed=120 << 20, transcendentals=0),
    )(tally, row, heat, lane, vertex, share)
    near = pl.pallas_call(
        sum_kernel, out_shape=jax.ShapeDtypeStruct((GROUPS * BS, NB), F32),
        in_specs=[VM, ANY, ANY], out_specs=VM, compiler_params=PARAMS, name="near",
    )(from_all(partial, ("z", "core"), 8), rhi, rlo)
    flux = from_all(near, ("y", "rad"), 16)
    source, sup, sdown, srup, srdown, height = pl.pallas_call(
        front_kernel,
        out_shape=(plane(T), plane(H - 1), plane(H - 1), tile(T), tile(T),
                   jax.ShapeDtypeStruct((BS, NB), F32)),
        in_specs=[SM, SM, SM] + [VM] * 9 + [ANY] * 5, out_specs=(VM,) * 6,
        scratch_shapes=[pltpu.VMEM((GROUPS, 304, NB), F32), pltpu.VMEM((GROUPS, BS, NB), F32),
                        pltpu.VMEM((GROUPS, BS, NB), F32), pltpu.VMEM((GROUPS, SLOTS, 128), F32),
                        pltpu.VMEM((GROUPS * BS, NB), F32)]
        + [pltpu.VMEM((T * R * 8, 128), F32)] * GROUPS,
        compiler_params=PARAMS, name="front",
        cost_estimate=pl.CostEstimate(flops=1000, bytes_accessed=30 << 20, transcendentals=0),
    )(kidx, tally, row, flux, *fronts, lane, vertex, share, outflow, lo, hi, side, clo, chi)
    slo, shi = shift_azim(sup, 1), shift_azim(sdown, -1)
    sside = ring_tile(shift_rad(srdown, -1), shift_rad(srup, 1))
    sclo, schi = shift_azim(sside[T - H + 1:], 1), shift_azim(sside[:H - 1], -1)
    ext = pltpu.VMEM((TE, RE, Z), F32)
    pressure = pl.pallas_call(
        sweep_kernel, out_shape=plane(T),
        in_specs=[SM] + [ANY] * 13, out_specs=VM,
        scratch_shapes=[ext] * 7 + [pltpu.SemaphoreType.DMA((3, 6))],
        compiler_params=PARAMS, name="sweeps",
        cost_estimate=pl.CostEstimate(flops=1000, bytes_accessed=30 << 20, transcendentals=0),
    )(kidx, load, beta, lo, hi, side, clo, chi, source, slo, shi, sside, sclo, schi)
    return pressure, height.T.reshape(NB * BS)


def solution(mesh):
    fine = jax.sharding.Mesh(mesh.devices.reshape(4, 4, 2, 4), AZIM + ("rad",))
    cells = P(AZIM, "rad", None)
    slots = P(AZIM, "rad", None, None)
    return jax.shard_map(
        per_device,
        mesh=fine,
        in_specs=(cells, cells, cells, cells, slots, slots, slots, cells,
                  P("rad"), P("rad"), P("rad"), P(None, None, "rad")),
        out_specs=(cells, P("rad")),
        check_vma=False,
    )
```

time: 190 us -> 287 us (1.51)
  Pallas kernels: 39.9 us -> 207 us
  starting transfers between devices: 93 us -> 51.8 us
  waiting for transfers between devices: 37.7 us -> 12 us
  local copies, waits for them, and re-layouts: 12.8 us -> 9.22 us
    pallas_call x2 -> x4, Pallas kernels: 30.4 us -> 199 us  [the longest x1 160 us: per_device(): pl.pallas_call(pack_kernel, out_shape=(plane(2 * H), plane(2 * H), tile(2...]
    ppermute x34 -> x12, starting transfers between devices: 89.5 us -> 33.9 us  [the longest x8 20.5 us: shift_azim(): return lax.ppermute(x, AZIM, [(i, (i + d) % 32) for i in range(32)])]
    ppermute x34 -> x12, waiting for transfers between devices: 37.7 us -> 7.31 us  [the longest x8 5.89 us: shift_azim(): return lax.ppermute(x, AZIM, [(i, (i + d) % 32) for i in range(32)])]
    all_to_all x0 -> x2, starting transfers between devices: none -> 11.7 us  [from_all(): lax.all_to_all(jnp.broadcast_to(x[None], (count,) + x.shape), axes, 0, 0)]
    slice x9 -> x2, local copies, waits for them, and re-layouts: 10.2 us -> 0.06 us  [the longest x1 0.04 us: per_device(): side[s:s + H]]
    ppermute x3, waiting for transfers between devices: 0.01 us -> 4.09 us  [per_device(): lax.ppermute(front, 'rad', [(i, (i + s) % 4) for i in range(4)])]
    broadcast_in_dim x0 -> x2, local copies, waits for them, and re-layouts: none -> 3.07 us  [from_all(): jnp.broadcast_to(x[None], (count,) + x.shape)]
  transfers between devices with their start and end apart: 37 -> 17, of which waited for: 12 -> 5; matrix products, arithmetic and copies ran while one was open for 7% -> 4% of each run, Pallas kernels for 5% -> 3%
where the time goes in v2:
time: 287 us; the launch traced here: 286 us
  Pallas kernels  207 us (72%)
  starting transfers between devices  51.8 us (18%)
  waiting for transfers between devices  12 us (4%)
  local copies, waits for them, and re-layouts  9.22 us (3%)
  other arithmetic  5.17 us (2%)
    pallas_call x1, Pallas kernels, per_device(): pl.pallas_call(pack_kernel, out_shape=(plane(2 * H), plane(2 * H), tile(2...  160 us
    pallas_call x1, Pallas kernels, per_device(): pl.pallas_call(sweep_kernel, out_shape=plane(T), in_specs=[SM] + [ANY] *...  27.9 us
    ppermute x8, starting transfers between devices, shift_azim(): return lax.ppermute(x, AZIM, [(i, (i + d) % 32) for i in range(32)])  20.5 us
    ppermute x4, starting transfers between devices, shift_rad(): lax.ppermute(x, 'rad', [(i, i + d) for i in range(4) if 0 <= i + d < 4])  13.4 us
    all_to_all x2, starting transfers between devices, from_all(): lax.all_to_all(jnp.broadcast_to(x[None], (count,) + x.shape), axes, 0, 0)  11.7 us
    pallas_call x1, Pallas kernels, per_device(): pl.pallas_call(front_kernel, out_shape=(plane(T), plane(H - 1), plane(H -...  9.29 us
    pallas_call x1, Pallas kernels, per_device(): pl.pallas_call(flux_kernel, out_shape=jax.ShapeDtypeStruct((GROUPS * BS,...  7.93 us
    ppermute x3, starting transfers between devices, per_device(): lax.ppermute(front, 'rad', [(i, (i + s) % 4) for i in range(4)])  6.23 us
  transfers between devices with their start and end apart: 17, of which 5 were waited for; matrix products, arithmetic and copies ran while one was open for 4% of the time, Pallas kernels for 3%

profile of v2, /device:TPU:2, one launch (start us, length us, event | category | flops | bytes accessed | tf_op | source)
XLA Modules:
  0.0 285.9 jit_solution(10492146751465105578)
XLA Ops:
  0.6 160.0 %pack.1 = (f32[8,64,1024]{2,1,0:T(8,128)}, f32[8,64,1024]{2,1,0:T(8,128)}, f32[16,8,1024]{2,1,0:T(8,128)}, f32[16,8,1024]{2,1,0:T(8,128)}) custom-call(f32[8,64,1024]{2,1,0:T(8,128)} %load.3, f32[8,64,1024]{2,1,0:T(8,128)} %beta_in.1), custom_call_target="tpu_custom_call" | custom-call | tf_op jit(solution)/shard_map/pack/pallas_call | solution.py:356
  160.6 0.0 copy-start.13
  160.7 0.0 copy-start.14
  160.7 0.0 copy-start.15
  160.7 0.1 collective-permute-start
  160.8 6.0 %collective-permute-start.1 = (f32[8,64,1024]{2,1,0:T(8,128)}, f32[8,64,1024]{2,1,0:T(8,128)}, u32[]{:S(2)}, u32[]{:S(2)}) collective-permute-start(f32[8,64,1024]{2,1,0:T(8,128)} %get-tuple-element.22), channel_id=1, source_target_pairs={{0,124},{4,0},{8,4},{12,8},{16,12},{20,16},{24,20},{28,24},{32,28}... | collective-permute-start | bytes 6291464 | tf_op jit(solution)/shard_map/ppermute | solution.py:187
  166.8 2.4 collective-permute-start.2
  169.2 3.4 %collective-permute-start.3 = (f32[16,8,1024]{2,1,0:T(8,128)}, f32[16,8,1024]{2,1,0:T(8,128)S(1)}, u32[]{:S(2)}, u32[]{:S(2)}) collective-permute-start(f32[16,8,1024]{2,1,0:T(8,128)} %get-tuple-element.24), channel_id=1, source_target_pairs={{0,1},{1,2},{2,3},{4,5},{5,6},{6,7},{8,9},{9,10},{10,11},{12,13},{... | collective-permute-start | bytes 1572872 | tf_op jit(solution)/shard_map/ppermute | solution.py:191
  172.6 0.6 broadcast_and_fusion
  173.2 7.9 %flux.1 = f32[64,128]{1,0:T(8,128)} custom-call(s32[4]{0:T(128)} %bitcast.49, s32[4,1024]{1,0:T(4,128)} %get-tuple-element.39.row, f32[8,64,1024]{2,1,0:T(8,128)} %heat, s32[4,1024]{1,0:T(4,128)} %get-tuple-element.38.lane, s32[4,1024]{1,0:T(4,128)} %bitcast.41, f32[4,1024]{1,0:T(4,128)} %bitcast.43), custom_call_target="tpu_custom_call" | custom-call | flops 20000000 | bytes 125829120 | tf_op jit(solution)/shard_map/flux/pallas_call | solution.py:367
  181.2 1.5 broadcast_in_dim.4
  182.6 3.4 %all-to-all-start = ((f32[8,64,128]{2,1,0:T(8,128)}), f32[8,64,128]{2,1,0:T(8,128)S(1)}, u32[]{:S(2)}, u32[]{:S(2)}) async-start(f32[8,64,128]{2,1,0:T(8,128)} %broadcast_in_dim.4), calls=%async_computation | async-start | bytes 524288 | tf_op jit(solution)/shard_map/all_to_all | solution.py:319
  186.1 0.1 reshape.43
  186.1 0.1 copy.14
  186.2 0.1 reshape.44
  186.3 0.1 copy.15
  186.4 0.1 reshape.45
  186.5 0.1 copy.16
  186.5 1.6 pad_maximum_fusion.2.f0
  188.1 4.7 %collective-permute-start.8 = (f32[304,128]{1,0:T(8,128)}, f32[304,128]{1,0:T(8,128)}, u32[]{:S(2)}, u32[]{:S(2)}) collective-permute-start(f32[304,128]{1,0:T(8,128)} %pad_maximum_fusion.2.f0), channel_id=1, source_target_pairs={{0,3},{1,0},{2,1},{3,2},{4,7},{5,4},{6,5},{7,6},{8,11},{9,8},{10,9... | collective-permute-start | bytes 466952 | tf_op jit(solution)/shard_map/ppermute | solution.py:352
  192.8 0.0 collective-permute-done.2.refs_0_
  192.8 0.1 collective-permute-start.7
  192.9 0.6 all-to-all-done.parts
  193.5 0.0 collective-permute-done.3.refs_1_
  193.5 0.1 copy-done.3
  193.6 0.6 copy-done.7
  194.2 0.8 copy-done.4
  195.0 1.6 near.1
  196.6 1.6 broadcast_in_dim.5
  198.2 8.3 %all-to-all-start.1 = ((f32[16,64,128]{2,1,0:T(8,128)}), f32[16,64,128]{2,1,0:T(8,128)S(1)}, u32[]{:S(2)}, u32[]{:S(2)}) async-start(f32[16,64,128]{2,1,0:T(8,128)} %broadcast_in_dim.5), calls=%async_computation.1 | async-start | bytes 1048576 | tf_op jit(solution)/shard_map/all_to_all | solution.py:319
  206.4 1.3 broadcast_select_fusion.refs_2_.side
  207.8 0.8 pad_maximum_fusion
  208.6 0.0 collective-permute-start.4
  208.6 0.7 pad_maximum_fusion.1
  209.4 0.0 collective-permute-done.8.f3
  209.4 5.1 %collective-permute-start.5 = (f32[8,8,1024]{2,1,0:T(8,128)}, f32[8,8,1024]{2,1,0:T(8,128)}, u32[]{:S(2)}, u32[]{:S(2)}) collective-permute-start(f32[8,8,1024]{2,1,0:T(8,128)} %pad_maximum_fusion.1), channel_id=1, source_target_pairs={{0,124},{4,0},{8,4},{12,8},{16,12},{20,16},{24,20},{28,24},{32,28}... | collective-permute-start | bytes 786440 | tf_op jit(solution)/shard_map/ppermute | solution.py:187
  214.4 1.5 collective-permute-start.6
  215.9 4.1 %collective-permute-done.6.f1 = f32[304,128]{1,0:T(8,128)} collective-permute-done((f32[304,128]{1,0:T(8,128)}, f32[304,128]{1,0:T(8,128)}, u32[]{:S(2)}, u32[]{:S(2)}) %collective-permute-start.6) | collective-permute-done | bytes 155680 | tf_op jit(solution)/shard_map/ppermute | solution.py:352
  220.0 0.0 collective-permute-done.4.refs_3_.clo
  220.0 0.0 collective-permute-done.5.refs_4_.chi
  220.0 0.0 collective-permute-done.refs_0_.lo
  220.0 0.0 collective-permute-done.1.refs_1_.hi
  220.0 0.7 copy-done.6
  220.7 0.2 copy-done.2
  220.9 0.7 copy-done
  221.6 9.3 %front.1 = (f32[8,64,1024]{2,1,0:T(8,128)}, f32[3,64,1024]{2,1,0:T(8,128)}, f32[3,64,1024]{2,1,0:T(8,128)}, f32[8,8,1024]{2,1,0:T(8,128)}, f32[8,8,1024]{2,1,0:T(8,128)}, /*index=5*/f32[16,128]{1,0:T(8,128)}) custom-call(s32[1]{0:T(128)} %bitcast.kref, s32[4]{0:T(128)} %bitcast.50, s32[4,1024]{1,0:T(4,128)} %get-tuple-element.39.row, ...), custom_call_target="tpu_custom_call" | custom-call | flops 1000 | bytes 31457280 | tf_op jit(solution)/shard_map/front/pallas_call | solution.py:379
  230.9 5.7 %collective-permute-start.11 = (f32[8,8,1024]{2,1,0:T(8,128)}, f32[8,8,1024]{2,1,0:T(8,128)S(1)}, u32[]{:S(2)}, u32[]{:S(2)}) collective-permute-start(f32[8,8,1024]{2,1,0:T(8,128)} %get-tuple-element.29), channel_id=1, source_target_pairs={{1,0},{2,1},{3,2},{5,4},{6,5},{7,6},{9,8},{10,9},{11,10},{13,12},{... | collective-permute-start | bytes 786440 | tf_op jit(solution)/shard_map/ppermute | solution.py:191
  236.6 1.9 collective-permute-start.12
  238.5 0.1 collective-permute-start.9
  238.6 5.1 %collective-permute-start.10 = (f32[3,64,1024]{2,1,0:T(8,128)}, f32[3,64,1024]{2,1,0:T(8,128)S(1)}, u32[]{:S(2)}, u32[]{:S(2)}) collective-permute-start(f32[3,64,1024]{2,1,0:T(8,128)} %get-tuple-element.28), channel_id=1, source_target_pairs={{0,124},{4,0},{8,4},{12,8},{16,12},{20,16},{24,20},{28,24},{32,28}... | collective-permute-start | bytes 2359304 | tf_op jit(solution)/shard_map/ppermute | solution.py:187
  243.7 0.0 collective-permute-done.11
  243.7 1.4 collective-permute-done.12
  245.1 0.1 broadcast_select_fusion.1.sside
  245.2 4.2 %collective-permute-start.14 = (f32[3,8,1024]{2,1,0:T(8,128)S(1)}, f32[3,8,1024]{2,1,0:T(8,128)S(1)}, u32[]{:S(2)}, u32[]{:S(2)}) collective-permute-start(f32[3,8,1024]{2,1,0:T(8,128)S(1)} %get-tuple-element.36), channel_id=1, source_target_pairs={{0,124},{4,0},{8,4},{12,8},{16,12},{20,16},{24,20},{28,24},{32,28}... | collective-permute-start | bytes 294920 | tf_op jit(solution)/shard_map/ppermute | solution.py:187
  249.4 0.0 collective-permute-start.13
  249.4 0.8 copy.17
  250.2 0.7 reshape.46
  250.9 3.5 %collective-permute-done.14.schi = f32[3,8,1024]{2,1,0:T(8,128)S(1)} collective-permute-done((f32[3,8,1024]{2,1,0:T(8,128)S(1)}, f32[3,8,1024]{2,1,0:T(8,128)S(1)}, u32[]{:S(2)}, u32[]{:S(2)}) %collective-permute-start.14) | collective-permute-done | bytes 98336 | tf_op jit(solution)/shard_map/ppermute | solution.py:187
  254.4 2.3 collective-permute-done.13.sclo
  256.8 0.0 collective-permute-done.9.slo
  256.8 0.6 copy-done.11
  257.4 0.3 copy-done.8
  257.7 0.2 copy-done.9
  257.9 27.9 %sweeps.1 = f32[8,64,1024]{2,1,0:T(8,128)} custom-call(s32[1]{0:T(128)} %bitcast.kref, f32[8,64,1024]{2,1,0:T(8,128)} %load.3, f32[8,64,1024]{2,1,0:T(8,128)} %beta_in.1, f32[8,64,1024]{2,1,0:T(8,128)} %copy-done, f32[8,64,1024]{2,1,0:T(8,128)} %collective-permute-done.1.refs_1_.hi, f32[16,8,1024]{2,1,0:T(8,128)} %copy-done.1, f32[8,8,1024]{2,1,0:T(8,128)} %copy-done.6, ...), custom_call_target="tpu_custom_call" | custom-call | flops 1000 | bytes 31457280 | tf_op jit(solution)/shard_map/sweeps/pallas_call | solution.py:395
  (26 shorter events, 0.1 us)
Async XLA Ops:
  0.6 172.0 %copy-start.12 = (s32[1,1,4,1024]{3,2,1,0:T(4,128)S(1)}, s32[1,1,4,1024]{3,2,1,0:T(4,128)}, u32[]{:S(2)}) copy-start(s32[1,1,4,1024]{3,2,1,0:T(4,128)} %param.16) | copy-start | bytes 49156
  160.6 25.4 %copy-start.13 = (f32[2048]{0:T(1024)S(1)}, f32[2048]{0:T(1024)}, u32[]{:S(2)}) copy-start(f32[2048]{0:T(1024)} %param.20) | copy-start | bytes 24580
  160.7 25.5 %copy-start.14 = (f32[2048]{0:T(1024)S(1)}, f32[2048]{0:T(1024)}, u32[]{:S(2)}) copy-start(f32[2048]{0:T(1024)} %param.21) | copy-start | bytes 24580
  160.7 25.7 %copy-start.15 = (f32[2048]{0:T(1024)S(1)}, f32[2048]{0:T(1024)}, u32[]{:S(2)}) copy-start(f32[2048]{0:T(1024)} %param.22) | copy-start | bytes 24580
  160.7 59.3 %collective-permute-start = (f32[8,64,1024]{2,1,0:T(8,128)}, f32[8,64,1024]{2,1,0:T(8,128)S(1)}, u32[]{:S(2)}, u32[]{:S(2)}) collective-permute-start(f32[8,64,1024]{2,1,0:T(8,128)} %get-tuple-element.21), channel_id=1, source_target_pairs={{0,4},{4,8},{8,12},{12,16},{16,20},{20,24},{24,28},{28,32},{32,36}... | collective-permute-start | bytes 6291464 | tf_op jit(solution)/shard_map/ppermute | solution.py:187
  160.8 59.3 %collective-permute-start.1 = (f32[8,64,1024]{2,1,0:T(8,128)}, f32[8,64,1024]{2,1,0:T(8,128)}, u32[]{:S(2)}, u32[]{:S(2)}) collective-permute-start(f32[8,64,1024]{2,1,0:T(8,128)} %get-tuple-element.22), channel_id=1, source_target_pairs={{0,124},{4,0},{8,4},{12,8},{16,12},{20,16},{24,20},{28,24},{32,28}... | collective-permute-start | bytes 6291464 | tf_op jit(solution)/shard_map/ppermute | solution.py:187
  166.8 26.1 %collective-permute-start.2 = (f32[16,8,1024]{2,1,0:T(8,128)}, f32[16,8,1024]{2,1,0:T(8,128)S(1)}, u32[]{:S(2)}, u32[]{:S(2)}) collective-permute-start(f32[16,8,1024]{2,1,0:T(8,128)} %get-tuple-element.23), channel_id=1, source_target_pairs={{1,0},{2,1},{3,2},{5,4},{6,5},{7,6},{9,8},{10,9},{11,10},{13,12},{... | collective-permute-start | bytes 1572872 | tf_op jit(solution)/shard_map/ppermute | solution.py:191
  169.2 24.3 %collective-permute-start.3 = (f32[16,8,1024]{2,1,0:T(8,128)}, f32[16,8,1024]{2,1,0:T(8,128)S(1)}, u32[]{:S(2)}, u32[]{:S(2)}) collective-permute-start(f32[16,8,1024]{2,1,0:T(8,128)} %get-tuple-element.24), channel_id=1, source_target_pairs={{0,1},{1,2},{2,3},{4,5},{5,6},{6,7},{8,9},{9,10},{10,11},{12,13},{... | collective-permute-start | bytes 1572872 | tf_op jit(solution)/shard_map/ppermute | solution.py:191
  182.6 10.9 %all-to-all-start = ((f32[8,64,128]{2,1,0:T(8,128)}), f32[8,64,128]{2,1,0:T(8,128)S(1)}, u32[]{:S(2)}, u32[]{:S(2)}) async-start(f32[8,64,128]{2,1,0:T(8,128)} %broadcast_in_dim.4), calls=%async_computation | async-start | bytes 524288 | tf_op jit(solution)/shard_map/all_to_all | solution.py:319
  188.1 21.2 %collective-permute-start.8 = (f32[304,128]{1,0:T(8,128)}, f32[304,128]{1,0:T(8,128)}, u32[]{:S(2)}, u32[]{:S(2)}) collective-permute-start(f32[304,128]{1,0:T(8,128)} %pad_maximum_fusion.2.f0), channel_id=1, source_target_pairs={{0,3},{1,0},{2,1},{3,2},{4,7},{5,4},{6,5},{7,6},{8,11},{9,8},{10,9... | collective-permute-start | bytes 466952 | tf_op jit(solution)/shard_map/ppermute | solution.py:352
  192.8 0.8 copy-start.3
  192.8 21.6 %collective-permute-start.7 = (f32[304,128]{1,0:T(8,128)}, f32[304,128]{1,0:T(8,128)}, u32[]{:S(2)}, u32[]{:S(2)}) collective-permute-start(f32[304,128]{1,0:T(8,128)} %pad_maximum_fusion.2.f0), channel_id=1, source_target_pairs={{0,2},{1,3},{2,0},{3,1},{4,6},{5,7},{6,4},{7,5},{8,10},{9,11},{10,... | collective-permute-start | bytes 466952 | tf_op jit(solution)/shard_map/ppermute | solution.py:352
  193.5 0.7 copy-start.7
  194.2 0.8 copy-start.4
  198.2 21.8 %all-to-all-start.1 = ((f32[16,64,128]{2,1,0:T(8,128)}), f32[16,64,128]{2,1,0:T(8,128)S(1)}, u32[]{:S(2)}, u32[]{:S(2)}) async-start(f32[16,64,128]{2,1,0:T(8,128)} %broadcast_in_dim.5), calls=%async_computation.1 | async-start | bytes 1048576 | tf_op jit(solution)/shard_map/all_to_all | solution.py:319
  207.8 12.3 %copy-start.1 = (f32[16,8,1024]{2,1,0:T(8,128)}, f32[16,8,1024]{2,1,0:T(8,128)S(1)}, u32[]{:S(2)}) copy-start(f32[16,8,1024]{2,1,0:T(8,128)S(1)} %broadcast_select_fusion.refs_2_.side) | copy-start | bytes 1572868
  208.6 11.3 %collective-permute-start.4 = (f32[8,8,1024]{2,1,0:T(8,128)}, f32[8,8,1024]{2,1,0:T(8,128)S(1)}, u32[]{:S(2)}, u32[]{:S(2)}) collective-permute-start(f32[8,8,1024]{2,1,0:T(8,128)} %pad_maximum_fusion), channel_id=1, source_target_pairs={{0,4},{4,8},{8,12},{12,16},{16,20},{20,24},{24,28},{28,32},{32,36}... | collective-permute-start | bytes 786440 | tf_op jit(solution)/shard_map/ppermute | solution.py:187
  209.4 10.6 %collective-permute-start.5 = (f32[8,8,1024]{2,1,0:T(8,128)}, f32[8,8,1024]{2,1,0:T(8,128)}, u32[]{:S(2)}, u32[]{:S(2)}) collective-permute-start(f32[8,8,1024]{2,1,0:T(8,128)} %pad_maximum_fusion.1), channel_id=1, source_target_pairs={{0,124},{4,0},{8,4},{12,8},{16,12},{20,16},{24,20},{28,24},{32,28}... | collective-permute-start | bytes 786440 | tf_op jit(solution)/shard_map/ppermute | solution.py:187
  214.4 5.5 %collective-permute-start.6 = (f32[304,128]{1,0:T(8,128)}, f32[304,128]{1,0:T(8,128)}, u32[]{:S(2)}, u32[]{:S(2)}) collective-permute-start(f32[304,128]{1,0:T(8,128)} %pad_maximum_fusion.2.f0), channel_id=1, source_target_pairs={{0,1},{1,2},{2,3},{3,0},{4,5},{5,6},{6,7},{7,4},{8,9},{9,10},{10,1... | collective-permute-start | bytes 466952 | tf_op jit(solution)/shard_map/ppermute | solution.py:352
  220.0 0.7 copy-start.6
  220.0 0.9 copy-start.2
  220.0 1.6 copy-start
  230.9 12.8 %collective-permute-start.11 = (f32[8,8,1024]{2,1,0:T(8,128)}, f32[8,8,1024]{2,1,0:T(8,128)S(1)}, u32[]{:S(2)}, u32[]{:S(2)}) collective-permute-start(f32[8,8,1024]{2,1,0:T(8,128)} %get-tuple-element.29), channel_id=1, source_target_pairs={{1,0},{2,1},{3,2},{5,4},{6,5},{7,6},{9,8},{10,9},{11,10},{13,12},{... | collective-permute-start | bytes 786440 | tf_op jit(solution)/shard_map/ppermute | solution.py:191
  236.6 8.5 %collective-permute-start.12 = (f32[8,8,1024]{2,1,0:T(8,128)}, f32[8,8,1024]{2,1,0:T(8,128)S(1)}, u32[]{:S(2)}, u32[]{:S(2)}) collective-permute-start(f32[8,8,1024]{2,1,0:T(8,128)} %get-tuple-element.30), channel_id=1, source_target_pairs={{0,1},{1,2},{2,3},{4,5},{5,6},{6,7},{8,9},{9,10},{10,11},{12,13},{... | collective-permute-start | bytes 786440 | tf_op jit(solution)/shard_map/ppermute | solution.py:191
  238.5 18.3 %collective-permute-start.9 = (f32[3,64,1024]{2,1,0:T(8,128)}, f32[3,64,1024]{2,1,0:T(8,128)S(1)}, u32[]{:S(2)}, u32[]{:S(2)}) collective-permute-start(f32[3,64,1024]{2,1,0:T(8,128)} %get-tuple-element.27), channel_id=1, source_target_pairs={{0,4},{4,8},{8,12},{12,16},{16,20},{20,24},{24,28},{28,32},{32,36}... | collective-permute-start | bytes 2359304 | tf_op jit(solution)/shard_map/ppermute | solution.py:187
  238.6 18.2 %collective-permute-start.10 = (f32[3,64,1024]{2,1,0:T(8,128)}, f32[3,64,1024]{2,1,0:T(8,128)S(1)}, u32[]{:S(2)}, u32[]{:S(2)}) collective-permute-start(f32[3,64,1024]{2,1,0:T(8,128)} %get-tuple-element.28), channel_id=1, source_target_pairs={{0,124},{4,0},{8,4},{12,8},{16,12},{20,16},{24,20},{28,24},{32,28}... | collective-permute-start | bytes 2359304 | tf_op jit(solution)/shard_map/ppermute | solution.py:187
  245.2 11.6 %copy-start.5 = (f32[8,8,1024]{2,1,0:T(8,128)}, f32[8,8,1024]{2,1,0:T(8,128)S(1)}, u32[]{:S(2)}) copy-start(f32[8,8,1024]{2,1,0:T(8,128)S(1)} %broadcast_select_fusion.1.sside) | copy-start | bytes 786436
  245.2 9.2 %collective-permute-start.14 = (f32[3,8,1024]{2,1,0:T(8,128)S(1)}, f32[3,8,1024]{2,1,0:T(8,128)S(1)}, u32[]{:S(2)}, u32[]{:S(2)}) collective-permute-start(f32[3,8,1024]{2,1,0:T(8,128)S(1)} %get-tuple-element.36), channel_id=1, source_target_pairs={{0,124},{4,0},{8,4},{12,8},{16,12},{20,16},{24,20},{28,24},{32,28}... | collective-permute-start | bytes 294920 | tf_op jit(solution)/shard_map/ppermute | solution.py:187
  249.4 7.4 %collective-permute-start.13 = (f32[3,8,1024]{2,1,0:T(8,128)S(1)}, f32[3,8,1024]{2,1,0:T(8,128)S(1)}, u32[]{:S(2)}, u32[]{:S(2)}) collective-permute-start(f32[3,8,1024]{2,1,0:T(8,128)S(1)} %get-tuple-element.37), channel_id=1, source_target_pairs={{0,4},{4,8},{8,12},{12,16},{16,20},{20,24},{24,28},{28,32},{32,36}... | collective-permute-start | bytes 294920 | tf_op jit(solution)/shard_map/ppermute | solution.py:187
  254.4 2.4 copy-start.10
  256.8 0.6 copy-start.11
  256.8 1.0 copy-start.8
  256.8 1.1 copy-start.9

commit v3 on v2

v3 whole, which is shorter than its diff:
```python
import functools
import math

import jax
import jax.numpy as jnp
from jax import lax
from jax.experimental import pallas as pl
from jax.experimental.pallas import tpu as pltpu
from jax.sharding import PartitionSpec as P

SWEEPS = 4
ITERS = 4
OMEGA = 0.9
AXIAL = 0.25
STEFAN = 1.0
SHRINK = 0.3
COUPLE = 0.2

F32 = jnp.float32
I32 = jnp.int32
BF16 = jnp.bfloat16

T, R, Z = 8, 64, 1024
H = 4
TE = T + 2 * H
RE = R + 8
RT = RE // 8
GROUPS, SLOTS, NB, BS = 4, 1024, 128, 16
FT = 5
UNROLL = 16
AZIM = ("y", "z", "core")


def iota(shape, dim):
    return lax.broadcasted_iota(I32, shape, dim)


def pieces(x):
    h = x.astype(BF16)
    rest = x - h.astype(F32)
    m = rest.astype(BF16)
    return h, m, (rest - m.astype(F32)).astype(BF16)


def at8(i):
    return pl.ds(pl.multiple_of(i * 8, 8), 8)


def flux_kernel(cnt, row, heat_any, lane, vert, share, out, heat, diff, picked, sems):
    loads = [pltpu.make_async_copy(heat_any.at[t], heat.at[t], sems.at[t]) for t in range(T)]
    for c in loads:
        c.start()

    for t in range(T):
        loads[t].wait()

        def make(q, _):
            x = heat[t, at8(q), :]
            d = pltpu.roll(x, Z - 1, 1) - x
            for zc in range(8):
                diff[at8((t * 8 + q) * 8 + zc), :] = d[:, zc * 128:(zc + 1) * 128]
            return 0

        lax.fori_loop(0, R // 8, make, 0, unroll=4)
    for j in range(GROUPS):
        def body(b, _):
            base = pl.multiple_of(b * UNROLL, UNROLL)
            for u in range(UNROLL):
                picked[pl.ds(base + u, 1), :] = diff[pl.ds(row[j, base + u], 1), :]
            return 0

        lax.fori_loop(0, (cnt[j] + UNROLL - 1) // UNROLL, body, 0)
        vals = []
        for kb in range(SLOTS // 128):
            cut = slice(kb * 128, (kb + 1) * 128)
            hit = iota((128, 128), 0) == lane[j:j + 1, cut]
            vals.append(jnp.sum(jnp.where(hit, picked[cut, :].T, 0.0), axis=0, keepdims=True))
        live = iota((1, SLOTS), 1) < cnt[j]
        val = jnp.where(live, share[j:j + 1, :] * jnp.concatenate(vals, axis=1), 0.0)
        v = vert[j:j + 1, :]
        inner = iota((BS, SLOTS), 0) == (v & (BS - 1))
        left = jnp.concatenate(
            [jnp.where(inner, p.astype(F32), 0.0).astype(BF16) for p in pieces(val)], axis=0)
        right = jnp.where(iota((NB, SLOTS), 0) == (v >> 4), 1.0, 0.0).astype(BF16)
        o = lax.dot_general(left, right, (((1,), (1,)), ((), ())), preferred_element_type=F32)
        o = o[:BS] + o[BS:2 * BS] + o[2 * BS:]
        for n in range(out.shape[0]):
            out[n, j * BS:(j + 1) * BS, :] = o


def front_kernel(kref, cnt, row, parts, cross, lane, vert, share, pred_any, *refs):
    front_body(kref, cnt, row, parts, cross, lane, vert, share, pred_any, *refs[5:])


def front_body(kref, cnt, row, parts, cross, lane, vert, share, pred_any, src_any, sup, sdown, srup, srdown,
               hout, front, gtab, height, terms, flux, pred, zeros, flip, sems, zsems, *acc):
    k = kref[0]
    load = pltpu.make_async_copy(pred_any, pred, sems.at[0])
    load.start()
    params_in = pltpu.make_async_copy(cross.at[:, pl.ds(2 * T, FT)], front, sems.at[6])
    params_in.start()
    zeros[...] = jnp.zeros(zeros.shape, F32)
    count = zeros.shape[0]
    clears = [pltpu.make_async_copy(zeros, a.at[pl.ds(n * count, count)], zsems.at[m, n])
              for m, a in enumerate(acc) for n in range(T * R * 8 // count)]
    for c in clears:
        c.start()
    sums = parts[0]
    for n in range(1, parts.shape[0]):
        sums = sums + parts[n]
    flux[...] = sums
    params_in.wait()

    def held(g, n):
        return jnp.concatenate([front[g, m // 8, :, m % 8 * 128:m % 8 * 128 + 128]
                                for m in (2 * n, 2 * n + 1)], axis=0)

    def neighbours(h):
        last = jnp.concatenate([h[g][BS - 1:BS, :] for g in range(GROUPS)], axis=0)
        first = jnp.concatenate([h[g][0:1, :] for g in range(GROUPS)], axis=0)
        zrow = jnp.zeros((1, 128), F32)
        lr = pltpu.roll(last, 1, 1)
        fr = pltpu.roll(first, 127, 1)
        col = iota((GROUPS, 128), 1)
        lr = jnp.where(col == 0, jnp.concatenate([zrow, lr[:-1]], axis=0), lr)
        fr = jnp.where(col == 127, jnp.concatenate([fr[1:], zrow], axis=0), fr)
        down = [jnp.concatenate([lr[g:g + 1], h[g][:BS - 1]], axis=0) for g in range(GROUPS)]
        up = [jnp.concatenate([h[g][1:], fr[g:g + 1]], axis=0) for g in range(GROUPS)]
        return down, up

    prior = [held(g, BS) for g in range(GROUPS)]
    h = list(prior)
    for _ in range(ITERS):
        down, up = neighbours(h)
        for g in range(GROUPS):
            applied = (2.0 + held(g, BS + 1)) * h[g] - down[g] - up[g]
            res = held(g, BS + 2) + COUPLE * flux[g * BS:(g + 1) * BS, :] - applied
            h[g] = h[g] + jnp.concatenate(
                [jnp.sum(held(g, i) * res, axis=0, keepdims=True) for i in range(BS)], axis=0)
    down, up = neighbours(h)
    for g in range(GROUPS):
        slope = up[g] - down[g]
        growth = h[g] - prior[g]
        height[g] = h[g]
        gtab[g] = (flux[g * BS:(g + 1) * BS, :] - STEFAN * growth) * jnp.sqrt(1.0 + slope * slope)
    for j in range(GROUPS):
        v = vert[j:j + 1, :]
        right = jnp.where(iota((NB, SLOTS), 0) == (v >> 4), 1.0, 0.0).astype(BF16)
        x = jnp.dot(jnp.concatenate(pieces(gtab[j]), axis=0), right, preferred_element_type=F32)
        x = x[:BS] + x[BS:2 * BS] + x[2 * BS:]
        inner = iota((BS, SLOTS), 0) == (v & (BS - 1))
        term = jnp.sum(jnp.where(inner, x, 0.0), axis=0, keepdims=True) * share[j:j + 1, :]
        term = jnp.where(iota((1, SLOTS), 1) < cnt[j], term, 0.0)
        for kb in range(SLOTS // 128):
            cut = slice(kb * 128, (kb + 1) * 128)
            hit = iota((128, 128), 0) == lane[j:j + 1, cut]
            terms[j, cut, :] = jnp.where(hit, term[:, cut], 0.0).T
    for c in clears:
        c.wait()
    most = jnp.maximum(jnp.maximum(cnt[0], cnt[1]), jnp.maximum(cnt[2], cnt[3]))

    def add(b, _):
        for u in range(UNROLL):
            s = b * UNROLL + u
            for j in range(GROUPS):
                at = pl.ds(row[j, s], 1)
                acc[j][at, :] = acc[j][at, :] + terms[j, pl.ds(s, 1), :]
        return 0

    lax.fori_loop(0, (most + UNROLL - 1) // UNROLL, add, 0)

    load.wait()
    src = pred
    sends = []

    def send(m, a, b):
        sends.append(pltpu.make_async_copy(a, b, sems.at[m]))
        sends[-1].start()

    for d in range(T):
        def finish(q, _):
            for zc in range(8):
                a = at8((d * 8 + q) * 8 + zc)
                s = (acc[0][a, :] + acc[1][a, :]) + (acc[2][a, :] + acc[3][a, :])
                cut = slice(zc * 128, (zc + 1) * 128)
                src[d, at8(q), cut] = pred[d, at8(q), cut] + SHRINK * s
            return 0

        lax.fori_loop(0, R // 8, finish, 0, unroll=2)
        if d == H - 2:
            send(1, src.at[pl.ds(0, H - 1)], sdown)
    send(2, src.at[pl.ds(T - H + 1, H - 1)], sup)
    send(3, src.at[:, pl.ds(R - 8, 8)], srup)
    send(4, src.at[:, pl.ds(0, 8)], srdown)
    send(5, src, src_any)
    flip[...] = jnp.concatenate([height[k], jnp.zeros((128 - BS, 128), F32)], axis=0).T
    nodes = flip[pl.ds(0, BS, stride=8), :]
    for m in range(1, 8):
        nodes = nodes + pltpu.roll(flip[pl.ds(m, BS, stride=8), :], m * BS, 1)
    hout[...] = nodes
    for c in sends:
        c.wait()


def pack_kernel(kref, load_any, beta_any, solve, prior, weight, jump, label, up, down, cross,
                row, lane, load, beta, front, flip, isems, osems, fsems):
    k = kref[0]
    loads = [pltpu.make_async_copy(a, b, isems.at[n])
             for n, (a, b) in enumerate(((load_any, load), (beta_any, beta)))]
    for c in loads:
        c.start()
    lab = label[...]
    hi = lab >> 10
    low = hi + (lab & 1023)
    carry = (low >= Z - 1).astype(I32)
    column, axial = hi + carry, low - (Z - 1) * carry
    row[...] = ((column >> 3) << 6) + ((axial >> 7) << 3) + (column & 7)
    lane[...] = axial & 127

    def keep(n, x):
        front[n // 8, :, n % 8 * 128:n % 8 * 128 + 128] = x

    for n in range(FT * 8):
        keep(n, solve[n * 8:n * 8 + 8, :] if n < BS * BS // 8 else jnp.zeros((8, 128), F32))
    for n, x in enumerate((prior, weight, jump)):
        for m in range(8):
            flip[pl.ds(m, BS, stride=8), :] = pltpu.roll(x[...], (128 - m * BS) % 128, 1)
        turned = flip[...].T
        keep(BS * BS // 8 + 2 * n, turned[:8, :])
        keep(BS * BS // 8 + 2 * n + 1, turned[8:16, :])
    sends = []
    for d in range(GROUPS):
        sends.append(pltpu.make_async_copy(front, cross.at[d, pl.ds(2 * T, FT)], fsems.at[d]))
        sends[-1].start()
    count = 0
    for n, f in enumerate((load, beta)):
        loads[n].wait()
        pairs = [(f.at[pl.ds(T - H, H)], up.at[pl.ds(n * H, H)]), (f.at[pl.ds(0, H)], down.at[pl.ds(n * H, H)])]
        for d in range(GROUPS):
            first = pl.multiple_of(jnp.where(d < k, 0, R - 8), 8)
            pairs.append((f.at[:, pl.ds(first, 8)], cross.at[d, pl.ds(n * T, T)]))
        for a, b in pairs:
            sends.append(pltpu.make_async_copy(a, b, osems.at[count]))
            sends[-1].start()
            count += 1
    for c in sends:
        c.wait()


def side_kernel(kref, cross, side, eup, edown, below, sems):
    k = kref[0]
    loads = [pltpu.make_async_copy(cross.at[jnp.minimum(k + 1, GROUPS - 1), pl.ds(0, 2 * T)], side, sems.at[0]),
             pltpu.make_async_copy(cross.at[jnp.maximum(k - 1, 0), pl.ds(0, 2 * T)], below, sems.at[1])]
    for c in loads:
        c.start()
    for c in loads:
        c.wait()
    first = iota((8, Z), 0) < 4
    for t in range(2 * T):
        above_t = jnp.where(k < GROUPS - 1, side[t], 0.0)
        below_t = jnp.where(k > 0, below[t], 0.0)
        side[t] = jnp.where(first, above_t, below_t)
    for n in range(2):
        eup[n * H:(n + 1) * H] = side[n * T + T - H:n * T + T]
        edown[n * H:(n + 1) * H] = side[n * T:n * T + H]


def shift_azim(x, d):
    return lax.ppermute(x, AZIM, [(i, (i + d) % 32) for i in range(32)])


def shift_rad(x, d):
    return lax.ppermute(x, "rad", [(i, i + d) for i in range(4) if 0 <= i + d < 4])


def ring_tile(from_above, from_below):
    return jnp.where(iota(from_above.shape, 1) < 4, from_above, from_below)


def wide(x):
    return jnp.concatenate([x] * (Z // 128), axis=1)


def sweep_kernel(kref, load, beta_in, lo, hi, side, clo, chi, src, slo, shi, sside, sclo, schi,
                 out, pa, pb, beta, th, rr, zz, ww, ss, rads, sems):
    k = kref[0]
    rows, ring = pl.ds(0, R), pl.ds(R, 8)
    half = T // 2

    def planes(own, tile_own, low, tile_low, high, tile_high, first):
        return [(low, tile_low, first, H - first), (own.at[pl.ds(0, half)], tile_own.at[pl.ds(0, half)], H, half),
                (own.at[pl.ds(half, half)], tile_own.at[pl.ds(half, half)], H + half, half),
                (high, tile_high, H + T, H - first)]

    def both(x, n, count):
        return x.at[pl.ds(n * count, count)]

    fields = [(ref, planes(own, both(side, n, T), both(lo, n, H), both(clo, n, H), both(hi, n, H), both(chi, n, H), 0))
              for ref, own, n in ((beta, beta_in, 1), (pa, load, 0))]
    fields.append((ss, planes(src, sside, slo, sclo, shi, schi, 1)))
    waits = []
    for g in range(4):
        cs = []
        for f, (ref, parts) in enumerate(fields):
            main, tile, first, count = parts[g]
            cs.append(pltpu.make_async_copy(main, ref.at[pl.ds(first, count), rows], sems.at[g, f, 0]))
            cs.append(pltpu.make_async_copy(tile, ref.at[pl.ds(first, count), ring], sems.at[g, f, 1]))
        for c in cs:
            c.start()
        waits.append(cs)
    sub, lanes = iota((8, 128), 0), iota((8, 128), 1)
    top, bottom, last_lane, first_lane = sub == 7, sub == 0, lanes == 127, lanes == 0
    angular = (256 / (2.0 * math.pi)) ** 2
    for it in range(RT):
        gi = k * R + (it * 8 + sub if it < RT - 1 else jnp.where(sub < 4, R + sub, sub - 8))
        ra = 0.25 * 256 + gi.astype(F32) + 0.5
        rads[0, it] = ra
        rads[1, it] = (0.5 * angular) / ra
        rads[2, it] = jnp.where((gi >= 0) & (gi < 255), 0.5 * (ra + 0.5), 0.0)
    nothing = jnp.zeros((8, 128), F32)
    columns = range(Z // 128)

    def cut(it):
        it = it % RT
        return slice(it * 8, it * 8 + 8)

    def vec(ref, t, it, v):
        return ref[t, cut(it), v * 128:v * 128 + 128]

    def put(ref, t, it, v, x):
        ref[t, cut(it), v * 128:v * 128 + 128] = x

    def up_row(x):
        return pltpu.roll(x, 7, 0)

    def down_row(x):
        return pltpu.roll(x, 1, 0)

    def next_lane(ref, t, it, v, cur):
        nxt = pltpu.roll(vec(ref, t, it, v + 1), 127, 1) if v + 1 < Z // 128 else cur
        return jnp.where(last_lane, nxt, cur), nxt

    def relaxed(old, t, it, v, p, pz, pu, prev, zprev, tu, td, r, z, w, s):
        acc = (tu * vec(old, t + 1, it, v) + td * vec(old, t - 1, it, v)) + r * pu
        rp = down_row(r * p)
        acc = acc + jnp.where(bottom, prev, rp)
        zu, pz = next_lane(old, t, it, v, pz)
        zp = pltpu.roll(z * p, 1, 1)
        acc = acc + (z * zu + jnp.where(first_lane, zprev, zp))
        return (1.0 - OMEGA) * p + w * (acc - s), pz, rp, zp

    def first_sweep(t, _):
        last = RT - 1
        bup = [up_row(vec(beta, t, 0, v)) for v in columns]
        pup = [up_row(vec(pa, t, 0, v)) for v in columns]
        fprev, prev = [], []
        for v in columns:
            b = vec(beta, t, last, v)
            face = (b + jnp.where(top, bup[v], up_row(b))) * rads[2, last]
            fprev.append(down_row(face))
            prev.append(down_row(face * vec(pa, t, last, v)))
        for it in range(RT):
            ra, ang, rad = rads[0, it], rads[1, it], rads[2, it]
            axi = (0.5 * AXIAL) * ra
            bz = pltpu.roll(vec(beta, t, it, 0), 127, 1)
            pz = pltpu.roll(vec(pa, t, it, 0), 127, 1)
            zfprev = zprev = nothing
            for v in columns:
                b, p = vec(beta, t, it, v), vec(pa, t, it, v)
                nb, np_ = up_row(vec(beta, t, it + 1, v)), up_row(vec(pa, t, it + 1, v))
                tu = (b + vec(beta, t + 1, it, v)) * ang
                td = vec(th, t - 1, it, v)
                r = (b + jnp.where(top, nb, bup[v])) * rad
                froll = down_row(r)
                other = jnp.where(bottom, fprev[v], froll)
                bu, bz = next_lane(beta, t, it, v, bz)
                zf = (b + bu) * axi
                z = zf
                if v == Z // 128 - 1:
                    zf = jnp.where(last_lane, 2.0 * (b * axi), zf)
                    z = jnp.where(last_lane, 0.0, zf)
                zr = pltpu.roll(z, 1, 1)
                d = (tu + td) + (r + other) + (zf + jnp.where(first_lane, zfprev, zr))
                if it == last:
                    d = jnp.where(d > 0.0, d, 1.0)
                w = pl.reciprocal(d, approx=True)
                w = w * (2.0 - d * w)
                w = (w * (2.0 - d * w)) * OMEGA
                sc = vec(ss, t, it, v) * ra
                put(th, t, it, v, tu)
                put(rr, t, it, v, r)
                put(zz, t, it, v, z)
                put(ww, t, it, v, w)
                put(ss, t, it, v, sc)
                pu = jnp.where(top, np_, pup[v])
                new, pz, prev[v], zprev = relaxed(pa, t, it, v, p, pz, pu, prev[v], zprev, tu, td, r, z, w, sc)
                put(pb, t, it, v, new)
                bup[v], pup[v], fprev[v], zfprev = nb, np_, froll, zr
        return 0

    def sweep(old, new, t, tiles, shift):
        pup = [up_row(vec(old, t, 0, v)) for v in columns]
        prev = [down_row(vec(rr, t, -1, v) * vec(old, t, -1, v)) for v in columns]
        for it in range(tiles):
            pz = pltpu.roll(vec(old, t, it, 0), 127, 1)
            zprev = nothing
            for v in columns:
                p = vec(old, t, it, v)
                np_ = up_row(vec(old, t, it + 1, v))
                pu = jnp.where(top, np_, pup[v])
                x, pz, prev[v], zprev = relaxed(
                    old, t, it, v, p, pz, pu, prev[v], zprev, vec(th, t, it, v), vec(th, t - 1, it, v),
                    vec(rr, t, it, v), vec(zz, t, it, v), vec(ww, t, it, v), vec(ss, t, it, v))
                put(new, t - shift, it, v, x)
                pup[v] = np_
        return 0

    ends = (H - 1, H + half - 1, H + T - 1, TE - 1)
    start = 1
    for g in range(4):
        for c in waits[g]:
            c.wait()
        if g == 0:
            for it in range(RT):
                th[0, cut(it), :] = (beta[0, cut(it), :] + beta[1, cut(it), :]) * wide(rads[1, it])
        lax.fori_loop(start, ends[g], first_sweep, 0)
        start = ends[g]
    lax.fori_loop(2, TE - 2, lambda t, _: sweep(pb, pa, t, RT, 0), 0)
    lax.fori_loop(3, TE - 3, lambda t, _: sweep(pa, pb, t, RT, 0), 0)
    lax.fori_loop(4, TE - 4, lambda t, _: sweep(pb, out, t, RT - 1, H), 0)


def from_all(copies, axes):
    return lax.all_to_all(copies, axes, 0, 0)


def sum_kernel(parts, *refs):
    out = refs[-1]
    s = parts[0]
    for n in range(1, parts.shape[0]):
        s = s + parts[n]
    for n in range(out.shape[0]):
        out[n] = s


VM = pl.BlockSpec(memory_space=pltpu.VMEM)
SM = pl.BlockSpec(memory_space=pltpu.SMEM)
ANY = pl.BlockSpec(memory_space=pl.ANY)


def params(mib):
    return pltpu.CompilerParams(vmem_limit_bytes=mib << 20)


def cost(us):
    return pl.CostEstimate(flops=1000, bytes_accessed=us * 3000000, transcendentals=0)


def per_device(load, outflow, beta, heat, label, vertex, share, tally, prior, weight, jump, solve):
    label = label.reshape(GROUPS, SLOTS)
    vertex = vertex.reshape(GROUPS, SLOTS)
    share = share.reshape(GROUPS, SLOTS)
    tally = tally.reshape(GROUPS)
    kidx = lax.axis_index("rad").astype(I32).reshape(1)
    nodes = lambda v: v.reshape(BS, NB)

    shape = lambda *d: jax.ShapeDtypeStruct(d, F32)
    slot = jax.ShapeDtypeStruct((GROUPS, SLOTS), I32)
    plane = lambda n: shape(n, R, Z)
    tile = lambda n: shape(n, 8, Z)
    block = pltpu.VMEM((T, R, Z), F32)
    up, down, cross, row, lane = pl.pallas_call(
        pack_kernel,
        out_shape=(plane(2 * H), plane(2 * H), shape(GROUPS, 2 * T + FT, 8, Z), slot, slot),
        in_specs=[SM] + [ANY] * 2 + [VM] * 5, out_specs=(ANY,) * 3 + (VM,) * 2,
        scratch_shapes=[block, block, pltpu.VMEM((FT, 8, Z), F32), pltpu.VMEM((128, 128), F32),
                        pltpu.SemaphoreType.DMA((2,)), pltpu.SemaphoreType.DMA((12,)),
                        pltpu.SemaphoreType.DMA((GROUPS,))],
        compiler_params=params(10), cost_estimate=cost(4), name="pack",
    )(kidx, load, beta, solve.reshape(BS * BS, NB), nodes(prior), nodes(weight), nodes(jump), label)
    lo, hi = shift_azim(up, 1), shift_azim(down, -1)
    cross = from_all(cross, "rad")

    partial = pl.pallas_call(
        flux_kernel, out_shape=shape(8, GROUPS * BS, NB),
        in_specs=[SM, SM, ANY, VM, VM, VM], out_specs=VM,
        scratch_shapes=[block, pltpu.VMEM((T * R * 8, 128), F32), pltpu.VMEM((SLOTS, 128), F32),
                        pltpu.SemaphoreType.DMA((T,))],
        compiler_params=params(12), cost_estimate=cost(10), name="flux",
    )(tally, row, heat, lane, vertex, share)
    side, eup, edown = pl.pallas_call(
        side_kernel, out_shape=(tile(2 * T), tile(2 * H), tile(2 * H)),
        in_specs=[SM, ANY], out_specs=(VM,) * 3,
        scratch_shapes=[pltpu.VMEM((2 * T, 8, Z), F32), pltpu.SemaphoreType.DMA((2,))],
        compiler_params=params(4), cost_estimate=cost(2), name="side",
    )(kidx, cross)
    clo, chi = shift_azim(eup, 1), shift_azim(edown, -1)
    near = pl.pallas_call(
        sum_kernel, out_shape=shape(16, GROUPS * BS, NB),
        in_specs=[VM, ANY], out_specs=VM, compiler_params=params(4), name="near",
    )(from_all(partial, ("z", "core")), side)
    flux = from_all(near, ("y", "rad"))
    source, sup, sdown, srup, srdown, height = pl.pallas_call(
        front_kernel,
        out_shape=(plane(T), plane(H - 1), plane(H - 1), tile(T), tile(T), shape(BS, NB)),
        in_specs=[SM, SM, SM, VM, ANY, VM, VM, VM] + [ANY] * 6, out_specs=(ANY,) * 5 + (VM,),
        scratch_shapes=[pltpu.VMEM((GROUPS, FT, 8, Z), F32),
                        pltpu.VMEM((GROUPS, BS, NB), F32), pltpu.VMEM((GROUPS, BS, NB), F32),
                        pltpu.VMEM((GROUPS, SLOTS, 128), F32), pltpu.VMEM((GROUPS * BS, NB), F32),
                        block, pltpu.VMEM((R * 8, 128), F32), pltpu.VMEM((128, 128), F32),
                        pltpu.SemaphoreType.DMA((7,)), pltpu.SemaphoreType.DMA((GROUPS, T))]
        + [pltpu.VMEM((T * R * 8, 128), F32)] * GROUPS,
        compiler_params=params(20), cost_estimate=cost(10), name="front",
    )(kidx, tally, row, flux, cross, lane, vertex, share, outflow, lo, hi, side, clo, chi)
    slo, shi = shift_azim(sup, 1), shift_azim(sdown, -1)
    sside = ring_tile(shift_rad(srdown, -1), shift_rad(srup, 1))
    sclo, schi = shift_azim(sside[T - H + 1:], 1), shift_azim(sside[:H - 1], -1)
    ext = pltpu.VMEM((TE, RE, Z), F32)
    pressure = pl.pallas_call(
        sweep_kernel, out_shape=plane(T),
        in_specs=[SM] + [ANY] * 13, out_specs=VM,
        scratch_shapes=[ext] * 8 + [pltpu.VMEM((3, RT, 8, 128), F32), pltpu.SemaphoreType.DMA((4, 3, 2))],
        compiler_params=params(46), cost_estimate=cost(20), name="sweeps",
    )(kidx, load, beta, lo, hi, side, clo, chi, source, slo, shi, sside, sclo, schi)
    return pressure, height.reshape(NB * BS)


def solution(mesh):
    fine = jax.sharding.Mesh(mesh.devices.reshape(4, 4, 2, 4), AZIM + ("rad",))
    cells = P(AZIM, "rad", None)
    slots = P(AZIM, "rad", None, None)
    return jax.shard_map(
        per_device,
        mesh=fine,
        in_specs=(cells, cells, cells, cells, slots, slots, slots, cells,
                  P("rad"), P("rad"), P("rad"), P(None, None, "rad")),
        out_specs=(cells, P("rad")),
        check_vma=False,
    )
```

time: 287 us -> 147 us (0.51)
  Pallas kernels: 207 us -> 40.6 us
  waiting for transfers between devices: 12 us -> 35.3 us
  local copies, waits for them, and re-layouts: 9.22 us -> 22.4 us
  starting transfers between devices: 51.8 us -> 45.1 us
  other arithmetic: 5.17 us -> 0.1 us
    pallas_call x3 -> x4, Pallas kernels: 169 us -> 10.1 us  [the longest x1 7.91 us: per_device(): pl.pallas_call(flux_kernel, out_shape=shape(8, GROUPS * BS, NB), in_specs...]
    all_to_all x2 -> x3, waiting for transfers between devices: 0.6 us -> 22.9 us  [from_all(): return lax.all_to_all(copies, axes, 0, 0)]
    unnamed x32 -> x58, local copies, waits for them, and re-layouts: 4.19 us -> 22.4 us
    ppermute x3 -> x0, starting transfers between devices: 6.23 us -> none  [per_device(): lax.ppermute(front, 'rad', [(i, (i + s) % 4) for i in range(4)])]
    ppermute x4 -> x2, starting transfers between devices: 13.4 us -> 7.61 us  [shift_rad(): lax.ppermute(x, 'rad', [(i, i + d) for i in range(4) if 0 <= i + d < 4])]
    pallas_call x1, Pallas kernels: 27.9 us -> 22.2 us  [per_device(): pl.pallas_call(sweep_kernel, out_shape=plane(T), in_specs=[SM] + [ANY] *...]
    ppermute x8, waiting for transfers between devices: 5.89 us -> 11.2 us  [shift_azim(): return lax.ppermute(x, AZIM, [(i, (i + d) % 32) for i in range(32)])]
    all_to_all x2 -> x3, starting transfers between devices: 11.7 us -> 16.8 us  [from_all(): return lax.all_to_all(copies, axes, 0, 0)]
  transfers between devices with their start and end apart: 17 -> 13, of which waited for: 5 -> 5; matrix products, arithmetic and copies ran while one was open for 4% -> 0% of each run, Pallas kernels for 3% -> 6%
where the time goes in v3:
time: 147 us; the launch traced here: 145 us
  starting transfers between devices  45.1 us (31%)
  Pallas kernels  40.6 us (28%)
  waiting for transfers between devices  35.3 us (24%)
  local copies, waits for them, and re-layouts  22.4 us (15%)
    all_to_all x3, waiting for transfers between devices, from_all(): return lax.all_to_all(copies, axes, 0, 0)  22.9 us
    unnamed x58, local copies, waits for them, and re-layouts  22.4 us
    pallas_call x1, Pallas kernels, per_device(): pl.pallas_call(sweep_kernel, out_shape=plane(T), in_specs=[SM] + [ANY] *...  22.2 us
    ppermute x8, starting transfers between devices, shift_azim(): return lax.ppermute(x, AZIM, [(i, (i + d) % 32) for i in range(32)])  20.7 us
    all_to_all x3, starting transfers between devices, from_all(): return lax.all_to_all(copies, axes, 0, 0)  16.8 us
    ppermute x8, waiting for transfers between devices, shift_azim(): return lax.ppermute(x, AZIM, [(i, (i + d) % 32) for i in range(32)])  11.2 us
    pallas_call x1, Pallas kernels, per_device(): pl.pallas_call(front_kernel, out_shape=(plane(T), plane(H - 1), plane(H -...  8.3 us
    pallas_call x1, Pallas kernels, per_device(): pl.pallas_call(flux_kernel, out_shape=shape(8, GROUPS * BS, NB), in_specs...  7.91 us
  transfers between devices with their start and end apart: 13, of which 5 were waited for; matrix products, arithmetic and copies ran while one was open for 0% of the time, Pallas kernels for 6%

profile of v3, /device:TPU:2, one launch (start us, length us, event | category | flops | bytes accessed | tf_op | source)
XLA Modules:
  0.0 144.5 jit_solution(15382165830674397833)
XLA Ops:
  0.6 0.0 copy-start
  0.6 1.6 %copy-done = f32[8,64,1024]{2,1,0:T(8,128)S(1)} copy-done((f32[8,64,1024]{2,1,0:T(8,128)S(1)}, f32[8,64,1024]{2,1,0:T(8,128)}, u32[]{:S(2)}) %copy-start) | copy-done | bytes 2097176
  2.2 1.6 %copy-done.2 = f32[8,64,1024]{2,1,0:T(8,128)S(1)} copy-done((f32[8,64,1024]{2,1,0:T(8,128)S(1)}, f32[8,64,1024]{2,1,0:T(8,128)}, u32[]{:S(2)}) %copy-start.2) | copy-done | bytes 2097176
  3.8 0.9 copy-done.11
  4.7 0.7 copy-done.19
  5.4 0.7 copy-done.20
  6.1 0.7 copy-done.21
  6.8 0.7 copy-done.22
  7.5 1.9 %pack.1 = (f32[8,64,1024]{2,1,0:T(8,128)S(1)}, f32[8,64,1024]{2,1,0:T(8,128)S(1)}, f32[4,21,8,1024]{3,2,1,0:T(8,128)S(1)}, s32[4,1024]{1,0:T(4,128)S(1)}, s32[4,1024]{1,0:T(4,128)S(1)}) custom-call(s32[1]{0:T(128)} %bitcast.kref, f32[8,64,1024]{2,1,0:T(8,128)S(1)} %copy-done, f32[8,64,1024]{2,1,0:T(8,128)S(1)} %copy-done.2, f32[256,128]{1,0:T(8,128)S(1)} %bitcast.10, ...), custom_call_target="tpu_custom_call" | custom-call | flops 1000 | bytes 12000000 | tf_op jit(solution)/shard_map/pack/pallas_call | solution.py:472
  9.5 0.0 copy-start.4
  9.5 1.5 %copy-done.4 = f32[4,21,8,1024]{3,2,1,0:T(8,128)} copy-done((f32[4,21,8,1024]{3,2,1,0:T(8,128)}, f32[4,21,8,1024]{3,2,1,0:T(8,128)S(1)}, u32[]{:S(2)}) %copy-start.4) | copy-done | bytes 2752536
  11.0 1.4 copy-done.25
  12.4 1.3 copy-done.26
  13.7 0.0 copy-start.23
  13.7 5.0 %all-to-all-start = ((f32[4,21,8,1024]{3,2,1,0:T(8,128)}), f32[4,21,8,1024]{3,2,1,0:T(8,128)S(1)}, u32[]{:S(2)}, u32[]{:S(2)}) async-start(f32[4,21,8,1024]{3,2,1,0:T(8,128)} %copy-done.4), calls=%async_computation | async-start | bytes 5505024 | tf_op jit(solution)/shard_map/all_to_all | solution.py:434
  18.7 0.0 collective-permute-start
  18.7 5.4 %collective-permute-start.1 = (f32[8,64,1024]{2,1,0:T(8,128)}, f32[8,64,1024]{2,1,0:T(8,128)}, u32[]{:S(2)}, u32[]{:S(2)}) collective-permute-start(f32[8,64,1024]{2,1,0:T(8,128)} %copy-done.25), channel_id=1, source_target_pairs={{0,124},{4,0},{8,4},{12,8},{16,12},{20,16},{24,20},{28,24},{32,28}... | collective-permute-start | bytes 6291464 | tf_op jit(solution)/shard_map/ppermute | solution.py:269
  24.1 0.0 copy-done.15
  24.1 0.0 copy-done.17
  24.1 0.0 copy-done.12
  24.1 0.0 copy-done.13
  24.1 0.0 copy-done.23
  24.1 0.0 copy-start.6
  24.1 1.6 %copy-done.6 = f32[8,64,1024]{2,1,0:T(8,128)S(1)} copy-done((f32[8,64,1024]{2,1,0:T(8,128)S(1)}, f32[8,64,1024]{2,1,0:T(8,128)}, u32[]{:S(2)}) %copy-start.6) | copy-done | bytes 2097176
  25.7 7.9 %flux.1 = f32[8,64,128]{2,1,0:T(8,128)} custom-call(s32[4]{0:T(128)S(1)} %bitcast.19, s32[4,1024]{1,0:T(4,128)S(1)} %get-tuple-element.22.row, f32[8,64,1024]{2,1,0:T(8,128)S(1)} %copy-done.6, s32[4,1024]{1,0:T(4,128)S(1)} %get-tuple-element.23.lane, s32[4,1024]{1,0:T(4,128)S(1)} %bitcast.11, f32[4,1024]{1,0:T(4,128)S(1)} %bitcast.13), custom_call_target="tpu_custom_call" | custom-call | flops 1000 | bytes 30000000 | tf_op jit(solution)/shard_map/flux/pallas_call | solution.py:484
  33.6 17.0 %all-to-all-done.cross = f32[4,21,8,1024]{3,2,1,0:T(8,128)S(1)} async-done(((f32[4,21,8,1024]{3,2,1,0:T(8,128)}), f32[4,21,8,1024]{3,2,1,0:T(8,128)S(1)}, u32[]{:S(2)}, u32[]{:S(2)}) %all-to-all-start) | async-done | bytes 2752544 | tf_op jit(solution)/shard_map/all_to_all | solution.py:434
  50.6 5.3 %all-to-all-start.1 = ((f32[8,64,128]{2,1,0:T(8,128)}), f32[8,64,128]{2,1,0:T(8,128)S(1)}, u32[]{:S(2)}, u32[]{:S(2)}) async-start(f32[8,64,128]{2,1,0:T(8,128)} %flux.1), calls=%async_computation.1 | async-start | bytes 524288 | tf_op jit(solution)/shard_map/all_to_all | solution.py:434
  55.9 0.2 side.1
  56.1 0.7 copy-done.27
  56.8 0.7 copy-done.28
  57.5 5.9 %all-to-all-done.1.parts = f32[8,64,128]{2,1,0:T(8,128)S(1)} async-done(((f32[8,64,128]{2,1,0:T(8,128)}), f32[8,64,128]{2,1,0:T(8,128)S(1)}, u32[]{:S(2)}, u32[]{:S(2)}) %all-to-all-start.1) | async-done | bytes 262176 | tf_op jit(solution)/shard_map/all_to_all | solution.py:434
  63.4 0.1 near.1
  63.5 0.8 copy-done.7
  64.3 6.5 %all-to-all-start.2 = ((f32[16,64,128]{2,1,0:T(8,128)}), f32[16,64,128]{2,1,0:T(8,128)}, u32[]{:S(2)}, u32[]{:S(2)}) async-start(f32[16,64,128]{2,1,0:T(8,128)} %copy-done.7), calls=%async_computation.2 | async-start | bytes 1048576 | tf_op jit(solution)/shard_map/all_to_all | solution.py:434
  70.9 0.0 collective-permute-start.2
  70.9 5.1 %collective-permute-start.3 = (f32[8,8,1024]{2,1,0:T(8,128)}, f32[8,8,1024]{2,1,0:T(8,128)S(1)}, u32[]{:S(2)}, u32[]{:S(2)}) collective-permute-start(f32[8,8,1024]{2,1,0:T(8,128)} %copy-done.27), channel_id=1, source_target_pairs={{0,124},{4,0},{8,4},{12,8},{16,12},{20,16},{24,20},{28,24},{32,28}... | collective-permute-start | bytes 786440 | tf_op jit(solution)/shard_map/ppermute | solution.py:269
  75.9 0.0 collective-permute-done.refs_0_.lo
  75.9 0.0 collective-permute-done.1.refs_1_.hi
  75.9 6.9 %collective-permute-done.2.refs_3_.clo = f32[8,8,1024]{2,1,0:T(8,128)S(1)} collective-permute-done((f32[8,8,1024]{2,1,0:T(8,128)}, f32[8,8,1024]{2,1,0:T(8,128)S(1)}, u32[]{:S(2)}, u32[]{:S(2)}) %collective-permute-start.2) | collective-permute-done | bytes 262176 | tf_op jit(solution)/shard_map/ppermute | solution.py:269
  82.9 0.0 collective-permute-done.3.refs_4_.chi
  82.9 0.7 copy-done.9
  83.6 0.0 all-to-all-done.2.parts
  83.6 1.6 %copy-done.8 = f32[8,64,1024]{2,1,0:T(8,128)S(1)} copy-done((f32[8,64,1024]{2,1,0:T(8,128)S(1)}, f32[8,64,1024]{2,1,0:T(8,128)}, u32[]{:S(2)}) %copy-start.8) | copy-done | bytes 2097176
  85.2 0.9 copy-done.10
  86.1 0.7 copy-done.14
  86.9 0.7 copy-done.16
  87.6 0.7 copy-done.18
  88.3 0.7 copy-done.24
  89.0 8.3 %front.1 = (f32[8,64,1024]{2,1,0:T(8,128)S(1)}, f32[3,64,1024]{2,1,0:T(8,128)S(1)}, f32[3,64,1024]{2,1,0:T(8,128)S(1)}, f32[8,8,1024]{2,1,0:T(8,128)S(1)}, f32[8,8,1024]{2,1,0:T(8,128)S(1)}, /*index=5*/f32[16,128]{1,0:T(8,128)}) custom-call(s32[1]{0:T(128)} %bitcast.kref, s32[4]{0:T(128)S(1)} %bitcast.20, s32[4,1024]{1,0:T(4,128)S(1)} %copy-done.16, ...), custom_call_target="tpu_custom_call" | custom-call | flops 1000 | bytes 30000000 | tf_op jit(solution)/shard_map/front/pallas_call | solution.py:503
  97.3 1.3 copy-done.5
  98.6 5.7 %collective-permute-start.6 = (f32[8,8,1024]{2,1,0:T(8,128)S(1)}, f32[8,8,1024]{2,1,0:T(8,128)S(1)}, u32[]{:S(2)}, u32[]{:S(2)}) collective-permute-start(f32[8,8,1024]{2,1,0:T(8,128)S(1)} %get-tuple-element.27), channel_id=1, source_target_pairs={{1,0},{2,1},{3,2},{5,4},{6,5},{7,6},{9,8},{10,9},{11,10},{13,12},{... | collective-permute-start | bytes 786440 | tf_op jit(solution)/shard_map/ppermute | solution.py:273
  104.3 1.9 %collective-permute-start.7 = (f32[8,8,1024]{2,1,0:T(8,128)S(1)}, f32[8,8,1024]{2,1,0:T(8,128)S(1)}, u32[]{:S(2)}, u32[]{:S(2)}) collective-permute-start(f32[8,8,1024]{2,1,0:T(8,128)S(1)} %get-tuple-element.28), channel_id=1, source_target_pairs={{0,1},{1,2},{2,3},{4,5},{5,6},{6,7},{8,9},{9,10},{10,11},{12,13},{... | collective-permute-start | bytes 786440 | tf_op jit(solution)/shard_map/ppermute | solution.py:273
  106.2 0.1 collective-permute-start.4
  106.3 5.1 %collective-permute-start.5 = (f32[3,64,1024]{2,1,0:T(8,128)S(1)}, f32[3,64,1024]{2,1,0:T(8,128)S(1)}, u32[]{:S(2)}, u32[]{:S(2)}) collective-permute-start(f32[3,64,1024]{2,1,0:T(8,128)S(1)} %get-tuple-element.26), channel_id=1, source_target_pairs={{0,124},{4,0},{8,4},{12,8},{16,12},{20,16},{24,20},{28,24},{32,28}... | collective-permute-start | bytes 2359304 | tf_op jit(solution)/shard_map/ppermute | solution.py:269
  111.4 0.0 collective-permute-done.6
  111.4 1.2 collective-permute-done.7
  112.6 0.1 broadcast_select_fusion.sside
  112.7 0.1 collective-permute-start.8
  112.8 5.1 %collective-permute-start.9 = (f32[3,8,1024]{2,1,0:T(8,128)S(1)}, f32[3,8,1024]{2,1,0:T(8,128)S(1)}, u32[]{:S(2)}, u32[]{:S(2)}) collective-permute-start(f32[3,8,1024]{2,1,0:T(8,128)S(1)} %get-tuple-element.30), channel_id=1, source_target_pairs={{0,124},{4,0},{8,4},{12,8},{16,12},{20,16},{24,20},{28,24},{32,28}... | collective-permute-start | bytes 294920 | tf_op jit(solution)/shard_map/ppermute | solution.py:269
  117.8 4.3 %collective-permute-done.8.sclo = f32[3,8,1024]{2,1,0:T(8,128)S(1)} collective-permute-done((f32[3,8,1024]{2,1,0:T(8,128)S(1)}, f32[3,8,1024]{2,1,0:T(8,128)S(1)}, u32[]{:S(2)}, u32[]{:S(2)}) %collective-permute-start.8) | collective-permute-done | bytes 98336 | tf_op jit(solution)/shard_map/ppermute | solution.py:269
  122.1 0.0 collective-permute-done.9.schi
  122.1 0.0 collective-permute-done.4.slo
  122.1 0.0 collective-permute-done.5.shi
  122.1 22.2 %sweeps.1 = f32[8,64,1024]{2,1,0:T(8,128)} custom-call(s32[1]{0:T(128)} %bitcast.kref, f32[8,64,1024]{2,1,0:T(8,128)S(1)} %copy-done.1, f32[8,64,1024]{2,1,0:T(8,128)S(1)} %copy-done.3, f32[8,64,1024]{2,1,0:T(8,128)} %collective-permute-done.refs_0_.lo, f32[8,64,1024]{2,1,0:T(8,128)} %collective-permute-done.1.refs_1_.hi, ...), custom_call_target="tpu_custom_call" | custom-call | flops 1000 | bytes 60000000 | tf_op jit(solution)/shard_map/sweeps/pallas_call | solution.py:519
  (29 shorter events, 0.1 us)
Async XLA Ops:
  0.6 1.6 %copy-start = (f32[8,64,1024]{2,1,0:T(8,128)S(1)}, f32[8,64,1024]{2,1,0:T(8,128)}, u32[]{:S(2)}) copy-start(f32[8,64,1024]{2,1,0:T(8,128)} %load.1) | copy-start | bytes 6291460
  2.2 1.6 %copy-start.2 = (f32[8,64,1024]{2,1,0:T(8,128)S(1)}, f32[8,64,1024]{2,1,0:T(8,128)}, u32[]{:S(2)}) copy-start(f32[8,64,1024]{2,1,0:T(8,128)} %beta_in.1) | copy-start | bytes 6291460
  3.8 0.9 copy-start.11
  4.7 0.7 copy-start.19
  5.4 0.7 copy-start.20
  6.1 0.7 copy-start.21
  6.8 0.7 copy-start.22
  9.5 1.5 %copy-start.4 = (f32[4,21,8,1024]{3,2,1,0:T(8,128)}, f32[4,21,8,1024]{3,2,1,0:T(8,128)S(1)}, u32[]{:S(2)}) copy-start(f32[4,21,8,1024]{3,2,1,0:T(8,128)S(1)} %get-tuple-element.18) | copy-start | bytes 8257540
  11.0 1.4 copy-start.25
  12.4 1.3 copy-start.26
  13.7 10.4 %copy-start.15 = (s32[4,1024]{1,0:T(4,128)}, s32[4,1024]{1,0:T(4,128)S(1)}, u32[]{:S(2)}) copy-start(s32[4,1024]{1,0:T(4,128)S(1)} %get-tuple-element.22.row) | copy-start | bytes 49156
  13.7 10.4 %copy-start.17 = (s32[4,1024]{1,0:T(4,128)}, s32[4,1024]{1,0:T(4,128)S(1)}, u32[]{:S(2)}) copy-start(s32[4,1024]{1,0:T(4,128)S(1)} %get-tuple-element.23.lane) | copy-start | bytes 49156
  13.7 10.4 %copy-start.12 = (s32[1,1,4,1024]{3,2,1,0:T(4,128)S(1)}, s32[1,1,4,1024]{3,2,1,0:T(4,128)}, u32[]{:S(2)}) copy-start(s32[1,1,4,1024]{3,2,1,0:T(4,128)} %param.17) | copy-start | bytes 49156
  13.7 10.4 %copy-start.13 = (f32[1,1,4,1024]{3,2,1,0:T(4,128)S(1)}, f32[1,1,4,1024]{3,2,1,0:T(4,128)}, u32[]{:S(2)}) copy-start(f32[1,1,4,1024]{3,2,1,0:T(4,128)} %param.18) | copy-start | bytes 49156
  13.7 10.4 %copy-start.23 = (s32[1,1,4]{2,1,0:T(1,128)S(1)}, s32[1,1,4]{2,1,0:T(1,128)}, u32[]{:S(2)}) copy-start(s32[1,1,4]{2,1,0:T(1,128)} %param.19) | copy-start | bytes 52
  13.7 36.9 %all-to-all-start = ((f32[4,21,8,1024]{3,2,1,0:T(8,128)}), f32[4,21,8,1024]{3,2,1,0:T(8,128)S(1)}, u32[]{:S(2)}, u32[]{:S(2)}) async-start(f32[4,21,8,1024]{3,2,1,0:T(8,128)} %copy-done.4), calls=%async_computation | async-start | bytes 5505024 | tf_op jit(solution)/shard_map/all_to_all | solution.py:434
  18.7 57.3 %collective-permute-start = (f32[8,64,1024]{2,1,0:T(8,128)}, f32[8,64,1024]{2,1,0:T(8,128)}, u32[]{:S(2)}, u32[]{:S(2)}) collective-permute-start(f32[8,64,1024]{2,1,0:T(8,128)} %copy-done.26), channel_id=1, source_target_pairs={{0,4},{4,8},{8,12},{12,16},{16,20},{20,24},{24,28},{28,32},{32,36}... | collective-permute-start | bytes 6291464 | tf_op jit(solution)/shard_map/ppermute | solution.py:269
  18.7 57.3 %collective-permute-start.1 = (f32[8,64,1024]{2,1,0:T(8,128)}, f32[8,64,1024]{2,1,0:T(8,128)}, u32[]{:S(2)}, u32[]{:S(2)}) collective-permute-start(f32[8,64,1024]{2,1,0:T(8,128)} %copy-done.25), channel_id=1, source_target_pairs={{0,124},{4,0},{8,4},{12,8},{16,12},{20,16},{24,20},{28,24},{32,28}... | collective-permute-start | bytes 6291464 | tf_op jit(solution)/shard_map/ppermute | solution.py:269
  24.1 1.6 %copy-start.6 = (f32[8,64,1024]{2,1,0:T(8,128)S(1)}, f32[8,64,1024]{2,1,0:T(8,128)}, u32[]{:S(2)}) copy-start(f32[8,64,1024]{2,1,0:T(8,128)} %heat_any.1) | copy-start | bytes 6291460
  50.6 12.9 %all-to-all-start.1 = ((f32[8,64,128]{2,1,0:T(8,128)}), f32[8,64,128]{2,1,0:T(8,128)S(1)}, u32[]{:S(2)}, u32[]{:S(2)}) async-start(f32[8,64,128]{2,1,0:T(8,128)} %flux.1), calls=%async_computation.1 | async-start | bytes 524288 | tf_op jit(solution)/shard_map/all_to_all | solution.py:434
  56.1 0.7 copy-start.27
  56.8 0.7 copy-start.28
  63.5 0.8 copy-start.7
  64.3 19.3 %all-to-all-start.2 = ((f32[16,64,128]{2,1,0:T(8,128)}), f32[16,64,128]{2,1,0:T(8,128)}, u32[]{:S(2)}, u32[]{:S(2)}) async-start(f32[16,64,128]{2,1,0:T(8,128)} %copy-done.7), calls=%async_computation.2 | async-start | bytes 1048576 | tf_op jit(solution)/shard_map/all_to_all | solution.py:434
  70.9 12.0 %collective-permute-start.2 = (f32[8,8,1024]{2,1,0:T(8,128)}, f32[8,8,1024]{2,1,0:T(8,128)S(1)}, u32[]{:S(2)}, u32[]{:S(2)}) collective-permute-start(f32[8,8,1024]{2,1,0:T(8,128)} %copy-done.28), channel_id=1, source_target_pairs={{0,4},{4,8},{8,12},{12,16},{16,20},{20,24},{24,28},{28,32},{32,36}... | collective-permute-start | bytes 786440 | tf_op jit(solution)/shard_map/ppermute | solution.py:269
  70.9 12.0 %collective-permute-start.3 = (f32[8,8,1024]{2,1,0:T(8,128)}, f32[8,8,1024]{2,1,0:T(8,128)S(1)}, u32[]{:S(2)}, u32[]{:S(2)}) collective-permute-start(f32[8,8,1024]{2,1,0:T(8,128)} %copy-done.27), channel_id=1, source_target_pairs={{0,124},{4,0},{8,4},{12,8},{16,12},{20,16},{24,20},{28,24},{32,28}... | collective-permute-start | bytes 786440 | tf_op jit(solution)/shard_map/ppermute | solution.py:269
  82.9 0.7 copy-start.9
  83.6 1.6 %copy-start.8 = (f32[8,64,1024]{2,1,0:T(8,128)S(1)}, f32[8,64,1024]{2,1,0:T(8,128)}, u32[]{:S(2)}) copy-start(f32[8,64,1024]{2,1,0:T(8,128)} %pred_any.1) | copy-start | bytes 6291460
  85.2 0.9 copy-start.10
  86.1 0.7 copy-start.14
  86.9 0.7 copy-start.16
  87.6 0.7 copy-start.18
  88.3 0.7 copy-start.24
  88.9 33.1 %copy-start.1 = (f32[8,64,1024]{2,1,0:T(8,128)S(1)}, f32[8,64,1024]{2,1,0:T(8,128)}, u32[]{:S(2)}) copy-start(f32[8,64,1024]{2,1,0:T(8,128)} %load.1) | copy-start | bytes 6291460
  88.9 33.1 %copy-start.3 = (f32[8,64,1024]{2,1,0:T(8,128)S(1)}, f32[8,64,1024]{2,1,0:T(8,128)}, u32[]{:S(2)}) copy-start(f32[8,64,1024]{2,1,0:T(8,128)} %beta_in.1) | copy-start | bytes 6291460
  97.3 1.3 copy-start.5
  98.6 12.8 %collective-permute-start.6 = (f32[8,8,1024]{2,1,0:T(8,128)S(1)}, f32[8,8,1024]{2,1,0:T(8,128)S(1)}, u32[]{:S(2)}, u32[]{:S(2)}) collective-permute-start(f32[8,8,1024]{2,1,0:T(8,128)S(1)} %get-tuple-element.27), channel_id=1, source_target_pairs={{1,0},{2,1},{3,2},{5,4},{6,5},{7,6},{9,8},{10,9},{11,10},{13,12},{... | collective-permute-start | bytes 786440 | tf_op jit(solution)/shard_map/ppermute | solution.py:273
  104.3 8.3 %collective-permute-start.7 = (f32[8,8,1024]{2,1,0:T(8,128)S(1)}, f32[8,8,1024]{2,1,0:T(8,128)S(1)}, u32[]{:S(2)}, u32[]{:S(2)}) collective-permute-start(f32[8,8,1024]{2,1,0:T(8,128)S(1)} %get-tuple-element.28), channel_id=1, source_target_pairs={{0,1},{1,2},{2,3},{4,5},{5,6},{6,7},{8,9},{9,10},{10,11},{12,13},{... | collective-permute-start | bytes 786440 | tf_op jit(solution)/shard_map/ppermute | solution.py:273
  106.2 15.9 %collective-permute-start.4 = (f32[3,64,1024]{2,1,0:T(8,128)S(1)}, f32[3,64,1024]{2,1,0:T(8,128)S(1)}, u32[]{:S(2)}, u32[]{:S(2)}) collective-permute-start(f32[3,64,1024]{2,1,0:T(8,128)S(1)} %get-tuple-element.25), channel_id=1, source_target_pairs={{0,4},{4,8},{8,12},{12,16},{16,20},{20,24},{24,28},{28,32},{32,36}... | collective-permute-start | bytes 2359304 | tf_op jit(solution)/shard_map/ppermute | solution.py:269
  106.3 15.8 %collective-permute-start.5 = (f32[3,64,1024]{2,1,0:T(8,128)S(1)}, f32[3,64,1024]{2,1,0:T(8,128)S(1)}, u32[]{:S(2)}, u32[]{:S(2)}) collective-permute-start(f32[3,64,1024]{2,1,0:T(8,128)S(1)} %get-tuple-element.26), channel_id=1, source_target_pairs={{0,124},{4,0},{8,4},{12,8},{16,12},{20,16},{24,20},{28,24},{32,28}... | collective-permute-start | bytes 2359304 | tf_op jit(solution)/shard_map/ppermute | solution.py:269
  112.7 9.4 %collective-permute-start.8 = (f32[3,8,1024]{2,1,0:T(8,128)S(1)}, f32[3,8,1024]{2,1,0:T(8,128)S(1)}, u32[]{:S(2)}, u32[]{:S(2)}) collective-permute-start(f32[3,8,1024]{2,1,0:T(8,128)S(1)} %get-tuple-element.31), channel_id=1, source_target_pairs={{0,4},{4,8},{8,12},{12,16},{16,20},{20,24},{24,28},{28,32},{32,36}... | collective-permute-start | bytes 294920 | tf_op jit(solution)/shard_map/ppermute | solution.py:269
  112.8 9.3 %collective-permute-start.9 = (f32[3,8,1024]{2,1,0:T(8,128)S(1)}, f32[3,8,1024]{2,1,0:T(8,128)S(1)}, u32[]{:S(2)}, u32[]{:S(2)}) collective-permute-start(f32[3,8,1024]{2,1,0:T(8,128)S(1)} %get-tuple-element.30), channel_id=1, source_target_pairs={{0,124},{4,0},{8,4},{12,8},{16,12},{20,16},{24,20},{28,24},{32,28}... | collective-permute-start | bytes 294920 | tf_op jit(solution)/shard_map/ppermute | solution.py:269

commit v4 on v3

--- a/solution.py
+++ b/solution.py
@@ -26,7 +26,7 @@
 RE = R + 8
 RT = RE // 8
 GROUPS, SLOTS, NB, BS = 4, 1024, 128, 16
-FT = 5
+FROWS = BS * BS + 3 * BS
 UNROLL = 16
 AZIM = ("y", "z", "core")
 
@@ -88,17 +88,15 @@
             out[n, j * BS:(j + 1) * BS, :] = o
 
 
-def front_kernel(kref, cnt, row, parts, cross, lane, vert, share, pred_any, *refs):
-    front_body(kref, cnt, row, parts, cross, lane, vert, share, pred_any, *refs[5:])
-
-
-def front_body(kref, cnt, row, parts, cross, lane, vert, share, pred_any, src_any, sup, sdown, srup, srdown,
+def front_kernel(kref, cnt, row, parts, f0, f1, f2, f3, lane, vert, share, pred_any, *refs):
+    front_body(kref, cnt, row, parts, (f0, f1, f2, f3), lane, vert, share, pred_any, *refs[5:])
+
+
+def front_body(kref, cnt, row, parts, fronts, lane, vert, share, pred_any, src_any, sup, sdown, srup, srdown,
                hout, front, gtab, height, terms, flux, pred, zeros, flip, sems, zsems, *acc):
     k = kref[0]
     load = pltpu.make_async_copy(pred_any, pred, sems.at[0])
     load.start()
-    params_in = pltpu.make_async_copy(cross.at[:, pl.ds(2 * T, FT)], front, sems.at[6])
-    params_in.start()
     zeros[...] = jnp.zeros(zeros.shape, F32)
     count = zeros.shape[0]
     clears = [pltpu.make_async_copy(zeros, a.at[pl.ds(n * count, count)], zsems.at[m, n])
@@ -109,11 +107,11 @@
     for n in range(1, parts.shape[0]):
         sums = sums + parts[n]
     flux[...] = sums
-    params_in.wait()
+    for n, f in enumerate(fronts):
+        front[lax.rem(k + GROUPS - n, GROUPS)] = f[...]
 
     def held(g, n):
-        return jnp.concatenate([front[g, m // 8, :, m % 8 * 128:m % 8 * 128 + 128]
-                                for m in (2 * n, 2 * n + 1)], axis=0)
+        return front[g, n * BS:n * BS + BS, :]
 
     def neighbours(h):
         last = jnp.concatenate([h[g][BS - 1:BS, :] for g in range(GROUPS)], axis=0)
@@ -202,9 +200,8 @@
         c.wait()
 
 
-def pack_kernel(kref, load_any, beta_any, solve, prior, weight, jump, label, up, down, cross,
-                row, lane, load, beta, front, flip, isems, osems, fsems):
-    k = kref[0]
+def pack_kernel(load_any, beta_any, solve, prior, weight, jump, label, up, down, rup, rdown,
+                front, row, lane, load, beta, flip, isems, osems):
     loads = [pltpu.make_async_copy(a, b, isems.at[n])
              for n, (a, b) in enumerate(((load_any, load), (beta_any, beta)))]
     for c in loads:
@@ -217,49 +214,34 @@
     row[...] = ((column >> 3) << 6) + ((axial >> 7) << 3) + (column & 7)
     lane[...] = axial & 127
 
-    def keep(n, x):
-        front[n // 8, :, n % 8 * 128:n % 8 * 128 + 128] = x
-
-    for n in range(FT * 8):
-        keep(n, solve[n * 8:n * 8 + 8, :] if n < BS * BS // 8 else jnp.zeros((8, 128), F32))
+    front[0:BS * BS, :] = solve[...]
     for n, x in enumerate((prior, weight, jump)):
         for m in range(8):
             flip[pl.ds(m, BS, stride=8), :] = pltpu.roll(x[...], (128 - m * BS) % 128, 1)
-        turned = flip[...].T
-        keep(BS * BS // 8 + 2 * n, turned[:8, :])
-        keep(BS * BS // 8 + 2 * n + 1, turned[8:16, :])
+        at = BS * BS + n * BS
+        front[at:at + BS, :] = flip[...].T[:BS, :]
     sends = []
-    for d in range(GROUPS):
-        sends.append(pltpu.make_async_copy(front, cross.at[d, pl.ds(2 * T, FT)], fsems.at[d]))
-        sends[-1].start()
-    count = 0
     for n, f in enumerate((load, beta)):
         loads[n].wait()
-        pairs = [(f.at[pl.ds(T - H, H)], up.at[pl.ds(n * H, H)]), (f.at[pl.ds(0, H)], down.at[pl.ds(n * H, H)])]
-        for d in range(GROUPS):
-            first = pl.multiple_of(jnp.where(d < k, 0, R - 8), 8)
-            pairs.append((f.at[:, pl.ds(first, 8)], cross.at[d, pl.ds(n * T, T)]))
-        for a, b in pairs:
-            sends.append(pltpu.make_async_copy(a, b, osems.at[count]))
+        for a, b in ((f.at[pl.ds(T - H, H)], up.at[pl.ds(n * H, H)]),
+                     (f.at[pl.ds(0, H)], down.at[pl.ds(n * H, H)]),
+                     (f.at[:, pl.ds(R - 8, 8)], rup.at[pl.ds(n * T, T)]),
+                     (f.at[:, pl.ds(0, 8)], rdown.at[pl.ds(n * T, T)])):
+            sends.append(pltpu.make_async_copy(a, b, osems.at[len(sends)]))
             sends[-1].start()
-            count += 1
     for c in sends:
         c.wait()
 
 
-def side_kernel(kref, cross, side, eup, edown, below, sems):
-    k = kref[0]
-    loads = [pltpu.make_async_copy(cross.at[jnp.minimum(k + 1, GROUPS - 1), pl.ds(0, 2 * T)], side, sems.at[0]),
-             pltpu.make_async_copy(cross.at[jnp.maximum(k - 1, 0), pl.ds(0, 2 * T)], below, sems.at[1])]
+def side_kernel(above, below_any, side, eup, edown, below, sems):
+    loads = [pltpu.make_async_copy(above, side, sems.at[0]), pltpu.make_async_copy(below_any, below, sems.at[1])]
     for c in loads:
         c.start()
     for c in loads:
         c.wait()
     first = iota((8, Z), 0) < 4
     for t in range(2 * T):
-        above_t = jnp.where(k < GROUPS - 1, side[t], 0.0)
-        below_t = jnp.where(k > 0, below[t], 0.0)
-        side[t] = jnp.where(first, above_t, below_t)
+        side[t] = jnp.where(first, side[t], below[t])
     for n in range(2):
         eup[n * H:(n + 1) * H] = side[n * T + T - H:n * T + T]
         edown[n * H:(n + 1) * H] = side[n * T:n * T + H]
@@ -305,9 +287,14 @@
             main, tile, first, count = parts[g]
             cs.append(pltpu.make_async_copy(main, ref.at[pl.ds(first, count), rows], sems.at[g, f, 0]))
             cs.append(pltpu.make_async_copy(tile, ref.at[pl.ds(first, count), ring], sems.at[g, f, 1]))
-        for c in cs:
+        waits.append(cs)
+
+    def begin(g):
+        for c in waits[g] if g < 4 else ():
             c.start()
-        waits.append(cs)
+
+    begin(0)
+    begin(1)
     sub, lanes = iota((8, 128), 0), iota((8, 128), 1)
     top, bottom, last_lane, first_lane = sub == 7, sub == 0, lanes == 127, lanes == 0
     angular = (256 / (2.0 * math.pi)) ** 2
@@ -420,6 +407,7 @@
     for g in range(4):
         for c in waits[g]:
             c.wait()
+        begin(g + 2)
         if g == 0:
             for it in range(RT):
                 th[0, cut(it), :] = (beta[0, cut(it), :] + beta[1, cut(it), :]) * wide(rads[1, it])
@@ -445,11 +433,11 @@
 
 VM = pl.BlockSpec(memory_space=pltpu.VMEM)
 SM = pl.BlockSpec(memory_space=pltpu.SMEM)
-ANY = pl.BlockSpec(memory_space=pl.ANY)
+ANY = pl.BlockSpec(memory_space=pltpu.HBM)
 
 
 def params(mib):
-    return pltpu.CompilerParams(vmem_limit_bytes=mib << 20)
+    return pltpu.CompilerParams(vmem_limit_bytes=62 << 20)
 
 
 def cost(us):
@@ -469,17 +457,18 @@
     plane = lambda n: shape(n, R, Z)
     tile = lambda n: shape(n, 8, Z)
     block = pltpu.VMEM((T, R, Z), F32)
-    up, down, cross, row, lane = pl.pallas_call(
+    up, down, rup, rdown, front, row, lane = pl.pallas_call(
         pack_kernel,
-        out_shape=(plane(2 * H), plane(2 * H), shape(GROUPS, 2 * T + FT, 8, Z), slot, slot),
-        in_specs=[SM] + [ANY] * 2 + [VM] * 5, out_specs=(ANY,) * 3 + (VM,) * 2,
-        scratch_shapes=[block, block, pltpu.VMEM((FT, 8, Z), F32), pltpu.VMEM((128, 128), F32),
-                        pltpu.SemaphoreType.DMA((2,)), pltpu.SemaphoreType.DMA((12,)),
-                        pltpu.SemaphoreType.DMA((GROUPS,))],
+        out_shape=(plane(2 * H), plane(2 * H), tile(2 * T), tile(2 * T), shape(FROWS, NB), slot, slot),
+        in_specs=[ANY] * 2 + [VM] * 5, out_specs=(ANY,) * 4 + (VM,) * 3,
+        scratch_shapes=[block, block, pltpu.VMEM((128, 128), F32),
+                        pltpu.SemaphoreType.DMA((2,)), pltpu.SemaphoreType.DMA((8,))],
         compiler_params=params(10), cost_estimate=cost(4), name="pack",
-    )(kidx, load, beta, solve.reshape(BS * BS, NB), nodes(prior), nodes(weight), nodes(jump), label)
+    )(load, beta, solve.reshape(BS * BS, NB), nodes(prior), nodes(weight), nodes(jump), label)
     lo, hi = shift_azim(up, 1), shift_azim(down, -1)
-    cross = from_all(cross, "rad")
+    rhi, rlo = shift_rad(rdown, -1), shift_rad(rup, 1)
+    fronts = [front] + [
+        lax.ppermute(front, "rad", [(i, (i + s) % 4) for i in range(4)]) for s in (1, 2, 3)]
 
     partial = pl.pallas_call(
         flux_kernel, out_shape=shape(8, GROUPS * BS, NB),
@@ -490,10 +479,10 @@
     )(tally, row, heat, lane, vertex, share)
     side, eup, edown = pl.pallas_call(
         side_kernel, out_shape=(tile(2 * T), tile(2 * H), tile(2 * H)),
-        in_specs=[SM, ANY], out_specs=(VM,) * 3,
+        in_specs=[ANY, ANY], out_specs=(VM,) * 3,
         scratch_shapes=[pltpu.VMEM((2 * T, 8, Z), F32), pltpu.SemaphoreType.DMA((2,))],
         compiler_params=params(4), cost_estimate=cost(2), name="side",
-    )(kidx, cross)
+    )(rhi, rlo)
     clo, chi = shift_azim(eup, 1), shift_azim(edown, -1)
     near = pl.pallas_call(
         sum_kernel, out_shape=shape(16, GROUPS * BS, NB),
@@ -503,15 +492,15 @@
     source, sup, sdown, srup, srdown, height = pl.pallas_call(
         front_kernel,
         out_shape=(plane(T), plane(H - 1), plane(H - 1), tile(T), tile(T), shape(BS, NB)),
-        in_specs=[SM, SM, SM, VM, ANY, VM, VM, VM] + [ANY] * 6, out_specs=(ANY,) * 5 + (VM,),
-        scratch_shapes=[pltpu.VMEM((GROUPS, FT, 8, Z), F32),
+        in_specs=[SM, SM, SM] + [VM] * 8 + [ANY] * 6, out_specs=(ANY,) * 5 + (VM,),
+        scratch_shapes=[pltpu.VMEM((GROUPS, FROWS, NB), F32),
                         pltpu.VMEM((GROUPS, BS, NB), F32), pltpu.VMEM((GROUPS, BS, NB), F32),
                         pltpu.VMEM((GROUPS, SLOTS, 128), F32), pltpu.VMEM((GROUPS * BS, NB), F32),
                         block, pltpu.VMEM((R * 8, 128), F32), pltpu.VMEM((128, 128), F32),
-                        pltpu.SemaphoreType.DMA((7,)), pltpu.SemaphoreType.DMA((GROUPS, T))]
+                        pltpu.SemaphoreType.DMA((6,)), pltpu.SemaphoreType.DMA((GROUPS, T))]
         + [pltpu.VMEM((T * R * 8, 128), F32)] * GROUPS,
         compiler_params=params(20), cost_estimate=cost(10), name="front",
-    )(kidx, tally, row, flux, cross, lane, vertex, share, outflow, lo, hi, side, clo, chi)
+    )(kidx, tally, row, flux, *fronts, lane, vertex, share, outflow, lo, hi, side, clo, chi)
     slo, shi = shift_azim(sup, 1), shift_azim(sdown, -1)
     sside = ring_tile(shift_rad(srdown, -1), shift_rad(srup, 1))
     sclo, schi = shift_azim(sside[T - H + 1:], 1), shift_azim(sside[:H - 1], -1)

time: 147 us -> 128 us (0.87)
  local copies, waits for them, and re-layouts: 22.4 us -> 4.42 us
  Pallas kernels: 40.6 us -> 51.1 us
  waiting for transfers between devices: 35.3 us -> 26.7 us
  starting transfers between devices: 45.1 us -> 43 us
    all_to_all x3 -> x2, waiting for transfers between devices: 22.9 us -> 4.2 us  [from_all(): return lax.all_to_all(copies, axes, 0, 0)]
    unnamed x58 -> x32, local copies, waits for them, and re-layouts: 22.4 us -> 4.4 us
    ppermute x0 -> x3, waiting for transfers between devices: none -> 13.8 us  [per_device(): lax.ppermute(front, 'rad', [(i, (i + s) % 4) for i in range(4)])]
    all_to_all x3 -> x2, starting transfers between devices: 16.8 us -> 10.8 us  [from_all(): return lax.all_to_all(copies, axes, 0, 0)]
    ppermute x2 -> x4, starting transfers between devices: 7.61 us -> 11.9 us  [shift_rad(): lax.ppermute(x, 'rad', [(i, i + d) for i in range(4) if 0 <= i + d < 4])]
    ppermute x8, waiting for transfers between devices: 11.2 us -> 7.37 us  [shift_azim(): return lax.ppermute(x, AZIM, [(i, (i + d) % 32) for i in range(32)])]
    pallas_call x1, Pallas kernels: 1.92 us -> 5.63 us  [per_device(): pl.pallas_call(pack_kernel, out_shape=(plane(2 * H), plane(2 * H), tile(2...]
    ppermute x8, starting transfers between devices: 20.7 us -> 17.4 us  [shift_azim(): return lax.ppermute(x, AZIM, [(i, (i + d) % 32) for i in range(32)])]
  transfers between devices with their start and end apart: 13 -> 17, of which waited for: 5 -> 6; matrix products, arithmetic and copies ran while one was open for 0% -> 0% of each run, Pallas kernels for 6% -> 10%
where the time goes in v4:
time: 128 us; the launch traced here: 126 us
  Pallas kernels  51.1 us (40%)
  starting transfers between devices  43 us (34%)
  waiting for transfers between devices  26.7 us (21%)
  local copies, waits for them, and re-layouts  4.42 us (3%)
    pallas_call x1, Pallas kernels, per_device(): pl.pallas_call(sweep_kernel, out_shape=plane(T), in_specs=[SM] + [ANY] *...  22.5 us
    ppermute x8, starting transfers between devices, shift_azim(): return lax.ppermute(x, AZIM, [(i, (i + d) % 32) for i in range(32)])  17.4 us
    ppermute x3, waiting for transfers between devices, per_device(): lax.ppermute(front, 'rad', [(i, (i + s) % 4) for i in range(4)])  13.8 us
    ppermute x4, starting transfers between devices, shift_rad(): lax.ppermute(x, 'rad', [(i, i + d) for i in range(4) if 0 <= i + d < 4])  11.9 us
    all_to_all x2, starting transfers between devices, from_all(): return lax.all_to_all(copies, axes, 0, 0)  10.8 us
    pallas_call x1, Pallas kernels, per_device(): pl.pallas_call(front_kernel, out_shape=(plane(T), plane(H - 1), plane(H -...  9.73 us
    pallas_call x1, Pallas kernels, per_device(): pl.pallas_call(flux_kernel, out_shape=shape(8, GROUPS * BS, NB), in_specs...  9.09 us
    ppermute x8, waiting for transfers between devices, shift_azim(): return lax.ppermute(x, AZIM, [(i, (i + d) % 32) for i in range(32)])  7.37 us
  transfers between devices with their start and end apart: 17, of which 6 were waited for; matrix products, arithmetic and copies ran while one was open for 0% of the time, Pallas kernels for 10%

profile of v4, /device:TPU:2, one launch (start us, length us, event | category | flops | bytes accessed | tf_op | source)
XLA Modules:
  0.0 126.5 jit_solution(7027100619305043935)
XLA Ops:
  0.6 5.6 %pack.1 = (f32[8,64,1024]{2,1,0:T(8,128)}, f32[8,64,1024]{2,1,0:T(8,128)}, f32[16,8,1024]{2,1,0:T(8,128)}, f32[16,8,1024]{2,1,0:T(8,128)}, f32[304,128]{1,0:T(8,...) custom-call(f32[8,64,1024]{2,1,0:T(8,128)} %load.1, f32[8,64,1024]{2,1,0:T(8,128)} %beta_in.1, f32[256,128]{1,0:T(8,128)} %bitcast.10, ...), custom_call_target="tpu_custom_call" | custom-call | flops 1000 | bytes 12000000 | tf_op jit(solution)/shard_map/pack/pallas_call | solution.py:460
  6.3 0.1 collective-permute-start
  6.4 6.0 %collective-permute-start.1 = (f32[8,64,1024]{2,1,0:T(8,128)}, f32[8,64,1024]{2,1,0:T(8,128)}, u32[]{:S(2)}, u32[]{:S(2)}) collective-permute-start(f32[8,64,1024]{2,1,0:T(8,128)} %get-tuple-element.19), channel_id=1, source_target_pairs={{0,124},{4,0},{8,4},{12,8},{16,12},{20,16},{24,20},{28,24},{32,28}... | collective-permute-start | bytes 6291464 | tf_op jit(solution)/shard_map/ppermute | solution.py:251
  12.3 2.4 %collective-permute-start.2 = (f32[16,8,1024]{2,1,0:T(8,128)}, f32[16,8,1024]{2,1,0:T(8,128)S(1)}, u32[]{:S(2)}, u32[]{:S(2)}) collective-permute-start(f32[16,8,1024]{2,1,0:T(8,128)} %get-tuple-element.20), channel_id=1, source_target_pairs={{1,0},{2,1},{3,2},{5,4},{6,5},{7,6},{9,8},{10,9},{11,10},{13,12},{... | collective-permute-start | bytes 1572872 | tf_op jit(solution)/shard_map/ppermute | solution.py:255
  14.8 3.4 %collective-permute-start.3 = (f32[16,8,1024]{2,1,0:T(8,128)}, f32[16,8,1024]{2,1,0:T(8,128)S(1)}, u32[]{:S(2)}, u32[]{:S(2)}) collective-permute-start(f32[16,8,1024]{2,1,0:T(8,128)} %get-tuple-element.21), channel_id=1, source_target_pairs={{0,1},{1,2},{2,3},{4,5},{5,6},{6,7},{8,9},{9,10},{10,11},{12,13},{... | collective-permute-start | bytes 1572872 | tf_op jit(solution)/shard_map/ppermute | solution.py:255
  18.2 9.1 %flux.1 = f32[8,64,128]{2,1,0:T(8,128)} custom-call(s32[4]{0:T(128)} %bitcast.19, s32[4,1024]{1,0:T(4,128)} %get-tuple-element.25.row, f32[8,64,1024]{2,1,0:T(8,128)} %heat_any.1, s32[4,1024]{1,0:T(4,128)} %get-tuple-element.26.lane, s32[4,1024]{1,0:T(4,128)} %bitcast.11, f32[4,1024]{1,0:T(4,128)} %bitcast.13), custom_call_target="tpu_custom_call" | custom-call | flops 1000 | bytes 30000000 | tf_op jit(solution)/shard_map/flux/pallas_call | solution.py:473
  27.3 0.0 copy-start.9
  27.3 3.6 %all-to-all-start = ((f32[8,64,128]{2,1,0:T(8,128)}), f32[8,64,128]{2,1,0:T(8,128)S(1)}, u32[]{:S(2)}, u32[]{:S(2)}) async-start(f32[8,64,128]{2,1,0:T(8,128)} %flux.1), calls=%async_computation | async-start | bytes 524288 | tf_op jit(solution)/shard_map/all_to_all | solution.py:422
  30.9 0.0 collective-permute-done.2.above
  30.9 0.0 copy-start.7
  30.9 0.0 collective-permute-done.3.below_any
  30.9 0.8 copy-done.7
  31.7 0.8 copy-done.8
  32.5 2.3 %side.1 = (f32[16,8,1024]{2,1,0:T(8,128)}, f32[8,8,1024]{2,1,0:T(8,128)}, f32[8,8,1024]{2,1,0:T(8,128)}) custom-call(f32[16,8,1024]{2,1,0:T(8,128)} %copy-done.7, f32[16,8,1024]{2,1,0:T(8,128)} %copy-done.8), custom_call_target="tpu_custom_call" | custom-call | flops 1000 | bytes 6000000 | tf_op jit(solution)/shard_map/side/pallas_call | solution.py:480
  34.8 0.0 copy-start.15
  34.8 4.2 %all-to-all-done.parts = f32[8,64,128]{2,1,0:T(8,128)S(1)} async-done(((f32[8,64,128]{2,1,0:T(8,128)}), f32[8,64,128]{2,1,0:T(8,128)S(1)}, u32[]{:S(2)}, u32[]{:S(2)}) %all-to-all-start) | async-done | bytes 262176 | tf_op jit(solution)/shard_map/all_to_all | solution.py:422
  39.0 0.7 copy-done.4
  39.7 1.8 %near.1 = f32[16,64,128]{2,1,0:T(8,128)} custom-call(f32[8,64,128]{2,1,0:T(8,128)} %copy-done.4, f32[16,8,1024]{2,1,0:T(8,128)} %get-tuple-element.22.refs_0_.refs_2_.side), custom_call_target="tpu_custom_call" | custom-call | tf_op jit(solution)/shard_map/near/pallas_call | solution.py:487
  41.5 7.2 %all-to-all-start.1 = ((f32[16,64,128]{2,1,0:T(8,128)}), f32[16,64,128]{2,1,0:T(8,128)S(1)}, u32[]{:S(2)}, u32[]{:S(2)}) async-start(f32[16,64,128]{2,1,0:T(8,128)} %near.1), calls=%async_computation.1 | async-start | bytes 1048576 | tf_op jit(solution)/shard_map/all_to_all | solution.py:422
  48.7 0.0 copy-done.9
  48.7 0.2 collective-permute-start.8
  48.9 2.8 %collective-permute-start.7 = (f32[304,128]{1,0:T(8,128)S(1)}, f32[304,128]{1,0:T(8,128)S(1)}, u32[]{:S(2)}, u32[]{:S(2)}) collective-permute-start(f32[304,128]{1,0:T(8,128)S(1)} %copy-done.9), channel_id=1, source_target_pairs={{0,2},{1,3},{2,0},{3,1},{4,6},{5,7},{6,4},{7,5},{8,10},{9,11},{10,... | collective-permute-start | bytes 466952 | tf_op jit(solution)/shard_map/ppermute | solution.py:471
  51.7 0.0 collective-permute-start.4
  51.7 8.5 %collective-permute-done.8.f3 = f32[304,128]{1,0:T(8,128)S(1)} collective-permute-done((f32[304,128]{1,0:T(8,128)S(1)}, f32[304,128]{1,0:T(8,128)S(1)}, u32[]{:S(2)}, u32[]{:S(2)}) %collective-permute-start.8) | collective-permute-done | bytes 155680 | tf_op jit(solution)/shard_map/ppermute | solution.py:471
  60.3 0.0 copy-done.15
  60.3 3.5 %collective-permute-start.5 = (f32[8,8,1024]{2,1,0:T(8,128)S(1)}, f32[8,8,1024]{2,1,0:T(8,128)S(1)}, u32[]{:S(2)}, u32[]{:S(2)}) collective-permute-start(f32[8,8,1024]{2,1,0:T(8,128)S(1)} %copy-done.15), channel_id=1, source_target_pairs={{0,124},{4,0},{8,4},{12,8},{16,12},{20,16},{24,20},{28,24},{32,28}... | collective-permute-start | bytes 786440 | tf_op jit(solution)/shard_map/ppermute | solution.py:251
  63.8 0.0 collective-permute-done.7.f2
  63.8 0.0 collective-permute-start.6
  63.8 5.2 %collective-permute-done.6.f1 = f32[304,128]{1,0:T(8,128)S(1)} collective-permute-done((f32[304,128]{1,0:T(8,128)S(1)}, f32[304,128]{1,0:T(8,128)S(1)}, u32[]{:S(2)}, u32[]{:S(2)}) %collective-permute-start.6) | collective-permute-done | bytes 155680 | tf_op jit(solution)/shard_map/ppermute | solution.py:471
  69.0 0.0 collective-permute-done.4.refs_3_.clo
  69.0 0.0 collective-permute-done.5.refs_4_.chi
  69.0 0.0 copy-start.3
  69.1 0.0 all-to-all-done.1.parts
  69.1 0.0 copy-start
  69.1 0.0 collective-permute-done.refs_0_.lo
  69.1 0.0 collective-permute-done.1.refs_1_.hi
  69.1 0.0 copy-done.10
  69.1 0.0 copy-done.11
  69.1 0.6 copy-done.12
  69.7 0.1 copy-done.2
  69.8 0.1 copy-done.3
  69.9 0.2 copy-done
  70.1 9.7 %front.1 = (f32[8,64,1024]{2,1,0:T(8,128)}, f32[3,64,1024]{2,1,0:T(8,128)}, f32[3,64,1024]{2,1,0:T(8,128)}, f32[8,8,1024]{2,1,0:T(8,128)}, f32[8,8,1024]{2,1,0:T(8,128)}, /*index=5*/f32[16,128]{1,0:T(8,128)}) custom-call(s32[1]{0:T(128)} %bitcast.kref, s32[4]{0:T(128)} %bitcast.20, s32[4,1024]{1,0:T(4,128)} %get-tuple-element.25.row, ...), custom_call_target="tpu_custom_call" | custom-call | flops 1000 | bytes 30000000 | tf_op jit(solution)/shard_map/front/pallas_call | solution.py:492
  79.8 4.1 %collective-permute-start.11 = (f32[8,8,1024]{2,1,0:T(8,128)}, f32[8,8,1024]{2,1,0:T(8,128)S(1)}, u32[]{:S(2)}, u32[]{:S(2)}) collective-permute-start(f32[8,8,1024]{2,1,0:T(8,128)} %get-tuple-element.31), channel_id=1, source_target_pairs={{1,0},{2,1},{3,2},{5,4},{6,5},{7,6},{9,8},{10,9},{11,10},{13,12},{... | collective-permute-start | bytes 786440 | tf_op jit(solution)/shard_map/ppermute | solution.py:255
  84.0 1.9 %collective-permute-start.12 = (f32[8,8,1024]{2,1,0:T(8,128)}, f32[8,8,1024]{2,1,0:T(8,128)S(1)}, u32[]{:S(2)}, u32[]{:S(2)}) collective-permute-start(f32[8,8,1024]{2,1,0:T(8,128)} %get-tuple-element.32), channel_id=1, source_target_pairs={{0,1},{1,2},{2,3},{4,5},{5,6},{6,7},{8,9},{9,10},{10,11},{12,13},{... | collective-permute-start | bytes 786440 | tf_op jit(solution)/shard_map/ppermute | solution.py:255
  85.9 0.1 collective-permute-start.9
  86.0 5.1 %collective-permute-start.10 = (f32[3,64,1024]{2,1,0:T(8,128)}, f32[3,64,1024]{2,1,0:T(8,128)S(1)}, u32[]{:S(2)}, u32[]{:S(2)}) collective-permute-start(f32[3,64,1024]{2,1,0:T(8,128)} %get-tuple-element.30), channel_id=1, source_target_pairs={{0,124},{4,0},{8,4},{12,8},{16,12},{20,16},{24,20},{28,24},{32,28}... | collective-permute-start | bytes 2359304 | tf_op jit(solution)/shard_map/ppermute | solution.py:251
  91.0 0.0 collective-permute-done.11
  91.0 1.4 %collective-permute-done.12 = f32[8,8,1024]{2,1,0:T(8,128)S(1)} collective-permute-done((f32[8,8,1024]{2,1,0:T(8,128)}, f32[8,8,1024]{2,1,0:T(8,128)S(1)}, u32[]{:S(2)}, u32[]{:S(2)}) %collective-permute-start.12) | collective-permute-done | bytes 262176 | tf_op jit(solution)/shard_map/ppermute | solution.py:255
  92.4 0.1 broadcast_select_fusion.sside
  92.5 0.0 copy-start.1
  92.6 2.7 %collective-permute-start.14 = (f32[3,8,1024]{2,1,0:T(8,128)S(1)}, f32[3,8,1024]{2,1,0:T(8,128)S(1)}, u32[]{:S(2)}, u32[]{:S(2)}) collective-permute-start(f32[3,8,1024]{2,1,0:T(8,128)S(1)} %get-tuple-element.34), channel_id=1, source_target_pairs={{0,124},{4,0},{8,4},{12,8},{16,12},{20,16},{24,20},{28,24},{32,28}... | collective-permute-start | bytes 294920 | tf_op jit(solution)/shard_map/ppermute | solution.py:251
  95.3 0.0 collective-permute-start.13
  95.3 6.6 %collective-permute-done.14.schi = f32[3,8,1024]{2,1,0:T(8,128)S(1)} collective-permute-done((f32[3,8,1024]{2,1,0:T(8,128)S(1)}, f32[3,8,1024]{2,1,0:T(8,128)S(1)}, u32[]{:S(2)}, u32[]{:S(2)}) %collective-permute-start.14) | collective-permute-done | bytes 98336 | tf_op jit(solution)/shard_map/ppermute | solution.py:251
  101.8 0.8 collective-permute-done.13.sclo
  102.6 0.0 collective-permute-done.9.slo
  102.6 0.0 collective-permute-done.10.shi
  102.6 0.0 copy-start.6
  102.6 0.0 copy-done.1
  102.6 0.0 copy-done.13
  102.7 0.6 copy-done.14
  103.3 0.3 copy-done.5
  103.6 0.2 copy-done.6
  103.8 22.5 %sweeps.1 = f32[8,64,1024]{2,1,0:T(8,128)} custom-call(s32[1]{0:T(128)} %bitcast.kref, f32[8,64,1024]{2,1,0:T(8,128)} %load.1, f32[8,64,1024]{2,1,0:T(8,128)} %beta_in.1, f32[8,64,1024]{2,1,0:T(8,128)} %collective-permute-done.refs_0_.lo, f32[8,64,1024]{2,1,0:T(8,128)} %collective-permute-done.1.refs_1_.hi, ...), custom_call_target="tpu_custom_call" | custom-call | flops 1000 | bytes 60000000 | tf_op jit(solution)/shard_map/sweeps/pallas_call | solution.py:508
  (11 shorter events, 0.0 us)
Async XLA Ops:
  6.3 62.8 %collective-permute-start = (f32[8,64,1024]{2,1,0:T(8,128)}, f32[8,64,1024]{2,1,0:T(8,128)}, u32[]{:S(2)}, u32[]{:S(2)}) collective-permute-start(f32[8,64,1024]{2,1,0:T(8,128)} %get-tuple-element.18), channel_id=1, source_target_pairs={{0,4},{4,8},{8,12},{12,16},{16,20},{20,24},{24,28},{28,32},{32,36}... | collective-permute-start | bytes 6291464 | tf_op jit(solution)/shard_map/ppermute | solution.py:251
  6.4 62.7 %collective-permute-start.1 = (f32[8,64,1024]{2,1,0:T(8,128)}, f32[8,64,1024]{2,1,0:T(8,128)}, u32[]{:S(2)}, u32[]{:S(2)}) collective-permute-start(f32[8,64,1024]{2,1,0:T(8,128)} %get-tuple-element.19), channel_id=1, source_target_pairs={{0,124},{4,0},{8,4},{12,8},{16,12},{20,16},{24,20},{28,24},{32,28}... | collective-permute-start | bytes 6291464 | tf_op jit(solution)/shard_map/ppermute | solution.py:251
  12.3 18.5 %collective-permute-start.2 = (f32[16,8,1024]{2,1,0:T(8,128)}, f32[16,8,1024]{2,1,0:T(8,128)S(1)}, u32[]{:S(2)}, u32[]{:S(2)}) collective-permute-start(f32[16,8,1024]{2,1,0:T(8,128)} %get-tuple-element.20), channel_id=1, source_target_pairs={{1,0},{2,1},{3,2},{5,4},{6,5},{7,6},{9,8},{10,9},{11,10},{13,12},{... | collective-permute-start | bytes 1572872 | tf_op jit(solution)/shard_map/ppermute | solution.py:255
  14.8 16.1 %collective-permute-start.3 = (f32[16,8,1024]{2,1,0:T(8,128)}, f32[16,8,1024]{2,1,0:T(8,128)S(1)}, u32[]{:S(2)}, u32[]{:S(2)}) collective-permute-start(f32[16,8,1024]{2,1,0:T(8,128)} %get-tuple-element.21), channel_id=1, source_target_pairs={{0,1},{1,2},{2,3},{4,5},{5,6},{6,7},{8,9},{9,10},{10,11},{12,13},{... | collective-permute-start | bytes 1572872 | tf_op jit(solution)/shard_map/ppermute | solution.py:255
  27.3 21.4 %copy-start.9 = (f32[304,128]{1,0:T(8,128)S(1)}, f32[304,128]{1,0:T(8,128)}, u32[]{:S(2)}) copy-start(f32[304,128]{1,0:T(8,128)} %get-tuple-element.27.f0) | copy-start | bytes 466948
  27.3 11.7 %all-to-all-start = ((f32[8,64,128]{2,1,0:T(8,128)}), f32[8,64,128]{2,1,0:T(8,128)S(1)}, u32[]{:S(2)}, u32[]{:S(2)}) async-start(f32[8,64,128]{2,1,0:T(8,128)} %flux.1), calls=%async_computation | async-start | bytes 524288 | tf_op jit(solution)/shard_map/all_to_all | solution.py:422
  30.9 0.8 copy-start.7
  31.7 0.8 copy-start.8
  34.8 25.5 %copy-start.15 = (f32[8,8,1024]{2,1,0:T(8,128)S(1)}, f32[8,8,1024]{2,1,0:T(8,128)}, u32[]{:S(2)}) copy-start(f32[8,8,1024]{2,1,0:T(8,128)} %get-tuple-element.24) | copy-start | bytes 786436
  39.0 0.7 copy-start.4
  41.5 27.5 %all-to-all-start.1 = ((f32[16,64,128]{2,1,0:T(8,128)}), f32[16,64,128]{2,1,0:T(8,128)S(1)}, u32[]{:S(2)}, u32[]{:S(2)}) async-start(f32[16,64,128]{2,1,0:T(8,128)} %near.1), calls=%async_computation.1 | async-start | bytes 1048576 | tf_op jit(solution)/shard_map/all_to_all | solution.py:422
  48.7 11.5 %collective-permute-start.8 = (f32[304,128]{1,0:T(8,128)S(1)}, f32[304,128]{1,0:T(8,128)S(1)}, u32[]{:S(2)}, u32[]{:S(2)}) collective-permute-start(f32[304,128]{1,0:T(8,128)S(1)} %copy-done.9), channel_id=1, source_target_pairs={{0,3},{1,0},{2,1},{3,2},{4,7},{5,4},{6,5},{7,6},{8,11},{9,8},{10,9... | collective-permute-start | bytes 466952 | tf_op jit(solution)/shard_map/ppermute | solution.py:471
  48.9 14.9 %collective-permute-start.7 = (f32[304,128]{1,0:T(8,128)S(1)}, f32[304,128]{1,0:T(8,128)S(1)}, u32[]{:S(2)}, u32[]{:S(2)}) collective-permute-start(f32[304,128]{1,0:T(8,128)S(1)} %copy-done.9), channel_id=1, source_target_pairs={{0,2},{1,3},{2,0},{3,1},{4,6},{5,7},{6,4},{7,5},{8,10},{9,11},{10,... | collective-permute-start | bytes 466952 | tf_op jit(solution)/shard_map/ppermute | solution.py:471
  51.7 17.3 %collective-permute-start.4 = (f32[8,8,1024]{2,1,0:T(8,128)}, f32[8,8,1024]{2,1,0:T(8,128)S(1)}, u32[]{:S(2)}, u32[]{:S(2)}) collective-permute-start(f32[8,8,1024]{2,1,0:T(8,128)} %get-tuple-element.23), channel_id=1, source_target_pairs={{0,4},{4,8},{8,12},{12,16},{16,20},{20,24},{24,28},{28,32},{32,36}... | collective-permute-start | bytes 786440 | tf_op jit(solution)/shard_map/ppermute | solution.py:251
  60.3 8.8 %copy-start.10 = (f32[304,128]{1,0:T(8,128)}, f32[304,128]{1,0:T(8,128)S(1)}, u32[]{:S(2)}) copy-start(f32[304,128]{1,0:T(8,128)S(1)} %collective-permute-done.8.f3) | copy-start | bytes 466948
  60.3 8.8 %collective-permute-start.5 = (f32[8,8,1024]{2,1,0:T(8,128)S(1)}, f32[8,8,1024]{2,1,0:T(8,128)S(1)}, u32[]{:S(2)}, u32[]{:S(2)}) collective-permute-start(f32[8,8,1024]{2,1,0:T(8,128)S(1)} %copy-done.15), channel_id=1, source_target_pairs={{0,124},{4,0},{8,4},{12,8},{16,12},{20,16},{24,20},{28,24},{32,28}... | collective-permute-start | bytes 786440 | tf_op jit(solution)/shard_map/ppermute | solution.py:251
  63.8 5.3 %copy-start.11 = (f32[304,128]{1,0:T(8,128)}, f32[304,128]{1,0:T(8,128)S(1)}, u32[]{:S(2)}) copy-start(f32[304,128]{1,0:T(8,128)S(1)} %collective-permute-done.7.f2) | copy-start | bytes 466948
  63.8 5.2 %collective-permute-start.6 = (f32[304,128]{1,0:T(8,128)S(1)}, f32[304,128]{1,0:T(8,128)S(1)}, u32[]{:S(2)}, u32[]{:S(2)}) collective-permute-start(f32[304,128]{1,0:T(8,128)S(1)} %copy-done.9), channel_id=1, source_target_pairs={{0,1},{1,2},{2,3},{3,0},{4,5},{5,6},{6,7},{7,4},{8,9},{9,10},{10,1... | collective-permute-start | bytes 466952 | tf_op jit(solution)/shard_map/ppermute | solution.py:471
  69.0 0.7 copy-start.12
  69.0 0.8 copy-start.2
  69.0 0.9 copy-start.3
  69.1 1.0 copy-start
  79.8 11.2 %collective-permute-start.11 = (f32[8,8,1024]{2,1,0:T(8,128)}, f32[8,8,1024]{2,1,0:T(8,128)S(1)}, u32[]{:S(2)}, u32[]{:S(2)}) collective-permute-start(f32[8,8,1024]{2,1,0:T(8,128)} %get-tuple-element.31), channel_id=1, source_target_pairs={{1,0},{2,1},{3,2},{5,4},{6,5},{7,6},{9,8},{10,9},{11,10},{13,12},{... | collective-permute-start | bytes 786440 | tf_op jit(solution)/shard_map/ppermute | solution.py:255
  84.0 8.5 %collective-permute-start.12 = (f32[8,8,1024]{2,1,0:T(8,128)}, f32[8,8,1024]{2,1,0:T(8,128)S(1)}, u32[]{:S(2)}, u32[]{:S(2)}) collective-permute-start(f32[8,8,1024]{2,1,0:T(8,128)} %get-tuple-element.32), channel_id=1, source_target_pairs={{0,1},{1,2},{2,3},{4,5},{5,6},{6,7},{8,9},{9,10},{10,11},{12,13},{... | collective-permute-start | bytes 786440 | tf_op jit(solution)/shard_map/ppermute | solution.py:255
  85.9 16.7 %collective-permute-start.9 = (f32[3,64,1024]{2,1,0:T(8,128)}, f32[3,64,1024]{2,1,0:T(8,128)S(1)}, u32[]{:S(2)}, u32[]{:S(2)}) collective-permute-start(f32[3,64,1024]{2,1,0:T(8,128)} %get-tuple-element.29), channel_id=1, source_target_pairs={{0,4},{4,8},{8,12},{12,16},{16,20},{20,24},{24,28},{28,32},{32,36}... | collective-permute-start | bytes 2359304 | tf_op jit(solution)/shard_map/ppermute | solution.py:251
  86.0 16.6 %collective-permute-start.10 = (f32[3,64,1024]{2,1,0:T(8,128)}, f32[3,64,1024]{2,1,0:T(8,128)S(1)}, u32[]{:S(2)}, u32[]{:S(2)}) collective-permute-start(f32[3,64,1024]{2,1,0:T(8,128)} %get-tuple-element.30), channel_id=1, source_target_pairs={{0,124},{4,0},{8,4},{12,8},{16,12},{20,16},{24,20},{28,24},{32,28}... | collective-permute-start | bytes 2359304 | tf_op jit(solution)/shard_map/ppermute | solution.py:251
  92.5 10.1 %copy-start.1 = (f32[8,8,1024]{2,1,0:T(8,128)}, f32[8,8,1024]{2,1,0:T(8,128)S(1)}, u32[]{:S(2)}) copy-start(f32[8,8,1024]{2,1,0:T(8,128)S(1)} %broadcast_select_fusion.sside) | copy-start | bytes 786436
  92.6 9.2 %collective-permute-start.14 = (f32[3,8,1024]{2,1,0:T(8,128)S(1)}, f32[3,8,1024]{2,1,0:T(8,128)S(1)}, u32[]{:S(2)}, u32[]{:S(2)}) collective-permute-start(f32[3,8,1024]{2,1,0:T(8,128)S(1)} %get-tuple-element.34), channel_id=1, source_target_pairs={{0,124},{4,0},{8,4},{12,8},{16,12},{20,16},{24,20},{28,24},{32,28}... | collective-permute-start | bytes 294920 | tf_op jit(solution)/shard_map/ppermute | solution.py:251
  95.3 7.4 %collective-permute-start.13 = (f32[3,8,1024]{2,1,0:T(8,128)S(1)}, f32[3,8,1024]{2,1,0:T(8,128)S(1)}, u32[]{:S(2)}, u32[]{:S(2)}) collective-permute-start(f32[3,8,1024]{2,1,0:T(8,128)S(1)} %get-tuple-element.35), channel_id=1, source_target_pairs={{0,4},{4,8},{8,12},{12,16},{16,20},{20,24},{24,28},{28,32},{32,36}... | collective-permute-start | bytes 294920 | tf_op jit(solution)/shard_map/ppermute | solution.py:251
  101.8 0.8 copy-start.13
  102.6 0.6 copy-start.14
  102.6 0.9 copy-start.5
  102.6 1.2 copy-start.6

commit v5 on v4

--- a/solution.py
+++ b/solution.py
@@ -26,7 +26,7 @@
 RE = R + 8
 RT = RE // 8
 GROUPS, SLOTS, NB, BS = 4, 1024, 128, 16
-FROWS = BS * BS + 3 * BS
+FT = 5
 UNROLL = 16
 AZIM = ("y", "z", "core")
 
@@ -93,10 +93,15 @@
 
 
 def front_body(kref, cnt, row, parts, fronts, lane, vert, share, pred_any, src_any, sup, sdown, srup, srdown,
-               hout, front, gtab, height, terms, flux, pred, zeros, flip, sems, zsems, *acc):
+               hout, front, gtab, height, terms, flux, pred, zeros, flip, sems, zsems, fsems, *acc):
     k = kref[0]
     load = pltpu.make_async_copy(pred_any, pred, sems.at[0])
     load.start()
+    own, above, below, across = fronts
+    copies = [(own, 0), (above.at[pl.ds(2 * T, FT)], 1), (across, 2), (below.at[pl.ds(2 * T, FT)], 3)]
+    copies = [pltpu.make_async_copy(f, front.at[lax.rem(k + n, GROUPS)], fsems.at[n]) for f, n in copies]
+    for c in copies:
+        c.start()
     zeros[...] = jnp.zeros(zeros.shape, F32)
     count = zeros.shape[0]
     clears = [pltpu.make_async_copy(zeros, a.at[pl.ds(n * count, count)], zsems.at[m, n])
@@ -107,11 +112,12 @@
     for n in range(1, parts.shape[0]):
         sums = sums + parts[n]
     flux[...] = sums
-    for n, f in enumerate(fronts):
-        front[lax.rem(k + GROUPS - n, GROUPS)] = f[...]
+    for c in copies:
+        c.wait()
 
     def held(g, n):
-        return front[g, n * BS:n * BS + BS, :]
+        return jnp.concatenate([front[g, m // 8, :, m % 8 * 128:m % 8 * 128 + 128]
+                                for m in (2 * n, 2 * n + 1)], axis=0)
 
     def neighbours(h):
         last = jnp.concatenate([h[g][BS - 1:BS, :] for g in range(GROUPS)], axis=0)
@@ -201,7 +207,7 @@
 
 
 def pack_kernel(load_any, beta_any, solve, prior, weight, jump, label, up, down, rup, rdown,
-                front, row, lane, load, beta, flip, isems, osems):
+                front_any, row, lane, load, beta, front, flip, isems, osems, fsems):
     loads = [pltpu.make_async_copy(a, b, isems.at[n])
              for n, (a, b) in enumerate(((load_any, load), (beta_any, beta)))]
     for c in loads:
@@ -214,13 +220,23 @@
     row[...] = ((column >> 3) << 6) + ((axial >> 7) << 3) + (column & 7)
     lane[...] = axial & 127
 
-    front[0:BS * BS, :] = solve[...]
+
+    def keep(n, x):
+        front[n // 8, :, n % 8 * 128:n % 8 * 128 + 128] = x
+
+    for n in range(FT * 8):
+        keep(n, solve[n * 8:n * 8 + 8, :] if n < BS * BS // 8 else jnp.zeros((8, 128), F32))
     for n, x in enumerate((prior, weight, jump)):
         for m in range(8):
             flip[pl.ds(m, BS, stride=8), :] = pltpu.roll(x[...], (128 - m * BS) % 128, 1)
-        at = BS * BS + n * BS
-        front[at:at + BS, :] = flip[...].T[:BS, :]
+        turned = flip[...].T
+        keep(BS * BS // 8 + 2 * n, turned[:8, :])
+        keep(BS * BS // 8 + 2 * n + 1, turned[8:16, :])
     sends = []
+    fcopies = [pltpu.make_async_copy(front, b, fsems.at[n]) for n, b in enumerate(
+        (front_any, rup.at[pl.ds(2 * T, FT)], rdown.at[pl.ds(2 * T, FT)]))]
+    for c in fcopies:
+        c.start()
     for n, f in enumerate((load, beta)):
         loads[n].wait()
         for a, b in ((f.at[pl.ds(T - H, H)], up.at[pl.ds(n * H, H)]),
@@ -229,19 +245,23 @@
                      (f.at[:, pl.ds(0, 8)], rdown.at[pl.ds(n * T, T)])):
             sends.append(pltpu.make_async_copy(a, b, osems.at[len(sends)]))
             sends[-1].start()
-    for c in sends:
+    for c in sends + fcopies:
         c.wait()
 
 
-def side_kernel(above, below_any, side, eup, edown, below, sems):
-    loads = [pltpu.make_async_copy(above, side, sems.at[0]), pltpu.make_async_copy(below_any, below, sems.at[1])]
+def side_kernel(kref, above, below_any, side, eup, edown, below, sems):
+    loads = [pltpu.make_async_copy(above.at[pl.ds(0, 2 * T)], side, sems.at[0]),
+             pltpu.make_async_copy(below_any.at[pl.ds(0, 2 * T)], below, sems.at[1])]
     for c in loads:
         c.start()
     for c in loads:
         c.wait()
-    first = iota((8, Z), 0) < 4
+    k = kref[0]
+    sub = iota((8, Z), 0)
+    first = (sub < 4) & (k < GROUPS - 1)
+    second = (sub >= 4) & (k > 0)
     for t in range(2 * T):
-        side[t] = jnp.where(first, side[t], below[t])
+        side[t] = jnp.where(first, side[t], jnp.where(second, below[t], 0.0))
     for n in range(2):
         eup[n * H:(n + 1) * H] = side[n * T + T - H:n * T + T]
         edown[n * H:(n + 1) * H] = side[n * T:n * T + H]
@@ -459,16 +479,15 @@
     block = pltpu.VMEM((T, R, Z), F32)
     up, down, rup, rdown, front, row, lane = pl.pallas_call(
         pack_kernel,
-        out_shape=(plane(2 * H), plane(2 * H), tile(2 * T), tile(2 * T), shape(FROWS, NB), slot, slot),
-        in_specs=[ANY] * 2 + [VM] * 5, out_specs=(ANY,) * 4 + (VM,) * 3,
-        scratch_shapes=[block, block, pltpu.VMEM((128, 128), F32),
-                        pltpu.SemaphoreType.DMA((2,)), pltpu.SemaphoreType.DMA((8,))],
+        out_shape=(plane(2 * H), plane(2 * H), tile(2 * T + FT), tile(2 * T + FT), tile(FT), slot, slot),
+        in_specs=[ANY] * 2 + [VM] * 5, out_specs=(ANY,) * 5 + (VM,) * 2,
+        scratch_shapes=[block, block, pltpu.VMEM((FT, 8, Z), F32), pltpu.VMEM((128, 128), F32),
+                        pltpu.SemaphoreType.DMA((2,)), pltpu.SemaphoreType.DMA((8,)), pltpu.SemaphoreType.DMA((3,))],
         compiler_params=params(10), cost_estimate=cost(4), name="pack",
     )(load, beta, solve.reshape(BS * BS, NB), nodes(prior), nodes(weight), nodes(jump), label)
     lo, hi = shift_azim(up, 1), shift_azim(down, -1)
-    rhi, rlo = shift_rad(rdown, -1), shift_rad(rup, 1)
-    fronts = [front] + [
-        lax.ppermute(front, "rad", [(i, (i + s) % 4) for i in range(4)]) for s in (1, 2, 3)]
+    ring = lambda x, d: lax.ppermute(x, "rad", [(i, (i + d) % 4) for i in range(4)])
+    rhi, rlo, across = ring(rdown, -1), ring(rup, 1), ring(front, 2)
 
     partial = pl.pallas_call(
         flux_kernel, out_shape=shape(8, GROUPS * BS, NB),
@@ -479,28 +498,29 @@
     )(tally, row, heat, lane, vertex, share)
     side, eup, edown = pl.pallas_call(
         side_kernel, out_shape=(tile(2 * T), tile(2 * H), tile(2 * H)),
-        in_specs=[ANY, ANY], out_specs=(VM,) * 3,
+        in_specs=[SM, ANY, ANY], out_specs=(VM,) * 3,
         scratch_shapes=[pltpu.VMEM((2 * T, 8, Z), F32), pltpu.SemaphoreType.DMA((2,))],
         compiler_params=params(4), cost_estimate=cost(2), name="side",
-    )(rhi, rlo)
+    )(kidx, rhi, rlo)
     clo, chi = shift_azim(eup, 1), shift_azim(edown, -1)
     near = pl.pallas_call(
         sum_kernel, out_shape=shape(16, GROUPS * BS, NB),
-        in_specs=[VM, ANY], out_specs=VM, compiler_params=params(4), name="near",
-    )(from_all(partial, ("z", "core")), side)
+        in_specs=[VM, ANY, ANY], out_specs=VM, compiler_params=params(4), name="near",
+    )(from_all(partial, ("z", "core")), side, across)
     flux = from_all(near, ("y", "rad"))
     source, sup, sdown, srup, srdown, height = pl.pallas_call(
         front_kernel,
         out_shape=(plane(T), plane(H - 1), plane(H - 1), tile(T), tile(T), shape(BS, NB)),
-        in_specs=[SM, SM, SM] + [VM] * 8 + [ANY] * 6, out_specs=(ANY,) * 5 + (VM,),
-        scratch_shapes=[pltpu.VMEM((GROUPS, FROWS, NB), F32),
+        in_specs=[SM, SM, SM, VM] + [ANY] * 4 + [VM] * 3 + [ANY] * 6, out_specs=(ANY,) * 5 + (VM,),
+        scratch_shapes=[pltpu.VMEM((GROUPS, FT, 8, Z), F32),
                         pltpu.VMEM((GROUPS, BS, NB), F32), pltpu.VMEM((GROUPS, BS, NB), F32),
                         pltpu.VMEM((GROUPS, SLOTS, 128), F32), pltpu.VMEM((GROUPS * BS, NB), F32),
                         block, pltpu.VMEM((R * 8, 128), F32), pltpu.VMEM((128, 128), F32),
-                        pltpu.SemaphoreType.DMA((6,)), pltpu.SemaphoreType.DMA((GROUPS, T))]
+                        pltpu.SemaphoreType.DMA((6,)), pltpu.SemaphoreType.DMA((GROUPS, T)),
+                        pltpu.SemaphoreType.DMA((GROUPS,))]
         + [pltpu.VMEM((T * R * 8, 128), F32)] * GROUPS,
         compiler_params=params(20), cost_estimate=cost(10), name="front",
-    )(kidx, tally, row, flux, *fronts, lane, vertex, share, outflow, lo, hi, side, clo, chi)
+    )(kidx, tally, row, flux, front, rhi, rlo, across, lane, vertex, share, outflow, lo, hi, side, clo, chi)
     slo, shi = shift_azim(sup, 1), shift_azim(sdown, -1)
     sside = ring_tile(shift_rad(srdown, -1), shift_rad(srup, 1))
     sclo, schi = shift_azim(sside[T - H + 1:], 1), shift_azim(sside[:H - 1], -1)

time: 128 us -> 121 us (0.945); the launches traced: 126 us -> 121 us
  waiting for transfers between devices: 26.7 us -> 21.9 us
    ppermute x3, waiting for transfers between devices: 13.8 us -> 2.91 us  [per_device(): lax.ppermute(x, 'rad', [(i, (i + d) % 4) for i in range(4)])]
    ppermute x8, waiting for transfers between devices: 7.37 us -> 14.9 us  [shift_azim(): return lax.ppermute(x, AZIM, [(i, (i + d) % 32) for i in range(32)])]
    ppermute x4 -> x2, starting transfers between devices: 11.9 us -> 6.66 us  [shift_rad(): lax.ppermute(x, 'rad', [(i, i + d) for i in range(4) if 0 <= i + d < 4])]
    ppermute x8, starting transfers between devices: 17.4 us -> 21.4 us  [shift_azim(): return lax.ppermute(x, AZIM, [(i, (i + d) % 32) for i in range(32)])]
    ppermute x4 -> x2, waiting for transfers between devices: 1.41 us -> 0.01 us  [shift_rad(): lax.ppermute(x, 'rad', [(i, i + d) for i in range(4) if 0 <= i + d < 4])]
    unnamed x32 -> x28, local copies, waits for them, and re-layouts: 4.4 us -> 3.93 us
  transfers between devices with their start and end apart: 17 -> 15, of which waited for: 6 -> 4; matrix products, arithmetic and copies ran while one was open for 0% -> 0% of each run, Pallas kernels for 10% -> 11%
where the time goes in v5:
time: 121 us
  Pallas kernels  51.8 us (43%)
  starting transfers between devices  42.1 us (35%)
  waiting for transfers between devices  21.9 us (18%)
  local copies, waits for them, and re-layouts  3.95 us (3%)
    pallas_call x1, Pallas kernels, per_device(): pl.pallas_call(sweep_kernel, out_shape=plane(T), in_specs=[SM] + [ANY] *...  22.5 us
    ppermute x8, starting transfers between devices, shift_azim(): return lax.ppermute(x, AZIM, [(i, (i + d) % 32) for i in range(32)])  21.4 us
    ppermute x8, waiting for transfers between devices, shift_azim(): return lax.ppermute(x, AZIM, [(i, (i + d) % 32) for i in range(32)])  14.9 us
    all_to_all x2, starting transfers between devices, from_all(): return lax.all_to_all(copies, axes, 0, 0)  10.4 us
    pallas_call x1, Pallas kernels, per_device(): pl.pallas_call(front_kernel, out_shape=(plane(T), plane(H - 1), plane(H -...  10.3 us
    pallas_call x1, Pallas kernels, per_device(): pl.pallas_call(flux_kernel, out_shape=shape(8, GROUPS * BS, NB), in_specs...  9.12 us
    ppermute x2, starting transfers between devices, shift_rad(): lax.ppermute(x, 'rad', [(i, i + d) for i in range(4) if 0 <= i + d < 4])  6.66 us
    pallas_call x1, Pallas kernels, per_device(): pl.pallas_call(pack_kernel, out_shape=(plane(2 * H), plane(2 * H), tile(2...  5.78 us
  transfers between devices with their start and end apart: 15, of which 4 were waited for; matrix products, arithmetic and copies ran while one was open for 0% of the time, Pallas kernels for 11%

profile of v5, /device:TPU:2, one launch (start us, length us, event | category | flops | bytes accessed | tf_op | source)
XLA Modules:
  0.0 120.9 jit_solution(9631034641696862340)
XLA Ops:
  0.6 5.8 %pack.1 = (f32[8,64,1024]{2,1,0:T(8,128)}, f32[8,64,1024]{2,1,0:T(8,128)}, f32[21,8,1024]{2,1,0:T(8,128)}, f32[21,8,1024]{2,1,0:T(8,128)}, f32[5,8,1024]{2,1,0:T...) custom-call(f32[8,64,1024]{2,1,0:T(8,128)} %load.1, f32[8,64,1024]{2,1,0:T(8,128)} %beta_in.1, f32[256,128]{1,0:T(8,128)} %bitcast.10, ...), custom_call_target="tpu_custom_call" | custom-call | flops 1000 | bytes 12000000 | tf_op jit(solution)/shard_map/pack/pallas_call | solution.py:480
  6.4 0.0 copy-start.10
  6.4 0.1 collective-permute-start
  6.5 6.0 %collective-permute-start.1 = (f32[8,64,1024]{2,1,0:T(8,128)}, f32[8,64,1024]{2,1,0:T(8,128)}, u32[]{:S(2)}, u32[]{:S(2)}) collective-permute-start(f32[8,64,1024]{2,1,0:T(8,128)} %get-tuple-element.19), channel_id=1, source_target_pairs={{0,124},{4,0},{8,4},{12,8},{16,12},{20,16},{24,20},{28,24},{32,28}... | collective-permute-start | bytes 6291464 | tf_op jit(solution)/shard_map/ppermute | solution.py:271
  12.5 0.5 collective-permute-start.2
  13.0 1.5 %collective-permute-start.3 = (f32[21,8,1024]{2,1,0:T(8,128)}, f32[21,8,1024]{2,1,0:T(8,128)S(1)}, u32[]{:S(2)}, u32[]{:S(2)}) collective-permute-start(f32[21,8,1024]{2,1,0:T(8,128)} %get-tuple-element.21), channel_id=1, source_target_pairs={{0,1},{1,2},{2,3},{3,0},{4,5},{5,6},{6,7},{7,4},{8,9},{9,10},{10,1... | collective-permute-start | bytes 2064392 | tf_op jit(solution)/shard_map/ppermute | solution.py:489
  14.5 9.1 %flux.1 = f32[8,64,128]{2,1,0:T(8,128)} custom-call(s32[4]{0:T(128)} %bitcast.19, s32[4,1024]{1,0:T(4,128)} %get-tuple-element.25.row, f32[8,64,1024]{2,1,0:T(8,128)} %heat_any.1, s32[4,1024]{1,0:T(4,128)} %get-tuple-element.26.lane, s32[4,1024]{1,0:T(4,128)} %bitcast.11, f32[4,1024]{1,0:T(4,128)} %bitcast.13), custom_call_target="tpu_custom_call" | custom-call | flops 1000 | bytes 30000000 | tf_op jit(solution)/shard_map/flux/pallas_call | solution.py:492
  23.7 3.4 %all-to-all-start = ((f32[8,64,128]{2,1,0:T(8,128)}), f32[8,64,128]{2,1,0:T(8,128)S(1)}, u32[]{:S(2)}, u32[]{:S(2)}) async-start(f32[8,64,128]{2,1,0:T(8,128)} %flux.1), calls=%async_computation | async-start | bytes 524288 | tf_op jit(solution)/shard_map/all_to_all | solution.py:442
  27.1 0.0 copy-done.10
  27.1 1.6 %collective-permute-start.6 = (f32[5,8,1024]{2,1,0:T(8,128)S(1)}, f32[5,8,1024]{2,1,0:T(8,128)S(1)}, u32[]{:S(2)}, u32[]{:S(2)}) collective-permute-start(f32[5,8,1024]{2,1,0:T(8,128)S(1)} %copy-done.10), channel_id=1, source_target_pairs={{0,2},{1,3},{2,0},{3,1},{4,6},{5,7},{6,4},{7,5},{8,10},{9,11},{10,... | collective-permute-start | bytes 491528 | tf_op jit(solution)/shard_map/ppermute | solution.py:489
  28.7 0.0 collective-permute-done.2.above.f1
  28.7 0.0 copy-start
  28.7 0.0 collective-permute-done.3.below_any.f2
  28.8 0.0 copy-start.1
  28.8 0.9 copy-done
  29.6 0.3 copy-done.1
  29.9 2.3 %side.1 = (f32[16,8,1024]{2,1,0:T(8,128)}, f32[8,8,1024]{2,1,0:T(8,128)}, f32[8,8,1024]{2,1,0:T(8,128)}) custom-call(s32[1]{0:T(128)} %bitcast.kref, f32[21,8,1024]{2,1,0:T(8,128)} %copy-done, f32[21,8,1024]{2,1,0:T(8,128)} %copy-done.1), custom_call_target="tpu_custom_call" | custom-call | flops 1000 | bytes 6000000 | tf_op jit(solution)/shard_map/side/pallas_call | solution.py:499
  32.2 0.0 copy-start.13
  32.2 2.9 %collective-permute-done.6.refs_1_.f3 = f32[5,8,1024]{2,1,0:T(8,128)S(1)} collective-permute-done((f32[5,8,1024]{2,1,0:T(8,128)S(1)}, f32[5,8,1024]{2,1,0:T(8,128)S(1)}, u32[]{:S(2)}, u32[]{:S(2)}) %collective-permute-start.6) | collective-permute-done | bytes 163872 | tf_op jit(solution)/shard_map/ppermute | solution.py:489
  35.1 0.0 copy-start.9
  35.1 4.0 %all-to-all-done.parts = f32[8,64,128]{2,1,0:T(8,128)S(1)} async-done(((f32[8,64,128]{2,1,0:T(8,128)}), f32[8,64,128]{2,1,0:T(8,128)S(1)}, u32[]{:S(2)}, u32[]{:S(2)}) %all-to-all-start) | async-done | bytes 262176 | tf_op jit(solution)/shard_map/all_to_all | solution.py:442
  39.2 0.0 copy-start.6
  39.2 0.0 copy-done.9
  39.2 0.7 copy-done.6
  39.9 1.8 %near.1 = f32[16,64,128]{2,1,0:T(8,128)} custom-call(f32[8,64,128]{2,1,0:T(8,128)} %copy-done.6, f32[16,8,1024]{2,1,0:T(8,128)} %get-tuple-element.22.refs_0_.refs_2_.side, f32[5,8,1024]{2,1,0:T(8,128)} %copy-done.9), custom_call_target="tpu_custom_call" | custom-call | tf_op jit(solution)/shard_map/near/pallas_call | solution.py:506
  41.7 7.0 %all-to-all-start.1 = ((f32[16,64,128]{2,1,0:T(8,128)}), f32[16,64,128]{2,1,0:T(8,128)S(1)}, u32[]{:S(2)}, u32[]{:S(2)}) async-start(f32[16,64,128]{2,1,0:T(8,128)} %near.1), calls=%async_computation.1 | async-start | bytes 1048576 | tf_op jit(solution)/shard_map/all_to_all | solution.py:442
  48.6 0.0 collective-permute-start.4
  48.7 0.0 copy-done.13
  48.7 5.1 %collective-permute-start.5 = (f32[8,8,1024]{2,1,0:T(8,128)S(1)}, f32[8,8,1024]{2,1,0:T(8,128)S(1)}, u32[]{:S(2)}, u32[]{:S(2)}) collective-permute-start(f32[8,8,1024]{2,1,0:T(8,128)S(1)} %copy-done.13), channel_id=1, source_target_pairs={{0,124},{4,0},{8,4},{12,8},{16,12},{20,16},{24,20},{28,24},{32,28}... | collective-permute-start | bytes 786440 | tf_op jit(solution)/shard_map/ppermute | solution.py:271
  53.7 9.3 %collective-permute-done.4.refs_3_.clo = f32[8,8,1024]{2,1,0:T(8,128)S(1)} collective-permute-done((f32[8,8,1024]{2,1,0:T(8,128)}, f32[8,8,1024]{2,1,0:T(8,128)S(1)}, u32[]{:S(2)}, u32[]{:S(2)}) %collective-permute-start.4) | collective-permute-done | bytes 262176 | tf_op jit(solution)/shard_map/ppermute | solution.py:271
  63.0 0.0 copy-start.4
  63.0 0.0 collective-permute-done.5.refs_4_.chi
  63.0 0.0 copy-start.5
  63.0 0.0 all-to-all-done.1.parts
  63.0 0.0 copy-start.2
  63.0 0.0 collective-permute-done.refs_0_.lo
  63.0 0.0 collective-permute-done.1.refs_1_.hi
  63.0 0.6 copy-done.4
  63.7 0.1 copy-done.5
  63.8 0.2 copy-done.2
  64.0 10.3 %front.1 = (f32[8,64,1024]{2,1,0:T(8,128)}, f32[3,64,1024]{2,1,0:T(8,128)}, f32[3,64,1024]{2,1,0:T(8,128)}, f32[8,8,1024]{2,1,0:T(8,128)}, f32[8,8,1024]{2,1,0:T(8,128)}, /*index=5*/f32[16,128]{1,0:T(8,128)}) custom-call(s32[1]{0:T(128)} %bitcast.kref, s32[4]{0:T(128)} %bitcast.20, s32[4,1024]{1,0:T(4,128)} %get-tuple-element.25.row, ...), custom_call_target="tpu_custom_call" | custom-call | flops 1000 | bytes 30000000 | tf_op jit(solution)/shard_map/front/pallas_call | solution.py:511
  74.2 2.5 %collective-permute-start.10 = (f32[8,8,1024]{2,1,0:T(8,128)}, f32[8,8,1024]{2,1,0:T(8,128)S(1)}, u32[]{:S(2)}, u32[]{:S(2)}) collective-permute-start(f32[8,8,1024]{2,1,0:T(8,128)} %get-tuple-element.32), channel_id=1, source_target_pairs={{0,1},{1,2},{2,3},{4,5},{5,6},{6,7},{8,9},{9,10},{10,11},{12,13},{... | collective-permute-start | bytes 786440 | tf_op jit(solution)/shard_map/ppermute | solution.py:275
  76.7 4.2 %collective-permute-start.9 = (f32[8,8,1024]{2,1,0:T(8,128)}, f32[8,8,1024]{2,1,0:T(8,128)S(1)}, u32[]{:S(2)}, u32[]{:S(2)}) collective-permute-start(f32[8,8,1024]{2,1,0:T(8,128)} %get-tuple-element.31), channel_id=1, source_target_pairs={{1,0},{2,1},{3,2},{5,4},{6,5},{7,6},{9,8},{10,9},{11,10},{13,12},{... | collective-permute-start | bytes 786440 | tf_op jit(solution)/shard_map/ppermute | solution.py:275
  80.9 0.1 collective-permute-start.7
  81.0 5.1 %collective-permute-start.8 = (f32[3,64,1024]{2,1,0:T(8,128)}, f32[3,64,1024]{2,1,0:T(8,128)S(1)}, u32[]{:S(2)}, u32[]{:S(2)}) collective-permute-start(f32[3,64,1024]{2,1,0:T(8,128)} %get-tuple-element.30), channel_id=1, source_target_pairs={{0,124},{4,0},{8,4},{12,8},{16,12},{20,16},{24,20},{28,24},{32,28}... | collective-permute-start | bytes 2359304 | tf_op jit(solution)/shard_map/ppermute | solution.py:271
  86.1 0.0 collective-permute-done.10
  86.1 0.0 collective-permute-done.9
  86.1 0.1 broadcast_select_fusion.sside
  86.2 0.0 copy-start.3
  86.2 0.1 collective-permute-start.11
  86.3 5.1 %collective-permute-start.12 = (f32[3,8,1024]{2,1,0:T(8,128)S(1)}, f32[3,8,1024]{2,1,0:T(8,128)S(1)}, u32[]{:S(2)}, u32[]{:S(2)}) collective-permute-start(f32[3,8,1024]{2,1,0:T(8,128)S(1)} %get-tuple-element.34), channel_id=1, source_target_pairs={{0,124},{4,0},{8,4},{12,8},{16,12},{20,16},{24,20},{28,24},{32,28}... | collective-permute-start | bytes 294920 | tf_op jit(solution)/shard_map/ppermute | solution.py:271
  91.3 5.7 %collective-permute-done.11.sclo = f32[3,8,1024]{2,1,0:T(8,128)S(1)} collective-permute-done((f32[3,8,1024]{2,1,0:T(8,128)S(1)}, f32[3,8,1024]{2,1,0:T(8,128)S(1)}, u32[]{:S(2)}, u32[]{:S(2)}) %collective-permute-start.11) | collective-permute-done | bytes 98336 | tf_op jit(solution)/shard_map/ppermute | solution.py:271
  97.0 0.0 collective-permute-done.12.schi
  97.0 0.0 copy-start.12
  97.0 0.0 collective-permute-done.7.slo
  97.0 0.0 copy-start.7
  97.0 0.0 collective-permute-done.8.shi
  97.0 0.0 copy-start.8
  97.0 0.0 copy-done.3
  97.0 0.6 copy-done.11
  97.6 0.0 copy-done.12
  97.7 0.3 copy-done.7
  98.0 0.2 copy-done.8
  98.2 22.5 %sweeps.1 = f32[8,64,1024]{2,1,0:T(8,128)} custom-call(s32[1]{0:T(128)} %bitcast.kref, f32[8,64,1024]{2,1,0:T(8,128)} %load.1, f32[8,64,1024]{2,1,0:T(8,128)} %beta_in.1, f32[8,64,1024]{2,1,0:T(8,128)} %collective-permute-done.refs_0_.lo, f32[8,64,1024]{2,1,0:T(8,128)} %collective-permute-done.1.refs_1_.hi, ...), custom_call_target="tpu_custom_call" | custom-call | flops 1000 | bytes 60000000 | tf_op jit(solution)/shard_map/sweeps/pallas_call | solution.py:528
  (3 shorter events, 0.0 us)
Async XLA Ops:
  6.4 20.7 %copy-start.10 = (f32[5,8,1024]{2,1,0:T(8,128)S(1)}, f32[5,8,1024]{2,1,0:T(8,128)}, u32[]{:S(2)}) copy-start(f32[5,8,1024]{2,1,0:T(8,128)} %get-tuple-element.27.f0) | copy-start | bytes 491524
  6.4 56.6 %collective-permute-start = (f32[8,64,1024]{2,1,0:T(8,128)}, f32[8,64,1024]{2,1,0:T(8,128)}, u32[]{:S(2)}, u32[]{:S(2)}) collective-permute-start(f32[8,64,1024]{2,1,0:T(8,128)} %get-tuple-element.18), channel_id=1, source_target_pairs={{0,4},{4,8},{8,12},{12,16},{16,20},{20,24},{24,28},{28,32},{32,36}... | collective-permute-start | bytes 6291464 | tf_op jit(solution)/shard_map/ppermute | solution.py:271
  6.5 56.5 %collective-permute-start.1 = (f32[8,64,1024]{2,1,0:T(8,128)}, f32[8,64,1024]{2,1,0:T(8,128)}, u32[]{:S(2)}, u32[]{:S(2)}) collective-permute-start(f32[8,64,1024]{2,1,0:T(8,128)} %get-tuple-element.19), channel_id=1, source_target_pairs={{0,124},{4,0},{8,4},{12,8},{16,12},{20,16},{24,20},{28,24},{32,28}... | collective-permute-start | bytes 6291464 | tf_op jit(solution)/shard_map/ppermute | solution.py:271
  12.5 16.2 %collective-permute-start.2 = (f32[21,8,1024]{2,1,0:T(8,128)}, f32[21,8,1024]{2,1,0:T(8,128)S(1)}, u32[]{:S(2)}, u32[]{:S(2)}) collective-permute-start(f32[21,8,1024]{2,1,0:T(8,128)} %get-tuple-element.20), channel_id=1, source_target_pairs={{0,3},{1,0},{2,1},{3,2},{4,7},{5,4},{6,5},{7,6},{8,11},{9,8},{10,9... | collective-permute-start | bytes 2064392 | tf_op jit(solution)/shard_map/ppermute | solution.py:489
  13.0 15.7 %collective-permute-start.3 = (f32[21,8,1024]{2,1,0:T(8,128)}, f32[21,8,1024]{2,1,0:T(8,128)S(1)}, u32[]{:S(2)}, u32[]{:S(2)}) collective-permute-start(f32[21,8,1024]{2,1,0:T(8,128)} %get-tuple-element.21), channel_id=1, source_target_pairs={{0,1},{1,2},{2,3},{3,0},{4,5},{5,6},{6,7},{7,4},{8,9},{9,10},{10,1... | collective-permute-start | bytes 2064392 | tf_op jit(solution)/shard_map/ppermute | solution.py:489
  23.7 15.5 %all-to-all-start = ((f32[8,64,128]{2,1,0:T(8,128)}), f32[8,64,128]{2,1,0:T(8,128)S(1)}, u32[]{:S(2)}, u32[]{:S(2)}) async-start(f32[8,64,128]{2,1,0:T(8,128)} %flux.1), calls=%async_computation | async-start | bytes 524288 | tf_op jit(solution)/shard_map/all_to_all | solution.py:442
  27.1 8.0 %collective-permute-start.6 = (f32[5,8,1024]{2,1,0:T(8,128)S(1)}, f32[5,8,1024]{2,1,0:T(8,128)S(1)}, u32[]{:S(2)}, u32[]{:S(2)}) collective-permute-start(f32[5,8,1024]{2,1,0:T(8,128)S(1)} %copy-done.10), channel_id=1, source_target_pairs={{0,2},{1,3},{2,0},{3,1},{4,6},{5,7},{6,4},{7,5},{8,10},{9,11},{10,... | collective-permute-start | bytes 491528 | tf_op jit(solution)/shard_map/ppermute | solution.py:489
  28.7 0.9 copy-start
  28.8 1.2 copy-start.1
  32.2 16.5 %copy-start.13 = (f32[8,8,1024]{2,1,0:T(8,128)S(1)}, f32[8,8,1024]{2,1,0:T(8,128)}, u32[]{:S(2)}) copy-start(f32[8,8,1024]{2,1,0:T(8,128)} %get-tuple-element.24) | copy-start | bytes 786436
  35.1 4.1 %copy-start.9 = (f32[5,8,1024]{2,1,0:T(8,128)}, f32[5,8,1024]{2,1,0:T(8,128)S(1)}, u32[]{:S(2)}) copy-start(f32[5,8,1024]{2,1,0:T(8,128)S(1)} %collective-permute-done.6.refs_1_.f3) | copy-start | bytes 491524
  39.2 0.7 copy-start.6
  41.7 21.3 %all-to-all-start.1 = ((f32[16,64,128]{2,1,0:T(8,128)}), f32[16,64,128]{2,1,0:T(8,128)S(1)}, u32[]{:S(2)}, u32[]{:S(2)}) async-start(f32[16,64,128]{2,1,0:T(8,128)} %near.1), calls=%async_computation.1 | async-start | bytes 1048576 | tf_op jit(solution)/shard_map/all_to_all | solution.py:442
  48.6 14.3 %collective-permute-start.4 = (f32[8,8,1024]{2,1,0:T(8,128)}, f32[8,8,1024]{2,1,0:T(8,128)S(1)}, u32[]{:S(2)}, u32[]{:S(2)}) collective-permute-start(f32[8,8,1024]{2,1,0:T(8,128)} %get-tuple-element.23), channel_id=1, source_target_pairs={{0,4},{4,8},{8,12},{12,16},{16,20},{20,24},{24,28},{28,32},{32,36}... | collective-permute-start | bytes 786440 | tf_op jit(solution)/shard_map/ppermute | solution.py:271
  48.7 14.3 %collective-permute-start.5 = (f32[8,8,1024]{2,1,0:T(8,128)S(1)}, f32[8,8,1024]{2,1,0:T(8,128)S(1)}, u32[]{:S(2)}, u32[]{:S(2)}) collective-permute-start(f32[8,8,1024]{2,1,0:T(8,128)S(1)} %copy-done.13), channel_id=1, source_target_pairs={{0,124},{4,0},{8,4},{12,8},{16,12},{20,16},{24,20},{28,24},{32,28}... | collective-permute-start | bytes 786440 | tf_op jit(solution)/shard_map/ppermute | solution.py:271
  63.0 0.7 copy-start.4
  63.0 0.8 copy-start.5
  63.0 0.9 copy-start.2
  74.2 11.8 %collective-permute-start.10 = (f32[8,8,1024]{2,1,0:T(8,128)}, f32[8,8,1024]{2,1,0:T(8,128)S(1)}, u32[]{:S(2)}, u32[]{:S(2)}) collective-permute-start(f32[8,8,1024]{2,1,0:T(8,128)} %get-tuple-element.32), channel_id=1, source_target_pairs={{0,1},{1,2},{2,3},{4,5},{5,6},{6,7},{8,9},{9,10},{10,11},{12,13},{... | collective-permute-start | bytes 786440 | tf_op jit(solution)/shard_map/ppermute | solution.py:275
  76.7 9.4 %collective-permute-start.9 = (f32[8,8,1024]{2,1,0:T(8,128)}, f32[8,8,1024]{2,1,0:T(8,128)S(1)}, u32[]{:S(2)}, u32[]{:S(2)}) collective-permute-start(f32[8,8,1024]{2,1,0:T(8,128)} %get-tuple-element.31), channel_id=1, source_target_pairs={{1,0},{2,1},{3,2},{5,4},{6,5},{7,6},{9,8},{10,9},{11,10},{13,12},{... | collective-permute-start | bytes 786440 | tf_op jit(solution)/shard_map/ppermute | solution.py:275
  80.9 16.1 %collective-permute-start.7 = (f32[3,64,1024]{2,1,0:T(8,128)}, f32[3,64,1024]{2,1,0:T(8,128)S(1)}, u32[]{:S(2)}, u32[]{:S(2)}) collective-permute-start(f32[3,64,1024]{2,1,0:T(8,128)} %get-tuple-element.29), channel_id=1, source_target_pairs={{0,4},{4,8},{8,12},{12,16},{16,20},{20,24},{24,28},{28,32},{32,36}... | collective-permute-start | bytes 2359304 | tf_op jit(solution)/shard_map/ppermute | solution.py:271
  81.0 16.0 %collective-permute-start.8 = (f32[3,64,1024]{2,1,0:T(8,128)}, f32[3,64,1024]{2,1,0:T(8,128)S(1)}, u32[]{:S(2)}, u32[]{:S(2)}) collective-permute-start(f32[3,64,1024]{2,1,0:T(8,128)} %get-tuple-element.30), channel_id=1, source_target_pairs={{0,124},{4,0},{8,4},{12,8},{16,12},{20,16},{24,20},{28,24},{32,28}... | collective-permute-start | bytes 2359304 | tf_op jit(solution)/shard_map/ppermute | solution.py:271
  86.2 10.9 %copy-start.3 = (f32[8,8,1024]{2,1,0:T(8,128)}, f32[8,8,1024]{2,1,0:T(8,128)S(1)}, u32[]{:S(2)}) copy-start(f32[8,8,1024]{2,1,0:T(8,128)S(1)} %broadcast_select_fusion.sside) | copy-start | bytes 786436
  86.2 10.8 %collective-permute-start.11 = (f32[3,8,1024]{2,1,0:T(8,128)S(1)}, f32[3,8,1024]{2,1,0:T(8,128)S(1)}, u32[]{:S(2)}, u32[]{:S(2)}) collective-permute-start(f32[3,8,1024]{2,1,0:T(8,128)S(1)} %get-tuple-element.35), channel_id=1, source_target_pairs={{0,4},{4,8},{8,12},{12,16},{16,20},{20,24},{24,28},{28,32},{32,36}... | collective-permute-start | bytes 294920 | tf_op jit(solution)/shard_map/ppermute | solution.py:271
  86.3 10.7 %collective-permute-start.12 = (f32[3,8,1024]{2,1,0:T(8,128)S(1)}, f32[3,8,1024]{2,1,0:T(8,128)S(1)}, u32[]{:S(2)}, u32[]{:S(2)}) collective-permute-start(f32[3,8,1024]{2,1,0:T(8,128)S(1)} %get-tuple-element.34), channel_id=1, source_target_pairs={{0,124},{4,0},{8,4},{12,8},{16,12},{20,16},{24,20},{28,24},{32,28}... | collective-permute-start | bytes 294920 | tf_op jit(solution)/shard_map/ppermute | solution.py:271
  97.0 0.6 copy-start.11
  97.0 0.7 copy-start.12
  97.0 1.0 copy-start.7
  97.0 1.2 copy-start.8

commit v6 on v5

--- a/solution.py
+++ b/solution.py
@@ -89,7 +89,7 @@
 
 
 def front_kernel(kref, cnt, row, parts, f0, f1, f2, f3, lane, vert, share, pred_any, *refs):
-    front_body(kref, cnt, row, parts, (f0, f1, f2, f3), lane, vert, share, pred_any, *refs[5:])
+    front_body(kref, cnt, row, parts, (f0, f1, f2, f3), lane, vert, share, pred_any, *refs[6:])
 
 
 def front_body(kref, cnt, row, parts, fronts, lane, vert, share, pred_any, src_any, sup, sdown, srup, srdown,
@@ -275,88 +275,98 @@
     return lax.ppermute(x, "rad", [(i, i + d) for i in range(4) if 0 <= i + d < 4])
 
 
-def ring_tile(from_above, from_below):
-    return jnp.where(iota(from_above.shape, 1) < 4, from_above, from_below)
-
-
-def wide(x):
-    return jnp.concatenate([x] * (Z // 128), axis=1)
-
-
-def sweep_kernel(kref, load, beta_in, lo, hi, side, clo, chi, src, slo, shi, sside, sclo, schi,
-                 out, pa, pb, beta, th, rr, zz, ww, ss, rads, sems):
+def ring_kernel(above, below, unread, side, eup, edown):
+    side[...] = jnp.where(iota((T, 8, Z), 1) < 4, above[...], below[...])
+    eup[...] = side[T - H + 1:]
+    edown[...] = side[:H - 1]
+
+
+nothing = lambda: jnp.zeros((8, 128), F32)
+columns = range(Z // 128)
+
+
+def cut(it):
+    it = it % RT
+    return slice(it * 8, it * 8 + 8)
+
+
+def vec(ref, t, it, v):
+    return ref[t, cut(it), v * 128:v * 128 + 128]
+
+
+def put(ref, t, it, v, x):
+    ref[t, cut(it), v * 128:v * 128 + 128] = x
+
+
+def up_row(x):
+    return pltpu.roll(x, 7, 0)
+
+
+def down_row(x):
+    return pltpu.roll(x, 1, 0)
+
+
+def next_lane(ref, t, it, v, cur):
+    nxt = pltpu.roll(vec(ref, t, it, v + 1), 127, 1) if v + 1 < Z // 128 else cur
+    return jnp.where(iota((8, 128), 1) == 127, nxt, cur), nxt
+
+
+def ring_rows(k, it):
+    sub = iota((8, 128), 0)
+    return k * R + (it * 8 + sub if it < RT - 1 else jnp.where(sub < 4, R + sub, sub - 8))
+
+
+def radii(k, it):
+    return 0.25 * 256 + ring_rows(k, it).astype(F32) + 0.5
+
+
+def relaxed(old, t, it, v, p, pz, pu, prev, zprev, tu, td, r, z, w):
+    acc = (tu * vec(old, t + 1, it, v) + td * vec(old, t - 1, it, v)) + r * pu
+    rp = down_row(r * p)
+    acc = acc + jnp.where(iota((8, 128), 0) == 0, prev, rp)
+    zu, pz = next_lane(old, t, it, v, pz)
+    zp = pltpu.roll(z * p, 1, 1)
+    acc = acc + (z * zu + jnp.where(iota((8, 128), 1) == 0, zprev, zp))
+    return (1.0 - OMEGA) * p + w * acc, pz, rp, zp
+
+
+PARTS = ((1, 6), (7, 4), (11, 4))
+
+
+def coef_kernel(first, count, kref, load, beta_in, lo, hi, side, clo, chi,
+                h_out, w_out, r_out, z_out, t_out, pa, beta, hh, ww, rr, zz, th, rads, sems, osems):
     k = kref[0]
     rows, ring = pl.ds(0, R), pl.ds(R, 8)
-    half = T // 2
-
-    def planes(own, tile_own, low, tile_low, high, tile_high, first):
-        return [(low, tile_low, first, H - first), (own.at[pl.ds(0, half)], tile_own.at[pl.ds(0, half)], H, half),
-                (own.at[pl.ds(half, half)], tile_own.at[pl.ds(half, half)], H + half, half),
-                (high, tile_high, H + T, H - first)]
-
-    def both(x, n, count):
-        return x.at[pl.ds(n * count, count)]
-
-    fields = [(ref, planes(own, both(side, n, T), both(lo, n, H), both(clo, n, H), both(hi, n, H), both(chi, n, H), 0))
-              for ref, own, n in ((beta, beta_in, 1), (pa, load, 0))]
-    fields.append((ss, planes(src, sside, slo, sclo, shi, schi, 1)))
-    waits = []
-    for g in range(4):
-        cs = []
-        for f, (ref, parts) in enumerate(fields):
-            main, tile, first, count = parts[g]
-            cs.append(pltpu.make_async_copy(main, ref.at[pl.ds(first, count), rows], sems.at[g, f, 0]))
-            cs.append(pltpu.make_async_copy(tile, ref.at[pl.ds(first, count), ring], sems.at[g, f, 1]))
-        waits.append(cs)
-
-    def begin(g):
-        for c in waits[g] if g < 4 else ():
-            c.start()
-
-    begin(0)
-    begin(1)
-    sub, lanes = iota((8, 128), 0), iota((8, 128), 1)
-    top, bottom, last_lane, first_lane = sub == 7, sub == 0, lanes == 127, lanes == 0
+    copies = []
+    begin, end = first - 1, first + count + 1
+    for f, (ref, own, n) in enumerate(((beta, beta_in, 1), (pa, load, 0))):
+        spans = ((max(begin, 0), min(end, H), lo, clo, n * H, 0, n * H),
+                 (max(begin, H), min(end, H + T), own, side, 0, H, n * T),
+                 (max(begin, H + T), min(end, TE), hi, chi, n * H, H + T, n * H))
+        for m, (x, y, main, tile, base, origin, tbase) in enumerate(spans):
+            if x < y:
+                copies.append(pltpu.make_async_copy(
+                    main.at[pl.ds(base + x - origin, y - x)], ref.at[pl.ds(x - begin, y - x), rows], sems.at[f, m, 0]))
+                copies.append(pltpu.make_async_copy(
+                    tile.at[pl.ds(tbase + x - origin, y - x)], ref.at[pl.ds(x - begin, y - x), ring], sems.at[f, m, 1]))
+    for c in copies:
+        c.start()
+    lanes = iota((8, 128), 1)
+    top, bottom, last_lane, first_lane = iota((8, 128), 0) == 7, iota((8, 128), 0) == 0, lanes == 127, lanes == 0
     angular = (256 / (2.0 * math.pi)) ** 2
     for it in range(RT):
-        gi = k * R + (it * 8 + sub if it < RT - 1 else jnp.where(sub < 4, R + sub, sub - 8))
-        ra = 0.25 * 256 + gi.astype(F32) + 0.5
-        rads[0, it] = ra
+        ra, gi = radii(k, it), ring_rows(k, it)
+        rads[0, it] = (0.5 * AXIAL) * ra
         rads[1, it] = (0.5 * angular) / ra
         rads[2, it] = jnp.where((gi >= 0) & (gi < 255), 0.5 * (ra + 0.5), 0.0)
-    nothing = jnp.zeros((8, 128), F32)
-    columns = range(Z // 128)
-
-    def cut(it):
-        it = it % RT
-        return slice(it * 8, it * 8 + 8)
-
-    def vec(ref, t, it, v):
-        return ref[t, cut(it), v * 128:v * 128 + 128]
-
-    def put(ref, t, it, v, x):
-        ref[t, cut(it), v * 128:v * 128 + 128] = x
-
-    def up_row(x):
-        return pltpu.roll(x, 7, 0)
-
-    def down_row(x):
-        return pltpu.roll(x, 1, 0)
-
-    def next_lane(ref, t, it, v, cur):
-        nxt = pltpu.roll(vec(ref, t, it, v + 1), 127, 1) if v + 1 < Z // 128 else cur
-        return jnp.where(last_lane, nxt, cur), nxt
-
-    def relaxed(old, t, it, v, p, pz, pu, prev, zprev, tu, td, r, z, w, s):
-        acc = (tu * vec(old, t + 1, it, v) + td * vec(old, t - 1, it, v)) + r * pu
-        rp = down_row(r * p)
-        acc = acc + jnp.where(bottom, prev, rp)
-        zu, pz = next_lane(old, t, it, v, pz)
-        zp = pltpu.roll(z * p, 1, 1)
-        acc = acc + (z * zu + jnp.where(first_lane, zprev, zp))
-        return (1.0 - OMEGA) * p + w * (acc - s), pz, rp, zp
-
-    def first_sweep(t, _):
+    for c in copies:
+        c.wait()
+    for it in range(RT):
+        for v in columns:
+            put(th, 0, it, v, (vec(beta, 0, it, v) + vec(beta, 1, it, v)) * rads[1, it])
+
+    def plane(t, _):
+        o = t - 1
         last = RT - 1
         bup = [up_row(vec(beta, t, 0, v)) for v in columns]
         pup = [up_row(vec(pa, t, 0, v)) for v in columns]
@@ -367,11 +377,10 @@
             fprev.append(down_row(face))
             prev.append(down_row(face * vec(pa, t, last, v)))
         for it in range(RT):
-            ra, ang, rad = rads[0, it], rads[1, it], rads[2, it]
-            axi = (0.5 * AXIAL) * ra
+            axi, ang, rad = rads[0, it], rads[1, it], rads[2, it]
             bz = pltpu.roll(vec(beta, t, it, 0), 127, 1)
             pz = pltpu.roll(vec(pa, t, it, 0), 127, 1)
-            zfprev = zprev = nothing
+            zfprev = zprev = nothing()
             for v in columns:
                 b, p = vec(beta, t, it, v), vec(pa, t, it, v)
                 nb, np_ = up_row(vec(beta, t, it + 1, v)), up_row(vec(pa, t, it + 1, v))
@@ -393,16 +402,64 @@
                 w = pl.reciprocal(d, approx=True)
                 w = w * (2.0 - d * w)
                 w = (w * (2.0 - d * w)) * OMEGA
-                sc = vec(ss, t, it, v) * ra
                 put(th, t, it, v, tu)
-                put(rr, t, it, v, r)
-                put(zz, t, it, v, z)
-                put(ww, t, it, v, w)
-                put(ss, t, it, v, sc)
+                put(rr, o, it, v, r)
+                put(zz, o, it, v, z)
+                put(ww, o, it, v, w)
                 pu = jnp.where(top, np_, pup[v])
-                new, pz, prev[v], zprev = relaxed(pa, t, it, v, p, pz, pu, prev[v], zprev, tu, td, r, z, w, sc)
-                put(pb, t, it, v, new)
+                new, pz, prev[v], zprev = relaxed(pa, t, it, v, p, pz, pu, prev[v], zprev, tu, td, r, z, w)
+                put(hh, o, it, v, new)
                 bup[v], pup[v], fprev[v], zfprev = nb, np_, froll, zr
+        for c in results(o):
+            c.start()
+        return 0
+
+    def results(o):
+        pairs = ((hh.at[o], h_out.at[o]), (ww.at[o], w_out.at[o]), (rr.at[o], r_out.at[o]),
+                 (zz.at[o], z_out.at[o]), (th.at[o + 1], t_out.at[o]))
+        return [pltpu.make_async_copy(a, b, osems.at[m, o]) for m, (a, b) in enumerate(pairs)]
+
+    lax.fori_loop(1, count + 1, plane, 0)
+    for o in range(count):
+        for c in results(o):
+            c.wait()
+
+
+def sweep_kernel(kref, *refs):
+    given, (src, slo, shi, sside, sclo, schi, out_any) = refs[:15], refs[15:22]
+    pa, pb, th, rr, zz, ww, ss, out, sems, osems = refs[22:]
+    k = kref[0]
+    rows, ring = pl.ds(0, R), pl.ds(R, 8)
+    waits = []
+    for g, (first, count) in enumerate(PARTS):
+        cs = []
+
+        def fetch(a, b):
+            cs.append(pltpu.make_async_copy(a, b, sems.at[g, len(cs)]))
+
+        for a, ref in zip(given[5 * g:5 * g + 2], (pb, ww)):
+            fetch(a, ref.at[pl.ds(first, count)])
+        for x, y, main, tile, origin in ((first, min(first + count, H), slo, sclo, 1),
+                                         (max(first, H), min(first + count, H + T), src, sside, H),
+                                         (max(first, H + T), first + count, shi, schi, H + T)):
+            if x < y:
+                fetch(main.at[pl.ds(x - origin, y - x)], ss.at[pl.ds(x, y - x), rows])
+                fetch(tile.at[pl.ds(x - origin, y - x)], ss.at[pl.ds(x, y - x), ring])
+        for a, ref in zip(given[5 * g + 2:5 * g + 5], (rr, zz, th)):
+            fetch(a, ref.at[pl.ds(first, count)])
+        waits.append(cs)
+
+    def begin(g):
+        for c in waits[g] if g < len(PARTS) else ():
+            c.start()
+
+    def add_source(t, _):
+        for it in range(RT):
+            ra = radii(k, it)
+            for v in columns:
+                s = vec(ww, t, it, v) * (vec(ss, t, it, v) * ra)
+                put(ss, t, it, v, s)
+                put(pb, t, it, v, vec(pb, t, it, v) - s)
         return 0
 
     def sweep(old, new, t, tiles, shift):
@@ -410,32 +467,38 @@
         prev = [down_row(vec(rr, t, -1, v) * vec(old, t, -1, v)) for v in columns]
         for it in range(tiles):
             pz = pltpu.roll(vec(old, t, it, 0), 127, 1)
-            zprev = nothing
+            zprev = nothing()
             for v in columns:
                 p = vec(old, t, it, v)
                 np_ = up_row(vec(old, t, it + 1, v))
-                pu = jnp.where(top, np_, pup[v])
+                pu = jnp.where(iota((8, 128), 0) == 7, np_, pup[v])
                 x, pz, prev[v], zprev = relaxed(
                     old, t, it, v, p, pz, pu, prev[v], zprev, vec(th, t, it, v), vec(th, t - 1, it, v),
-                    vec(rr, t, it, v), vec(zz, t, it, v), vec(ww, t, it, v), vec(ss, t, it, v))
-                put(new, t - shift, it, v, x)
+                    vec(rr, t, it, v), vec(zz, t, it, v), vec(ww, t, it, v))
+                put(new, t - shift, it, v, x - vec(ss, t, it, v))
                 pup[v] = np_
         return 0
 
-    ends = (H - 1, H + half - 1, H + T - 1, TE - 1)
-    start = 1
-    for g in range(4):
+    begin(0)
+    begin(1)
+    start = 2
+    for g, (first, count) in enumerate(PARTS):
         for c in waits[g]:
             c.wait()
         begin(g + 2)
-        if g == 0:
-            for it in range(RT):
-                th[0, cut(it), :] = (beta[0, cut(it), :] + beta[1, cut(it), :]) * wide(rads[1, it])
-        lax.fori_loop(start, ends[g], first_sweep, 0)
-        start = ends[g]
-    lax.fori_loop(2, TE - 2, lambda t, _: sweep(pb, pa, t, RT, 0), 0)
+        lax.fori_loop(first, first + count, add_source, 0)
+        lax.fori_loop(start, first + count - 1, lambda t, _: sweep(pb, pa, t, RT, 0), 0)
+        start = first + count - 1
     lax.fori_loop(3, TE - 3, lambda t, _: sweep(pa, pb, t, RT, 0), 0)
-    lax.fori_loop(4, TE - 4, lambda t, _: sweep(pb, out, t, RT - 1, H), 0)
+
+    def final(t, _):
+        sweep(pb, out, t, RT - 1, H)
+        pltpu.make_async_copy(out.at[t - H], out_any.at[t - H], osems.at[t - H]).start()
+        return 0
+
+    lax.fori_loop(4, TE - 4, final, 0)
+    for t in range(T):
+        pltpu.make_async_copy(out.at[t], out_any.at[t], osems.at[t]).wait()
 
 
 def from_all(copies, axes):
@@ -507,11 +570,22 @@
         sum_kernel, out_shape=shape(16, GROUPS * BS, NB),
         in_specs=[VM, ANY, ANY], out_specs=VM, compiler_params=params(4), name="near",
     )(from_all(partial, ("z", "core")), side, across)
+    def coefficients(first, count):
+        ext = lambda n: pltpu.VMEM((n, RE, Z), F32)
+        return pl.pallas_call(
+            functools.partial(coef_kernel, first, count), out_shape=(shape(count, RE, Z),) * 5,
+            in_specs=[SM] + [ANY] * 7, out_specs=(ANY,) * 5,
+            scratch_shapes=[ext(count + 2)] * 2 + [ext(count)] * 4 + [ext(count + 1), pltpu.VMEM((3, RT, 8, 128), F32),
+                            pltpu.SemaphoreType.DMA((2, 3, 2)), pltpu.SemaphoreType.DMA((5, count))],
+            compiler_params=params(40), cost_estimate=cost(1 + count), name="coef",
+        )(kidx, load, beta, lo, hi, side, clo, chi)
+
+    given = [coefficients(first, count) for first, count in PARTS]
     flux = from_all(near, ("y", "rad"))
     source, sup, sdown, srup, srdown, height = pl.pallas_call(
         front_kernel,
         out_shape=(plane(T), plane(H - 1), plane(H - 1), tile(T), tile(T), shape(BS, NB)),
-        in_specs=[SM, SM, SM, VM] + [ANY] * 4 + [VM] * 3 + [ANY] * 6, out_specs=(ANY,) * 5 + (VM,),
+        in_specs=[SM, SM, SM, VM] + [ANY] * 4 + [VM] * 3 + [ANY] * 7, out_specs=(ANY,) * 5 + (VM,),
         scratch_shapes=[pltpu.VMEM((GROUPS, FT, 8, Z), F32),
                         pltpu.VMEM((GROUPS, BS, NB), F32), pltpu.VMEM((GROUPS, BS, NB), F32),
                         pltpu.VMEM((GROUPS, SLOTS, 128), F32), pltpu.VMEM((GROUPS * BS, NB), F32),
@@ -520,17 +594,20 @@
                         pltpu.SemaphoreType.DMA((GROUPS,))]
         + [pltpu.VMEM((T * R * 8, 128), F32)] * GROUPS,
         compiler_params=params(20), cost_estimate=cost(10), name="front",
-    )(kidx, tally, row, flux, front, rhi, rlo, across, lane, vertex, share, outflow, lo, hi, side, clo, chi)
+    )(kidx, tally, row, flux, front, rhi, rlo, across, lane, vertex, share, outflow, lo, hi, side, clo, chi, given[0][0])
     slo, shi = shift_azim(sup, 1), shift_azim(sdown, -1)
-    sside = ring_tile(shift_rad(srdown, -1), shift_rad(srup, 1))
-    sclo, schi = shift_azim(sside[T - H + 1:], 1), shift_azim(sside[:H - 1], -1)
+    sside, seup, sedown = pl.pallas_call(
+        ring_kernel, out_shape=(tile(T), tile(H - 1), tile(H - 1)),
+        in_specs=[VM, VM, ANY], out_specs=(VM,) * 3, compiler_params=params(4), cost_estimate=cost(1), name="ring",
+    )(shift_rad(srdown, -1), shift_rad(srup, 1), given[1][0])
+    sclo, schi = shift_azim(seup, 1), shift_azim(sedown, -1)
     ext = pltpu.VMEM((TE, RE, Z), F32)
     pressure = pl.pallas_call(
         sweep_kernel, out_shape=plane(T),
-        in_specs=[SM] + [ANY] * 13, out_specs=VM,
-        scratch_shapes=[ext] * 8 + [pltpu.VMEM((3, RT, 8, 128), F32), pltpu.SemaphoreType.DMA((4, 3, 2))],
+        in_specs=[SM] + [ANY] * 21, out_specs=ANY,
+        scratch_shapes=[ext] * 7 + [block, pltpu.SemaphoreType.DMA((len(PARTS), 9)), pltpu.SemaphoreType.DMA((T,))],
         compiler_params=params(46), cost_estimate=cost(20), name="sweeps",
-    )(kidx, load, beta, lo, hi, side, clo, chi, source, slo, shi, sside, sclo, schi)
+    )(kidx, *[x for part in given for x in part], source, slo, shi, sside, sclo, schi)
     return pressure, height.reshape(NB * BS)
 
 

time: 121 us -> 133 us (1.099)
  Pallas kernels: 51.8 us -> 67.4 us
  waiting for transfers between devices: 21.9 us -> 16.2 us
    pallas_call x0 -> x4, Pallas kernels: none -> 24.2 us  [the longest x3 22.3 us: coefficients(): pl.pallas_call(functools.partial(coef_kernel, first, count), out_shape=(s...]
    pallas_call x1, Pallas kernels: 22.5 us -> 14.9 us  [per_device(): pl.pallas_call(sweep_kernel, out_shape=plane(T), in_specs=[SM] + [ANY] *...]
    ppermute x8, waiting for transfers between devices: 14.9 us -> 9.29 us  [shift_azim(): return lax.ppermute(x, AZIM, [(i, (i + d) % 32) for i in range(32)])]
  transfers between devices with their start and end apart: 15 -> 15, of which waited for: 4 -> 3; matrix products, arithmetic and copies ran while one was open for 0% -> 0% of each run, Pallas kernels for 11% -> 28%
where the time goes in v6:
time: 133 us; the launch traced here: 132 us
  Pallas kernels  67.4 us (51%)
  starting transfers between devices  42.3 us (32%)
  waiting for transfers between devices  16.2 us (12%)
  local copies, waits for them, and re-layouts  5.21 us (4%)
    pallas_call x3, Pallas kernels, coefficients(): pl.pallas_call(functools.partial(coef_kernel, first, count), out_shape=(s...  22.3 us
    ppermute x8, starting transfers between devices, shift_azim(): return lax.ppermute(x, AZIM, [(i, (i + d) % 32) for i in range(32)])  21.3 us
    pallas_call x1, Pallas kernels, per_device(): pl.pallas_call(sweep_kernel, out_shape=plane(T), in_specs=[SM] + [ANY] *...  14.9 us
    all_to_all x2, starting transfers between devices, from_all(): return lax.all_to_all(copies, axes, 0, 0)  10.4 us
    pallas_call x1, Pallas kernels, per_device(): pl.pallas_call(front_kernel, out_shape=(plane(T), plane(H - 1), plane(H -...  9.64 us
    ppermute x8, waiting for transfers between devices, shift_azim(): return lax.ppermute(x, AZIM, [(i, (i + d) % 32) for i in range(32)])  9.29 us
    pallas_call x1, Pallas kernels, per_device(): pl.pallas_call(flux_kernel, out_shape=shape(8, GROUPS * BS, NB), in_specs...  8.87 us
    ppermute x2, starting transfers between devices, shift_rad(): lax.ppermute(x, 'rad', [(i, i + d) for i in range(4) if 0 <= i + d < 4])  6.47 us
  transfers between devices with their start and end apart: 15, of which 3 were waited for; matrix products, arithmetic and copies ran while one was open for 0% of the time, Pallas kernels for 28%

profile of v6, /device:TPU:2, one launch (start us, length us, event | category | flops | bytes accessed | tf_op | source)
XLA Modules:
  0.0 132.2 jit_solution(1958206873596820943)
XLA Ops:
  0.6 5.8 %pack.1 = (f32[8,64,1024]{2,1,0:T(8,128)}, f32[8,64,1024]{2,1,0:T(8,128)}, f32[21,8,1024]{2,1,0:T(8,128)}, f32[21,8,1024]{2,1,0:T(8,128)}, f32[5,8,1024]{2,1,0:T...) custom-call(f32[8,64,1024]{2,1,0:T(8,128)} %load.5, f32[8,64,1024]{2,1,0:T(8,128)} %beta_in.5, f32[256,128]{1,0:T(8,128)} %bitcast.10, ...), custom_call_target="tpu_custom_call" | custom-call | flops 1000 | bytes 12000000 | tf_op jit(solution)/shard_map/pack/pallas_call | solution.py:543
  6.4 0.0 copy-start.10
  6.4 0.1 collective-permute-start
  6.5 6.0 %collective-permute-start.1 = (f32[8,64,1024]{2,1,0:T(8,128)}, f32[8,64,1024]{2,1,0:T(8,128)}, u32[]{:S(2)}, u32[]{:S(2)}) collective-permute-start(f32[8,64,1024]{2,1,0:T(8,128)} %get-tuple-element.37), channel_id=1, source_target_pairs={{0,124},{4,0},{8,4},{12,8},{16,12},{20,16},{24,20},{28,24},{32,28}... | collective-permute-start | bytes 6291464 | tf_op jit(solution)/shard_map/ppermute | solution.py:271
  12.5 0.5 collective-permute-start.2
  13.0 1.5 %collective-permute-start.3 = (f32[21,8,1024]{2,1,0:T(8,128)}, f32[21,8,1024]{2,1,0:T(8,128)S(1)}, u32[]{:S(2)}, u32[]{:S(2)}) collective-permute-start(f32[21,8,1024]{2,1,0:T(8,128)} %get-tuple-element.39), channel_id=1, source_target_pairs={{0,1},{1,2},{2,3},{3,0},{4,5},{5,6},{6,7},{7,4},{8,9},{9,10},{10,1... | collective-permute-start | bytes 2064392 | tf_op jit(solution)/shard_map/ppermute | solution.py:552
  14.5 8.9 %flux.1 = f32[8,64,128]{2,1,0:T(8,128)} custom-call(s32[4]{0:T(128)} %bitcast.19, s32[4,1024]{1,0:T(4,128)} %get-tuple-element.58.row, f32[8,64,1024]{2,1,0:T(8,128)} %heat_any.1, s32[4,1024]{1,0:T(4,128)} %get-tuple-element.59.lane, s32[4,1024]{1,0:T(4,128)} %bitcast.11, f32[4,1024]{1,0:T(4,128)} %bitcast.13), custom_call_target="tpu_custom_call" | custom-call | flops 1000 | bytes 30000000 | tf_op jit(solution)/shard_map/flux/pallas_call | solution.py:555
  23.4 3.4 %all-to-all-start = ((f32[8,64,128]{2,1,0:T(8,128)}), f32[8,64,128]{2,1,0:T(8,128)S(1)}, u32[]{:S(2)}, u32[]{:S(2)}) async-start(f32[8,64,128]{2,1,0:T(8,128)} %flux.1), calls=%async_computation | async-start | bytes 524288 | tf_op jit(solution)/shard_map/all_to_all | solution.py:505
  26.8 0.0 copy-done.10
  26.8 2.1 %collective-permute-start.6 = (f32[5,8,1024]{2,1,0:T(8,128)S(1)}, f32[5,8,1024]{2,1,0:T(8,128)S(1)}, u32[]{:S(2)}, u32[]{:S(2)}) collective-permute-start(f32[5,8,1024]{2,1,0:T(8,128)S(1)} %copy-done.10), channel_id=1, source_target_pairs={{0,2},{1,3},{2,0},{3,1},{4,6},{5,7},{6,4},{7,5},{8,10},{9,11},{10,... | collective-permute-start | bytes 491528 | tf_op jit(solution)/shard_map/ppermute | solution.py:552
  28.9 0.0 collective-permute-done.2.above.f1
  28.9 0.0 copy-start.2
  28.9 0.0 collective-permute-done.3.below_any.f2
  29.0 0.0 copy-start.3
  29.0 0.9 copy-done.2
  29.8 0.2 copy-done.3
  30.0 2.2 %side.1 = (f32[16,8,1024]{2,1,0:T(8,128)}, f32[8,8,1024]{2,1,0:T(8,128)}, f32[8,8,1024]{2,1,0:T(8,128)}) custom-call(s32[1]{0:T(128)} %bitcast.kref, f32[21,8,1024]{2,1,0:T(8,128)} %copy-done.2, f32[21,8,1024]{2,1,0:T(8,128)} %copy-done.3), custom_call_target="tpu_custom_call" | custom-call | flops 1000 | bytes 6000000 | tf_op jit(solution)/shard_map/side/pallas_call | solution.py:562
  32.3 0.0 copy-start.13
  32.3 2.6 %collective-permute-done.6.refs_1_.f3 = f32[5,8,1024]{2,1,0:T(8,128)S(1)} collective-permute-done((f32[5,8,1024]{2,1,0:T(8,128)S(1)}, f32[5,8,1024]{2,1,0:T(8,128)S(1)}, u32[]{:S(2)}, u32[]{:S(2)}) %collective-permute-start.6) | collective-permute-done | bytes 163872 | tf_op jit(solution)/shard_map/ppermute | solution.py:552
  34.9 4.3 %all-to-all-done.parts = f32[8,64,128]{2,1,0:T(8,128)S(1)} async-done(((f32[8,64,128]{2,1,0:T(8,128)}), f32[8,64,128]{2,1,0:T(8,128)S(1)}, u32[]{:S(2)}, u32[]{:S(2)}) %all-to-all-start) | async-done | bytes 262176 | tf_op jit(solution)/shard_map/all_to_all | solution.py:505
  39.2 0.0 copy-done.8
  39.2 0.7 copy-done.5
  39.9 1.8 %near.1 = f32[16,64,128]{2,1,0:T(8,128)} custom-call(f32[8,64,128]{2,1,0:T(8,128)} %copy-done.5, f32[16,8,1024]{2,1,0:T(8,128)} %get-tuple-element.40.side.refs_0_.refs_2_, f32[5,8,1024]{2,1,0:T(8,128)} %copy-done.8), custom_call_target="tpu_custom_call" | custom-call | tf_op jit(solution)/shard_map/near/pallas_call | solution.py:569
  41.7 7.0 %all-to-all-start.1 = ((f32[16,64,128]{2,1,0:T(8,128)}), f32[16,64,128]{2,1,0:T(8,128)S(1)}, u32[]{:S(2)}, u32[]{:S(2)}) async-start(f32[16,64,128]{2,1,0:T(8,128)} %near.1), calls=%async_computation.1 | async-start | bytes 1048576 | tf_op jit(solution)/shard_map/all_to_all | solution.py:505
  48.7 0.0 collective-permute-start.4
  48.7 0.0 copy-done.13
  48.7 5.1 %collective-permute-start.5 = (f32[8,8,1024]{2,1,0:T(8,128)S(1)}, f32[8,8,1024]{2,1,0:T(8,128)S(1)}, u32[]{:S(2)}, u32[]{:S(2)}) collective-permute-start(f32[8,8,1024]{2,1,0:T(8,128)S(1)} %copy-done.13), channel_id=1, source_target_pairs={{0,124},{4,0},{8,4},{12,8},{16,12},{20,16},{24,20},{28,24},{32,28}... | collective-permute-start | bytes 786440 | tf_op jit(solution)/shard_map/ppermute | solution.py:271
  53.7 9.3 %collective-permute-done.4.clo.refs_3_ = f32[8,8,1024]{2,1,0:T(8,128)S(1)} collective-permute-done((f32[8,8,1024]{2,1,0:T(8,128)}, f32[8,8,1024]{2,1,0:T(8,128)S(1)}, u32[]{:S(2)}, u32[]{:S(2)}) %collective-permute-start.4) | collective-permute-done | bytes 262176 | tf_op jit(solution)/shard_map/ppermute | solution.py:271
  63.0 0.0 collective-permute-done.5.chi.refs_4_
  63.0 0.0 collective-permute-done.lo.refs_0_
  63.0 0.0 collective-permute-done.1.hi.refs_1_
  63.0 0.7 copy-done
  63.7 0.1 copy-done.1
  63.8 8.8 %coef.3 = (f32[6,72,1024]{2,1,0:T(8,128)}, f32[6,72,1024]{2,1,0:T(8,128)}, f32[6,72,1024]{2,1,0:T(8,128)}, f32[6,72,1024]{2,1,0:T(8,128)}, f32[6,72,1024]{2,1,0:T(8,128)}) custom-call(s32[1]{0:T(128)} %bitcast.kref, f32[8,64,1024]{2,1,0:T(8,128)} %load.5, f32[8,64,1024]{2,1,0:T(8,128)} %beta_in.5, f32[8,64,1024]{2,1,0:T(8,128)} %collective-permute-done.lo.refs_0_, ...), custom_call_target="tpu_custom_call" | custom-call | flops 1000 | bytes 21000000 | tf_op jit(solution)/shard_map/coef/pallas_call | solution.py:575
  72.6 0.0 all-to-all-done.1.parts
  72.7 0.0 copy-start.4
  72.7 0.8 copy-done.4
  73.5 9.6 %front.1 = (f32[8,64,1024]{2,1,0:T(8,128)}, f32[3,64,1024]{2,1,0:T(8,128)}, f32[3,64,1024]{2,1,0:T(8,128)}, f32[8,8,1024]{2,1,0:T(8,128)}, f32[8,8,1024]{2,1,0:T(8,128)}, /*index=5*/f32[16,128]{1,0:T(8,128)}) custom-call(s32[1]{0:T(128)} %bitcast.kref, s32[4]{0:T(128)} %bitcast.20, s32[4,1024]{1,0:T(4,128)} %get-tuple-element.58.row, ...), custom_call_target="tpu_custom_call" | custom-call | flops 1000 | bytes 30000000 | tf_op jit(solution)/shard_map/front/pallas_call | solution.py:585
  83.1 0.1 collective-permute-start.7
  83.2 5.1 %collective-permute-start.8 = (f32[3,64,1024]{2,1,0:T(8,128)}, f32[3,64,1024]{2,1,0:T(8,128)S(1)}, u32[]{:S(2)}, u32[]{:S(2)}) collective-permute-start(f32[3,64,1024]{2,1,0:T(8,128)} %get-tuple-element.63), channel_id=1, source_target_pairs={{0,124},{4,0},{8,4},{12,8},{16,12},{20,16},{24,20},{28,24},{32,28}... | collective-permute-start | bytes 2359304 | tf_op jit(solution)/shard_map/ppermute | solution.py:271
  88.3 2.8 %collective-permute-start.10 = (f32[8,8,1024]{2,1,0:T(8,128)}, f32[8,8,1024]{2,1,0:T(8,128)S(1)}, u32[]{:S(2)}, u32[]{:S(2)}) collective-permute-start(f32[8,8,1024]{2,1,0:T(8,128)} %get-tuple-element.65), channel_id=1, source_target_pairs={{0,1},{1,2},{2,3},{4,5},{5,6},{6,7},{8,9},{9,10},{10,11},{12,13},{... | collective-permute-start | bytes 786440 | tf_op jit(solution)/shard_map/ppermute | solution.py:275
  91.1 3.7 %collective-permute-start.9 = (f32[8,8,1024]{2,1,0:T(8,128)}, f32[8,8,1024]{2,1,0:T(8,128)}, u32[]{:S(2)}, u32[]{:S(2)}) collective-permute-start(f32[8,8,1024]{2,1,0:T(8,128)} %get-tuple-element.64), channel_id=1, source_target_pairs={{1,0},{2,1},{3,2},{5,4},{6,5},{7,6},{9,8},{10,9},{11,10},{13,12},{... | collective-permute-start | bytes 786440 | tf_op jit(solution)/shard_map/ppermute | solution.py:275
  94.7 6.7 %coef.4 = (f32[4,72,1024]{2,1,0:T(8,128)}, f32[4,72,1024]{2,1,0:T(8,128)}, f32[4,72,1024]{2,1,0:T(8,128)}, f32[4,72,1024]{2,1,0:T(8,128)}, f32[4,72,1024]{2,1,0:T(8,128)}) custom-call(s32[1]{0:T(128)} %bitcast.kref, f32[8,64,1024]{2,1,0:T(8,128)} %load.5, f32[8,64,1024]{2,1,0:T(8,128)} %beta_in.5, f32[8,64,1024]{2,1,0:T(8,128)} %collective-permute-done.lo.refs_0_, ...), custom_call_target="tpu_custom_call" | custom-call | flops 1000 | bytes 15000000 | tf_op jit(solution)/shard_map/coef/pallas_call | solution.py:575
  101.5 0.0 collective-permute-done.10.below
  101.5 0.0 copy-start.9
  101.5 0.0 collective-permute-done.9.above
  101.5 0.7 copy-done.9
  102.2 1.9 %ring.1 = (f32[8,8,1024]{2,1,0:T(8,128)}, f32[3,8,1024]{2,1,0:T(8,128)}, f32[3,8,1024]{2,1,0:T(8,128)}) custom-call(f32[8,8,1024]{2,1,0:T(8,128)} %collective-permute-done.9.above, f32[8,8,1024]{2,1,0:T(8,128)} %copy-done.9, f32[4,72,1024]{2,1,0:T(8,128)} %get-tuple-element.48.unread.refs_5_), custom_call_target="tpu_custom_call" | custom-call | flops 1000 | bytes 3000000 | tf_op jit(solution)/shard_map/ring/pallas_call | solution.py:599
  104.0 0.0 collective-permute-start.11
  104.0 5.1 %collective-permute-start.12 = (f32[3,8,1024]{2,1,0:T(8,128)}, f32[3,8,1024]{2,1,0:T(8,128)S(1)}, u32[]{:S(2)}, u32[]{:S(2)}) collective-permute-start(f32[3,8,1024]{2,1,0:T(8,128)} %get-tuple-element.68), channel_id=1, source_target_pairs={{0,124},{4,0},{8,4},{12,8},{16,12},{20,16},{24,20},{28,24},{32,28}... | collective-permute-start | bytes 294920 | tf_op jit(solution)/shard_map/ppermute | solution.py:271
  109.1 6.8 %coef.5 = (f32[4,72,1024]{2,1,0:T(8,128)}, f32[4,72,1024]{2,1,0:T(8,128)}, f32[4,72,1024]{2,1,0:T(8,128)}, f32[4,72,1024]{2,1,0:T(8,128)}, f32[4,72,1024]{2,1,0:T(8,128)}) custom-call(s32[1]{0:T(128)} %bitcast.kref, f32[8,64,1024]{2,1,0:T(8,128)} %load.5, f32[8,64,1024]{2,1,0:T(8,128)} %beta_in.5, f32[8,64,1024]{2,1,0:T(8,128)} %collective-permute-done.lo.refs_0_, ...), custom_call_target="tpu_custom_call" | custom-call | flops 1000 | bytes 15000000 | tf_op jit(solution)/shard_map/coef/pallas_call | solution.py:575
  115.9 0.0 collective-permute-done.11.refs_19_
  115.9 0.0 copy-start.11
  115.9 0.0 collective-permute-done.12.refs_20_
  115.9 0.0 copy-start.12
  115.9 0.0 collective-permute-done.7.refs_16_
  115.9 0.0 copy-start.6
  115.9 0.0 collective-permute-done.8.refs_17_
  115.9 0.0 copy-start.7
  115.9 0.6 copy-done.11
  116.5 0.0 copy-done.12
  116.5 0.3 copy-done.6
  116.8 0.3 copy-done.7
  117.1 14.9 %sweeps.1 = f32[8,64,1024]{2,1,0:T(8,128)} custom-call(s32[1]{0:T(128)} %bitcast.kref, f32[6,72,1024]{2,1,0:T(8,128)} %get-tuple-element.43.refs_5_.refs_0_, f32[6,72,1024]{2,1,0:T(8,128)} %get-tuple-element.44.refs_1_, f32[6,72,1024]{2,1,0:T(8,128)} %get-tuple-element.45.refs_2_, f32[6,72,1024]{2,1,0:T(8,128)} %get-tuple-element.46.refs_3_, ...), custom_call_target="tpu_custom_call" | custom-call | flops 1000 | bytes 60000000 | tf_op jit(solution)/shard_map/sweeps/pallas_call | solution.py:605
  (4 shorter events, 0.0 us)
Async XLA Ops:
  6.4 20.4 %copy-start.10 = (f32[5,8,1024]{2,1,0:T(8,128)S(1)}, f32[5,8,1024]{2,1,0:T(8,128)}, u32[]{:S(2)}) copy-start(f32[5,8,1024]{2,1,0:T(8,128)} %get-tuple-element.60.f0) | copy-start | bytes 491524
  6.4 56.6 %collective-permute-start = (f32[8,64,1024]{2,1,0:T(8,128)}, f32[8,64,1024]{2,1,0:T(8,128)}, u32[]{:S(2)}, u32[]{:S(2)}) collective-permute-start(f32[8,64,1024]{2,1,0:T(8,128)} %get-tuple-element.36), channel_id=1, source_target_pairs={{0,4},{4,8},{8,12},{12,16},{16,20},{20,24},{24,28},{28,32},{32,36}... | collective-permute-start | bytes 6291464 | tf_op jit(solution)/shard_map/ppermute | solution.py:271
  6.5 56.5 %collective-permute-start.1 = (f32[8,64,1024]{2,1,0:T(8,128)}, f32[8,64,1024]{2,1,0:T(8,128)}, u32[]{:S(2)}, u32[]{:S(2)}) collective-permute-start(f32[8,64,1024]{2,1,0:T(8,128)} %get-tuple-element.37), channel_id=1, source_target_pairs={{0,124},{4,0},{8,4},{12,8},{16,12},{20,16},{24,20},{28,24},{32,28}... | collective-permute-start | bytes 6291464 | tf_op jit(solution)/shard_map/ppermute | solution.py:271
  12.5 16.4 %collective-permute-start.2 = (f32[21,8,1024]{2,1,0:T(8,128)}, f32[21,8,1024]{2,1,0:T(8,128)S(1)}, u32[]{:S(2)}, u32[]{:S(2)}) collective-permute-start(f32[21,8,1024]{2,1,0:T(8,128)} %get-tuple-element.38), channel_id=1, source_target_pairs={{0,3},{1,0},{2,1},{3,2},{4,7},{5,4},{6,5},{7,6},{8,11},{9,8},{10,9... | collective-permute-start | bytes 2064392 | tf_op jit(solution)/shard_map/ppermute | solution.py:552
  13.0 15.9 %collective-permute-start.3 = (f32[21,8,1024]{2,1,0:T(8,128)}, f32[21,8,1024]{2,1,0:T(8,128)S(1)}, u32[]{:S(2)}, u32[]{:S(2)}) collective-permute-start(f32[21,8,1024]{2,1,0:T(8,128)} %get-tuple-element.39), channel_id=1, source_target_pairs={{0,1},{1,2},{2,3},{3,0},{4,5},{5,6},{6,7},{7,4},{8,9},{9,10},{10,1... | collective-permute-start | bytes 2064392 | tf_op jit(solution)/shard_map/ppermute | solution.py:552
  23.4 15.8 %all-to-all-start = ((f32[8,64,128]{2,1,0:T(8,128)}), f32[8,64,128]{2,1,0:T(8,128)S(1)}, u32[]{:S(2)}, u32[]{:S(2)}) async-start(f32[8,64,128]{2,1,0:T(8,128)} %flux.1), calls=%async_computation | async-start | bytes 524288 | tf_op jit(solution)/shard_map/all_to_all | solution.py:505
  26.8 8.0 %collective-permute-start.6 = (f32[5,8,1024]{2,1,0:T(8,128)S(1)}, f32[5,8,1024]{2,1,0:T(8,128)S(1)}, u32[]{:S(2)}, u32[]{:S(2)}) collective-permute-start(f32[5,8,1024]{2,1,0:T(8,128)S(1)} %copy-done.10), channel_id=1, source_target_pairs={{0,2},{1,3},{2,0},{3,1},{4,6},{5,7},{6,4},{7,5},{8,10},{9,11},{10,... | collective-permute-start | bytes 491528 | tf_op jit(solution)/shard_map/ppermute | solution.py:552
  28.9 0.9 copy-start.2
  29.0 1.1 copy-start.3
  32.3 16.4 %copy-start.13 = (f32[8,8,1024]{2,1,0:T(8,128)S(1)}, f32[8,8,1024]{2,1,0:T(8,128)}, u32[]{:S(2)}) copy-start(f32[8,8,1024]{2,1,0:T(8,128)} %get-tuple-element.42) | copy-start | bytes 786436
  34.9 4.3 %copy-start.8 = (f32[5,8,1024]{2,1,0:T(8,128)}, f32[5,8,1024]{2,1,0:T(8,128)S(1)}, u32[]{:S(2)}) copy-start(f32[5,8,1024]{2,1,0:T(8,128)S(1)} %collective-permute-done.6.refs_1_.f3) | copy-start | bytes 491524
  39.2 0.7 copy-start.5
  41.7 31.0 %all-to-all-start.1 = ((f32[16,64,128]{2,1,0:T(8,128)}), f32[16,64,128]{2,1,0:T(8,128)S(1)}, u32[]{:S(2)}, u32[]{:S(2)}) async-start(f32[16,64,128]{2,1,0:T(8,128)} %near.1), calls=%async_computation.1 | async-start | bytes 1048576 | tf_op jit(solution)/shard_map/all_to_all | solution.py:505
  48.7 14.3 %collective-permute-start.4 = (f32[8,8,1024]{2,1,0:T(8,128)}, f32[8,8,1024]{2,1,0:T(8,128)S(1)}, u32[]{:S(2)}, u32[]{:S(2)}) collective-permute-start(f32[8,8,1024]{2,1,0:T(8,128)} %get-tuple-element.41), channel_id=1, source_target_pairs={{0,4},{4,8},{8,12},{12,16},{16,20},{20,24},{24,28},{28,32},{32,36}... | collective-permute-start | bytes 786440 | tf_op jit(solution)/shard_map/ppermute | solution.py:271
  48.7 14.3 %collective-permute-start.5 = (f32[8,8,1024]{2,1,0:T(8,128)S(1)}, f32[8,8,1024]{2,1,0:T(8,128)S(1)}, u32[]{:S(2)}, u32[]{:S(2)}) collective-permute-start(f32[8,8,1024]{2,1,0:T(8,128)S(1)} %copy-done.13), channel_id=1, source_target_pairs={{0,124},{4,0},{8,4},{12,8},{16,12},{20,16},{24,20},{28,24},{32,28}... | collective-permute-start | bytes 786440 | tf_op jit(solution)/shard_map/ppermute | solution.py:271
  63.0 0.7 copy-start
  63.0 0.8 copy-start.1
  72.7 0.8 copy-start.4
  83.1 32.8 %collective-permute-start.7 = (f32[3,64,1024]{2,1,0:T(8,128)}, f32[3,64,1024]{2,1,0:T(8,128)S(1)}, u32[]{:S(2)}, u32[]{:S(2)}) collective-permute-start(f32[3,64,1024]{2,1,0:T(8,128)} %get-tuple-element.62), channel_id=1, source_target_pairs={{0,4},{4,8},{8,12},{12,16},{16,20},{20,24},{24,28},{28,32},{32,36}... | collective-permute-start | bytes 2359304 | tf_op jit(solution)/shard_map/ppermute | solution.py:271
  83.2 32.7 %collective-permute-start.8 = (f32[3,64,1024]{2,1,0:T(8,128)}, f32[3,64,1024]{2,1,0:T(8,128)S(1)}, u32[]{:S(2)}, u32[]{:S(2)}) collective-permute-start(f32[3,64,1024]{2,1,0:T(8,128)} %get-tuple-element.63), channel_id=1, source_target_pairs={{0,124},{4,0},{8,4},{12,8},{16,12},{20,16},{24,20},{28,24},{32,28}... | collective-permute-start | bytes 2359304 | tf_op jit(solution)/shard_map/ppermute | solution.py:271
  88.3 13.2 %collective-permute-start.10 = (f32[8,8,1024]{2,1,0:T(8,128)}, f32[8,8,1024]{2,1,0:T(8,128)S(1)}, u32[]{:S(2)}, u32[]{:S(2)}) collective-permute-start(f32[8,8,1024]{2,1,0:T(8,128)} %get-tuple-element.65), channel_id=1, source_target_pairs={{0,1},{1,2},{2,3},{4,5},{5,6},{6,7},{8,9},{9,10},{10,11},{12,13},{... | collective-permute-start | bytes 786440 | tf_op jit(solution)/shard_map/ppermute | solution.py:275
  91.1 10.4 %collective-permute-start.9 = (f32[8,8,1024]{2,1,0:T(8,128)}, f32[8,8,1024]{2,1,0:T(8,128)}, u32[]{:S(2)}, u32[]{:S(2)}) collective-permute-start(f32[8,8,1024]{2,1,0:T(8,128)} %get-tuple-element.64), channel_id=1, source_target_pairs={{1,0},{2,1},{3,2},{5,4},{6,5},{7,6},{9,8},{10,9},{11,10},{13,12},{... | collective-permute-start | bytes 786440 | tf_op jit(solution)/shard_map/ppermute | solution.py:275
  101.5 0.7 copy-start.9
  104.0 11.8 %collective-permute-start.11 = (f32[3,8,1024]{2,1,0:T(8,128)}, f32[3,8,1024]{2,1,0:T(8,128)S(1)}, u32[]{:S(2)}, u32[]{:S(2)}) collective-permute-start(f32[3,8,1024]{2,1,0:T(8,128)} %get-tuple-element.67), channel_id=1, source_target_pairs={{0,4},{4,8},{8,12},{12,16},{16,20},{20,24},{24,28},{28,32},{32,36}... | collective-permute-start | bytes 294920 | tf_op jit(solution)/shard_map/ppermute | solution.py:271
  104.0 11.9 %collective-permute-start.12 = (f32[3,8,1024]{2,1,0:T(8,128)}, f32[3,8,1024]{2,1,0:T(8,128)S(1)}, u32[]{:S(2)}, u32[]{:S(2)}) collective-permute-start(f32[3,8,1024]{2,1,0:T(8,128)} %get-tuple-element.68), channel_id=1, source_target_pairs={{0,124},{4,0},{8,4},{12,8},{16,12},{20,16},{24,20},{28,24},{32,28}... | collective-permute-start | bytes 294920 | tf_op jit(solution)/shard_map/ppermute | solution.py:271
  115.9 0.6 copy-start.11
  115.9 0.6 copy-start.12
  115.9 0.9 copy-start.6
  115.9 1.2 copy-start.7

commit v7 on v5

--- a/solution.py
+++ b/solution.py
@@ -46,11 +46,39 @@
     return pl.ds(pl.multiple_of(i * 8, 8), 8)
 
 
-def flux_kernel(cnt, row, heat_any, lane, vert, share, out, heat, diff, picked, sems):
+def flux_kernel(cnt, heat_any, label, vert, share, load_any, beta_any, solve, prior, weight, jump,
+                out, row_out, lane, up, down, rup, rdown, front_any,
+                heat, diff, picked, row, load, beta, front, flip, sems, isems, osems, fsems):
     loads = [pltpu.make_async_copy(heat_any.at[t], heat.at[t], sems.at[t]) for t in range(T)]
-    for c in loads:
+    fields = [pltpu.make_async_copy(a, b, isems.at[n])
+              for n, (a, b) in enumerate(((load_any, load), (beta_any, beta)))]
+    for c in loads + fields:
         c.start()
-
+    lab = label[...]
+    hi = lab >> 10
+    low = hi + (lab & 1023)
+    carry = (low >= Z - 1).astype(I32)
+    column, axial = hi + carry, low - (Z - 1) * carry
+    row_out[...] = ((column >> 3) << 6) + ((axial >> 7) << 3) + (column & 7)
+    lane[...] = axial & 127
+    index = pltpu.make_async_copy(row_out, row, isems.at[2])
+    index.start()
+
+    def keep(n, x):
+        front[n // 8, :, n % 8 * 128:n % 8 * 128 + 128] = x
+
+    for n in range(FT * 8):
+        keep(n, solve[n * 8:n * 8 + 8, :] if n < BS * BS // 8 else jnp.zeros((8, 128), F32))
+    for n, x in enumerate((prior, weight, jump)):
+        for m in range(8):
+            flip[pl.ds(m, BS, stride=8), :] = pltpu.roll(x[...], (128 - m * BS) % 128, 1)
+        turned = flip[...].T
+        keep(BS * BS // 8 + 2 * n, turned[:8, :])
+        keep(BS * BS // 8 + 2 * n + 1, turned[8:16, :])
+    sends = [pltpu.make_async_copy(front, b, fsems.at[n]) for n, b in enumerate(
+        (front_any, rup.at[pl.ds(2 * T, FT)], rdown.at[pl.ds(2 * T, FT)]))]
+    for c in sends:
+        c.start()
     for t in range(T):
         loads[t].wait()
 
@@ -62,6 +90,15 @@
             return 0
 
         lax.fori_loop(0, R // 8, make, 0, unroll=4)
+    for n, f in enumerate((load, beta)):
+        fields[n].wait()
+        for m, (a, b) in enumerate(((f.at[pl.ds(T - H, H)], up.at[pl.ds(n * H, H)]),
+                                    (f.at[pl.ds(0, H)], down.at[pl.ds(n * H, H)]),
+                                    (f.at[:, pl.ds(R - 8, 8)], rup.at[pl.ds(n * T, T)]),
+                                    (f.at[:, pl.ds(0, 8)], rdown.at[pl.ds(n * T, T)]))):
+            sends.append(pltpu.make_async_copy(a, b, osems.at[4 * n + m]))
+            sends[-1].start()
+    index.wait()
     for j in range(GROUPS):
         def body(b, _):
             base = pl.multiple_of(b * UNROLL, UNROLL)
@@ -86,6 +123,8 @@
         o = o[:BS] + o[BS:2 * BS] + o[2 * BS:]
         for n in range(out.shape[0]):
             out[n, j * BS:(j + 1) * BS, :] = o
+    for c in sends:
+        c.wait()
 
 
 def front_kernel(kref, cnt, row, parts, f0, f1, f2, f3, lane, vert, share, pred_any, *refs):
@@ -206,49 +245,6 @@
         c.wait()
 
 
-def pack_kernel(load_any, beta_any, solve, prior, weight, jump, label, up, down, rup, rdown,
-                front_any, row, lane, load, beta, front, flip, isems, osems, fsems):
-    loads = [pltpu.make_async_copy(a, b, isems.at[n])
-             for n, (a, b) in enumerate(((load_any, load), (beta_any, beta)))]
-    for c in loads:
-        c.start()
-    lab = label[...]
-    hi = lab >> 10
-    low = hi + (lab & 1023)
-    carry = (low >= Z - 1).astype(I32)
-    column, axial = hi + carry, low - (Z - 1) * carry
-    row[...] = ((column >> 3) << 6) + ((axial >> 7) << 3) + (column & 7)
-    lane[...] = axial & 127
-
-
-    def keep(n, x):
-        front[n // 8, :, n % 8 * 128:n % 8 * 128 + 128] = x
-
-    for n in range(FT * 8):
-        keep(n, solve[n * 8:n * 8 + 8, :] if n < BS * BS // 8 else jnp.zeros((8, 128), F32))
-    for n, x in enumerate((prior, weight, jump)):
-        for m in range(8):
-            flip[pl.ds(m, BS, stride=8), :] = pltpu.roll(x[...], (128 - m * BS) % 128, 1)
-        turned = flip[...].T
-        keep(BS * BS // 8 + 2 * n, turned[:8, :])
-        keep(BS * BS // 8 + 2 * n + 1, turned[8:16, :])
-    sends = []
-    fcopies = [pltpu.make_async_copy(front, b, fsems.at[n]) for n, b in enumerate(
-        (front_any, rup.at[pl.ds(2 * T, FT)], rdown.at[pl.ds(2 * T, FT)]))]
-    for c in fcopies:
-        c.start()
-    for n, f in enumerate((load, beta)):
-        loads[n].wait()
-        for a, b in ((f.at[pl.ds(T - H, H)], up.at[pl.ds(n * H, H)]),
-                     (f.at[pl.ds(0, H)], down.at[pl.ds(n * H, H)]),
-                     (f.at[:, pl.ds(R - 8, 8)], rup.at[pl.ds(n * T, T)]),
-                     (f.at[:, pl.ds(0, 8)], rdown.at[pl.ds(n * T, T)])):
-            sends.append(pltpu.make_async_copy(a, b, osems.at[len(sends)]))
-            sends[-1].start()
-    for c in sends + fcopies:
-        c.wait()
-
-
 def side_kernel(kref, above, below_any, side, eup, edown, below, sems):
     loads = [pltpu.make_async_copy(above.at[pl.ds(0, 2 * T)], side, sems.at[0]),
              pltpu.make_async_copy(below_any.at[pl.ds(0, 2 * T)], below, sems.at[1])]
@@ -284,7 +280,7 @@
 
 
 def sweep_kernel(kref, load, beta_in, lo, hi, side, clo, chi, src, slo, shi, sside, sclo, schi,
-                 out, pa, pb, beta, th, rr, zz, ww, ss, rads, sems):
+                 out_any, pa, pb, beta, th, rr, zz, ww, ss, rads, out, sems, osems):
     k = kref[0]
     rows, ring = pl.ds(0, R), pl.ds(R, 8)
     half = T // 2
@@ -435,7 +431,15 @@
         start = ends[g]
     lax.fori_loop(2, TE - 2, lambda t, _: sweep(pb, pa, t, RT, 0), 0)
     lax.fori_loop(3, TE - 3, lambda t, _: sweep(pa, pb, t, RT, 0), 0)
-    lax.fori_loop(4, TE - 4, lambda t, _: sweep(pb, out, t, RT - 1, H), 0)
+
+    def final(t, _):
+        sweep(pb, out, t, RT - 1, H)
+        pltpu.make_async_copy(out.at[t - H], out_any.at[t - H], osems.at[t - H]).start()
+        return 0
+
+    lax.fori_loop(4, TE - 4, final, 0)
+    for t in range(T):
+        pltpu.make_async_copy(out.at[t], out_any.at[t], osems.at[t]).wait()
 
 
 def from_all(copies, axes):
@@ -477,25 +481,21 @@
     plane = lambda n: shape(n, R, Z)
     tile = lambda n: shape(n, 8, Z)
     block = pltpu.VMEM((T, R, Z), F32)
-    up, down, rup, rdown, front, row, lane = pl.pallas_call(
-        pack_kernel,
-        out_shape=(plane(2 * H), plane(2 * H), tile(2 * T + FT), tile(2 * T + FT), tile(FT), slot, slot),
-        in_specs=[ANY] * 2 + [VM] * 5, out_specs=(ANY,) * 5 + (VM,) * 2,
-        scratch_shapes=[block, block, pltpu.VMEM((FT, 8, Z), F32), pltpu.VMEM((128, 128), F32),
-                        pltpu.SemaphoreType.DMA((2,)), pltpu.SemaphoreType.DMA((8,)), pltpu.SemaphoreType.DMA((3,))],
-        compiler_params=params(10), cost_estimate=cost(4), name="pack",
-    )(load, beta, solve.reshape(BS * BS, NB), nodes(prior), nodes(weight), nodes(jump), label)
+    partial, row, lane, up, down, rup, rdown, front = pl.pallas_call(
+        flux_kernel,
+        out_shape=(shape(8, GROUPS * BS, NB), slot, slot, plane(2 * H), plane(2 * H),
+                   tile(2 * T + FT), tile(2 * T + FT), tile(FT)),
+        in_specs=[SM, ANY, VM, VM, VM, ANY, ANY] + [VM] * 4, out_specs=(VM,) * 3 + (ANY,) * 5,
+        scratch_shapes=[block, pltpu.VMEM((T * R * 8, 128), F32), pltpu.VMEM((SLOTS, 128), F32),
+                        pltpu.SMEM((GROUPS, SLOTS), I32), block, block, pltpu.VMEM((FT, 8, Z), F32),
+                        pltpu.VMEM((128, 128), F32), pltpu.SemaphoreType.DMA((T,)), pltpu.SemaphoreType.DMA((3,)),
+                        pltpu.SemaphoreType.DMA((8,)), pltpu.SemaphoreType.DMA((3,))],
+        compiler_params=params(20), cost_estimate=cost(10), name="flux",
+    )(tally, heat, label, vertex, share, load, beta, solve.reshape(BS * BS, NB), nodes(prior), nodes(weight), nodes(jump))
     lo, hi = shift_azim(up, 1), shift_azim(down, -1)
     ring = lambda x, d: lax.ppermute(x, "rad", [(i, (i + d) % 4) for i in range(4)])
     rhi, rlo, across = ring(rdown, -1), ring(rup, 1), ring(front, 2)
 
-    partial = pl.pallas_call(
-        flux_kernel, out_shape=shape(8, GROUPS * BS, NB),
-        in_specs=[SM, SM, ANY, VM, VM, VM], out_specs=VM,
-        scratch_shapes=[block, pltpu.VMEM((T * R * 8, 128), F32), pltpu.VMEM((SLOTS, 128), F32),
-                        pltpu.SemaphoreType.DMA((T,))],
-        compiler_params=params(12), cost_estimate=cost(10), name="flux",
-    )(tally, row, heat, lane, vertex, share)
     side, eup, edown = pl.pallas_call(
         side_kernel, out_shape=(tile(2 * T), tile(2 * H), tile(2 * H)),
         in_specs=[SM, ANY, ANY], out_specs=(VM,) * 3,
@@ -527,8 +527,9 @@
     ext = pltpu.VMEM((TE, RE, Z), F32)
     pressure = pl.pallas_call(
         sweep_kernel, out_shape=plane(T),
-        in_specs=[SM] + [ANY] * 13, out_specs=VM,
-        scratch_shapes=[ext] * 8 + [pltpu.VMEM((3, RT, 8, 128), F32), pltpu.SemaphoreType.DMA((4, 3, 2))],
+        in_specs=[SM] + [ANY] * 13, out_specs=ANY,
+        scratch_shapes=[ext] * 8 + [pltpu.VMEM((3, RT, 8, 128), F32), block, pltpu.SemaphoreType.DMA((4, 3, 2)),
+                        pltpu.SemaphoreType.DMA((T,))],
         compiler_params=params(46), cost_estimate=cost(20), name="sweeps",
     )(kidx, load, beta, lo, hi, side, clo, chi, source, slo, shi, sside, sclo, schi)
     return pressure, height.reshape(NB * BS)

time: 121 us -> 127 us (1.050)
  starting transfers between devices: 42.1 us -> 49 us
  Pallas kernels: 51.8 us -> 46 us
  waiting for transfers between devices: 21.9 us -> 26.6 us
    ppermute x3, waiting for transfers between devices: 2.91 us -> 9.97 us  [per_device(): lax.ppermute(x, 'rad', [(i, (i + d) % 4) for i in range(4)])]
    pallas_call x2 -> x1, Pallas kernels: 14.9 us -> 9.7 us  [per_device(): pl.pallas_call(flux_kernel, out_shape=(shape(8, GROUPS * BS, NB), slot, s...]
    ppermute x3, starting transfers between devices: 3.66 us -> 8.35 us  [per_device(): lax.ppermute(x, 'rad', [(i, (i + d) % 4) for i in range(4)])]
    all_to_all x2, starting transfers between devices: 10.4 us -> 13.6 us  [from_all(): return lax.all_to_all(copies, axes, 0, 0)]
    all_to_all x2, waiting for transfers between devices: 4.05 us -> 1.7 us  [from_all(): return lax.all_to_all(copies, axes, 0, 0)]
    unnamed x28 -> x26, local copies, waits for them, and re-layouts: 3.93 us -> 3.67 us
  transfers between devices with their start and end apart: 15 -> 15, of which waited for: 4 -> 5; matrix products, arithmetic and copies ran while one was open for 0% -> 0% of each run, Pallas kernels for 11% -> 3%
where the time goes in v7:
time: 127 us; the launch traced here: 126 us
  starting transfers between devices  49 us (39%)
  Pallas kernels  46 us (36%)
  waiting for transfers between devices  26.6 us (21%)
  local copies, waits for them, and re-layouts  3.69 us (3%)
    pallas_call x1, Pallas kernels, per_device(): pl.pallas_call(sweep_kernel, out_shape=plane(T), in_specs=[SM] + [ANY] *...  22 us
    ppermute x8, starting transfers between devices, shift_azim(): return lax.ppermute(x, AZIM, [(i, (i + d) % 32) for i in range(32)])  21.2 us
    ppermute x8, waiting for transfers between devices, shift_azim(): return lax.ppermute(x, AZIM, [(i, (i + d) % 32) for i in range(32)])  14.9 us
    all_to_all x2, starting transfers between devices, from_all(): return lax.all_to_all(copies, axes, 0, 0)  13.6 us
    pallas_call x1, Pallas kernels, per_device(): pl.pallas_call(front_kernel, out_shape=(plane(T), plane(H - 1), plane(H -...  10.2 us
    ppermute x3, waiting for transfers between devices, per_device(): lax.ppermute(x, 'rad', [(i, (i + d) % 4) for i in range(4)])  9.97 us
    pallas_call x1, Pallas kernels, per_device(): pl.pallas_call(flux_kernel, out_shape=(shape(8, GROUPS * BS, NB), slot, s...  9.7 us
    ppermute x3, starting transfers between devices, per_device(): lax.ppermute(x, 'rad', [(i, (i + d) % 4) for i in range(4)])  8.35 us
  transfers between devices with their start and end apart: 15, of which 5 were waited for; matrix products, arithmetic and copies ran while one was open for 0% of the time, Pallas kernels for 3%

profile of v7, /device:TPU:2, one launch (start us, length us, event | category | flops | bytes accessed | tf_op | source)
XLA Modules:
  0.0 126.3 jit_solution(2687613167968251975)
XLA Ops:
  0.6 9.7 %flux.1 = (f32[8,64,128]{2,1,0:T(8,128)}, s32[4,1024]{1,0:T(4,128)}, s32[4,1024]{1,0:T(4,128)}, f32[8,64,1024]{2,1,0:T(8,128)}, f32[8,64,1024]{2,1,0:T(8,128)}, ...) custom-call(s32[4]{0:T(128)} %bitcast.19, f32[8,64,1024]{2,1,0:T(8,128)} %heat_any.1, ...), custom_call_target="tpu_custom_call" | custom-call | flops 1000 | bytes 30000000 | tf_op jit(solution)/shard_map/flux/pallas_call | solution.py:484
  10.3 0.1 collective-permute-start
  10.4 5.8 %collective-permute-start.1 = (f32[8,64,1024]{2,1,0:T(8,128)}, f32[8,64,1024]{2,1,0:T(8,128)}, u32[]{:S(2)}, u32[]{:S(2)}) collective-permute-start(f32[8,64,1024]{2,1,0:T(8,128)} %get-tuple-element.20), channel_id=1, source_target_pairs={{0,124},{4,0},{8,4},{12,8},{16,12},{20,16},{24,20},{28,24},{32,28}... | collective-permute-start | bytes 6291464 | tf_op jit(solution)/shard_map/ppermute | solution.py:267
  16.2 6.2 %collective-permute-start.2 = (f32[21,8,1024]{2,1,0:T(8,128)}, f32[21,8,1024]{2,1,0:T(8,128)S(1)}, u32[]{:S(2)}, u32[]{:S(2)}) collective-permute-start(f32[21,8,1024]{2,1,0:T(8,128)} %get-tuple-element.21), channel_id=1, source_target_pairs={{0,3},{1,0},{2,1},{3,2},{4,7},{5,4},{6,5},{7,6},{8,11},{9,8},{10,9... | collective-permute-start | bytes 2064392 | tf_op jit(solution)/shard_map/ppermute | solution.py:496
  22.4 0.0 collective-permute-start.3
  22.4 3.4 %all-to-all-start = ((f32[8,64,128]{2,1,0:T(8,128)}), f32[8,64,128]{2,1,0:T(8,128)S(1)}, u32[]{:S(2)}, u32[]{:S(2)}) async-start(f32[8,64,128]{2,1,0:T(8,128)} %get-tuple-element.27), calls=%async_computation | async-start | bytes 524288 | tf_op jit(solution)/shard_map/all_to_all | solution.py:446
  25.8 2.1 %collective-permute-start.6 = (f32[5,8,1024]{2,1,0:T(8,128)}, f32[5,8,1024]{2,1,0:T(8,128)S(1)}, u32[]{:S(2)}, u32[]{:S(2)}) collective-permute-start(f32[5,8,1024]{2,1,0:T(8,128)} %get-tuple-element.28.f0), channel_id=1, source_target_pairs={{0,2},{1,3},{2,0},{3,1},{4,6},{5,7},{6,4},{7,5},{8,10},{9,11},{10,... | collective-permute-start | bytes 491528 | tf_op jit(solution)/shard_map/ppermute | solution.py:496
  28.0 7.9 %collective-permute-done.2.above.f1 = f32[21,8,1024]{2,1,0:T(8,128)S(1)} collective-permute-done((f32[21,8,1024]{2,1,0:T(8,128)}, f32[21,8,1024]{2,1,0:T(8,128)S(1)}, u32[]{:S(2)}, u32[]{:S(2)}) %collective-permute-start.2) | collective-permute-done | bytes 688160 | tf_op jit(solution)/shard_map/ppermute | solution.py:496
  35.8 0.0 copy-start
  35.8 2.1 %collective-permute-done.3.below_any.f2 = f32[21,8,1024]{2,1,0:T(8,128)S(1)} collective-permute-done((f32[21,8,1024]{2,1,0:T(8,128)}, f32[21,8,1024]{2,1,0:T(8,128)S(1)}, u32[]{:S(2)}, u32[]{:S(2)}) %collective-permute-start.3) | collective-permute-done | bytes 688160 | tf_op jit(solution)/shard_map/ppermute | solution.py:496
  37.9 0.0 copy-start.1
  37.9 0.0 copy-done
  37.9 0.9 copy-done.1
  38.8 2.3 %side.1 = (f32[16,8,1024]{2,1,0:T(8,128)}, f32[8,8,1024]{2,1,0:T(8,128)}, f32[8,8,1024]{2,1,0:T(8,128)}) custom-call(s32[1]{0:T(128)} %bitcast.kref, f32[21,8,1024]{2,1,0:T(8,128)} %copy-done, f32[21,8,1024]{2,1,0:T(8,128)} %copy-done.1), custom_call_target="tpu_custom_call" | custom-call | flops 1000 | bytes 6000000 | tf_op jit(solution)/shard_map/side/pallas_call | solution.py:499
  41.1 0.0 copy-start.12
  41.1 0.0 collective-permute-done.6.refs_1_.f3
  41.1 0.0 copy-start.9
  41.1 1.7 %all-to-all-done.parts = f32[8,64,128]{2,1,0:T(8,128)S(1)} async-done(((f32[8,64,128]{2,1,0:T(8,128)}), f32[8,64,128]{2,1,0:T(8,128)S(1)}, u32[]{:S(2)}, u32[]{:S(2)}) %all-to-all-start) | async-done | bytes 262176 | tf_op jit(solution)/shard_map/all_to_all | solution.py:446
  42.8 0.0 copy-start.6
  42.8 0.0 copy-done.9
  42.8 0.7 copy-done.6
  43.5 1.8 %near.1 = f32[16,64,128]{2,1,0:T(8,128)} custom-call(f32[8,64,128]{2,1,0:T(8,128)} %copy-done.6, f32[16,8,1024]{2,1,0:T(8,128)} %get-tuple-element.23.refs_0_.refs_2_.side, f32[5,8,1024]{2,1,0:T(8,128)} %copy-done.9), custom_call_target="tpu_custom_call" | custom-call | tf_op jit(solution)/shard_map/near/pallas_call | solution.py:506
  45.4 10.2 %all-to-all-start.1 = ((f32[16,64,128]{2,1,0:T(8,128)}), f32[16,64,128]{2,1,0:T(8,128)S(1)}, u32[]{:S(2)}, u32[]{:S(2)}) async-start(f32[16,64,128]{2,1,0:T(8,128)} %near.1), calls=%async_computation.1 | async-start | bytes 1048576 | tf_op jit(solution)/shard_map/all_to_all | solution.py:446
  55.5 0.0 collective-permute-start.4
  55.5 0.0 copy-done.12
  55.5 5.1 %collective-permute-start.5 = (f32[8,8,1024]{2,1,0:T(8,128)S(1)}, f32[8,8,1024]{2,1,0:T(8,128)S(1)}, u32[]{:S(2)}, u32[]{:S(2)}) collective-permute-start(f32[8,8,1024]{2,1,0:T(8,128)S(1)} %copy-done.12), channel_id=1, source_target_pairs={{0,124},{4,0},{8,4},{12,8},{16,12},{20,16},{24,20},{28,24},{32,28}... | collective-permute-start | bytes 786440 | tf_op jit(solution)/shard_map/ppermute | solution.py:267
  60.6 9.3 %collective-permute-done.4.refs_3_.clo = f32[8,8,1024]{2,1,0:T(8,128)S(1)} collective-permute-done((f32[8,8,1024]{2,1,0:T(8,128)}, f32[8,8,1024]{2,1,0:T(8,128)S(1)}, u32[]{:S(2)}, u32[]{:S(2)}) %collective-permute-start.4) | collective-permute-done | bytes 262176 | tf_op jit(solution)/shard_map/ppermute | solution.py:267
  69.9 0.0 copy-start.4
  69.9 0.0 collective-permute-done.5.refs_4_.chi
  69.9 0.0 copy-start.5
  69.9 0.0 all-to-all-done.1.parts
  69.9 0.0 copy-start.2
  69.9 0.0 collective-permute-done.refs_0_.lo
  69.9 0.0 collective-permute-done.1.refs_1_.hi
  69.9 0.6 copy-done.4
  70.6 0.1 copy-done.5
  70.6 0.2 copy-done.2
  70.8 10.2 %front.1 = (f32[8,64,1024]{2,1,0:T(8,128)}, f32[3,64,1024]{2,1,0:T(8,128)}, f32[3,64,1024]{2,1,0:T(8,128)}, f32[8,8,1024]{2,1,0:T(8,128)}, f32[8,8,1024]{2,1,0:T(8,128)}, /*index=5*/f32[16,128]{1,0:T(8,128)}) custom-call(s32[1]{0:T(128)} %bitcast.kref, s32[4]{0:T(128)} %bitcast.20, s32[4,1024]{1,0:T(4,128)} %get-tuple-element.26.row, ...), custom_call_target="tpu_custom_call" | custom-call | flops 1000 | bytes 30000000 | tf_op jit(solution)/shard_map/front/pallas_call | solution.py:511
  81.0 1.9 %collective-permute-start.10 = (f32[8,8,1024]{2,1,0:T(8,128)}, f32[8,8,1024]{2,1,0:T(8,128)S(1)}, u32[]{:S(2)}, u32[]{:S(2)}) collective-permute-start(f32[8,8,1024]{2,1,0:T(8,128)} %get-tuple-element.34), channel_id=1, source_target_pairs={{0,1},{1,2},{2,3},{4,5},{5,6},{6,7},{8,9},{9,10},{10,11},{12,13},{... | collective-permute-start | bytes 786440 | tf_op jit(solution)/shard_map/ppermute | solution.py:271
  83.0 3.9 %collective-permute-start.9 = (f32[8,8,1024]{2,1,0:T(8,128)}, f32[8,8,1024]{2,1,0:T(8,128)S(1)}, u32[]{:S(2)}, u32[]{:S(2)}) collective-permute-start(f32[8,8,1024]{2,1,0:T(8,128)} %get-tuple-element.33), channel_id=1, source_target_pairs={{1,0},{2,1},{3,2},{5,4},{6,5},{7,6},{9,8},{10,9},{11,10},{13,12},{... | collective-permute-start | bytes 786440 | tf_op jit(solution)/shard_map/ppermute | solution.py:271
  86.9 0.1 collective-permute-start.7
  87.0 5.1 %collective-permute-start.8 = (f32[3,64,1024]{2,1,0:T(8,128)}, f32[3,64,1024]{2,1,0:T(8,128)S(1)}, u32[]{:S(2)}, u32[]{:S(2)}) collective-permute-start(f32[3,64,1024]{2,1,0:T(8,128)} %get-tuple-element.32), channel_id=1, source_target_pairs={{0,124},{4,0},{8,4},{12,8},{16,12},{20,16},{24,20},{28,24},{32,28}... | collective-permute-start | bytes 2359304 | tf_op jit(solution)/shard_map/ppermute | solution.py:267
  92.0 0.0 collective-permute-done.10
  92.1 0.0 collective-permute-done.9
  92.1 0.1 broadcast_select_fusion.sside
  92.2 0.0 copy-start.3
  92.2 0.1 collective-permute-start.11
  92.3 5.1 %collective-permute-start.12 = (f32[3,8,1024]{2,1,0:T(8,128)S(1)}, f32[3,8,1024]{2,1,0:T(8,128)S(1)}, u32[]{:S(2)}, u32[]{:S(2)}) collective-permute-start(f32[3,8,1024]{2,1,0:T(8,128)S(1)} %get-tuple-element.36), channel_id=1, source_target_pairs={{0,124},{4,0},{8,4},{12,8},{16,12},{20,16},{24,20},{28,24},{32,28}... | collective-permute-start | bytes 294920 | tf_op jit(solution)/shard_map/ppermute | solution.py:267
  97.3 5.7 %collective-permute-done.11.sclo = f32[3,8,1024]{2,1,0:T(8,128)S(1)} collective-permute-done((f32[3,8,1024]{2,1,0:T(8,128)S(1)}, f32[3,8,1024]{2,1,0:T(8,128)S(1)}, u32[]{:S(2)}, u32[]{:S(2)}) %collective-permute-start.11) | collective-permute-done | bytes 98336 | tf_op jit(solution)/shard_map/ppermute | solution.py:267
  103.0 0.0 copy-start.10
  103.0 0.0 collective-permute-done.12.schi
  103.0 0.0 copy-start.11
  103.0 0.0 collective-permute-done.7.slo
  103.0 0.0 copy-start.7
  103.0 0.0 collective-permute-done.8.shi
  103.0 0.0 copy-start.8
  103.0 0.0 copy-done.3
  103.0 0.6 copy-done.10
  103.6 0.1 copy-done.11
  103.7 0.3 copy-done.7
  103.9 0.2 copy-done.8
  104.2 22.0 %sweeps.1 = f32[8,64,1024]{2,1,0:T(8,128)} custom-call(s32[1]{0:T(128)} %bitcast.kref, f32[8,64,1024]{2,1,0:T(8,128)} %load.1, f32[8,64,1024]{2,1,0:T(8,128)} %beta_in.1, f32[8,64,1024]{2,1,0:T(8,128)} %collective-permute-done.refs_0_.lo, f32[8,64,1024]{2,1,0:T(8,128)} %collective-permute-done.1.refs_1_.hi, ...), custom_call_target="tpu_custom_call" | custom-call | flops 1000 | bytes 60000000 | tf_op jit(solution)/shard_map/sweeps/pallas_call | solution.py:528
  (2 shorter events, 0.0 us)
Async XLA Ops:
  10.3 59.6 %collective-permute-start = (f32[8,64,1024]{2,1,0:T(8,128)}, f32[8,64,1024]{2,1,0:T(8,128)}, u32[]{:S(2)}, u32[]{:S(2)}) collective-permute-start(f32[8,64,1024]{2,1,0:T(8,128)} %get-tuple-element.19), channel_id=1, source_target_pairs={{0,4},{4,8},{8,12},{12,16},{16,20},{20,24},{24,28},{28,32},{32,36}... | collective-permute-start | bytes 6291464 | tf_op jit(solution)/shard_map/ppermute | solution.py:267
  10.4 59.5 %collective-permute-start.1 = (f32[8,64,1024]{2,1,0:T(8,128)}, f32[8,64,1024]{2,1,0:T(8,128)}, u32[]{:S(2)}, u32[]{:S(2)}) collective-permute-start(f32[8,64,1024]{2,1,0:T(8,128)} %get-tuple-element.20), channel_id=1, source_target_pairs={{0,124},{4,0},{8,4},{12,8},{16,12},{20,16},{24,20},{28,24},{32,28}... | collective-permute-start | bytes 6291464 | tf_op jit(solution)/shard_map/ppermute | solution.py:267
  16.2 19.6 %collective-permute-start.2 = (f32[21,8,1024]{2,1,0:T(8,128)}, f32[21,8,1024]{2,1,0:T(8,128)S(1)}, u32[]{:S(2)}, u32[]{:S(2)}) collective-permute-start(f32[21,8,1024]{2,1,0:T(8,128)} %get-tuple-element.21), channel_id=1, source_target_pairs={{0,3},{1,0},{2,1},{3,2},{4,7},{5,4},{6,5},{7,6},{8,11},{9,8},{10,9... | collective-permute-start | bytes 2064392 | tf_op jit(solution)/shard_map/ppermute | solution.py:496
  22.4 15.5 %collective-permute-start.3 = (f32[21,8,1024]{2,1,0:T(8,128)}, f32[21,8,1024]{2,1,0:T(8,128)S(1)}, u32[]{:S(2)}, u32[]{:S(2)}) collective-permute-start(f32[21,8,1024]{2,1,0:T(8,128)} %get-tuple-element.22), channel_id=1, source_target_pairs={{0,1},{1,2},{2,3},{3,0},{4,5},{5,6},{6,7},{7,4},{8,9},{9,10},{10,1... | collective-permute-start | bytes 2064392 | tf_op jit(solution)/shard_map/ppermute | solution.py:496
  22.4 20.5 %all-to-all-start = ((f32[8,64,128]{2,1,0:T(8,128)}), f32[8,64,128]{2,1,0:T(8,128)S(1)}, u32[]{:S(2)}, u32[]{:S(2)}) async-start(f32[8,64,128]{2,1,0:T(8,128)} %get-tuple-element.27), calls=%async_computation | async-start | bytes 524288 | tf_op jit(solution)/shard_map/all_to_all | solution.py:446
  25.8 15.3 %collective-permute-start.6 = (f32[5,8,1024]{2,1,0:T(8,128)}, f32[5,8,1024]{2,1,0:T(8,128)S(1)}, u32[]{:S(2)}, u32[]{:S(2)}) collective-permute-start(f32[5,8,1024]{2,1,0:T(8,128)} %get-tuple-element.28.f0), channel_id=1, source_target_pairs={{0,2},{1,3},{2,0},{3,1},{4,6},{5,7},{6,4},{7,5},{8,10},{9,11},{10,... | collective-permute-start | bytes 491528 | tf_op jit(solution)/shard_map/ppermute | solution.py:496
  35.8 2.1 %copy-start = (f32[21,8,1024]{2,1,0:T(8,128)}, f32[21,8,1024]{2,1,0:T(8,128)S(1)}, u32[]{:S(2)}) copy-start(f32[21,8,1024]{2,1,0:T(8,128)S(1)} %collective-permute-done.2.above.f1) | copy-start | bytes 2064388
  37.9 0.9 copy-start.1
  41.1 14.4 %copy-start.12 = (f32[8,8,1024]{2,1,0:T(8,128)S(1)}, f32[8,8,1024]{2,1,0:T(8,128)}, u32[]{:S(2)}) copy-start(f32[8,8,1024]{2,1,0:T(8,128)} %get-tuple-element.25) | copy-start | bytes 786436
  41.1 1.7 %copy-start.9 = (f32[5,8,1024]{2,1,0:T(8,128)}, f32[5,8,1024]{2,1,0:T(8,128)S(1)}, u32[]{:S(2)}) copy-start(f32[5,8,1024]{2,1,0:T(8,128)S(1)} %collective-permute-done.6.refs_1_.f3) | copy-start | bytes 491524
  42.8 0.7 copy-start.6
  45.4 24.5 %all-to-all-start.1 = ((f32[16,64,128]{2,1,0:T(8,128)}), f32[16,64,128]{2,1,0:T(8,128)S(1)}, u32[]{:S(2)}, u32[]{:S(2)}) async-start(f32[16,64,128]{2,1,0:T(8,128)} %near.1), calls=%async_computation.1 | async-start | bytes 1048576 | tf_op jit(solution)/shard_map/all_to_all | solution.py:446
  55.5 14.3 %collective-permute-start.4 = (f32[8,8,1024]{2,1,0:T(8,128)}, f32[8,8,1024]{2,1,0:T(8,128)S(1)}, u32[]{:S(2)}, u32[]{:S(2)}) collective-permute-start(f32[8,8,1024]{2,1,0:T(8,128)} %get-tuple-element.24), channel_id=1, source_target_pairs={{0,4},{4,8},{8,12},{12,16},{16,20},{20,24},{24,28},{28,32},{32,36}... | collective-permute-start | bytes 786440 | tf_op jit(solution)/shard_map/ppermute | solution.py:267
  55.5 14.3 %collective-permute-start.5 = (f32[8,8,1024]{2,1,0:T(8,128)S(1)}, f32[8,8,1024]{2,1,0:T(8,128)S(1)}, u32[]{:S(2)}, u32[]{:S(2)}) collective-permute-start(f32[8,8,1024]{2,1,0:T(8,128)S(1)} %copy-done.12), channel_id=1, source_target_pairs={{0,124},{4,0},{8,4},{12,8},{16,12},{20,16},{24,20},{28,24},{32,28}... | collective-permute-start | bytes 786440 | tf_op jit(solution)/shard_map/ppermute | solution.py:267
  69.9 0.7 copy-start.4
  69.9 0.8 copy-start.5
  69.9 0.9 copy-start.2
  81.0 11.0 %collective-permute-start.10 = (f32[8,8,1024]{2,1,0:T(8,128)}, f32[8,8,1024]{2,1,0:T(8,128)S(1)}, u32[]{:S(2)}, u32[]{:S(2)}) collective-permute-start(f32[8,8,1024]{2,1,0:T(8,128)} %get-tuple-element.34), channel_id=1, source_target_pairs={{0,1},{1,2},{2,3},{4,5},{5,6},{6,7},{8,9},{9,10},{10,11},{12,13},{... | collective-permute-start | bytes 786440 | tf_op jit(solution)/shard_map/ppermute | solution.py:271
  83.0 9.1 %collective-permute-start.9 = (f32[8,8,1024]{2,1,0:T(8,128)}, f32[8,8,1024]{2,1,0:T(8,128)S(1)}, u32[]{:S(2)}, u32[]{:S(2)}) collective-permute-start(f32[8,8,1024]{2,1,0:T(8,128)} %get-tuple-element.33), channel_id=1, source_target_pairs={{1,0},{2,1},{3,2},{5,4},{6,5},{7,6},{9,8},{10,9},{11,10},{13,12},{... | collective-permute-start | bytes 786440 | tf_op jit(solution)/shard_map/ppermute | solution.py:271
  86.9 16.1 %collective-permute-start.7 = (f32[3,64,1024]{2,1,0:T(8,128)}, f32[3,64,1024]{2,1,0:T(8,128)S(1)}, u32[]{:S(2)}, u32[]{:S(2)}) collective-permute-start(f32[3,64,1024]{2,1,0:T(8,128)} %get-tuple-element.31), channel_id=1, source_target_pairs={{0,4},{4,8},{8,12},{12,16},{16,20},{20,24},{24,28},{28,32},{32,36}... | collective-permute-start | bytes 2359304 | tf_op jit(solution)/shard_map/ppermute | solution.py:267
  87.0 16.0 %collective-permute-start.8 = (f32[3,64,1024]{2,1,0:T(8,128)}, f32[3,64,1024]{2,1,0:T(8,128)S(1)}, u32[]{:S(2)}, u32[]{:S(2)}) collective-permute-start(f32[3,64,1024]{2,1,0:T(8,128)} %get-tuple-element.32), channel_id=1, source_target_pairs={{0,124},{4,0},{8,4},{12,8},{16,12},{20,16},{24,20},{28,24},{32,28}... | collective-permute-start | bytes 2359304 | tf_op jit(solution)/shard_map/ppermute | solution.py:267
  92.2 10.9 %copy-start.3 = (f32[8,8,1024]{2,1,0:T(8,128)}, f32[8,8,1024]{2,1,0:T(8,128)S(1)}, u32[]{:S(2)}) copy-start(f32[8,8,1024]{2,1,0:T(8,128)S(1)} %broadcast_select_fusion.sside) | copy-start | bytes 786436
  92.2 10.8 %collective-permute-start.11 = (f32[3,8,1024]{2,1,0:T(8,128)S(1)}, f32[3,8,1024]{2,1,0:T(8,128)S(1)}, u32[]{:S(2)}, u32[]{:S(2)}) collective-permute-start(f32[3,8,1024]{2,1,0:T(8,128)S(1)} %get-tuple-element.37), channel_id=1, source_target_pairs={{0,4},{4,8},{8,12},{12,16},{16,20},{20,24},{24,28},{28,32},{32,36}... | collective-permute-start | bytes 294920 | tf_op jit(solution)/shard_map/ppermute | solution.py:267
  92.3 10.7 %collective-permute-start.12 = (f32[3,8,1024]{2,1,0:T(8,128)S(1)}, f32[3,8,1024]{2,1,0:T(8,128)S(1)}, u32[]{:S(2)}, u32[]{:S(2)}) collective-permute-start(f32[3,8,1024]{2,1,0:T(8,128)S(1)} %get-tuple-element.36), channel_id=1, source_target_pairs={{0,124},{4,0},{8,4},{12,8},{16,12},{20,16},{24,20},{28,24},{32,28}... | collective-permute-start | bytes 294920 | tf_op jit(solution)/shard_map/ppermute | solution.py:267
  103.0 0.6 copy-start.10
  103.0 0.7 copy-start.11
  103.0 0.9 copy-start.7
  103.0 1.2 copy-start.8

commit v8 on v5

--- a/solution.py
+++ b/solution.py
@@ -46,11 +46,13 @@
     return pl.ds(pl.multiple_of(i * 8, 8), 8)
 
 
-def flux_kernel(cnt, row, heat_any, lane, vert, share, out, heat, diff, picked, sems):
+def flux_kernel(cnt, row, heat_any, lane, vert, share, out, heat, diff, picked, vals, sems):
     loads = [pltpu.make_async_copy(heat_any.at[t], heat.at[t], sems.at[t]) for t in range(T)]
     for c in loads:
         c.start()
 
+    picked[...] = jnp.zeros((128, 128), F32)
+    vals[...] = jnp.zeros((8, SLOTS), F32)
     for t in range(T):
         loads[t].wait()
 
@@ -63,20 +65,25 @@
 
         lax.fori_loop(0, R // 8, make, 0, unroll=4)
     for j in range(GROUPS):
+        blocks = (cnt[j] + 127) // 128
+
+        def pick(b, rows):
+            at = pl.ds(pl.multiple_of(jnp.maximum(b, 0) * 128, 128), 128)
+            hit = iota((128, 128), 0) == lane[j:j + 1, at]
+            vals[0:1, at] = jnp.sum(jnp.where(hit, rows.T, 0.0), axis=0, keepdims=True)
+
         def body(b, _):
-            base = pl.multiple_of(b * UNROLL, UNROLL)
-            for u in range(UNROLL):
-                picked[pl.ds(base + u, 1), :] = diff[pl.ds(row[j, base + u], 1), :]
+            rows = picked[...]
+            base = b * 128
+            for u in range(128):
+                picked[u:u + 1, :] = diff[pl.ds(row[j, base + u], 1), :]
+            pick(b - 1, rows)
             return 0
 
-        lax.fori_loop(0, (cnt[j] + UNROLL - 1) // UNROLL, body, 0)
-        vals = []
-        for kb in range(SLOTS // 128):
-            cut = slice(kb * 128, (kb + 1) * 128)
-            hit = iota((128, 128), 0) == lane[j:j + 1, cut]
-            vals.append(jnp.sum(jnp.where(hit, picked[cut, :].T, 0.0), axis=0, keepdims=True))
+        lax.fori_loop(0, blocks, body, 0)
+        pick(blocks - 1, picked[...])
         live = iota((1, SLOTS), 1) < cnt[j]
-        val = jnp.where(live, share[j:j + 1, :] * jnp.concatenate(vals, axis=1), 0.0)
+        val = jnp.where(live, share[j:j + 1, :] * vals[0:1, :], 0.0)
         v = vert[j:j + 1, :]
         inner = iota((BS, SLOTS), 0) == (v & (BS - 1))
         left = jnp.concatenate(
@@ -93,7 +100,7 @@
 
 
 def front_body(kref, cnt, row, parts, fronts, lane, vert, share, pred_any, src_any, sup, sdown, srup, srdown,
-               hout, front, gtab, height, terms, flux, pred, zeros, flip, sems, zsems, fsems, *acc):
+               hout, front, gtab, height, terms, flux, pred, zeros, flip, sems, zsems, fsems, osems, *acc):
     k = kref[0]
     load = pltpu.make_async_copy(pred_any, pred, sems.at[0])
     load.start()
@@ -177,11 +184,11 @@
     src = pred
     sends = []
 
-    def send(m, a, b):
-        sends.append(pltpu.make_async_copy(a, b, sems.at[m]))
+    def send(m, n, a, b):
+        sends.append(pltpu.make_async_copy(a, b, osems.at[m, n]))
         sends[-1].start()
 
-    for d in range(T):
+    for n, d in enumerate((0, 1, 2, 5, 6, 7, 3, 4)):
         def finish(q, _):
             for zc in range(8):
                 a = at8((d * 8 + q) * 8 + zc)
@@ -191,12 +198,13 @@
             return 0
 
         lax.fori_loop(0, R // 8, finish, 0, unroll=2)
-        if d == H - 2:
-            send(1, src.at[pl.ds(0, H - 1)], sdown)
-    send(2, src.at[pl.ds(T - H + 1, H - 1)], sup)
-    send(3, src.at[:, pl.ds(R - 8, 8)], srup)
-    send(4, src.at[:, pl.ds(0, 8)], srdown)
-    send(5, src, src_any)
+        if d < H - 1:
+            send(0, n, src.at[d], sdown.at[d])
+        if d >= T - H + 1:
+            send(0, n, src.at[d], sup.at[d - (T - H + 1)])
+        send(1, n, src.at[d, pl.ds(R - 8, 8)], srup.at[d])
+        send(2, n, src.at[d, pl.ds(0, 8)], srdown.at[d])
+        send(3, n, src.at[d], src_any.at[d])
     flip[...] = jnp.concatenate([height[k], jnp.zeros((128 - BS, 128), F32)], axis=0).T
     nodes = flip[pl.ds(0, BS, stride=8), :]
     for m in range(1, 8):
@@ -284,7 +292,7 @@
 
 
 def sweep_kernel(kref, load, beta_in, lo, hi, side, clo, chi, src, slo, shi, sside, sclo, schi,
-                 out, pa, pb, beta, th, rr, zz, ww, ss, rads, sems):
+                 out_any, pa, pb, beta, th, rr, zz, ww, ss, rads, out, sems, osems):
     k = kref[0]
     rows, ring = pl.ds(0, R), pl.ds(R, 8)
     half = T // 2
@@ -343,44 +351,44 @@
     def down_row(x):
         return pltpu.roll(x, 1, 0)
 
-    def next_lane(ref, t, it, v, cur):
-        nxt = pltpu.roll(vec(ref, t, it, v + 1), 127, 1) if v + 1 < Z // 128 else cur
+    def next_lane(row, v, cur):
+        nxt = pltpu.roll(row[v + 1], 127, 1) if v + 1 < Z // 128 else cur
         return jnp.where(last_lane, nxt, cur), nxt
 
-    def relaxed(old, t, it, v, p, pz, pu, prev, zprev, tu, td, r, z, w, s):
+    def relaxed(old, row, t, it, v, p, pz, pu, prev, zprev, tu, td, r, z, w, s):
         acc = (tu * vec(old, t + 1, it, v) + td * vec(old, t - 1, it, v)) + r * pu
         rp = down_row(r * p)
         acc = acc + jnp.where(bottom, prev, rp)
-        zu, pz = next_lane(old, t, it, v, pz)
+        zu, pz = next_lane(row, v, pz)
         zp = pltpu.roll(z * p, 1, 1)
         acc = acc + (z * zu + jnp.where(first_lane, zprev, zp))
         return (1.0 - OMEGA) * p + w * (acc - s), pz, rp, zp
 
     def first_sweep(t, _):
         last = RT - 1
-        bup = [up_row(vec(beta, t, 0, v)) for v in columns]
-        pup = [up_row(vec(pa, t, 0, v)) for v in columns]
+        bc = [vec(beta, t, 0, v) for v in columns]
+        pc = [vec(pa, t, 0, v) for v in columns]
         fprev, prev = [], []
         for v in columns:
             b = vec(beta, t, last, v)
-            face = (b + jnp.where(top, bup[v], up_row(b))) * rads[2, last]
+            face = (b + jnp.where(top, up_row(bc[v]), up_row(b))) * rads[2, last]
             fprev.append(down_row(face))
             prev.append(down_row(face * vec(pa, t, last, v)))
         for it in range(RT):
             ra, ang, rad = rads[0, it], rads[1, it], rads[2, it]
             axi = (0.5 * AXIAL) * ra
-            bz = pltpu.roll(vec(beta, t, it, 0), 127, 1)
-            pz = pltpu.roll(vec(pa, t, it, 0), 127, 1)
+            bz = pltpu.roll(bc[0], 127, 1)
+            pz = pltpu.roll(pc[0], 127, 1)
             zfprev = zprev = nothing
             for v in columns:
-                b, p = vec(beta, t, it, v), vec(pa, t, it, v)
-                nb, np_ = up_row(vec(beta, t, it + 1, v)), up_row(vec(pa, t, it + 1, v))
+                b, p = bc[v], pc[v]
+                nb, np_ = vec(beta, t, it + 1, v), vec(pa, t, it + 1, v)
                 tu = (b + vec(beta, t + 1, it, v)) * ang
                 td = vec(th, t - 1, it, v)
-                r = (b + jnp.where(top, nb, bup[v])) * rad
+                r = (b + jnp.where(top, up_row(nb), up_row(b))) * rad
                 froll = down_row(r)
                 other = jnp.where(bottom, fprev[v], froll)
-                bu, bz = next_lane(beta, t, it, v, bz)
+                bu, bz = next_lane(bc, v, bz)
                 zf = (b + bu) * axi
                 z = zf
                 if v == Z // 128 - 1:
@@ -399,27 +407,29 @@
                 put(zz, t, it, v, z)
                 put(ww, t, it, v, w)
                 put(ss, t, it, v, sc)
-                pu = jnp.where(top, np_, pup[v])
-                new, pz, prev[v], zprev = relaxed(pa, t, it, v, p, pz, pu, prev[v], zprev, tu, td, r, z, w, sc)
+                pu = jnp.where(top, up_row(np_), up_row(p))
+                new, pz, prev[v], zprev = relaxed(pa, pc, t, it, v, p, pz, pu, prev[v], zprev, tu, td, r, z, w, sc)
                 put(pb, t, it, v, new)
-                bup[v], pup[v], fprev[v], zfprev = nb, np_, froll, zr
+                bc[v], pc[v], fprev[v], zfprev = nb, np_, froll, zr
         return 0
 
     def sweep(old, new, t, tiles, shift):
-        pup = [up_row(vec(old, t, 0, v)) for v in columns]
+        pc = [vec(old, t, 0, v) for v in columns]
+        pup = [up_row(p) for p in pc]
         prev = [down_row(vec(rr, t, -1, v) * vec(old, t, -1, v)) for v in columns]
         for it in range(tiles):
-            pz = pltpu.roll(vec(old, t, it, 0), 127, 1)
+            pz = pltpu.roll(pc[0], 127, 1)
             zprev = nothing
             for v in columns:
-                p = vec(old, t, it, v)
-                np_ = up_row(vec(old, t, it + 1, v))
-                pu = jnp.where(top, np_, pup[v])
+                p = pc[v]
+                np_ = vec(old, t, it + 1, v)
+                nup = up_row(np_)
+                pu = jnp.where(top, nup, pup[v])
                 x, pz, prev[v], zprev = relaxed(
-                    old, t, it, v, p, pz, pu, prev[v], zprev, vec(th, t, it, v), vec(th, t - 1, it, v),
+                    old, pc, t, it, v, p, pz, pu, prev[v], zprev, vec(th, t, it, v), vec(th, t - 1, it, v),
                     vec(rr, t, it, v), vec(zz, t, it, v), vec(ww, t, it, v), vec(ss, t, it, v))
                 put(new, t - shift, it, v, x)
-                pup[v] = np_
+                pc[v], pup[v] = np_, nup
         return 0
 
     ends = (H - 1, H + half - 1, H + T - 1, TE - 1)
@@ -435,7 +445,15 @@
         start = ends[g]
     lax.fori_loop(2, TE - 2, lambda t, _: sweep(pb, pa, t, RT, 0), 0)
     lax.fori_loop(3, TE - 3, lambda t, _: sweep(pa, pb, t, RT, 0), 0)
-    lax.fori_loop(4, TE - 4, lambda t, _: sweep(pb, out, t, RT - 1, H), 0)
+
+    def final(t, _):
+        sweep(pb, out, t, RT - 1, H)
+        pltpu.make_async_copy(out.at[t - H], out_any.at[t - H], osems.at[t - H]).start()
+        return 0
+
+    lax.fori_loop(4, TE - 4, final, 0)
+    for t in range(T):
+        pltpu.make_async_copy(out.at[t], out_any.at[t], osems.at[t]).wait()
 
 
 def from_all(copies, axes):
@@ -492,7 +510,8 @@
     partial = pl.pallas_call(
         flux_kernel, out_shape=shape(8, GROUPS * BS, NB),
         in_specs=[SM, SM, ANY, VM, VM, VM], out_specs=VM,
-        scratch_shapes=[block, pltpu.VMEM((T * R * 8, 128), F32), pltpu.VMEM((SLOTS, 128), F32),
+        scratch_shapes=[block, pltpu.VMEM((T * R * 8, 128), F32), pltpu.VMEM((128, 128), F32),
+                        pltpu.VMEM((8, SLOTS), F32),
                         pltpu.SemaphoreType.DMA((T,))],
         compiler_params=params(12), cost_estimate=cost(10), name="flux",
     )(tally, row, heat, lane, vertex, share)
@@ -516,8 +535,8 @@
                         pltpu.VMEM((GROUPS, BS, NB), F32), pltpu.VMEM((GROUPS, BS, NB), F32),
                         pltpu.VMEM((GROUPS, SLOTS, 128), F32), pltpu.VMEM((GROUPS * BS, NB), F32),
                         block, pltpu.VMEM((R * 8, 128), F32), pltpu.VMEM((128, 128), F32),
-                        pltpu.SemaphoreType.DMA((6,)), pltpu.SemaphoreType.DMA((GROUPS, T)),
-                        pltpu.SemaphoreType.DMA((GROUPS,))]
+                        pltpu.SemaphoreType.DMA((1,)), pltpu.SemaphoreType.DMA((GROUPS, T)),
+                        pltpu.SemaphoreType.DMA((GROUPS,)), pltpu.SemaphoreType.DMA((4, T))]
         + [pltpu.VMEM((T * R * 8, 128), F32)] * GROUPS,
         compiler_params=params(20), cost_estimate=cost(10), name="front",
     )(kidx, tally, row, flux, front, rhi, rlo, across, lane, vertex, share, outflow, lo, hi, side, clo, chi)
@@ -527,8 +546,9 @@
     ext = pltpu.VMEM((TE, RE, Z), F32)
     pressure = pl.pallas_call(
         sweep_kernel, out_shape=plane(T),
-        in_specs=[SM] + [ANY] * 13, out_specs=VM,
-        scratch_shapes=[ext] * 8 + [pltpu.VMEM((3, RT, 8, 128), F32), pltpu.SemaphoreType.DMA((4, 3, 2))],
+        in_specs=[SM] + [ANY] * 13, out_specs=ANY,
+        scratch_shapes=[ext] * 8 + [pltpu.VMEM((3, RT, 8, 128), F32), block, pltpu.SemaphoreType.DMA((4, 3, 2)),
+                        pltpu.SemaphoreType.DMA((T,))],
         compiler_params=params(46), cost_estimate=cost(20), name="sweeps",
     )(kidx, load, beta, lo, hi, side, clo, chi, source, slo, shi, sside, sclo, schi)
     return pressure, height.reshape(NB * BS)

time: 121 us -> 121 us (level)
  Pallas kernels: 51.8 us -> 50.1 us
  transfers between devices with their start and end apart: 15 -> 15, of which waited for: 4 -> 4; matrix products, arithmetic and copies ran while one was open for 0% -> 0% of each run, Pallas kernels for 11% -> 10%
where the time goes in v8:
time: 121 us; the launch traced here: 120 us
  Pallas kernels  50.1 us (41%)
  starting transfers between devices  42.8 us (35%)
  waiting for transfers between devices  22 us (18%)
  local copies, waits for them, and re-layouts  3.95 us (3%)
    pallas_call x1, Pallas kernels, per_device(): pl.pallas_call(sweep_kernel, out_shape=plane(T), in_specs=[SM] + [ANY] *...  22.3 us
    ppermute x8, starting transfers between devices, shift_azim(): return lax.ppermute(x, AZIM, [(i, (i + d) % 32) for i in range(32)])  21.4 us
    ppermute x8, waiting for transfers between devices, shift_azim(): return lax.ppermute(x, AZIM, [(i, (i + d) % 32) for i in range(32)])  14.9 us
    all_to_all x2, starting transfers between devices, from_all(): return lax.all_to_all(copies, axes, 0, 0)  10.4 us
    pallas_call x1, Pallas kernels, per_device(): pl.pallas_call(front_kernel, out_shape=(plane(T), plane(H - 1), plane(H -...  9.6 us
    pallas_call x1, Pallas kernels, per_device(): pl.pallas_call(flux_kernel, out_shape=shape(8, GROUPS * BS, NB), in_specs...  8.39 us
    ppermute x2, starting transfers between devices, shift_rad(): lax.ppermute(x, 'rad', [(i, i + d) for i in range(4) if 0 <= i + d < 4])  6.75 us
    pallas_call x1, Pallas kernels, per_device(): pl.pallas_call(pack_kernel, out_shape=(plane(2 * H), plane(2 * H), tile(2...  5.78 us
  transfers between devices with their start and end apart: 15, of which 4 were waited for; matrix products, arithmetic and copies ran while one was open for 0% of the time, Pallas kernels for 10%

profile of v8, /device:TPU:2, one launch (start us, length us, event | category | flops | bytes accessed | tf_op | source)
XLA Modules:
  0.0 120.0 jit_solution(4497349975142504868)
XLA Ops:
  0.6 5.8 %pack.1 = (f32[8,64,1024]{2,1,0:T(8,128)}, f32[8,64,1024]{2,1,0:T(8,128)}, f32[21,8,1024]{2,1,0:T(8,128)}, f32[21,8,1024]{2,1,0:T(8,128)}, f32[5,8,1024]{2,1,0:T...) custom-call(f32[8,64,1024]{2,1,0:T(8,128)} %load.1, f32[8,64,1024]{2,1,0:T(8,128)} %beta_in.1, f32[256,128]{1,0:T(8,128)} %bitcast.10, ...), custom_call_target="tpu_custom_call" | custom-call | flops 1000 | bytes 12000000 | tf_op jit(solution)/shard_map/pack/pallas_call | solution.py:498
  6.4 0.0 copy-start.10
  6.4 0.1 collective-permute-start
  6.5 6.0 %collective-permute-start.1 = (f32[8,64,1024]{2,1,0:T(8,128)}, f32[8,64,1024]{2,1,0:T(8,128)}, u32[]{:S(2)}, u32[]{:S(2)}) collective-permute-start(f32[8,64,1024]{2,1,0:T(8,128)} %get-tuple-element.19), channel_id=1, source_target_pairs={{0,124},{4,0},{8,4},{12,8},{16,12},{20,16},{24,20},{28,24},{32,28}... | collective-permute-start | bytes 6291464 | tf_op jit(solution)/shard_map/ppermute | solution.py:279
  12.5 0.5 collective-permute-start.2
  13.0 1.5 %collective-permute-start.3 = (f32[21,8,1024]{2,1,0:T(8,128)}, f32[21,8,1024]{2,1,0:T(8,128)S(1)}, u32[]{:S(2)}, u32[]{:S(2)}) collective-permute-start(f32[21,8,1024]{2,1,0:T(8,128)} %get-tuple-element.21), channel_id=1, source_target_pairs={{0,1},{1,2},{2,3},{3,0},{4,5},{5,6},{6,7},{7,4},{8,9},{9,10},{10,1... | collective-permute-start | bytes 2064392 | tf_op jit(solution)/shard_map/ppermute | solution.py:507
  14.5 8.4 %flux.1 = f32[8,64,128]{2,1,0:T(8,128)} custom-call(s32[4]{0:T(128)} %bitcast.19, s32[4,1024]{1,0:T(4,128)} %get-tuple-element.25.row, f32[8,64,1024]{2,1,0:T(8,128)} %heat_any.1, s32[4,1024]{1,0:T(4,128)} %get-tuple-element.26.lane, s32[4,1024]{1,0:T(4,128)} %bitcast.11, f32[4,1024]{1,0:T(4,128)} %bitcast.13), custom_call_target="tpu_custom_call" | custom-call | flops 1000 | bytes 30000000 | tf_op jit(solution)/shard_map/flux/pallas_call | solution.py:510
  22.9 3.4 %all-to-all-start = ((f32[8,64,128]{2,1,0:T(8,128)}), f32[8,64,128]{2,1,0:T(8,128)S(1)}, u32[]{:S(2)}, u32[]{:S(2)}) async-start(f32[8,64,128]{2,1,0:T(8,128)} %flux.1), calls=%async_computation | async-start | bytes 524288 | tf_op jit(solution)/shard_map/all_to_all | solution.py:460
  26.4 0.0 copy-done.10
  26.4 2.3 %collective-permute-start.6 = (f32[5,8,1024]{2,1,0:T(8,128)S(1)}, f32[5,8,1024]{2,1,0:T(8,128)S(1)}, u32[]{:S(2)}, u32[]{:S(2)}) collective-permute-start(f32[5,8,1024]{2,1,0:T(8,128)S(1)} %copy-done.10), channel_id=1, source_target_pairs={{0,2},{1,3},{2,0},{3,1},{4,6},{5,7},{6,4},{7,5},{8,10},{9,11},{10,... | collective-permute-start | bytes 491528 | tf_op jit(solution)/shard_map/ppermute | solution.py:507
  28.7 0.0 collective-permute-done.2.above.f1
  28.7 0.0 copy-start
  28.7 0.0 collective-permute-done.3.below_any.f2
  28.7 0.0 copy-start.1
  28.7 0.9 copy-done
  29.5 0.3 copy-done.1
  29.8 2.3 %side.1 = (f32[16,8,1024]{2,1,0:T(8,128)}, f32[8,8,1024]{2,1,0:T(8,128)}, f32[8,8,1024]{2,1,0:T(8,128)}) custom-call(s32[1]{0:T(128)} %bitcast.kref, f32[21,8,1024]{2,1,0:T(8,128)} %copy-done, f32[21,8,1024]{2,1,0:T(8,128)} %copy-done.1), custom_call_target="tpu_custom_call" | custom-call | flops 1000 | bytes 6000000 | tf_op jit(solution)/shard_map/side/pallas_call | solution.py:518
  32.1 0.0 copy-start.13
  32.1 2.2 %collective-permute-done.6.refs_1_.f3 = f32[5,8,1024]{2,1,0:T(8,128)S(1)} collective-permute-done((f32[5,8,1024]{2,1,0:T(8,128)S(1)}, f32[5,8,1024]{2,1,0:T(8,128)S(1)}, u32[]{:S(2)}, u32[]{:S(2)}) %collective-permute-start.6) | collective-permute-done | bytes 163872 | tf_op jit(solution)/shard_map/ppermute | solution.py:507
  34.4 0.0 copy-start.9
  34.4 4.8 %all-to-all-done.parts = f32[8,64,128]{2,1,0:T(8,128)S(1)} async-done(((f32[8,64,128]{2,1,0:T(8,128)}), f32[8,64,128]{2,1,0:T(8,128)S(1)}, u32[]{:S(2)}, u32[]{:S(2)}) %all-to-all-start) | async-done | bytes 262176 | tf_op jit(solution)/shard_map/all_to_all | solution.py:460
  39.2 0.0 copy-start.6
  39.2 0.0 copy-done.9
  39.2 0.7 copy-done.6
  39.9 1.8 %near.1 = f32[16,64,128]{2,1,0:T(8,128)} custom-call(f32[8,64,128]{2,1,0:T(8,128)} %copy-done.6, f32[16,8,1024]{2,1,0:T(8,128)} %get-tuple-element.22.refs_0_.refs_2_.side, f32[5,8,1024]{2,1,0:T(8,128)} %copy-done.9), custom_call_target="tpu_custom_call" | custom-call | tf_op jit(solution)/shard_map/near/pallas_call | solution.py:525
  41.7 7.0 %all-to-all-start.1 = ((f32[16,64,128]{2,1,0:T(8,128)}), f32[16,64,128]{2,1,0:T(8,128)S(1)}, u32[]{:S(2)}, u32[]{:S(2)}) async-start(f32[16,64,128]{2,1,0:T(8,128)} %near.1), calls=%async_computation.1 | async-start | bytes 1048576 | tf_op jit(solution)/shard_map/all_to_all | solution.py:460
  48.6 0.0 collective-permute-start.4
  48.7 0.0 copy-done.13
  48.7 5.1 %collective-permute-start.5 = (f32[8,8,1024]{2,1,0:T(8,128)S(1)}, f32[8,8,1024]{2,1,0:T(8,128)S(1)}, u32[]{:S(2)}, u32[]{:S(2)}) collective-permute-start(f32[8,8,1024]{2,1,0:T(8,128)S(1)} %copy-done.13), channel_id=1, source_target_pairs={{0,124},{4,0},{8,4},{12,8},{16,12},{20,16},{24,20},{28,24},{32,28}... | collective-permute-start | bytes 786440 | tf_op jit(solution)/shard_map/ppermute | solution.py:279
  53.7 9.3 %collective-permute-done.4.refs_3_.clo = f32[8,8,1024]{2,1,0:T(8,128)S(1)} collective-permute-done((f32[8,8,1024]{2,1,0:T(8,128)}, f32[8,8,1024]{2,1,0:T(8,128)S(1)}, u32[]{:S(2)}, u32[]{:S(2)}) %collective-permute-start.4) | collective-permute-done | bytes 262176 | tf_op jit(solution)/shard_map/ppermute | solution.py:279
  63.0 0.0 copy-start.4
  63.0 0.0 collective-permute-done.5.refs_4_.chi
  63.0 0.0 copy-start.5
  63.0 0.0 all-to-all-done.1.parts
  63.0 0.0 copy-start.2
  63.0 0.0 collective-permute-done.refs_0_.lo
  63.0 0.0 collective-permute-done.1.refs_1_.hi
  63.0 0.6 copy-done.4
  63.7 0.1 copy-done.5
  63.8 0.2 copy-done.2
  63.9 9.6 %front.1 = (f32[8,64,1024]{2,1,0:T(8,128)}, f32[3,64,1024]{2,1,0:T(8,128)}, f32[3,64,1024]{2,1,0:T(8,128)}, f32[8,8,1024]{2,1,0:T(8,128)}, f32[8,8,1024]{2,1,0:T(8,128)}, /*index=5*/f32[16,128]{1,0:T(8,128)}) custom-call(s32[1]{0:T(128)} %bitcast.kref, s32[4]{0:T(128)} %bitcast.20, s32[4,1024]{1,0:T(4,128)} %get-tuple-element.25.row, ...), custom_call_target="tpu_custom_call" | custom-call | flops 1000 | bytes 30000000 | tf_op jit(solution)/shard_map/front/pallas_call | solution.py:530
  73.6 3.1 %collective-permute-start.10 = (f32[8,8,1024]{2,1,0:T(8,128)}, f32[8,8,1024]{2,1,0:T(8,128)S(1)}, u32[]{:S(2)}, u32[]{:S(2)}) collective-permute-start(f32[8,8,1024]{2,1,0:T(8,128)} %get-tuple-element.32), channel_id=1, source_target_pairs={{0,1},{1,2},{2,3},{4,5},{5,6},{6,7},{8,9},{9,10},{10,11},{12,13},{... | collective-permute-start | bytes 786440 | tf_op jit(solution)/shard_map/ppermute | solution.py:283
  76.6 3.7 %collective-permute-start.9 = (f32[8,8,1024]{2,1,0:T(8,128)}, f32[8,8,1024]{2,1,0:T(8,128)S(1)}, u32[]{:S(2)}, u32[]{:S(2)}) collective-permute-start(f32[8,8,1024]{2,1,0:T(8,128)} %get-tuple-element.31), channel_id=1, source_target_pairs={{1,0},{2,1},{3,2},{5,4},{6,5},{7,6},{9,8},{10,9},{11,10},{13,12},{... | collective-permute-start | bytes 786440 | tf_op jit(solution)/shard_map/ppermute | solution.py:283
  80.3 0.1 collective-permute-start.7
  80.4 5.1 %collective-permute-start.8 = (f32[3,64,1024]{2,1,0:T(8,128)}, f32[3,64,1024]{2,1,0:T(8,128)S(1)}, u32[]{:S(2)}, u32[]{:S(2)}) collective-permute-start(f32[3,64,1024]{2,1,0:T(8,128)} %get-tuple-element.30), channel_id=1, source_target_pairs={{0,124},{4,0},{8,4},{12,8},{16,12},{20,16},{24,20},{28,24},{32,28}... | collective-permute-start | bytes 2359304 | tf_op jit(solution)/shard_map/ppermute | solution.py:279
  85.5 0.0 collective-permute-done.10
  85.5 0.0 collective-permute-done.9
  85.5 0.1 broadcast_select_fusion.sside
  85.6 0.0 copy-start.3
  85.6 0.1 collective-permute-start.11
  85.7 5.1 %collective-permute-start.12 = (f32[3,8,1024]{2,1,0:T(8,128)S(1)}, f32[3,8,1024]{2,1,0:T(8,128)S(1)}, u32[]{:S(2)}, u32[]{:S(2)}) collective-permute-start(f32[3,8,1024]{2,1,0:T(8,128)S(1)} %get-tuple-element.34), channel_id=1, source_target_pairs={{0,124},{4,0},{8,4},{12,8},{16,12},{20,16},{24,20},{28,24},{32,28}... | collective-permute-start | bytes 294920 | tf_op jit(solution)/shard_map/ppermute | solution.py:279
  90.7 5.7 %collective-permute-done.11.sclo = f32[3,8,1024]{2,1,0:T(8,128)S(1)} collective-permute-done((f32[3,8,1024]{2,1,0:T(8,128)S(1)}, f32[3,8,1024]{2,1,0:T(8,128)S(1)}, u32[]{:S(2)}, u32[]{:S(2)}) %collective-permute-start.11) | collective-permute-done | bytes 98336 | tf_op jit(solution)/shard_map/ppermute | solution.py:279
  96.4 0.0 copy-start.11
  96.4 0.0 collective-permute-done.12.schi
  96.4 0.0 collective-permute-done.7.slo
  96.4 0.0 copy-start.7
  96.4 0.0 collective-permute-done.8.shi
  96.4 0.0 copy-start.8
  96.4 0.0 copy-done.3
  96.4 0.6 copy-done.11
  97.0 0.0 copy-done.12
  97.1 0.3 copy-done.7
  97.4 0.2 copy-done.8
  97.6 22.3 %sweeps.1 = f32[8,64,1024]{2,1,0:T(8,128)} custom-call(s32[1]{0:T(128)} %bitcast.kref, f32[8,64,1024]{2,1,0:T(8,128)} %load.1, f32[8,64,1024]{2,1,0:T(8,128)} %beta_in.1, f32[8,64,1024]{2,1,0:T(8,128)} %collective-permute-done.refs_0_.lo, f32[8,64,1024]{2,1,0:T(8,128)} %collective-permute-done.1.refs_1_.hi, ...), custom_call_target="tpu_custom_call" | custom-call | flops 1000 | bytes 60000000 | tf_op jit(solution)/shard_map/sweeps/pallas_call | solution.py:547
  (3 shorter events, 0.0 us)
Async XLA Ops:
  6.4 19.9 %copy-start.10 = (f32[5,8,1024]{2,1,0:T(8,128)S(1)}, f32[5,8,1024]{2,1,0:T(8,128)}, u32[]{:S(2)}) copy-start(f32[5,8,1024]{2,1,0:T(8,128)} %get-tuple-element.27.f0) | copy-start | bytes 491524
  6.4 56.6 %collective-permute-start = (f32[8,64,1024]{2,1,0:T(8,128)}, f32[8,64,1024]{2,1,0:T(8,128)}, u32[]{:S(2)}, u32[]{:S(2)}) collective-permute-start(f32[8,64,1024]{2,1,0:T(8,128)} %get-tuple-element.18), channel_id=1, source_target_pairs={{0,4},{4,8},{8,12},{12,16},{16,20},{20,24},{24,28},{28,32},{32,36}... | collective-permute-start | bytes 6291464 | tf_op jit(solution)/shard_map/ppermute | solution.py:279
  6.5 56.5 %collective-permute-start.1 = (f32[8,64,1024]{2,1,0:T(8,128)}, f32[8,64,1024]{2,1,0:T(8,128)}, u32[]{:S(2)}, u32[]{:S(2)}) collective-permute-start(f32[8,64,1024]{2,1,0:T(8,128)} %get-tuple-element.19), channel_id=1, source_target_pairs={{0,124},{4,0},{8,4},{12,8},{16,12},{20,16},{24,20},{28,24},{32,28}... | collective-permute-start | bytes 6291464 | tf_op jit(solution)/shard_map/ppermute | solution.py:279
  12.5 16.2 %collective-permute-start.2 = (f32[21,8,1024]{2,1,0:T(8,128)}, f32[21,8,1024]{2,1,0:T(8,128)S(1)}, u32[]{:S(2)}, u32[]{:S(2)}) collective-permute-start(f32[21,8,1024]{2,1,0:T(8,128)} %get-tuple-element.20), channel_id=1, source_target_pairs={{0,3},{1,0},{2,1},{3,2},{4,7},{5,4},{6,5},{7,6},{8,11},{9,8},{10,9... | collective-permute-start | bytes 2064392 | tf_op jit(solution)/shard_map/ppermute | solution.py:507
  13.0 15.6 %collective-permute-start.3 = (f32[21,8,1024]{2,1,0:T(8,128)}, f32[21,8,1024]{2,1,0:T(8,128)S(1)}, u32[]{:S(2)}, u32[]{:S(2)}) collective-permute-start(f32[21,8,1024]{2,1,0:T(8,128)} %get-tuple-element.21), channel_id=1, source_target_pairs={{0,1},{1,2},{2,3},{3,0},{4,5},{5,6},{6,7},{7,4},{8,9},{9,10},{10,1... | collective-permute-start | bytes 2064392 | tf_op jit(solution)/shard_map/ppermute | solution.py:507
  22.9 16.2 %all-to-all-start = ((f32[8,64,128]{2,1,0:T(8,128)}), f32[8,64,128]{2,1,0:T(8,128)S(1)}, u32[]{:S(2)}, u32[]{:S(2)}) async-start(f32[8,64,128]{2,1,0:T(8,128)} %flux.1), calls=%async_computation | async-start | bytes 524288 | tf_op jit(solution)/shard_map/all_to_all | solution.py:460
  26.4 8.0 %collective-permute-start.6 = (f32[5,8,1024]{2,1,0:T(8,128)S(1)}, f32[5,8,1024]{2,1,0:T(8,128)S(1)}, u32[]{:S(2)}, u32[]{:S(2)}) collective-permute-start(f32[5,8,1024]{2,1,0:T(8,128)S(1)} %copy-done.10), channel_id=1, source_target_pairs={{0,2},{1,3},{2,0},{3,1},{4,6},{5,7},{6,4},{7,5},{8,10},{9,11},{10,... | collective-permute-start | bytes 491528 | tf_op jit(solution)/shard_map/ppermute | solution.py:507
  28.7 0.9 copy-start
  28.7 1.2 copy-start.1
  32.1 16.5 %copy-start.13 = (f32[8,8,1024]{2,1,0:T(8,128)S(1)}, f32[8,8,1024]{2,1,0:T(8,128)}, u32[]{:S(2)}) copy-start(f32[8,8,1024]{2,1,0:T(8,128)} %get-tuple-element.24) | copy-start | bytes 786436
  34.4 4.8 %copy-start.9 = (f32[5,8,1024]{2,1,0:T(8,128)}, f32[5,8,1024]{2,1,0:T(8,128)S(1)}, u32[]{:S(2)}) copy-start(f32[5,8,1024]{2,1,0:T(8,128)S(1)} %collective-permute-done.6.refs_1_.f3) | copy-start | bytes 491524
  39.2 0.7 copy-start.6
  41.7 21.3 %all-to-all-start.1 = ((f32[16,64,128]{2,1,0:T(8,128)}), f32[16,64,128]{2,1,0:T(8,128)S(1)}, u32[]{:S(2)}, u32[]{:S(2)}) async-start(f32[16,64,128]{2,1,0:T(8,128)} %near.1), calls=%async_computation.1 | async-start | bytes 1048576 | tf_op jit(solution)/shard_map/all_to_all | solution.py:460
  48.6 14.3 %collective-permute-start.4 = (f32[8,8,1024]{2,1,0:T(8,128)}, f32[8,8,1024]{2,1,0:T(8,128)S(1)}, u32[]{:S(2)}, u32[]{:S(2)}) collective-permute-start(f32[8,8,1024]{2,1,0:T(8,128)} %get-tuple-element.23), channel_id=1, source_target_pairs={{0,4},{4,8},{8,12},{12,16},{16,20},{20,24},{24,28},{28,32},{32,36}... | collective-permute-start | bytes 786440 | tf_op jit(solution)/shard_map/ppermute | solution.py:279
  48.7 14.3 %collective-permute-start.5 = (f32[8,8,1024]{2,1,0:T(8,128)S(1)}, f32[8,8,1024]{2,1,0:T(8,128)S(1)}, u32[]{:S(2)}, u32[]{:S(2)}) collective-permute-start(f32[8,8,1024]{2,1,0:T(8,128)S(1)} %copy-done.13), channel_id=1, source_target_pairs={{0,124},{4,0},{8,4},{12,8},{16,12},{20,16},{24,20},{28,24},{32,28}... | collective-permute-start | bytes 786440 | tf_op jit(solution)/shard_map/ppermute | solution.py:279
  63.0 0.7 copy-start.4
  63.0 0.8 copy-start.5
  63.0 0.9 copy-start.2
  73.6 11.9 %collective-permute-start.10 = (f32[8,8,1024]{2,1,0:T(8,128)}, f32[8,8,1024]{2,1,0:T(8,128)S(1)}, u32[]{:S(2)}, u32[]{:S(2)}) collective-permute-start(f32[8,8,1024]{2,1,0:T(8,128)} %get-tuple-element.32), channel_id=1, source_target_pairs={{0,1},{1,2},{2,3},{4,5},{5,6},{6,7},{8,9},{9,10},{10,11},{12,13},{... | collective-permute-start | bytes 786440 | tf_op jit(solution)/shard_map/ppermute | solution.py:283
  76.6 8.8 %collective-permute-start.9 = (f32[8,8,1024]{2,1,0:T(8,128)}, f32[8,8,1024]{2,1,0:T(8,128)S(1)}, u32[]{:S(2)}, u32[]{:S(2)}) collective-permute-start(f32[8,8,1024]{2,1,0:T(8,128)} %get-tuple-element.31), channel_id=1, source_target_pairs={{1,0},{2,1},{3,2},{5,4},{6,5},{7,6},{9,8},{10,9},{11,10},{13,12},{... | collective-permute-start | bytes 786440 | tf_op jit(solution)/shard_map/ppermute | solution.py:283
  80.3 16.1 %collective-permute-start.7 = (f32[3,64,1024]{2,1,0:T(8,128)}, f32[3,64,1024]{2,1,0:T(8,128)S(1)}, u32[]{:S(2)}, u32[]{:S(2)}) collective-permute-start(f32[3,64,1024]{2,1,0:T(8,128)} %get-tuple-element.29), channel_id=1, source_target_pairs={{0,4},{4,8},{8,12},{12,16},{16,20},{20,24},{24,28},{28,32},{32,36}... | collective-permute-start | bytes 2359304 | tf_op jit(solution)/shard_map/ppermute | solution.py:279
  80.4 16.0 %collective-permute-start.8 = (f32[3,64,1024]{2,1,0:T(8,128)}, f32[3,64,1024]{2,1,0:T(8,128)S(1)}, u32[]{:S(2)}, u32[]{:S(2)}) collective-permute-start(f32[3,64,1024]{2,1,0:T(8,128)} %get-tuple-element.30), channel_id=1, source_target_pairs={{0,124},{4,0},{8,4},{12,8},{16,12},{20,16},{24,20},{28,24},{32,28}... | collective-permute-start | bytes 2359304 | tf_op jit(solution)/shard_map/ppermute | solution.py:279
  85.6 10.9 %copy-start.3 = (f32[8,8,1024]{2,1,0:T(8,128)}, f32[8,8,1024]{2,1,0:T(8,128)S(1)}, u32[]{:S(2)}) copy-start(f32[8,8,1024]{2,1,0:T(8,128)S(1)} %broadcast_select_fusion.sside) | copy-start | bytes 786436
  85.6 10.8 %collective-permute-start.11 = (f32[3,8,1024]{2,1,0:T(8,128)S(1)}, f32[3,8,1024]{2,1,0:T(8,128)S(1)}, u32[]{:S(2)}, u32[]{:S(2)}) collective-permute-start(f32[3,8,1024]{2,1,0:T(8,128)S(1)} %get-tuple-element.35), channel_id=1, source_target_pairs={{0,4},{4,8},{8,12},{12,16},{16,20},{20,24},{24,28},{28,32},{32,36}... | collective-permute-start | bytes 294920 | tf_op jit(solution)/shard_map/ppermute | solution.py:279
  85.7 10.7 %collective-permute-start.12 = (f32[3,8,1024]{2,1,0:T(8,128)S(1)}, f32[3,8,1024]{2,1,0:T(8,128)S(1)}, u32[]{:S(2)}, u32[]{:S(2)}) collective-permute-start(f32[3,8,1024]{2,1,0:T(8,128)S(1)} %get-tuple-element.34), channel_id=1, source_target_pairs={{0,124},{4,0},{8,4},{12,8},{16,12},{20,16},{24,20},{28,24},{32,28}... | collective-permute-start | bytes 294920 | tf_op jit(solution)/shard_map/ppermute | solution.py:279
  96.4 0.6 copy-start.11
  96.4 0.7 copy-start.12
  96.4 1.0 copy-start.7
  96.4 1.2 copy-start.8
